TPU v7x, 128 devices: a whole 4x4x4 slice. The times are simulated.
128 devices in a mesh: seq: 8 (over z, core), shard: 16 (over x, y).
Axes of the slice: x: 4, y: 4, z: 4, core: 2. Of those that a mesh axis runs over, the one named last changes fastest.
Arguments:
- block_input: bfloat16 [16, 1024, 1536], P('shard', 'seq'), may hold values from -6 to 6
- lengths: int32 [16], P('shard'), may hold values from 256 to 1024, as said below
- routes: int32 [16, 1024, 6], P('shard', 'seq'), may hold values from 0 to 31, all different within a row; in each aligned block of 128 rows (0 to 127, 128 to 255, ..., all dimensions but the last counted through in order) at most 32 rows name the same one
- out_cotangent: bfloat16 [16, 1024, 1536], P('shard', 'seq'), may hold values from -6 to 6
- mixer_gain: bfloat16 [1536], P('shard'), may hold values from 0.5 to 1.5
- in_weight: bfloat16 [1536, 6448], P('shard'), may hold values from -0.15625 to 0.15625
- conv_weight: bfloat16 [4, 3328], P(None, 'shard'), may hold values from -3 to 3
- conv_bias: bfloat16 [3328], P('shard'), may hold values from -3 to 3
- step_bias: bfloat16 [48], P('shard'), may hold values from -5 to -1
- decay_log: bfloat16 [48], P('shard'), may hold values from 0 to 2.5
- skip_gain: bfloat16 [48], P('shard'), may hold values from 0.5 to 1.5
- norm_gain: bfloat16 [3072], P('shard'), may hold values from 0.5 to 1.5
- out_weight: bfloat16 [3072, 1536], P('shard'), may hold values from -0.109375 to 0.109375
- moe_gain: bfloat16 [1536], P('shard'), may hold values from 0.5 to 1.5
- router_weight: bfloat16 [1536, 32], P('shard'), may hold values from -0.078125 to 0.078125
- shared_gate: bfloat16 [1536, 1024], P('shard'), may hold values from -0.15625 to 0.15625
- shared_up: bfloat16 [1536, 1024], P('shard'), may hold values from -0.15625 to 0.15625
- shared_down: bfloat16 [1024, 1536], P('shard'), may hold values from -0.375 to 0.375
- expert_gate: bfloat16 [32, 1536, 512], P('shard'), may hold values from -0.15625 to 0.15625
- expert_up: bfloat16 [32, 1536, 512], P('shard'), may hold values from -0.15625 to 0.15625
- expert_down: bfloat16 [32, 512, 1536], P('shard'), may hold values from -1 to 1
Outputs:
- block_output: bfloat16 [16, 1024, 1536], P('shard', 'seq')
- input_grad: float32 [16, 1024, 1536], P('shard', 'seq')
- grad_mixer_gain: float32 [1536], P('shard')
- grad_in_weight: float32 [1536, 6448], P('shard')
- grad_conv_weight: float32 [4, 3328], P(None, 'shard')
- grad_conv_bias: float32 [3328], P('shard')
- grad_step_bias: float32 [48], P('shard')
- grad_decay_log: float32 [48], P('shard')
- grad_skip_gain: float32 [48], P('shard')
- grad_norm_gain: float32 [3072], P('shard')
- grad_out_weight: float32 [3072, 1536], P('shard')
- grad_moe_gain: float32 [1536], P('shard')
- grad_router_weight: float32 [1536, 32], P('shard')
- grad_shared_gate: float32 [1536, 1024], P('shard')
- grad_shared_up: float32 [1536, 1024], P('shard')
- grad_shared_down: float32 [1024, 1536], P('shard')
- grad_expert_gate: float32 [32, 1536, 512], P('shard')
- grad_expert_up: float32 [32, 1536, 512], P('shard')
- grad_expert_down: float32 [32, 512, 1536], P('shard')
Inputs may be any that keep to these rules, and one draw needn't show every extreme that they name: lengths[s] counts the live leading positions of sequence s; exactly 8 sequences, drawn from the seed, are full. `routes`: each row names 6 different experts; among the rows of one device no expert is named more than 32 times, and on some device some expert exactly 32 times.
All inputs are finite; a program needn't handle non-finite values.
Results may differ from a plain program's by a relative error of at most 0.035.
Values may be sent and summed in bfloat16 or wider, within the bound.
No kernel may reach another device: no remote copies, remote signals or barrier semaphores. Data moves between devices by JAX's collectives and lax.ppermute only.
A program may use at most 320 MiB of HBM per device.

v0:
```python
import jax
import jax.numpy as jnp
from jax import lax
from jax.sharding import PartitionSpec as P

BLOCK = 256


epsilon = 1e-05
highest = lax.Precision.HIGHEST


def rms_scale(values, gain):
    return values * lax.rsqrt(jnp.mean(values * values, axis=-1, keepdims=True) + epsilon) * gain


def times_transposed(left, right):
    return lax.dot_general(
        left, right, (((1,), (1,)), ((), ())), preferred_element_type=jnp.float32
    )


def transposed_times(left, right):
    return lax.dot_general(
        left, right, (((0,), (0,)), ((), ())), preferred_element_type=jnp.float32
    )


def silu_slope(values):
    sigma = jax.nn.sigmoid(values)
    return sigma * (1.0 + values * (1.0 - sigma))


def gate_norm(values, gate_input, gain):
    return rms_scale(values * jax.nn.silu(gate_input), gain)


def block_scan(ssm_state, block_piece, decay_rate):
    in_block, step_block, key_block, query_block = block_piece
    cumulative = jnp.cumsum(step_block * decay_rate[None, :], axis=0)
    positions = jnp.arange(cumulative.shape[0])
    causal = positions[:, None] >= positions[None, :]
    decay_gap = cumulative.T[:, :, None] - cumulative.T[:, None, :]
    decay_table = jnp.where(causal[None], jnp.exp(jnp.where(causal[None], decay_gap, 0.0)), 0.0)
    intersection = jnp.dot(query_block, key_block.T, precision=highest)
    scaled = in_block * step_block[:, :, None]
    within = jnp.einsum("hij,jhp->ihp", decay_table * intersection[None], scaled, precision=highest)
    across = (
        jnp.einsum("in,hpn->ihp", query_block, ssm_state, precision=highest)
        * jnp.exp(cumulative)[:, :, None]
    )
    to_end = jnp.exp(cumulative[-1][None, :] - cumulative)
    new_state = ssm_state * jnp.exp(cumulative[-1])[:, None, None] + jnp.einsum(
        "jn,jhp->hpn", key_block, scaled * to_end[:, :, None], precision=highest
    )
    return (new_state, within + across)


def mixer(
    mixer_raw, step_raw, keys_raw, conv_taps, conv_shift, step_offset, decay_logs, skip_scale
):
    seq_length, width = mixer_raw.shape
    head_count = step_raw.shape[1]
    head_size = width // head_count
    state_dim = keys_raw.shape[1] // 2
    kernel = conv_taps.shape[0]
    joined = jnp.concatenate([mixer_raw, keys_raw], axis=1)
    padded = jnp.pad(joined, ((kernel - 1, 0), (0, 0)))
    convolved = conv_shift[None, :]
    for tap_index in range(kernel):
        convolved = (
            convolved + conv_taps[tap_index][None, :] * padded[tap_index : tap_index + seq_length]
        )
    active = jax.nn.silu(convolved)
    mixer_in = active[:, :width]
    step_size = jax.nn.softplus(step_raw + step_offset[None, :])
    decay_rate = -jnp.exp(decay_logs)
    blocks = seq_length // BLOCK
    pieces = (
        mixer_in.reshape(blocks, BLOCK, head_count, head_size),
        step_size.reshape(blocks, BLOCK, head_count),
        active[:, width : width + state_dim].reshape(blocks, BLOCK, state_dim),
        active[:, width + state_dim :].reshape(blocks, BLOCK, state_dim),
    )

    def one_block(ssm_state, block_piece):
        return block_scan(ssm_state, block_piece, decay_rate)

    initial = jnp.zeros((head_count, head_size, state_dim), jnp.float32)
    final_state, outputs = lax.scan(jax.checkpoint(one_block), initial, pieces)
    result = outputs.reshape(seq_length, head_count, head_size) + skip_scale[
        None, :, None
    ] * mixer_in.reshape(seq_length, head_count, head_size)
    return result.reshape(seq_length, width)


def on_device(
    block_input,
    lengths,
    routes,
    out_cotangent,
    mixer_gain,
    in_weight,
    conv_weight,
    conv_bias,
    step_bias,
    decay_log,
    skip_gain,
    norm_gain,
    out_weight,
    moe_gain,
    router_weight,
    shared_gate,
    shared_up,
    shared_down,
    expert_gate,
    expert_up,
    expert_down,
):
    (
        gain_mixer,
        in_full,
        conv_full,
        offset_full,
        bias_full,
        decay_full,
        skip_full,
        gain_gate,
        out_full,
        gain_moe,
        route_full,
        share_gate,
        share_up,
        share_down,
    ) = (
        lax.all_gather(mixer_gain, "shard", axis=0, tiled=True),
        lax.all_gather(in_weight, "shard", axis=0, tiled=True),
        lax.all_gather(conv_weight, "shard", axis=1, tiled=True),
        lax.all_gather(conv_bias, "shard", axis=0, tiled=True),
        lax.all_gather(step_bias, "shard", axis=0, tiled=True),
        lax.all_gather(decay_log, "shard", axis=0, tiled=True),
        lax.all_gather(skip_gain, "shard", axis=0, tiled=True),
        lax.all_gather(norm_gain, "shard", axis=0, tiled=True),
        lax.all_gather(out_weight, "shard", axis=0, tiled=True),
        lax.all_gather(moe_gain, "shard", axis=0, tiled=True),
        lax.all_gather(router_weight, "shard", axis=0, tiled=True),
        lax.all_gather(shared_gate, "shard", axis=0, tiled=True),
        lax.all_gather(shared_up, "shard", axis=0, tiled=True),
        lax.all_gather(shared_down, "shard", axis=0, tiled=True),
    )
    seq_size = lax.axis_size("seq")
    seq_index = lax.axis_index("seq")
    tok_rows = block_input[0].astype(jnp.float32)
    tok_count, model_dim = tok_rows.shape
    inner_dim = gain_gate.shape[0]
    head_total = bias_full.shape[0]
    state_dim = (conv_full.shape[1] - inner_dim) // 2
    head_size = inner_dim // head_total
    group_heads = head_total // seq_size
    group_width = group_heads * head_size
    seq_rows = tok_count * seq_size
    normed, norm_back = jax.vjp(rms_scale, tok_rows, gain_mixer.astype(jnp.float32))
    normed_low = normed.astype(jnp.bfloat16)
    projected = jnp.dot(normed_low, in_full, preferred_element_type=jnp.float32)
    gate_input = projected[:, :inner_dim]
    mixer_part = (
        projected[:, inner_dim : 2 * inner_dim]
        .astype(jnp.bfloat16)
        .reshape(tok_count, seq_size, group_width)
    )
    keys_part = projected[:, 2 * inner_dim : 2 * inner_dim + 2 * state_dim].astype(jnp.bfloat16)
    step_part = (
        projected[:, 2 * inner_dim + 2 * state_dim :]
        .astype(jnp.bfloat16)
        .reshape(tok_count, seq_size, group_heads)
    )
    mixer_heads, step_heads = (
        lax.all_to_all(mixer_part, "seq", split_axis=1, concat_axis=0, tiled=True),
        lax.all_to_all(step_part, "seq", split_axis=1, concat_axis=0, tiled=True),
    )
    keys_whole = lax.all_gather(keys_part, "seq", axis=0, tiled=True)
    conv_group = lax.dynamic_slice_in_dim(conv_full, seq_index * group_width, group_width, 1)
    conv_local = jnp.concatenate([conv_group, conv_full[:, inner_dim:]], axis=1).astype(jnp.float32)
    offset_group = lax.dynamic_slice_in_dim(offset_full, seq_index * group_width, group_width, 0)
    offset_local = jnp.concatenate([offset_group, offset_full[inner_dim:]], axis=0).astype(
        jnp.float32
    )
    bias_local = lax.dynamic_slice_in_dim(
        bias_full, seq_index * group_heads, group_heads, 0
    ).astype(jnp.float32)
    decay_local = lax.dynamic_slice_in_dim(
        decay_full, seq_index * group_heads, group_heads, 0
    ).astype(jnp.float32)
    skip_local = lax.dynamic_slice_in_dim(
        skip_full, seq_index * group_heads, group_heads, 0
    ).astype(jnp.float32)
    mixed_out, mixer_back = jax.vjp(
        mixer,
        mixer_heads.reshape(seq_rows, group_width).astype(jnp.float32),
        step_heads.reshape(seq_rows, group_heads).astype(jnp.float32),
        keys_whole.astype(jnp.float32),
        conv_local,
        offset_local,
        bias_local,
        decay_local,
        skip_local,
    )
    mixed_send = mixed_out.astype(jnp.bfloat16).reshape(seq_size, tok_count, group_width)
    mixed_back = lax.all_to_all(mixed_send, "seq", split_axis=0, concat_axis=2, tiled=True)
    mixed_tok = mixed_back.reshape(tok_count, inner_dim).astype(jnp.float32)
    gated_out, gated_back = jax.vjp(gate_norm, mixed_tok, gate_input, gain_gate.astype(jnp.float32))
    gated_low = gated_out.astype(jnp.bfloat16)
    residual = tok_rows + jnp.dot(gated_low, out_full, preferred_element_type=jnp.float32)
    moe_norm, moe_back = jax.vjp(rms_scale, residual, gain_moe.astype(jnp.float32))
    moe_in = moe_norm.astype(jnp.bfloat16)
    route_ids = routes[0]
    topk = route_ids.shape[1]
    experts_all = route_full.shape[1]
    logits = jnp.dot(moe_in, route_full, preferred_element_type=jnp.float32)
    picks = (
        route_ids[:, :, None] == jnp.arange(experts_all, dtype=jnp.int32)[None, None, :]
    ).astype(jnp.float32)
    chosen = jnp.einsum("tke,te->tk", picks, logits, precision=highest)
    gate_weights = jax.nn.softmax(chosen, axis=1)
    shared_pre = jnp.dot(moe_in, share_gate, preferred_element_type=jnp.float32)
    shared_lin = jnp.dot(moe_in, share_up, preferred_element_type=jnp.float32)
    shared_act = (jax.nn.silu(shared_pre) * shared_lin).astype(jnp.bfloat16)
    shared_result = jnp.dot(shared_act, share_down, preferred_element_type=jnp.float32)
    capacity = tok_count * topk // experts_all * 4 // 3
    flat_ids = route_ids.reshape(-1)
    one_hot = (flat_ids[:, None] == jnp.arange(experts_all, dtype=jnp.int32)[None, :]).astype(
        jnp.int32
    )
    earlier = jnp.cumsum(one_hot, axis=0) - one_hot
    position = jnp.sum(earlier * one_hot, axis=1)
    slot = flat_ids * capacity + position
    sources = jnp.repeat(moe_in, topk, axis=0)
    send_rows = jnp.zeros((experts_all * capacity, model_dim), jnp.bfloat16).at[slot].set(sources)
    arrived = lax.all_to_all(
        send_rows.reshape(experts_all, capacity, model_dim),
        "shard",
        split_axis=0,
        concat_axis=1,
        tiled=True,
    )
    expert_pre = jnp.einsum(
        "ecd,edf->ecf", arrived, expert_gate, preferred_element_type=jnp.float32
    )
    expert_lin = jnp.einsum("ecd,edf->ecf", arrived, expert_up, preferred_element_type=jnp.float32)
    expert_act = (jax.nn.silu(expert_pre) * expert_lin).astype(jnp.bfloat16)
    expert_result = jnp.einsum(
        "ecf,efd->ecd", expert_act, expert_down, preferred_element_type=jnp.float32
    ).astype(jnp.bfloat16)
    returned = lax.all_to_all(expert_result, "shard", split_axis=1, concat_axis=0, tiled=True)
    flat_back = returned.reshape(experts_all * capacity, model_dim)[slot].reshape(
        tok_count, topk, model_dim
    )
    combined = jnp.sum(gate_weights[:, :, None] * flat_back.astype(jnp.float32), axis=1)
    live_mask = (
        seq_index * tok_count + jnp.arange(tok_count, dtype=jnp.int32) < lengths[0]
    ).astype(jnp.float32)
    block_output = ((residual + shared_result + combined) * live_mask[:, None]).astype(
        jnp.bfloat16
    )[None]
    in_back, out_back, route_back, share_gate_back, share_up_back, share_down_back = (
        lax.all_gather(in_weight, "shard", axis=0, tiled=True),
        lax.all_gather(out_weight, "shard", axis=0, tiled=True),
        lax.all_gather(router_weight, "shard", axis=0, tiled=True),
        lax.all_gather(shared_gate, "shard", axis=0, tiled=True),
        lax.all_gather(shared_up, "shard", axis=0, tiled=True),
        lax.all_gather(shared_down, "shard", axis=0, tiled=True),
    )
    d_total = out_cotangent[0].astype(jnp.float32) * live_mask[:, None]
    d_total_low = d_total.astype(jnp.bfloat16)
    d_gates = jnp.sum(d_total[:, None, :] * flat_back.astype(jnp.float32), axis=2)
    d_rows = (
        (gate_weights[:, :, None] * d_total[:, None, :])
        .astype(jnp.bfloat16)
        .reshape(tok_count * topk, model_dim)
    )
    d_send = jnp.zeros((experts_all * capacity, model_dim), jnp.bfloat16).at[slot].set(d_rows)
    d_arrived = lax.all_to_all(
        d_send.reshape(experts_all, capacity, model_dim),
        "shard",
        split_axis=0,
        concat_axis=1,
        tiled=True,
    )
    d_expert_act = jnp.einsum(
        "ecd,efd->ecf", d_arrived, expert_down, preferred_element_type=jnp.float32
    )
    grad_expert_down = jnp.einsum(
        "ecf,ecd->efd", expert_act, d_arrived, preferred_element_type=jnp.float32
    )
    d_expert_pre = (d_expert_act * expert_lin * silu_slope(expert_pre)).astype(jnp.bfloat16)
    d_expert_lin = (d_expert_act * jax.nn.silu(expert_pre)).astype(jnp.bfloat16)
    grad_expert_gate = jnp.einsum(
        "ecd,ecf->edf", arrived, d_expert_pre, preferred_element_type=jnp.float32
    )
    grad_expert_up = jnp.einsum(
        "ecd,ecf->edf", arrived, d_expert_lin, preferred_element_type=jnp.float32
    )
    d_inputs = (
        jnp.einsum("ecf,edf->ecd", d_expert_pre, expert_gate, preferred_element_type=jnp.float32)
        + jnp.einsum("ecf,edf->ecd", d_expert_lin, expert_up, preferred_element_type=jnp.float32)
    ).astype(jnp.bfloat16)
    d_returned = lax.all_to_all(d_inputs, "shard", split_axis=1, concat_axis=0, tiled=True)
    d_moe = jnp.sum(
        d_returned.reshape(experts_all * capacity, model_dim)[slot]
        .reshape(tok_count, topk, model_dim)
        .astype(jnp.float32),
        axis=1,
    )
    d_chosen = gate_weights * (d_gates - jnp.sum(gate_weights * d_gates, axis=1, keepdims=True))
    d_logits = jnp.einsum("tke,tk->te", picks, d_chosen, precision=highest)
    grad_route = jnp.dot(moe_in.astype(jnp.float32).T, d_logits, precision=highest)
    d_moe = d_moe + jnp.dot(d_logits, route_back.astype(jnp.float32).T, precision=highest)
    d_shared_act = times_transposed(d_total_low, share_down_back)
    d_shared_pre = (d_shared_act * shared_lin * silu_slope(shared_pre)).astype(jnp.bfloat16)
    d_shared_lin = (d_shared_act * jax.nn.silu(shared_pre)).astype(jnp.bfloat16)
    d_moe = (
        d_moe
        + times_transposed(d_shared_pre, share_gate_back)
        + times_transposed(d_shared_lin, share_up_back)
    )
    d_resid_norm, grad_gain_moe = moe_back(d_moe)
    d_resid = d_total + d_resid_norm
    d_out_low = d_resid.astype(jnp.bfloat16)
    d_gated = times_transposed(d_out_low, out_back)
    d_mixed_tok, d_gate_input, grad_gain_gate = gated_back(d_gated)
    d_mixed_send = d_mixed_tok.astype(jnp.bfloat16).reshape(tok_count, seq_size, group_width)
    d_mixed_heads = lax.all_to_all(d_mixed_send, "seq", split_axis=1, concat_axis=0, tiled=True)
    (
        d_mixer_raw,
        d_step_raw,
        d_keys_raw,
        grad_conv_local,
        grad_offset_local,
        grad_bias_local,
        grad_decay_local,
        grad_skip_local,
    ) = mixer_back(d_mixed_heads.reshape(seq_rows, group_width).astype(jnp.float32))
    d_mixer_send = d_mixer_raw.astype(jnp.bfloat16).reshape(seq_rows, 1, group_width)
    d_step_send = d_step_raw.astype(jnp.bfloat16).reshape(seq_rows, 1, group_heads)
    d_mixer_tok, d_step_tok = (
        lax.all_to_all(d_mixer_send, "seq", split_axis=0, concat_axis=1, tiled=True),
        lax.all_to_all(d_step_send, "seq", split_axis=0, concat_axis=1, tiled=True),
    )
    d_keys_tok = lax.psum_scatter(
        d_keys_raw.astype(jnp.bfloat16), "seq", scatter_dimension=0, tiled=True
    )
    d_proj = jnp.concatenate(
        [
            d_gate_input.astype(jnp.bfloat16),
            d_mixer_tok.reshape(tok_count, inner_dim),
            d_keys_tok,
            d_step_tok.reshape(tok_count, head_total),
        ],
        axis=1,
    )
    d_normed = times_transposed(d_proj, in_back)
    d_tok_norm, grad_gain_mixer = norm_back(d_normed)
    input_grad = (d_resid + d_tok_norm)[None]
    grad_conv = lax.dynamic_update_slice_in_dim(
        jnp.zeros(conv_full.shape, jnp.float32),
        grad_conv_local[:, :group_width],
        seq_index * group_width,
        1,
    )
    grad_conv = grad_conv.at[:, inner_dim:].set(grad_conv_local[:, group_width:])
    grad_offset = lax.dynamic_update_slice_in_dim(
        jnp.zeros(offset_full.shape, jnp.float32),
        grad_offset_local[:group_width],
        seq_index * group_width,
        0,
    )
    grad_offset = grad_offset.at[inner_dim:].set(grad_offset_local[group_width:])
    grad_bias = lax.dynamic_update_slice_in_dim(
        jnp.zeros((head_total,), jnp.float32), grad_bias_local, seq_index * group_heads, 0
    )
    grad_decay = lax.dynamic_update_slice_in_dim(
        jnp.zeros((head_total,), jnp.float32), grad_decay_local, seq_index * group_heads, 0
    )
    grad_skip = lax.dynamic_update_slice_in_dim(
        jnp.zeros((head_total,), jnp.float32), grad_skip_local, seq_index * group_heads, 0
    )
    grad_in = transposed_times(normed_low, d_proj)
    grad_out = transposed_times(gated_low, d_out_low)
    grad_share_down = transposed_times(shared_act, d_total_low)
    grad_share_gate = transposed_times(moe_in, d_shared_pre)
    grad_share_up = transposed_times(moe_in, d_shared_lin)
    (
        part_mixer_gain,
        part_in,
        part_conv,
        part_offset,
        part_bias,
        part_decay,
        part_skip,
        part_gain_gate,
        part_out,
        part_gain_moe,
        part_route,
        part_share_gate,
        part_share_up,
        part_share_down,
    ) = (
        lax.psum_scatter(grad_gain_mixer, "shard", scatter_dimension=0, tiled=True),
        lax.psum_scatter(grad_in, "shard", scatter_dimension=0, tiled=True),
        lax.psum_scatter(grad_conv, "shard", scatter_dimension=1, tiled=True),
        lax.psum_scatter(grad_offset, "shard", scatter_dimension=0, tiled=True),
        lax.psum_scatter(grad_bias, "shard", scatter_dimension=0, tiled=True),
        lax.psum_scatter(grad_decay, "shard", scatter_dimension=0, tiled=True),
        lax.psum_scatter(grad_skip, "shard", scatter_dimension=0, tiled=True),
        lax.psum_scatter(grad_gain_gate, "shard", scatter_dimension=0, tiled=True),
        lax.psum_scatter(grad_out, "shard", scatter_dimension=0, tiled=True),
        lax.psum_scatter(grad_gain_moe, "shard", scatter_dimension=0, tiled=True),
        lax.psum_scatter(grad_route, "shard", scatter_dimension=0, tiled=True),
        lax.psum_scatter(grad_share_gate, "shard", scatter_dimension=0, tiled=True),
        lax.psum_scatter(grad_share_up, "shard", scatter_dimension=0, tiled=True),
        lax.psum_scatter(grad_share_down, "shard", scatter_dimension=0, tiled=True),
    )
    summed = lax.psum(
        (
            part_mixer_gain,
            part_in,
            part_conv,
            part_offset,
            part_bias,
            part_decay,
            part_skip,
            part_gain_gate,
            part_out,
            part_gain_moe,
            part_route,
            part_share_gate,
            part_share_up,
            part_share_down,
            grad_expert_gate,
            grad_expert_up,
            grad_expert_down,
        ),
        "seq",
    )
    return (
        block_output,
        input_grad,
        summed[0],
        summed[1],
        summed[2],
        summed[3],
        summed[4],
        summed[5],
        summed[6],
        summed[7],
        summed[8],
        summed[9],
        summed[10],
        summed[11],
        summed[12],
        summed[13],
        summed[14],
        summed[15],
        summed[16],
    )


def solution(mesh):
    placed = (
        P("shard", "seq", None),
        P("shard"),
        P("shard", "seq", None),
        P("shard", "seq", None),
        P("shard"),
        P("shard", None),
        P(None, "shard"),
        P("shard"),
        P("shard"),
        P("shard"),
        P("shard"),
        P("shard"),
        P("shard", None),
        P("shard"),
        P("shard", None),
        P("shard", None),
        P("shard", None),
        P("shard", None),
        P("shard", None, None),
        P("shard", None, None),
        P("shard", None, None),
    )
    return jax.shard_map(
        on_device,
        mesh=mesh,
        in_specs=placed,
        out_specs=(
            P("shard", "seq", None),
            P("shard", "seq", None),
            P("shard"),
            P("shard", None),
            P(None, "shard"),
            P("shard"),
            P("shard"),
            P("shard"),
            P("shard"),
            P("shard"),
            P("shard", None),
            P("shard"),
            P("shard", None),
            P("shard", None),
            P("shard", None),
            P("shard", None),
            P("shard", None, None),
            P("shard", None, None),
            P("shard", None, None),
        ),
        check_vma=False,
    )
```

profile of v0, /device:TPU:1, one launch (start us, length us, event | category | flops | bytes accessed | tf_op | source)
XLA Modules:
  0.0 1910.4 jit_solution(8431778556288251838)
XLA Ops:
  22.3 62.9 %all-reduce.32 = (bf16[3072]{0:T(1024)(128)(2,1)}, bf16[1536]{0:T(1024)(128)(2,1)}, bf16[48]{0:T(256)(128)(2,1)}, bf16[48]{0:T(256)(128)(2,1)}, bf16[3328]{0:T(1...) all-reduce(bf16[3072]{0:T(1024)(128)(2,1)S(1)} %dynamic-update-slic, ...), channel_id=1, replica_groups=mesh['seq'=8,'shard'=16] {'shard'}, use_global_device_ids=true, to_apply=%add.19 | all-reduce | flops 9616 | bytes 38464
  87.1 18.1 all-gather
  113.2 29.6 %all-gather.8.cloned.1.call-done = bf16[1536,6448]{1,0:T(8,128)(2,1)} async-done(((bf16[96,6448]{1,0:T(8,128)(2,1)}), bf16[1536,6448]{1,0:T(8,128)(2,1)}) %all-gather.8.cloned.1.call-update) | async-done | bytes 19808272 | tf_op jit(solution)/shard_map/all_gather | solution.py:137
  142.8 13.7 fusion.176
  174.7 18.9 all_gather.57
  215.7 85.1 %while.46 = (s32[]{:T(128)}, f32[6,64,128]{2,1,0:T(8,128)S(1)}, f32[4,256,6,64]{1,0,3,2:T(4,128)}, f32[4,6,64,128]{3,2,1,0:T(8,128)}, f32[4,256,6]{1,2,0:T(8,128...) while((s32[]{:T(128)}, f32[6,64,128]{2,1,0:T(8,128)S(1)}, ...), condition=%wide.region_4.5_spmd.clone.clone, body=%wide.region_1.4_spmd.clone.clone.sunk | while | flops 707152896 | bytes 5768572 | solution.py:90
  227.4 9.6 dynamic_update_slice.97
  248.7 9.6 dynamic_update_slice.97
  270.0 9.5 dynamic_update_slice.97
  291.2 9.5 dynamic_update_slice.97
  371.5 39.8 %all-gather.1 = bf16[16,96,32]{1,2,0:T(8,128)(2,1)S(1)} all-gather(bf16[1,96,32]{1,2,0:T(8,128)(2,1)} %bitcast.641), channel_id=1, replica_groups=mesh['seq'=8,'shard'=16] {'shard'}, dimensions={0}, use_global_device_ids=true | all-gather | bytes 104448 | tf_op jit(solution)/shard_map/all_gather | solution.py:146
  422.0 13.3 scatter_custom_fusion.1
  450.0 24.1 %all-to-all-done.5 = bf16[32,32,1536]{2,1,0:T(8,128)(2,1)} async-done(((bf16[32,32,1536]{2,1,0:T(8,128)(2,1)}), bf16[32,32,1536]{2,1,0:T(8,128)(2,1)}, u32[]{:S(2)}, u32[]{:S(2)}) %all-to-all-start.5) | async-done | bytes 3145760 | tf_op jit(solution)/shard_map/all_to_all | solution.py:282
  488.9 10.5 all-to-all-start.4
  510.6 36.9 %all-to-all-done.4 = bf16[2,512,1536]{2,0,1:T(2,128)(2,1)S(1)} async-done(((bf16[2,512,1536]{2,0,1:T(2,128)(2,1)}), bf16[2,512,1536]{2,0,1:T(2,128)(2,1)S(1)}, u32[]{:S(2)}, u32[]{:S(2)}) %all-to-all-start.4) | async-done | bytes 3145760 | tf_op jit(solution)/shard_map/all_to_all | solution.py:254
  577.9 11.5 all-to-all-done.6
  624.6 9.8 all-to-all-start.7
  634.5 12.2 all-to-all-done.7
  654.0 145.9 %while.45 = (s32[]{:T(128)}, f32[6]{0:T(128)S(1)}, f32[6,64,128]{2,1,0:T(8,128)S(1)}, f32[4,256,6,64]{1,0,3,2:T(4,128)}, f32[4,256,6]{1,2,0:T(8,128)S(1)}, /*ind...) while((s32[]{:T(128)}, f32[6]{0:T(128)S(1)}, ...), condition=%wide.region_34.35_spmd.clone, body=%wide.region_20.34_spmd.clone.sunk | while | flops 1669043200 | bytes 14915856 | solution.py:90
  677.0 9.5 dynamic_update_slice.95
  839.9 10.3 fusion.134
  872.5 11.3 all-to-all-done.8
  886.3 17.6 fusion.129
  924.1 12.0 fusion.120
  941.9 80.7 %reduce-scatter.19.cloned.1.call-done = f32[96,1024]{1,0:T(8,128)} async-done(((f32[1536,1024]{1,0:T(8,128)}), f32[96,1024]{1,0:T(8,128)}) %reduce-scatter.19.cloned.1.call-update) | async-done | bytes 393232 | tf_op jit(solution)/shard_map/reduce_scatter | solution.py:420
  1022.6 85.2 %reduce-scatter.21.cloned.1.call-done = f32[64,1536]{1,0:T(8,128)} async-done(((f32[1024,1536]{1,0:T(8,128)}), f32[64,1536]{1,0:T(8,128)}) %reduce-scatter.21.cloned.1.call-update) | async-done | bytes 393232 | tf_op jit(solution)/shard_map/reduce_scatter | solution.py:421
  1107.8 125.1 %reduce-scatter.15.cloned.1.call-done = f32[192,1536]{1,0:T(8,128)} async-done(((f32[3072,1536]{1,0:T(8,128)}), f32[192,1536]{1,0:T(8,128)}) %reduce-scatter.15.cloned.1.call-update) | async-done | bytes 1179664 | tf_op jit(solution)/shard_map/reduce_scatter | solution.py:416
  1232.9 232.7 %reduce-scatter.13.cloned.1.call-done = f32[96,6448]{1,0:T(8,128)} async-done(((f32[1536,6448]{1,0:T(8,128)}), f32[96,6448]{1,0:T(8,128)}) %reduce-scatter.13.cloned.1.call-update) | async-done | bytes 2476048 | tf_op jit(solution)/shard_map/reduce_scatter | solution.py:409
  1471.8 68.1 %reduce-scatter.25.cloned.1.call-done = f32[96,32]{1,0:T(8,128)} async-done(((f32[1536,32]{1,0:T(8,128)}), f32[96,32]{1,0:T(8,128)}) %reduce-scatter.25.cloned.1.call-update) | async-done | bytes 12304
  1543.0 84.9 %all-reduce.36.cloned.1.call-done = (f32[1536]{0:T(1024)}, f32[4,3328]{1,0:T(4,128)}, f32[3328]{0:T(1024)}, f32[48]{0:T(128)}, f32[48]{0:T(128)}, /*index=5*/f32[48]{0:T(128)}, f32[3072]{0:T(1024)}, f32[1536]{0:T(1024)}) async-done(((f32[1536]{0:T(1024)}, f32[4,3328]{1,0:T(4,128)}, f32[3328]{0:T(1024)}, f32[48]{0:T(128)}, f32[48]{0:T(128)}, /*index=5*/f32[48]{0:T(128)}, f32[3072]{0:T(1024)}, ...) | async-done | bytes 91728
  1633.9 23.9 %all-reduce.30 = (f32[96]{0:T(128)}, f32[4,208]{1,0:T(4,128)}, f32[208]{0:T(256)}, f32[3]{0:T(128)}, f32[3]{0:T(128)}, /*index=5*/f32[3]{0:T(128)}, f32[192]{0:T(256)}, f32[96]{0:T(128)}, f32[96,32]{0,1:T(8,128)}) all-reduce(f32[96]{0:T(128)S(1)} %dynamic-slice.24, ...), channel_id=1, replica_groups=mesh['seq'=8,'shard'=16] {'seq'}, use_global_device_ids=true, to_apply=%region_39.40 | all-reduce | flops 4505 | bytes 36040 | tf_op jit(solution)/shard_map/psum | solution.py:423
  1657.8 225.4 %all-reduce.38.cloned.1.call-done = (f32[96,6448]{1,0:T(8,128)}, f32[192,1536]{1,0:T(8,128)}, f32[96,1024]{1,0:T(8,128)}, f32[96,1024]{1,0:T(8,128)}, f32[64,153...) async-done(((f32[96,6448]{1,0:T(8,128)}, f32[192,1536]{1,0:T(8,128)}, f32[96,1024]{1,0:T(8,128)}, f32[96,1024]{1,0:T(8,128)}, ...) | async-done | bytes 23709712 | tf_op jit(solution)/shard_map/psum | solution.py:423
  (774 shorter events, 561.4 us)
Async XLA Ops:
  7.2 469.3 %copy-start = (bf16[2,512,1536]{2,1,0:T(8,128)(2,1)S(1)}, bf16[2,512,1536]{2,1,0:T(8,128)(2,1)}, u32[]{:S(2)}) copy-start(bf16[2,512,1536]{2,1,0:T(8,128)(2,1)} %param.49) | copy-start | bytes 9437188
  7.2 78.6 %copy-start.16 = (bf16[1,128,1536]{2,1,0:T(8,128)(2,1)S(1)}, bf16[1,128,1536]{2,1,0:T(8,128)(2,1)}, u32[]{:S(2)}) copy-start(bf16[1,128,1536]{2,1,0:T(8,128)(2,1)} %param.29) | copy-start | bytes 1179652
  7.2 135.6 %all-gather.8.cloned.1.call-start = ((), (), s32[]{:S(2)}) async-start(), calls=%async_computation.17 | async-start | bytes 21307392 | tf_op jit(solution)/shard_map/all_gather | solution.py:137
  8.0 323.8 %all-gather.10.cloned.1.call-start = ((), (), s32[]{:S(2)}) async-start(), calls=%async_computation.18 | async-start | bytes 10027008 | tf_op jit(solution)/shard_map/all_gather | solution.py:144
  8.7 545.0 %all-gather.12.cloned.1.call-start = ((), (), s32[]{:S(2)}) async-start(), calls=%async_computation.19 | async-start | bytes 3342336 | tf_op jit(solution)/shard_map/all_gather | solution.py:147
  9.4 546.8 %all-gather.14.cloned.1.call-start = ((), (), s32[]{:S(2)}) async-start(), calls=%async_computation.20 | async-start | bytes 3342336 | tf_op jit(solution)/shard_map/all_gather | solution.py:148
  111.9 85.3 %copy-start.75 = (f32[640]{0:T(1024)}, f32[640]{0:T(1024)S(1)}, u32[]{:S(2)}) copy-start(f32[640]{0:T(1024)S(1)} %get-tuple-element.759) | copy-start | bytes 7684
  111.9 85.3 %copy-start.77 = (f32[640]{0:T(1024)}, f32[640]{0:T(1024)S(1)}, u32[]{:S(2)}) copy-start(f32[640]{0:T(1024)S(1)} %get-tuple-element.760) | copy-start | bytes 7684
  158.3 9.7 all-to-all-start
  168.1 26.3 %all-to-all-start.1 = ((bf16[128,8,384]{0,2,1:T(8,128)(2,1)}), bf16[128,8,384]{0,2,1:T(8,128)(2,1)}, u32[]{:S(2)}, u32[]{:S(2)}) async-start(bf16[128,8,384]{0,2,1:T(8,128)(2,1)} %bitcast.602), calls=%async_computation.1 | async-start | bytes 1572864 | tf_op jit(solution)/shard_map/all_to_all | solution.py:178
  173.9 129.0 %copy-start.83 = (f32[384]{0:T(512)}, f32[384]{0:T(512)S(1)}, u32[]{:S(2)}) copy-start(f32[384]{0:T(512)S(1)} %mul.860) | copy-start | bytes 4612
  308.9 16.8 all-to-all-start.2
  354.2 81.1 %all-to-all-start.3 = ((bf16[32,32,1536]{2,1,0:T(8,128)(2,1)}), bf16[32,32,1536]{2,1,0:T(8,128)(2,1)}, u32[]{:S(2)}, u32[]{:S(2)}) async-start(bf16[32,32,1536]{2,1,0:T(8,128)(2,1)} %bitcast.586), calls=%async_computation.3 | async-start | bytes 6291456 | tf_op jit(solution)/shard_map/all_to_all | solution.py:239
  435.3 38.8 %all-to-all-start.5 = ((bf16[32,32,1536]{2,1,0:T(8,128)(2,1)}), bf16[32,32,1536]{2,1,0:T(8,128)(2,1)}, u32[]{:S(2)}, u32[]{:S(2)}) async-start(bf16[32,32,1536]{2,1,0:T(8,128)(2,1)} %bitcast.584), calls=%async_computation.5 | async-start | bytes 6291456 | tf_op jit(solution)/shard_map/all_to_all | solution.py:282
  440.3 118.4 %all-gather.16.cloned.1.call-start = ((), (), s32[]{:S(2)}) async-start(), calls=%async_computation.21 | async-start | bytes 3342336 | tf_op jit(solution)/shard_map/all_gather | solution.py:149
  488.9 58.5 %all-to-all-start.4 = ((bf16[2,512,1536]{2,0,1:T(2,128)(2,1)}), bf16[2,512,1536]{2,0,1:T(2,128)(2,1)S(1)}, u32[]{:S(2)}, u32[]{:S(2)}) async-start(bf16[2,512,1536]{2,0,1:T(2,128)(2,1)} %copy.351), calls=%async_computation.4 | async-start | bytes 6291456 | tf_op jit(solution)/shard_map/all_to_all | solution.py:254
  549.1 40.3 %all-to-all-start.6 = ((bf16[2,512,1536]{2,0,1:T(2,128)(2,1)}), bf16[2,512,1536]{2,0,1:T(2,128)(2,1)}, u32[]{:S(2)}, u32[]{:S(2)}) async-start(bf16[2,512,1536]{2,0,1:T(2,128)(2,1)} %copy.354), calls=%async_computation.6 | async-start | bytes 6291456 | tf_op jit(solution)/shard_map/all_to_all | solution.py:307
  624.6 22.1 %all-to-all-start.7 = ((bf16[128,8,384]{0,2,1:T(8,128)(2,1)}), bf16[128,8,384]{0,2,1:T(8,128)(2,1)S(1)}, u32[]{:S(2)}, u32[]{:S(2)}) async-start(bf16[128,8,384]{0,2,1:T(8,128)(2,1)} %bitcast.50), calls=%async_computation.7 | async-start | bytes 1572864 | tf_op jit(solution)/shard_map/all_to_all | solution.py:332
  634.4 250.8 %reduce-scatter.23.cloned.1.call-start = ((), (), s32[]{:S(2)}) async-start(), calls=%async_computation.27 | async-start | bytes 589824
  824.7 117.1 %reduce-scatter.17.cloned.1.call-start = ((), (), s32[]{:S(2)}) async-start(), calls=%async_computation.24 | async-start | bytes 6684672 | tf_op jit(solution)/shard_map/reduce_scatter | solution.py:419
  829.5 193.1 %reduce-scatter.19.cloned.1.call-start = ((), (), s32[]{:S(2)}) async-start(), calls=%async_computation.25 | async-start | bytes 6684672 | tf_op jit(solution)/shard_map/reduce_scatter | solution.py:420
  834.1 273.6 %reduce-scatter.21.cloned.1.call-start = ((), (), s32[]{:S(2)}) async-start(), calls=%async_computation.26 | async-start | bytes 6684672 | tf_op jit(solution)/shard_map/reduce_scatter | solution.py:421
  839.8 393.1 %reduce-scatter.15.cloned.1.call-start = ((), (), s32[]{:S(2)}) async-start(), calls=%async_computation.23 | async-start | bytes 20054016 | tf_op jit(solution)/shard_map/reduce_scatter | solution.py:416
  853.5 13.2 all-to-all-start.9
  866.7 17.1 all-to-all-start.8
  871.5 594.1 %reduce-scatter.13.cloned.1.call-start = ((), (), s32[]{:S(2)}) async-start(), calls=%async_computation.22 | async-start | bytes 42614784 | tf_op jit(solution)/shard_map/reduce_scatter | solution.py:409
  903.9 635.9 %reduce-scatter.25.cloned.1.call-start = ((), (), s32[]{:S(2)}) async-start(), calls=%async_computation.28 | async-start | bytes 835584
  917.6 710.3 %all-reduce.36.cloned.1.call-start = ((), (), s32[]{:S(2)}) async-start(), calls=%async_computation.29 | async-start | bytes 199680
  936.1 947.0 %all-reduce.38.cloned.1.call-start = ((), (), s32[]{:S(2)}) async-start(), calls=%async_computation.30 | async-start | bytes 47480832 | tf_op jit(solution)/shard_map/psum | solution.py:423
  1468.4 72.3 %copy-start.108 = (f32[128]{0:T(128)S(1)}, f32[128]{0:T(128)}, u32[]{:S(2)}) copy-start(f32[128]{0:T(128)} %copy-done.107) | copy-start | bytes 1540
  1468.4 72.3 %copy-start.19 = (bf16[1,128,1536]{2,1,0:T(8,128)(2,1)S(1)}, bf16[1,128,1536]{2,1,0:T(8,128)(2,1)}, u32[]{:S(2)}) copy-start(bf16[1,128,1536]{2,1,0:T(8,128)(2,1)} %param.29) | copy-start | bytes 1179652
  1468.4 72.3 %copy-start.27 = (f32[128,1536]{1,0:T(8,128)S(1)}, f32[128,1536]{1,0:T(8,128)}, u32[]{:S(2)}) copy-start(f32[128,1536]{1,0:T(8,128)} %copy-done.26) | copy-start | bytes 2359300
  (117 other events, 651.9 us)
Sparse Core Ops, SparseCore 0:
  10.2 132.5 all-gather.7
  145.0 74.9 all-gather.9
  222.1 47.2 all-gather.11
  271.5 46.7 all-gather.13
  443.1 90.2 all-gather.15
  824.9 26.4 reduce-scatter.22
  855.8 81.6 reduce-scatter.16
  941.9 80.6 reduce-scatter.18
  1027.0 80.7 reduce-scatter.20
  1111.4 121.4 reduce-scatter.14
  1236.9 228.6 reduce-scatter.12
  1469.2 70.5 reduce-scatter.24
  1545.1 82.7 all-reduce.35
  1631.6 251.4 all-reduce.37
where the time goes:
time: 1920 us; the launch traced here: 1910 us
  waiting for transfers between devices  1040 us (54%)
  local copies, waits for them, and re-layouts  292 us (15%)
  matrix products  204 us (11%)
  blocking collectives  164 us (9%)
  other arithmetic  127 us (7%)
  starting transfers between devices  59.1 us (3%)
  between operations  21.5 us (1%)
    reduce_scatter x1, waiting for transfers between devices, on_device(): lax.psum_scatter(grad_in, 'shard', scatter_dimension=0, tiled=True)  233 us
    psum x1, waiting for transfers between devices, on_device(): lax.psum((part_mixer_gain, part_in, part_conv, part_offset, part_bias, pa...  225 us
    unnamed x17, waiting for transfers between devices  156 us
    reduce_scatter x1, waiting for transfers between devices, on_device(): lax.psum_scatter(grad_out, 'shard', scatter_dimension=0, tiled=True)  125 us
    reduce_scatter x1, waiting for transfers between devices, on_device(): lax.psum_scatter(grad_share_down, 'shard', scatter_dimension=0, tiled=True)  85.2 us
    dynamic_update_slice x16, local copies, waits for them, and re-layouts, mixer(): final_state, outputs = lax.scan(jax.checkpoint(one_block), initial, pieces)  82.6 us
    reduce_scatter x1, waiting for transfers between devices, on_device(): lax.psum_scatter(grad_share_up, 'shard', scatter_dimension=0, tiled=True)  80.7 us
    unnamed x300, local copies, waits for them, and re-layouts  77.5 us
  transfers between devices with their start and end apart: 24, of which 15 were waited for; matrix products, arithmetic and copies ran while one was open for 20% of the time, Pallas kernels for 0%

commit v1 on v0

v1 whole, which is shorter than its diff:
```python
import jax
import jax.numpy as jnp
from jax import lax
from jax.sharding import PartitionSpec as P

BLOCK = 256
CAP = 32


epsilon = 1e-05
highest = lax.Precision.HIGHEST
both_axes = ("seq", "shard")


def times(left, right):
    return jnp.dot(left, right, preferred_element_type=jnp.float32)


def times_transposed(left, right):
    return lax.dot_general(
        left, right, (((1,), (1,)), ((), ())), preferred_element_type=jnp.float32
    )


def transposed_times(left, right):
    return lax.dot_general(
        left, right, (((0,), (0,)), ((), ())), preferred_element_type=jnp.float32
    )


def silu_slope(values):
    sigma = jax.nn.sigmoid(values)
    return sigma * (1.0 + values * (1.0 - sigma))


def row_scale(values):
    return lax.rsqrt(jnp.mean(values * values, axis=-1, keepdims=True) + epsilon)


def block_scan(ssm_state, block_piece, decay_rate):
    in_block, step_block, key_block, query_block = block_piece
    cumulative = jnp.cumsum(step_block * decay_rate[None, :], axis=0)
    positions = jnp.arange(cumulative.shape[0])
    causal = positions[:, None] >= positions[None, :]
    decay_gap = cumulative.T[:, :, None] - cumulative.T[:, None, :]
    decay_table = jnp.where(causal[None], jnp.exp(jnp.where(causal[None], decay_gap, 0.0)), 0.0)
    intersection = jnp.dot(query_block, key_block.T, precision=highest)
    scaled = in_block * step_block[:, :, None]
    within = jnp.einsum("hij,jhp->ihp", decay_table * intersection[None], scaled, precision=highest)
    across = (
        jnp.einsum("in,hpn->ihp", query_block, ssm_state, precision=highest)
        * jnp.exp(cumulative)[:, :, None]
    )
    to_end = jnp.exp(cumulative[-1][None, :] - cumulative)
    new_state = ssm_state * jnp.exp(cumulative[-1])[:, None, None] + jnp.einsum(
        "jn,jhp->hpn", key_block, scaled * to_end[:, :, None], precision=highest
    )
    return (new_state, within + across)


def mixer(
    mixer_raw, step_raw, keys_raw, conv_taps, conv_shift, step_offset, decay_logs, skip_scale
):
    seq_length, width = mixer_raw.shape
    head_count = step_raw.shape[1]
    head_size = width // head_count
    state_dim = keys_raw.shape[1] // 2
    kernel = conv_taps.shape[0]
    joined = jnp.concatenate([mixer_raw, keys_raw], axis=1)
    padded = jnp.pad(joined, ((kernel - 1, 0), (0, 0)))
    convolved = conv_shift[None, :]
    for tap_index in range(kernel):
        convolved = (
            convolved + conv_taps[tap_index][None, :] * padded[tap_index : tap_index + seq_length]
        )
    active = jax.nn.silu(convolved)
    mixer_in = active[:, :width]
    step_size = jax.nn.softplus(step_raw + step_offset[None, :])
    decay_rate = -jnp.exp(decay_logs)
    blocks = seq_length // BLOCK
    pieces = (
        mixer_in.reshape(blocks, BLOCK, head_count, head_size),
        step_size.reshape(blocks, BLOCK, head_count),
        active[:, width : width + state_dim].reshape(blocks, BLOCK, state_dim),
        active[:, width + state_dim :].reshape(blocks, BLOCK, state_dim),
    )

    def one_block(ssm_state, block_piece):
        return block_scan(ssm_state, block_piece, decay_rate)

    initial = jnp.zeros((head_count, head_size, state_dim), jnp.float32)
    final_state, outputs = lax.scan(jax.checkpoint(one_block), initial, pieces)
    result = outputs.reshape(seq_length, head_count, head_size) + skip_scale[
        None, :, None
    ] * mixer_in.reshape(seq_length, head_count, head_size)
    return result.reshape(seq_length, width)


def on_device(
    block_input,
    lengths,
    routes,
    out_cotangent,
    mixer_gain,
    in_weight,
    conv_weight,
    conv_bias,
    step_bias,
    decay_log,
    skip_gain,
    norm_gain,
    out_weight,
    moe_gain,
    router_weight,
    shared_gate,
    shared_up,
    shared_down,
    expert_gate,
    expert_up,
    expert_down,
):
    sq = lax.axis_size("seq")
    sh = lax.axis_size("shard")
    q = lax.axis_index("seq")
    f32 = jnp.float32
    bf = jnp.bfloat16
    x_low = block_input[0]
    toks, dim = x_low.shape
    seq_rows = toks * sq
    heads = step_bias.shape[0] * sh
    inner = norm_gain.shape[0] * sh
    conv_all = conv_bias.shape[0] * sh
    keys_w = conv_all - inner
    gh = heads // sq
    gw = inner // sq
    rows_w = in_weight.shape[0]
    experts = router_weight.shape[1]
    local_e = expert_gate.shape[0]
    fs = shared_gate.shape[1]
    gf = fs // sq
    taps = conv_weight.shape[0]
    conv_own = conv_bias.shape[0]
    head_own = step_bias.shape[0]

    gain_col = mixer_gain.astype(f32)[:, None]

    def cols(start, width):
        return lax.dynamic_slice_in_dim(in_weight, start, width, 1)

    w_cols = jnp.concatenate(
        [
            cols(q * gw, gw),
            cols(inner + q * gw, gw),
            in_weight[:, 2 * inner : 2 * inner + keys_w],
            cols(2 * inner + keys_w + q * gh, gh),
        ],
        axis=1,
    )
    w_cols = (w_cols.astype(f32) * gain_col).astype(bf)
    used = 2 * gw + keys_w + gh
    small = jnp.concatenate(
        [conv_weight.reshape(-1), conv_bias, step_bias, decay_log, skip_gain]
    )
    small_cols = -(-small.shape[0] // rows_w)
    small = jnp.pad(small, (0, small_cols * rows_w - small.shape[0])).reshape(rows_w, small_cols)
    packed = jnp.concatenate(
        [w_cols, small, router_weight, moe_gain[:, None]], axis=1
    )
    at_small = used
    at_router = at_small + small_cols
    at_moe = at_router + experts
    total = -(-(at_moe + 1) // 128) * 128
    packed = jnp.pad(packed, ((0, 0), (0, total - packed.shape[1])))

    w_all = lax.all_gather(packed, "shard", axis=0, tiled=True)
    x_all = lax.all_gather(x_low, "seq", axis=0, tiled=True)

    out_scaled = (norm_gain.astype(f32)[:, None] * out_weight.astype(f32)).astype(bf)
    own_out = out_weight.shape[0] // sq
    own_down = shared_down.shape[0] // sq
    piece = jnp.concatenate(
        [
            lax.dynamic_slice_in_dim(out_scaled, q * own_out, own_out, 0),
            lax.dynamic_slice_in_dim(shared_down, q * own_down, own_down, 0),
        ],
        axis=0,
    )
    ratio = sh // sq
    forward_pairs = []
    for a in range(sh):
        for j in range(sq):
            s_to = sq * (a % ratio) + j
            q_to = a // ratio
            forward_pairs.append((j * sh + a, q_to * sh + s_to))
    backward_pairs = [(b, a) for a, b in forward_pairs]
    piece = lax.ppermute(piece, both_axes, forward_pairs)
    rows_all = lax.all_gather(piece, "shard", axis=0)
    w_out = rows_all[:, :own_out].reshape(gw, dim)
    w_down = rows_all[:, own_out:].reshape(gf, dim)
    shared_cols = jnp.concatenate(
        [
            lax.dynamic_slice_in_dim(shared_gate, q * gf, gf, 1),
            lax.dynamic_slice_in_dim(shared_up, q * gf, gf, 1),
        ],
        axis=1,
    )
    w_shared = lax.all_gather(shared_cols, "shard", axis=0, tiled=True)

    route_ids = routes[0]
    expert_ids = jnp.arange(experts, dtype=jnp.int32)
    named = jnp.any(route_ids[:, :, None] == expert_ids[None, None, :], axis=1).astype(f32)
    earlier = (
        jnp.arange(toks)[:, None] > jnp.arange(toks)[None, :]
    ).astype(f32)
    rank = jnp.dot(earlier, named)
    dispatch = (
        (named.T[:, None, :] > 0.0)
        & (rank.T[:, None, :] == jnp.arange(CAP, dtype=f32)[None, :, None])
    ).astype(bf)
    slots = experts * CAP
    dispatch_flat = dispatch.reshape(slots, toks)
    live = (q * toks + jnp.arange(toks, dtype=jnp.int32) < lengths[0]).astype(f32)
    cot = out_cotangent[0].astype(f32) * live[:, None]
    cot_low = cot.astype(bf)

    def to_experts(rows):
        return lax.all_to_all(
            rows.reshape(experts, CAP, rows.shape[-1]),
            "shard",
            split_axis=0,
            concat_axis=1,
            tiled=True,
        )

    cot_ext = jnp.concatenate(
        [cot_low, named.astype(bf), jnp.zeros((toks, 128 - experts), bf)], axis=1
    )
    cot_rows_ext = to_experts(times(dispatch_flat, cot_ext).astype(bf))
    cot_rows = cot_rows_ext[:, :, :dim]
    row_mask = cot_rows_ext[:, :, dim : dim + experts].astype(f32)
    cot_all = lax.all_gather(cot_low, "seq", axis=0, tiled=True)

    x_wide = x_all.astype(f32)
    x_r = row_scale(x_wide)
    proj = times(x_all, w_all) * x_r
    gate_in = proj[:, :gw]
    feed_low = proj[:, gw : 2 * gw + keys_w].astype(bf)
    step_low = proj[:, 2 * gw + keys_w : used].astype(bf)

    small_all = w_all.reshape(sh, rows_w, total)[:, :, at_small:at_router].reshape(sh, -1)
    at = taps * conv_own
    conv_full = (
        small_all[:, :at].reshape(sh, taps, conv_own).transpose(1, 0, 2).reshape(taps, conv_all)
    )
    offset_full = small_all[:, at : at + conv_own].reshape(conv_all)
    at = at + conv_own
    bias_full = small_all[:, at : at + head_own].reshape(heads)
    decay_full = small_all[:, at + head_own : at + 2 * head_own].reshape(heads)
    skip_full = small_all[:, at + 2 * head_own : at + 3 * head_own].reshape(heads)
    router_full = w_all[:, at_router:at_moe]
    moe_gain_full = w_all[:, at_moe].astype(f32)

    def group(values, width):
        return lax.dynamic_slice_in_dim(values, q * width, width, values.ndim - 1)

    conv_local = jnp.concatenate([group(conv_full, gw), conv_full[:, inner:]], axis=1).astype(f32)
    offset_local = jnp.concatenate([group(offset_full, gw), offset_full[inner:]]).astype(f32)
    bias_local = group(bias_full, gh).astype(f32)
    decay_local = group(decay_full, gh).astype(f32)
    skip_local = group(skip_full, gh).astype(f32)

    mixed_out, mixer_back = jax.vjp(
        mixer,
        feed_low[:, :gw].astype(f32),
        step_low.astype(f32),
        feed_low[:, gw:].astype(f32),
        conv_local,
        offset_local,
        bias_local,
        decay_local,
        skip_local,
    )
    mixed = mixed_out.astype(bf).astype(f32)

    gate_act = jax.nn.silu(gate_in)
    q_val = mixed * gate_act
    square = lax.psum(jnp.sum(q_val * q_val, axis=1).reshape(sq, toks), "seq")
    q_r = lax.rsqrt(square / inner + epsilon).reshape(seq_rows, 1)
    out_part = times(q_val.astype(bf), w_out).astype(bf)
    out_sum = lax.psum_scatter(out_part, "seq", scatter_dimension=0, tiled=True)
    tok_r = lax.dynamic_slice_in_dim(q_r, q * toks, toks, 0)
    x_tok = x_low.astype(f32)
    added = out_sum.astype(f32) * tok_r
    resid = x_tok + added

    resid_r = row_scale(resid)
    resid_n = resid * resid_r
    moe_in = (resid_n * moe_gain_full[None, :]).astype(bf)
    moe_all = lax.all_gather(moe_in, "seq", axis=0, tiled=True)
    logits = times(moe_in, router_full)

    def masked_softmax(values, mask):
        top = jnp.max(jnp.where(mask > 0.0, values, -jnp.inf), axis=-1, keepdims=True)
        top = jnp.where(top > -jnp.inf, top, 0.0)
        powers = jnp.where(mask > 0.0, jnp.exp(jnp.where(mask > 0.0, values - top, 0.0)), 0.0)
        return powers / jnp.maximum(jnp.sum(powers, axis=-1, keepdims=True), 1e-30)

    gates = masked_softmax(logits, named)
    rows = to_experts(times(dispatch_flat, moe_in).astype(bf))
    row_logits = lax.dot_general(
        rows, router_full, (((2,), (0,)), ((), ())), preferred_element_type=f32
    )
    row_gates = masked_softmax(row_logits, row_mask)
    own_ids = lax.axis_index("shard") * local_e + jnp.arange(local_e, dtype=jnp.int32)
    own_pick = (own_ids[:, None] == expert_ids[None, :]).astype(f32)
    row_gate = jnp.sum(row_gates * own_pick[:, None, :], axis=2, keepdims=True)

    d_raw = jnp.einsum("ecd,efd->ecf", cot_rows, expert_down, preferred_element_type=f32)
    e_gate = jnp.einsum("ecd,edf->ecf", rows, expert_gate, preferred_element_type=f32)
    e_up = jnp.einsum("ecd,edf->ecf", rows, expert_up, preferred_element_type=f32)
    e_sig = jax.nn.sigmoid(e_gate)
    e_silu = e_gate * e_sig
    e_act = (e_silu * e_up).astype(bf)
    d_gate_row = jnp.sum(e_act.astype(f32) * d_raw, axis=2, keepdims=True)
    d_act = row_gate * d_raw
    d_g = (d_act * e_up * (e_sig * (1.0 + e_gate * (1.0 - e_sig)))).astype(bf)
    d_v = (d_act * e_silu).astype(bf)
    d_row = jnp.einsum("ecf,edf->ecd", d_g, expert_gate, preferred_element_type=f32) + jnp.einsum(
        "ecf,edf->ecd", d_v, expert_up, preferred_element_type=f32
    )
    hi = d_gate_row.astype(bf)
    lo = (d_gate_row - hi.astype(f32)).astype(bf)
    back_rows = jnp.concatenate(
        [d_row.astype(bf), hi, lo, jnp.zeros(hi.shape[:2] + (126,), bf)], axis=2
    )

    def from_experts(values):
        return lax.all_to_all(values, "shard", split_axis=1, concat_axis=0, tiled=True)

    d_returned = from_experts(back_rows)
    e_out = jnp.einsum("ecf,efd->ecd", e_act, expert_down, preferred_element_type=f32).astype(bf)
    scaled_act = (row_gate * e_act.astype(f32)).astype(bf)
    grad_e_down = jnp.einsum("ecf,ecd->efd", scaled_act, cot_rows, preferred_element_type=f32)
    grad_e_gate = jnp.einsum("ecd,ecf->edf", rows, d_g, preferred_element_type=f32)
    grad_e_up = jnp.einsum("ecd,ecf->edf", rows, d_v, preferred_element_type=f32)
    e_sum = lax.psum(
        (grad_e_gate.astype(bf), grad_e_up.astype(bf), grad_e_down.astype(bf)), "seq"
    )

    s_both = times(moe_all, w_shared)
    s_gate, s_up = s_both[:, :gf], s_both[:, gf:]
    s_sig = jax.nn.sigmoid(s_gate)
    s_silu = s_gate * s_sig
    s_act = (s_silu * s_up).astype(bf)
    d_sh = times_transposed(cot_all, w_down)
    d_both = jnp.concatenate(
        [
            (d_sh * s_up * (s_sig * (1.0 + s_gate * (1.0 - s_sig)))).astype(bf),
            (d_sh * s_silu).astype(bf),
        ],
        axis=1,
    )
    d_moe_part = times_transposed(d_both, w_shared).astype(bf)
    d_moe_shared = lax.psum_scatter(d_moe_part, "seq", scatter_dimension=0, tiled=True)
    shared_part = times(s_act, w_down).astype(bf)
    shared_sum = lax.psum_scatter(shared_part, "seq", scatter_dimension=0, tiled=True)

    d_flat = d_returned.reshape(slots, dim + 128)
    gate_back = jnp.sum(
        d_flat[:, dim : dim + 2].astype(f32), axis=1
    ).reshape(experts, CAP)
    d_gates = jnp.sum(dispatch.astype(f32) * gate_back[:, :, None], axis=1).T
    d_logits = gates * (d_gates - jnp.sum(gates * d_gates, axis=1, keepdims=True))
    d_moe = (
        transposed_times(dispatch_flat, d_flat[:, :dim])
        + d_moe_shared.astype(f32)
        + jnp.dot(d_logits, router_full.astype(f32).T, precision=highest)
    )
    grad_router = jnp.dot(moe_in.astype(f32).T, d_logits, precision=highest)
    grad_moe = jnp.sum(d_moe * resid_n, axis=0)
    d_scaled = d_moe * moe_gain_full[None, :]
    d_resid = (
        cot
        + d_scaled * resid_r
        - resid_n * (resid_r * jnp.mean(d_scaled * resid_n, axis=1, keepdims=True))
    )
    d_o = d_resid.astype(bf)
    kappa = jnp.sum(d_o.astype(f32) * added, axis=1) / inner
    d_o_all = lax.all_gather(d_o, "seq", axis=0, tiled=True)
    kappa_all = lax.all_gather(kappa.reshape(1, toks), "seq", axis=0).reshape(seq_rows, 1)

    returned = from_experts(e_out)
    weighted = (gates.T[:, None, :] * dispatch.astype(f32)).reshape(slots, toks)
    combined = lax.dot_general(
        weighted,
        returned.reshape(slots, dim).astype(f32),
        (((0,), (0,)), ((), ())),
        preferred_element_type=f32,
    )
    block_output = ((resid + shared_sum.astype(f32) + combined) * live[:, None]).astype(bf)[None]

    d_gated = times_transposed(d_o_all, w_out)
    d_q = q_r * d_gated - q_val * (q_r * q_r * kappa_all)
    d_mixed = (d_q * gate_act).astype(bf)
    d_gate_in = d_q * mixed * silu_slope(gate_in)
    gated_low = (q_val * q_r).astype(bf)
    grad_out_part = transposed_times(gated_low, d_o_all)
    grad_down_part = transposed_times(s_act, cot_all)
    grad_shared_part = transposed_times(moe_all, d_both)

    def sum_over_shard(values):
        moved = lax.all_to_all(values.astype(bf), "shard", split_axis=0, concat_axis=0, tiled=True)
        return jnp.sum(moved.astype(f32), axis=0)

    rows_part = jnp.concatenate(
        [grad_out_part.reshape(sh, own_out, dim), grad_down_part.reshape(sh, own_down, dim)],
        axis=1,
    )
    rows_sum = sum_over_shard(rows_part)
    rows_sum = lax.ppermute(rows_sum.astype(bf), both_axes, backward_pairs)
    rows_grad = lax.all_gather(rows_sum, "seq", axis=0)
    grad_out_raw = rows_grad[:, :own_out].reshape(sq * own_out, dim).astype(f32)
    grad_down = rows_grad[:, own_out:].reshape(sq * own_down, dim).astype(f32)
    grad_out = norm_gain.astype(f32)[:, None] * grad_out_raw
    grad_norm = jnp.sum(out_weight.astype(f32) * grad_out_raw, axis=1)

    mid_part = jnp.concatenate(
        [
            grad_shared_part,
            grad_router,
            grad_moe[:, None],
            jnp.zeros((dim, 128 - experts - 1), f32),
        ],
        axis=1,
    )
    mid_sum = sum_over_shard(mid_part.reshape(sh, rows_w, 2 * gf + 128))
    mid_all = lax.all_gather(mid_sum.astype(bf), "seq", axis=0).astype(f32)
    grad_shared_gate = mid_all[:, :, :gf].transpose(1, 0, 2).reshape(rows_w, fs)
    grad_shared_up = mid_all[:, :, gf : 2 * gf].transpose(1, 0, 2).reshape(rows_w, fs)
    mid_rest = jnp.sum(mid_all[:, :, 2 * gf :], axis=0)
    grad_router_weight = mid_rest[:, :experts]
    grad_moe_gain = mid_rest[:, experts]

    (
        d_mixer_raw,
        d_step_raw,
        d_keys_raw,
        grad_conv_local,
        grad_offset_local,
        grad_bias_local,
        grad_decay_local,
        grad_skip_local,
    ) = mixer_back(d_mixed.astype(f32))
    d_proj = jnp.concatenate([d_gate_in, d_mixer_raw, d_keys_raw, d_step_raw], axis=1)
    d_proj = (d_proj * x_r).astype(bf)
    d_proj = jnp.pad(d_proj, ((0, 0), (0, total - used)))
    back_part = times_transposed(d_proj, w_all).astype(bf)
    back_sum = lax.psum_scatter(back_part, "seq", scatter_dimension=0, tiled=True).astype(f32)
    tok_x_r = row_scale(x_tok)
    x_n = x_tok * tok_x_r
    input_grad = (
        d_resid + back_sum - x_n * (tok_x_r * jnp.mean(back_sum * x_tok, axis=1, keepdims=True))
    )[None]

    grad_in_part = transposed_times(x_all, d_proj)[:, :used]

    def spread(local, count):
        wide = jnp.zeros(local.shape[:-1] + (count,), f32)
        return lax.dynamic_update_slice_in_dim(wide, local, q * local.shape[-1], local.ndim - 1)

    conv_rows = jnp.concatenate([grad_conv_local, grad_offset_local[None]], axis=0)
    conv_wide = jnp.concatenate([spread(conv_rows[:, :gw], inner), conv_rows[:, gw:]], axis=1)
    head_wide = spread(jnp.stack([grad_bias_local, grad_decay_local, grad_skip_local]), heads)
    small_part = jnp.concatenate(
        [
            conv_wide.reshape(taps + 1, sh, conv_own).transpose(1, 0, 2).reshape(sh, -1),
            head_wide.reshape(3, sh, head_own).transpose(1, 0, 2).reshape(sh, -1),
        ],
        axis=1,
    )
    small_count = small_part.shape[1]
    small_part = jnp.pad(
        small_part, ((0, 0), (0, rows_w * small_cols - small_count))
    ).reshape(sh, rows_w, small_cols)
    last_part = jnp.concatenate(
        [
            grad_in_part.reshape(sh, rows_w, used),
            small_part,
            jnp.zeros((sh, rows_w, total - used - small_cols), f32),
        ],
        axis=2,
    )
    last_sum = sum_over_shard(last_part)
    last_all = lax.all_gather(last_sum.astype(bf), "seq", axis=0).astype(f32)

    def side_by_side(start, width):
        return last_all[:, :, start : start + width].transpose(1, 0, 2).reshape(rows_w, sq * width)

    grad_in_raw = jnp.concatenate(
        [
            side_by_side(0, gw),
            side_by_side(gw, gw),
            jnp.sum(last_all[:, :, 2 * gw : 2 * gw + keys_w], axis=0),
            side_by_side(2 * gw + keys_w, gh),
        ],
        axis=1,
    )
    grad_in = gain_col * grad_in_raw
    grad_mixer_gain = jnp.sum(in_weight.astype(f32) * grad_in_raw, axis=1)
    small_sum = jnp.sum(last_all[:, :, used : used + small_cols], axis=0).reshape(-1)
    at = taps * conv_own
    grad_conv = small_sum[:at].reshape(taps, conv_own)
    grad_offset = small_sum[at : at + conv_own]
    at = at + conv_own
    grad_bias = small_sum[at : at + head_own]
    grad_decay = small_sum[at + head_own : at + 2 * head_own]
    grad_skip = small_sum[at + 2 * head_own : at + 3 * head_own]
    return (
        block_output,
        input_grad,
        grad_mixer_gain,
        grad_in,
        grad_conv,
        grad_offset,
        grad_bias,
        grad_decay,
        grad_skip,
        grad_norm,
        grad_out,
        grad_moe_gain,
        grad_router_weight,
        grad_shared_gate,
        grad_shared_up,
        grad_down,
        e_sum[0].astype(f32),
        e_sum[1].astype(f32),
        e_sum[2].astype(f32),
    )


def solution(mesh):
    placed = (
        P("shard", "seq", None),
        P("shard"),
        P("shard", "seq", None),
        P("shard", "seq", None),
        P("shard"),
        P("shard", None),
        P(None, "shard"),
        P("shard"),
        P("shard"),
        P("shard"),
        P("shard"),
        P("shard"),
        P("shard", None),
        P("shard"),
        P("shard", None),
        P("shard", None),
        P("shard", None),
        P("shard", None),
        P("shard", None, None),
        P("shard", None, None),
        P("shard", None, None),
    )
    return jax.shard_map(
        on_device,
        mesh=mesh,
        in_specs=placed,
        out_specs=(
            P("shard", "seq", None),
            P("shard", "seq", None),
            P("shard"),
            P("shard", None),
            P(None, "shard"),
            P("shard"),
            P("shard"),
            P("shard"),
            P("shard"),
            P("shard"),
            P("shard", None),
            P("shard"),
            P("shard", None),
            P("shard", None),
            P("shard", None),
            P("shard", None),
            P("shard", None, None),
            P("shard", None, None),
            P("shard", None, None),
        ),
        check_vma=False,
    )
```

time: 1920 us -> 1050 us (0.55)
  waiting for transfers between devices: 1040 us -> 251 us
  local copies, waits for them, and re-layouts: 292 us -> 245 us
  blocking collectives: 164 us -> 138 us
  matrix products: 204 us -> 184 us
    reduce_scatter x5 -> x4, waiting for transfers between devices: 524 us -> 17.3 us  [the longest x1 17.3 us: on_device(): out_sum = lax.psum_scatter(out_part, 'seq', scatter_dimension=0, tiled=True)]
    psum x1, waiting for transfers between devices: 225 us -> 0.01 us  [on_device(): lax.psum((grad_e_gate.astype(bf), grad_e_up.astype(bf), grad_e_down.astyp...]
    unnamed x17 -> x12, waiting for transfers between devices: 156 us -> 1.38 us
    all_gather x5 -> x7, waiting for transfers between devices: 29.7 us -> 119 us  [the longest x1 48.4 us: on_device(): w_all = lax.all_gather(packed, 'shard', axis=0, tiled=True)]
    unnamed x1 -> x0, blocking collectives: 62.9 us -> none
    unnamed x300 -> x259, local copies, waits for them, and re-layouts: 77.5 us -> 28.2 us
    all_gather x3 -> x4, blocking collectives: 76.9 us -> 125 us  [the longest x1 52.8 us: on_device(): w_shared = lax.all_gather(shared_cols, 'shard', axis=0, tiled=True)]
    concatenate x0 -> x9, local copies, waits for them, and re-layouts: none -> 27.5 us  [the longest x2 13.7 us: on_device(): jnp.concatenate([d_row.astype(bf), hi, lo, jnp.zeros(hi.shape[:2] + (126,...]
  transfers between devices with their start and end apart: 24 -> 21, of which waited for: 15 -> 10; matrix products, arithmetic and copies ran while one was open for 20% -> 37% of each run, Pallas kernels for 0% -> 0%
where the time goes in v1:
time: 1050 us; the launch traced here: 1030 us
  waiting for transfers between devices  251 us (24%)
  local copies, waits for them, and re-layouts  245 us (23%)
  matrix products  184 us (18%)
  other arithmetic  138 us (13%)
  blocking collectives  138 us (13%)
  starting transfers between devices  61 us (6%)
  between operations  16.8 us (2%)
    dynamic_update_slice x16, local copies, waits for them, and re-layouts, mixer(): final_state, outputs = lax.scan(jax.checkpoint(one_block), initial, pieces)  82.7 us
    all_gather x1, blocking collectives, on_device(): w_shared = lax.all_gather(shared_cols, 'shard', axis=0, tiled=True)  52.8 us
    all_gather x1, waiting for transfers between devices, on_device(): w_all = lax.all_gather(packed, 'shard', axis=0, tiled=True)  48.4 us
    another operation x37, other arithmetic  46.1 us
    all_gather x1, waiting for transfers between devices, on_device(): rows_all = lax.all_gather(piece, 'shard', axis=0)  42 us
    all_to_all x3, waiting for transfers between devices, sum_over_shard(): lax.all_to_all(values.astype(bf), 'shard', split_axis=0, concat_axis=0, t...  41 us
    all_to_all x2, waiting for transfers between devices, to_experts(): lax.all_to_all(rows.reshape(experts, CAP, rows.shape[-1]), 'shard', split...  34.5 us
    all_to_all x2, waiting for transfers between devices, from_experts(): lax.all_to_all(values, 'shard', split_axis=1, concat_axis=0, tiled=True)  34 us
  transfers between devices with their start and end apart: 21, of which 10 were waited for; matrix products, arithmetic and copies ran while one was open for 37% of the time, Pallas kernels for 0%

profile of v1, /device:TPU:1, one launch (start us, length us, event | category | flops | bytes accessed | tf_op | source)
XLA Modules:
  0.0 1034.6 jit_solution(16707008996625033785)
XLA Ops:
  28.8 42.0 %all-gather.25.cloned.1.call-done = bf16[512,1536]{1,0:T(8,128)(2,1)} async-done(((bf16[32,1536]{1,0:T(8,128)(2,1)}), bf16[512,1536]{1,0:T(8,128)(2,1)}) %all-gather.25.cloned.1.call-update) | async-done | bytes 1572880 | tf_op jit(solution)/shard_map/all_gather | solution.py:197
  73.2 28.1 %all-gather.23.cloned.1.call-done = bf16[1,1024,1536]{2,1,0:T(8,128)(2,1)} async-done(((bf16[1,128,1536]{2,1,0:T(8,128)(2,1)}), bf16[1,1024,1536]{2,1,0:T(8,128)(2,1)}) %all-gather.23.cloned.1.call-update) | async-done | bytes 3145744 | tf_op jit(solution)/shard_map/all_gather | solution.py:176
  103.9 48.4 %all-gather.15.cloned.1.call-done = bf16[1536,1152]{1,0:T(8,128)(2,1)} async-done(((bf16[96,1152]{1,0:T(8,128)(2,1)}), bf16[1536,1152]{1,0:T(8,128)(2,1)}) %all-gather.15.cloned.1.call-update) | async-done | bytes 3538960 | tf_op jit(solution)/shard_map/all_gather | solution.py:175
  156.2 9.4 fusion.200
  186.4 85.0 %while.44 = (s32[]{:T(128)}, f32[6,64,128]{2,1,0:T(8,128)S(1)}, f32[4,256,6,64]{1,0,3,2:T(4,128)}, f32[4,6,64,128]{3,2,1,0:T(8,128)}, f32[4,256,6]{1,2,0:T(8,128...) while((s32[]{:T(128)}, f32[6,64,128]{2,1,0:T(8,128)S(1)}, ...), condition=%wide.region_4.5_spmd.clone.clone, body=%wide.region_1.0_spmd.clone.clone.sunk | while | flops 707152896 | bytes 5768572 | solution.py:92
  198.1 9.5 dynamic_update_slice.84
  219.3 9.5 dynamic_update_slice.84
  240.5 9.5 dynamic_update_slice.84
  261.8 9.5 dynamic_update_slice.84
  286.3 13.1 %psum.28 = f32[8,128]{1,0:T(8,128)S(1)} all-reduce(f32[8,128]{1,0:T(8,128)S(1)} %bitcast.621), channel_id=1, replica_groups=mesh['seq'=8,'shard'=16] {'seq'}, use_global_device_ids=true, to_apply=%region_7.8 | all-reduce | flops 1024 | bytes 8192 | tf_op jit(solution)/shard_map/psum | solution.py:287
  301.3 17.3 %reduce-scatter.5.cloned.1.call-done = bf16[128,1536]{1,0:T(8,128)(2,1)} async-done(((bf16[1024,1536]{1,0:T(8,128)(2,1)}), bf16[128,1536]{1,0:T(8,128)(2,1)}) %reduce-scatter.5.cloned.1.call-update) | async-done | bytes 393232 | tf_op jit(solution)/shard_map/reduce_scatter | solution.py:290
  348.4 34.5 %all-to-all-done.2 = bf16[32,32,1664]{2,1,0:T(8,128)(2,1)} async-done(((bf16[32,32,1664]{2,1,0:T(8,128)(2,1)}), bf16[32,32,1664]{2,1,0:T(8,128)(2,1)}, u32[]{:S(2)}, u32[]{:S(2)}) %all-to-all-start.2) | async-done | bytes 3407904 | tf_op jit(solution)/shard_map/all_to_all | solution.py:227
  382.9 9.5 all-to-all-start
  393.3 52.8 %all_gather.50 = bf16[1536,256]{1,0:T(8,128)(2,1)} all-gather(bf16[96,256]{1,0:T(8,128)(2,1)S(1)} %pad_maximum_fusion.7), channel_id=1, replica_groups=mesh['seq'=8,'shard'=16] {'shard'}, dimensions={0}, use_global_device_ids=true | all-gather | bytes 835584 | tf_op jit(solution)/shard_map/all_gather | solution.py:207
  477.3 7.6 fusion.123
  517.9 34.0 %all-to-all-done.3 = bf16[2,512,1664]{2,0,1:T(2,128)(2,1)} async-done(((bf16[2,512,1664]{2,0,1:T(2,128)(2,1)}), bf16[2,512,1664]{2,0,1:T(2,128)(2,1)}, u32[]{:S(2)}, u32[]{:S(2)}) %all-to-all-start.3) | async-done | bytes 3407904 | tf_op jit(solution)/shard_map/all_to_all | solution.py:338
  593.9 8.8 all-to-all-start.1
  612.7 33.6 %all-gather.6 = f32[8,1,128]{2,1,0:T(1,128)S(1)} all-gather(f32[1,1,128]{2,1,0:T(1,128)S(1)} %multiply_bitcast_fusion.4), channel_id=4, replica_groups=mesh['seq'=8,'shard'=16] {'seq'}, dimensions={0}, use_global_device_ids=true | all-gather | bytes 4608 | tf_op jit(solution)/shard_map/all_gather | solution.py:390
  648.5 8.2 multiply_reduce_fusion.11
  663.5 146.2 %while.43 = (s32[]{:T(128)}, f32[6]{0:T(128)S(1)}, f32[6,64,128]{2,1,0:T(8,128)S(1)}, f32[4,256,6,64]{1,0,3,2:T(4,128)}, f32[4,256,6]{1,2,0:T(8,128)S(1)}, /*ind...) while((s32[]{:T(128)}, f32[6]{0:T(128)S(1)}, ...), condition=%wide.region_37.38_spmd.clone, body=%wide.region_23.37_spmd.clone.sunk | while | flops 1669043200 | bytes 14915856 | solution.py:92
  677.4 7.6 reduce-window.74
  686.3 9.6 dynamic_update_slice.82
  714.0 7.6 reduce-window.74
  722.9 9.5 dynamic_update_slice.82
  750.4 7.6 reduce-window.74
  759.3 9.6 dynamic_update_slice.82
  795.7 9.5 dynamic_update_slice.82
  865.1 8.4 all-to-all-done.6
  886.9 32.5 %all-to-all-done.4 = bf16[16,96,1152]{2,1,0:T(8,128)(2,1)} async-done(((bf16[16,96,1152]{2,1,0:T(8,128)(2,1)}), bf16[16,96,1152]{2,1,0:T(8,128)(2,1)}, u32[]{:S(2)}, u32[]{:S(2)}) %all-to-all-start.4) | async-done | bytes 3538976 | tf_op jit(solution)/shard_map/all_to_all | solution.py:412
  919.5 8.2 all-to-all-start.5
  954.1 19.7 %all-gather.5 = bf16[768,384]{1,0:T(8,128)(2,1)S(1)} all-gather(bf16[96,384]{1,0:T(8,128)(2,1)S(1)} %reduce_sum.520), channel_id=7, replica_groups=mesh['seq'=8,'shard'=16] {'seq'}, dimensions={0}, use_global_device_ids=true | all-gather | bytes 663552 | tf_op jit(solution)/shard_map/all_gather | solution.py:437
  984.9 18.5 %all-gather.4 = bf16[256,1536]{1,0:T(8,128)(2,1)S(1)} all-gather(bf16[32,1536]{1,0:T(8,128)(2,1)S(1)} %collective-permute-done.1), channel_id=6, replica_groups=mesh['seq'=8,'shard'=16] {'seq'}, dimensions={0}, use_global_device_ids=true | all-gather | bytes 884736 | tf_op jit(solution)/shard_map/all_gather | solution.py:421
  (783 shorter events, 483.2 us)
Async XLA Ops:
  7.2 470.1 %copy-start = (bf16[2,512,1536]{2,1,0:T(8,128)(2,1)S(1)}, bf16[2,512,1536]{2,1,0:T(8,128)(2,1)}, u32[]{:S(2)}) copy-start(bf16[2,512,1536]{2,1,0:T(8,128)(2,1)} %param.45) | copy-start | bytes 9437188
  7.3 63.5 %all-gather.25.cloned.1.call-start = ((), (), s32[]{:S(2)}) async-start(), calls=%async_computation.20 | async-start | bytes 1671168 | tf_op jit(solution)/shard_map/all_gather | solution.py:197
  12.2 8.5 collective-permute-start
  21.4 79.9 %all-gather.23.cloned.1.call-start = ((), (), s32[]{:S(2)}) async-start(), calls=%async_computation.19 | async-start | bytes 3538944 | tf_op jit(solution)/shard_map/all_gather | solution.py:176
  22.1 130.1 %all-gather.15.cloned.1.call-start = ((), (), s32[]{:S(2)}) async-start(), calls=%async_computation.11 | async-start | bytes 3760128 | tf_op jit(solution)/shard_map/all_gather | solution.py:175
  22.2 81.6 %copy-start.111 = (f32[96]{0:T(128)}, f32[96]{0:T(128)S(1)}, u32[]{:S(2)}) copy-start(f32[96]{0:T(128)S(1)} %convert_element_type.318) | copy-start | bytes 1156
  28.7 289.9 %reduce-scatter.5.cloned.1.call-start = ((), (), s32[]{:S(2)}) async-start(), calls=%async_computation.12 | async-start | bytes 3538944 | tf_op jit(solution)/shard_map/reduce_scatter | solution.py:290
  103.9 61.7 %copy-start.83 = (f32[1024]{0:T(1024)}, f32[1024]{0:T(1024)S(1)}, u32[]{:S(2)}) copy-start(f32[1024]{0:T(1024)S(1)} %add_rsqrt_fusion.1) | copy-start | bytes 12292
  286.2 178.1 %all-gather.17.cloned.1.call-start = ((), (), s32[]{:S(2)}) async-start(), calls=%async_computation.13 | async-start | bytes 3538944 | tf_op jit(solution)/shard_map/all_gather | solution.py:299
  337.5 45.4 %all-to-all-start.2 = ((bf16[32,32,1664]{2,1,0:T(8,128)(2,1)}), bf16[32,32,1664]{2,1,0:T(8,128)(2,1)}, u32[]{:S(2)}, u32[]{:S(2)}) async-start(bf16[32,32,1664]{2,1,0:T(8,128)(2,1)} %bitcast.563), calls=%async_computation.4 | async-start | bytes 6815744 | tf_op jit(solution)/shard_map/all_to_all | solution.py:227
  344.2 124.3 %all-gather.19.cloned.1.call-start = ((), (), s32[]{:S(2)}) async-start(), calls=%async_computation.15 | async-start | bytes 3538944 | tf_op jit(solution)/shard_map/all_gather | solution.py:241
  382.9 69.6 %all-to-all-start = ((bf16[32,32,1536]{2,1,0:T(8,128)(2,1)}), bf16[32,32,1536]{2,1,0:T(8,128)(2,1)}, u32[]{:S(2)}, u32[]{:S(2)}) async-start(bf16[32,32,1536]{2,1,0:T(8,128)(2,1)} %bitcast.570), calls=%async_computation.2 | async-start | bytes 6291456 | tf_op jit(solution)/shard_map/all_to_all | solution.py:227
  392.4 171.0 %reduce-scatter.9.cloned.1.call-start = ((), (), s32[]{:S(2)}) async-start(), calls=%async_computation.16 | async-start | bytes 3538944 | tf_op jit(solution)/shard_map/reduce_scatter | solution.py:364
  509.5 42.3 %all-to-all-start.3 = ((bf16[2,512,1664]{2,0,1:T(2,128)(2,1)}), bf16[2,512,1664]{2,0,1:T(2,128)(2,1)}, u32[]{:S(2)}, u32[]{:S(2)}) async-start(bf16[2,512,1664]{2,0,1:T(2,128)(2,1)} %copy.490), calls=%async_computation.5 | async-start | bytes 6815744 | tf_op jit(solution)/shard_map/all_to_all | solution.py:338
  514.4 134.1 %all-gather.21.cloned.1.call-start = ((), (), s32[]{:S(2)}) async-start(), calls=%async_computation.17 | async-start | bytes 3538944 | tf_op jit(solution)/shard_map/all_gather | solution.py:389
  569.5 364.1 %all-reduce.21.cloned.1.call-start = ((), (), s32[]{:S(2)}) async-start(), calls=%async_computation.22 | async-start | bytes 18874368 | tf_op jit(solution)/shard_map/psum | solution.py:346
  593.9 255.7 %all-to-all-start.1 = ((bf16[2,512,1536]{2,0,1:T(2,128)(2,1)}), bf16[2,512,1536]{2,0,1:T(2,128)(2,1)}, u32[]{:S(2)}, u32[]{:S(2)}) async-start(bf16[2,512,1536]{2,0,1:T(2,128)(2,1)} %copy.480), calls=%async_computation.3 | async-start | bytes 6291456 | tf_op jit(solution)/shard_map/all_to_all | solution.py:338
  602.6 347.3 %reduce-scatter.7.cloned.1.call-start = ((), (), s32[]{:S(2)}) async-start(), calls=%async_computation.14 | async-start | bytes 3538944 | tf_op jit(solution)/shard_map/reduce_scatter | solution.py:366
  606.6 41.8 %copy-start.6 = (f32[1024,640]{1,0:T(8,128)S(1)}, f32[1024,640]{1,0:T(8,128)}, u32[]{:S(2)}) copy-start(f32[1024,640]{1,0:T(8,128)} %copy-done.5) | copy-start | bytes 7864324
  606.6 41.8 %copy-start.59 = (f32[1024]{0:T(1024)S(1)}, f32[1024]{0:T(1024)}, u32[]{:S(2)}) copy-start(f32[1024]{0:T(1024)} %get-tuple-element.968) | copy-start | bytes 12292
  606.7 399.5 %reduce-scatter.11.cloned.1.call-start = ((), (), s32[]{:S(2)}) async-start(), calls=%async_computation.18 | async-start | bytes 3538944 | tf_op jit(solution)/shard_map/reduce_scatter | solution.py:458
  849.5 24.0 %all-to-all-start.6 = ((bf16[16,96,384]{2,1,0:T(8,128)(2,1)}), bf16[16,96,384]{2,1,0:T(8,128)(2,1)S(1)}, u32[]{:S(2)}, u32[]{:S(2)}) async-start(bf16[16,96,384]{2,1,0:T(8,128)(2,1)} %maximum_maximum_fusion), calls=%async_computation.10 | async-start | bytes 2359296 | tf_op jit(solution)/shard_map/all_to_all | solution.py:412
  874.5 44.9 %all-to-all-start.4 = ((bf16[16,96,1152]{2,1,0:T(8,128)(2,1)}), bf16[16,96,1152]{2,1,0:T(8,128)(2,1)}, u32[]{:S(2)}, u32[]{:S(2)}) async-start(bf16[16,96,1152]{2,1,0:T(8,128)(2,1)} %concatenate.93), calls=%async_computation.8 | async-start | bytes 7077888 | tf_op jit(solution)/shard_map/all_to_all | solution.py:412
  885.5 42.2 %copy-start.123 = (bf16[192]{0:T(256)(128)(2,1)S(1)}, bf16[192]{0:T(256)(128)(2,1)}, u32[]{:S(2)}) copy-start(bf16[192]{0:T(256)(128)(2,1)} %param.36) | copy-start | bytes 1156
  885.6 42.8 %copy-start.47 = (pred[128,32]{0,1:T(8,128)(4,1)S(1)}, pred[128,32]{0,1:T(8,128)(4,1)}, u32[]{:S(2)}) copy-start(pred[128,32]{0,1:T(8,128)(4,1)} %copy-done.45) | copy-start | bytes 12292
  885.6 42.7 %copy-start.86 = (f32[128]{0:T(128)S(1)}, f32[128]{0:T(128)}, u32[]{:S(2)}) copy-start(f32[128]{0:T(128)} %copy-done.84) | copy-start | bytes 1540
  885.6 42.7 %copy-start.89 = (f32[128]{0:T(128)S(1)}, f32[128]{0:T(128)}, u32[]{:S(2)}) copy-start(f32[128]{0:T(128)} %broadcast_maximum_fusion.1) | copy-start | bytes 1540
  885.6 42.7 %copy-start.53 = (f32[32,128]{1,0:T(8,128)S(1)}, f32[32,128]{1,0:T(8,128)}, u32[]{:S(2)}) copy-start(f32[32,128]{1,0:T(8,128)} %copy-done.52) | copy-start | bytes 49156
  885.6 42.7 %copy-start.62 = (pred[32,128]{1,0:T(8,128)(4,1)S(1)}, pred[32,128]{1,0:T(8,128)(4,1)}, u32[]{:S(2)}) copy-start(pred[32,128]{1,0:T(8,128)(4,1)} %copy-done.61) | copy-start | bytes 12292
  919.5 56.8 %all-to-all-start.5 = ((bf16[16,32,1536]{2,1,0:T(8,128)(2,1)}), bf16[16,32,1536]{2,1,0:T(8,128)(2,1)}, u32[]{:S(2)}, u32[]{:S(2)}) async-start(bf16[16,32,1536]{2,1,0:T(8,128)(2,1)} %pad_maximum_fusion.1), calls=%async_computation.9 | async-start | bytes 3145728 | tf_op jit(solution)/shard_map/all_to_all | solution.py:412
  927.7 81.9 %all-gather.27.cloned.1.call-start = ((), (), s32[]{:S(2)}) async-start(), calls=%async_computation.21 | async-start | bytes 1990656 | tf_op jit(solution)/shard_map/all_gather | solution.py:494
  977.9 6.9 collective-permute-start.1
  (117 other events, 809.5 us)
Sparse Core Ops, SparseCore 0:
  21.5 49.2 all-gather.24
  72.5 28.7 all-gather.22
  104.0 48.1 all-gather.14
  286.4 32.1 reduce-scatter.4
  323.1 30.2 all-gather.16
  355.6 27.8 all-gather.18
  476.4 52.4 reduce-scatter.8
  569.7 53.5 all-gather.20
  625.9 113.5 all-reduce.20
  741.7 32.9 reduce-scatter.6
  834.4 32.0 reduce-scatter.10
  950.1 33.2 all-gather.26

commit v2 on v1

--- a/solution.py
+++ b/solution.py
@@ -1,9 +1,10 @@
 import jax
 import jax.numpy as jnp
 from jax import lax
+from jax.experimental import pallas as pl
+from jax.experimental.pallas import tpu as pltpu
 from jax.sharding import PartitionSpec as P
 
-BLOCK = 256
 CAP = 32
 
 
@@ -37,63 +38,328 @@
     return lax.rsqrt(jnp.mean(values * values, axis=-1, keepdims=True) + epsilon)
 
 
-def block_scan(ssm_state, block_piece, decay_rate):
-    in_block, step_block, key_block, query_block = block_piece
-    cumulative = jnp.cumsum(step_block * decay_rate[None, :], axis=0)
-    positions = jnp.arange(cumulative.shape[0])
-    causal = positions[:, None] >= positions[None, :]
-    decay_gap = cumulative.T[:, :, None] - cumulative.T[:, None, :]
-    decay_table = jnp.where(causal[None], jnp.exp(jnp.where(causal[None], decay_gap, 0.0)), 0.0)
-    intersection = jnp.dot(query_block, key_block.T, precision=highest)
-    scaled = in_block * step_block[:, :, None]
-    within = jnp.einsum("hij,jhp->ihp", decay_table * intersection[None], scaled, precision=highest)
-    across = (
-        jnp.einsum("in,hpn->ihp", query_block, ssm_state, precision=highest)
-        * jnp.exp(cumulative)[:, :, None]
-    )
-    to_end = jnp.exp(cumulative[-1][None, :] - cumulative)
-    new_state = ssm_state * jnp.exp(cumulative[-1])[:, None, None] + jnp.einsum(
-        "jn,jhp->hpn", key_block, scaled * to_end[:, :, None], precision=highest
-    )
-    return (new_state, within + across)
-
-
-def mixer(
-    mixer_raw, step_raw, keys_raw, conv_taps, conv_shift, step_offset, decay_logs, skip_scale
+CHUNK = 128
+WIDE = 384
+CONVW = 640
+PAIRS = 3
+HEADS_HERE = 6
+
+
+def split_two(values):
+    high = values.astype(jnp.bfloat16)
+    return high, (values - high.astype(jnp.float32)).astype(jnp.bfloat16)
+
+
+def ones_times(ones, values):
+    high, low = split_two(values)
+    return times(ones, high) + times(ones, low)
+
+
+def times_ones(values, ones):
+    high, low = split_two(values)
+    return times(high, ones) + times(low, ones)
+
+
+def transposed_times_ones(values, ones):
+    high, low = split_two(values)
+    return transposed_times(high, ones) + transposed_times(low, ones)
+
+
+def grid_of(shape):
+    rows = lax.broadcasted_iota(jnp.int32, shape, 0)
+    columns = lax.broadcasted_iota(jnp.int32, shape, 1)
+    return rows, columns
+
+
+def mark(condition):
+    return jnp.where(condition, 1.0, 0.0).astype(jnp.bfloat16)
+
+
+def chunk_parts(proj, prev, has_prev, taps_ref, head_ref, pad_ref):
+    f32, bf = jnp.float32, jnp.bfloat16
+    feed = proj[:, WIDE : WIDE + CONVW].astype(bf).astype(f32)
+    before = prev[:, WIDE : WIDE + CONVW].astype(bf).astype(f32)
+    pad_ref[0:8, :] = jnp.where(has_prev, before, 0.0)
+    pad_ref[8 : 8 + CHUNK, :] = feed
+    conv = taps_ref[4:5, :]
+    for tap in range(4):
+        conv = conv + taps_ref[tap : tap + 1, :] * pad_ref[5 + tap : 5 + tap + CHUNK, :]
+    sig = jax.nn.sigmoid(conv)
+    act = conv * sig
+    u = act[:, :WIDE]
+    key = act[:, WIDE : WIDE + 128].astype(bf)
+    query = act[:, WIDE + 128 :].astype(bf)
+    step_low = proj[:, WIDE + CONVW :].astype(bf).astype(f32)
+    pre = step_low + head_ref[0:1, :]
+    rows, columns = grid_of((CHUNK, 128))
+    here = columns < HEADS_HERE
+    dt = jnp.where(here, jnp.maximum(pre, 0.0) + jnp.log1p(jnp.exp(-jnp.abs(pre))), 0.0)
+    la = dt * head_ref[1:2, :]
+    lower = mark(rows >= columns)
+    cum = ones_times(lower, la)
+    end = cum[CHUNK - 1 : CHUNK, :]
+    wide_rows, wide_columns = grid_of((128, WIDE))
+    widen = mark(wide_columns // 64 == wide_rows)
+    dt_w = times_ones(dt, widen)
+    e_w = times_ones(jnp.exp(cum), widen)
+    w_w = times_ones(jnp.exp(end - cum), widen)
+    full_rows, full_columns = grid_of((128, 2 * PAIRS * 128))
+    la_full = times_ones(la, mark(full_columns // 128 == full_rows))
+    scores = times_transposed(query, key)
+    return dict(
+        conv=conv, sig=sig, u=u, key=key, query=query, pre=pre, here=here, dt=dt, lower=lower,
+        dt_w=dt_w, e_w=e_w, w_w=w_w, la_full=la_full, scores=scores, xs=u * dt_w,
+    )
+
+
+def pair_table(parts, pair):
+    rows, columns = grid_of((CHUNK, 256))
+    local = columns % 128
+    steps = jnp.where(rows > local, parts["la_full"][:, 256 * pair : 256 * pair + 256], 0.0)
+    gap = ones_times(parts["lower"], steps)
+    causal = rows >= local
+    decay = jnp.where(causal, jnp.exp(jnp.where(causal, gap, 0.0)), 0.0)
+    scores = parts["scores"]
+    return decay, decay * jnp.concatenate([scores, scores], axis=1)
+
+
+def stack_heads(values, pair):
+    both = values[:, 128 * pair : 128 * pair + 128]
+    first = lax.broadcasted_iota(jnp.int32, both.shape, 1) < 64
+    return jnp.concatenate(
+        [jnp.where(first, both, 0.0), jnp.where(first, 0.0, both)], axis=0
+    ).astype(jnp.bfloat16)
+
+
+def scan_forward_kernel(
+    proj_ref, prev_ref, taps_ref, head_ref, skip_ref,
+    mixed_ref, q_ref, square_ref, start_ref, state_ref, pad_ref,
 ):
-    seq_length, width = mixer_raw.shape
-    head_count = step_raw.shape[1]
-    head_size = width // head_count
-    state_dim = keys_raw.shape[1] // 2
-    kernel = conv_taps.shape[0]
-    joined = jnp.concatenate([mixer_raw, keys_raw], axis=1)
-    padded = jnp.pad(joined, ((kernel - 1, 0), (0, 0)))
-    convolved = conv_shift[None, :]
-    for tap_index in range(kernel):
-        convolved = (
-            convolved + conv_taps[tap_index][None, :] * padded[tap_index : tap_index + seq_length]
+    f32, bf = jnp.float32, jnp.bfloat16
+    chunk = pl.program_id(0)
+
+    @pl.when(chunk == 0)
+    def _():
+        state_ref[...] = jnp.zeros(state_ref.shape, f32)
+
+    parts = chunk_parts(
+        proj_ref[...], prev_ref[...], chunk > 0, taps_ref, head_ref, pad_ref
+    )
+    state = state_ref[...]
+    start_ref[0] = state
+    xs = parts["xs"]
+    inside = []
+    for pair in range(PAIRS):
+        _, table = pair_table(parts, pair)
+        inside.append(times(table.astype(bf), stack_heads(xs, pair)))
+    across = times(parts["query"], state.astype(bf))
+    y = (
+        jnp.concatenate(inside, axis=1)
+        + parts["e_w"] * across
+        + skip_ref[0:1, :] * parts["u"]
+    )
+    mixed = y.astype(bf)
+    mixed_ref[...] = mixed
+    gate = proj_ref[:, :WIDE]
+    q_val = mixed.astype(f32) * (gate * jax.nn.sigmoid(gate))
+    q_ref[...] = q_val.astype(bf)
+    square_ref[...] = jnp.sum(q_val * q_val, axis=1, keepdims=True)
+    state_ref[...] = state * parts["e_w"][CHUNK - 1 : CHUNK, :] + transposed_times(
+        parts["key"], (xs * parts["w_w"]).astype(bf)
+    )
+
+
+def scan_backward_kernel(
+    proj_ref, prev_ref, mixed_ref, d_gated_ref, rows_ref, start_ref, taps_ref, head_ref, skip_ref,
+    d_proj_ref, d_taps_ref, d_head_ref, d_skip_ref,
+    state_ref, pad_ref, late_ref,
+):
+    f32, bf = jnp.float32, jnp.bfloat16
+    step = pl.program_id(0)
+    last = pl.num_programs(0) - 1
+
+    @pl.when(step == 0)
+    def _():
+        state_ref[...] = jnp.zeros(state_ref.shape, f32)
+        late_ref[CHUNK : CHUNK + 8, :] = jnp.zeros((8, CONVW), f32)
+        d_taps_ref[...] = jnp.zeros(d_taps_ref.shape, f32)
+        d_head_ref[...] = jnp.zeros(d_head_ref.shape, f32)
+        d_skip_ref[...] = jnp.zeros(d_skip_ref.shape, f32)
+
+    parts = chunk_parts(
+        proj_ref[...], prev_ref[...], step < last, taps_ref, head_ref, pad_ref
+    )
+    u, key, query, xs = parts["u"], parts["key"], parts["query"], parts["xs"]
+    e_w, w_w, dt_w = parts["e_w"], parts["w_w"], parts["dt_w"]
+
+    gate = proj_ref[:, :WIDE]
+    gate_sig = jax.nn.sigmoid(gate)
+    gate_act = gate * gate_sig
+    mixed = mixed_ref[...].astype(f32)
+    q_val = mixed * gate_act
+    q_r = rows_ref[:, 0:1]
+    d_q = q_r * d_gated_ref[...] - q_val * (q_r * q_r * rows_ref[:, 1:2])
+    d_gate = d_q * mixed * (gate_sig * (1.0 + gate * (1.0 - gate_sig)))
+    d_y = (d_q * gate_act).astype(bf).astype(f32)
+
+    start = start_ref[0]
+    start_low = start.astype(bf)
+    d_end = state_ref[...]
+    d_end_low = d_end.astype(bf)
+    xw = xs * w_w
+    ye = d_y * e_w
+    ye_low = ye.astype(bf)
+    across = times(query, start_low)
+    pulled = times(key, d_end_low)
+    d_query = times_transposed(ye_low, start_low)
+    d_key = times_transposed(xw.astype(bf), d_end_low)
+    state_ref[...] = d_end * e_w[CHUNK - 1 : CHUNK, :] + transposed_times(query, ye_low)
+    d_scores = jnp.zeros((CHUNK, 128), f32)
+    turns = jnp.zeros((CHUNK, 128), f32)
+    d_xs = []
+    for pair in range(PAIRS):
+        decay, table = pair_table(parts, pair)
+        xs_two = stack_heads(xs, pair)
+        dy_two = stack_heads(d_y, pair)
+        d_table = times_transposed(d_y[:, 128 * pair : 128 * pair + 128].astype(bf), xs_two)
+        d_decay = d_table * decay
+        d_scores = d_scores + d_decay[:, :128] + d_decay[:, 128:]
+        d_gap = d_table * table
+        table_low = table.astype(bf)
+        d_xs.append(
+            transposed_times(
+                jnp.concatenate([table_low[:, :128], table_low[:, 128:]], axis=0), dy_two
+            )
         )
-    active = jax.nn.silu(convolved)
-    mixer_in = active[:, :width]
-    step_size = jax.nn.softplus(step_raw + step_offset[None, :])
-    decay_rate = -jnp.exp(decay_logs)
-    blocks = seq_length // BLOCK
-    pieces = (
-        mixer_in.reshape(blocks, BLOCK, head_count, head_size),
-        step_size.reshape(blocks, BLOCK, head_count),
-        active[:, width : width + state_dim].reshape(blocks, BLOCK, state_dim),
-        active[:, width + state_dim :].reshape(blocks, BLOCK, state_dim),
-    )
-
-    def one_block(ssm_state, block_piece):
-        return block_scan(ssm_state, block_piece, decay_rate)
-
-    initial = jnp.zeros((head_count, head_size, state_dim), jnp.float32)
-    final_state, outputs = lax.scan(jax.checkpoint(one_block), initial, pieces)
-    result = outputs.reshape(seq_length, head_count, head_size) + skip_scale[
-        None, :, None
-    ] * mixer_in.reshape(seq_length, head_count, head_size)
-    return result.reshape(seq_length, width)
+        two_rows, two_columns = grid_of((256, 128))
+        own = mark(two_columns == 2 * pair + two_rows // 128)
+        turns = turns + times_ones(d_gap, own)
+        turns = turns - transposed_times_ones(
+            jnp.concatenate([d_gap[:, :128], d_gap[:, 128:]], axis=0), own
+        )
+    d_xs = jnp.concatenate(d_xs, axis=1) + w_w * pulled
+    d_scores_low = d_scores.astype(bf)
+    d_query = d_query + times(d_scores_low, key)
+    d_key = d_key + transposed_times(d_scores_low, query)
+
+    rows, columns = grid_of((CHUNK, 128))
+    upper = mark(columns >= rows)
+    strict = mark(columns < rows)
+    sum_rows, sum_columns = grid_of((WIDE, 128))
+    per_head = mark(sum_rows // 64 == sum_columns)
+    end_row = jnp.sum(d_end * start, axis=0, keepdims=True) * e_w[CHUNK - 1 : CHUNK, :]
+    wide = ones_times(upper, ye * across) + ones_times(strict, xw * pulled) + end_row
+    d_la = ones_times(upper, turns) + times_ones(wide, per_head)
+    d_dt = times_ones(d_xs * u, per_head) + d_la * head_ref[1:2, :]
+    d_pre = jnp.where(parts["here"], d_dt * jax.nn.sigmoid(parts["pre"]), 0.0)
+    d_head_ref[0:1, :] += jnp.sum(d_pre, axis=0, keepdims=True)
+    d_head_ref[1:2, :] += jnp.sum(d_la * parts["dt"], axis=0, keepdims=True)
+    d_skip_ref[0:1, :] += jnp.sum(d_y * u, axis=0, keepdims=True)
+
+    d_u = d_xs * dt_w + skip_ref[0:1, :] * d_y
+    conv, sig = parts["conv"], parts["sig"]
+    d_conv = jnp.concatenate([d_u, d_key, d_query], axis=1) * (sig * (1.0 + conv * (1.0 - sig)))
+    late_ref[0:CHUNK, :] = d_conv
+    d_feed = jnp.zeros((CHUNK, CONVW), f32)
+    for tap in range(4):
+        d_feed = d_feed + taps_ref[tap : tap + 1, :] * late_ref[3 - tap : 3 - tap + CHUNK, :]
+        d_taps_ref[tap : tap + 1, :] += jnp.sum(
+            d_conv * pad_ref[5 + tap : 5 + tap + CHUNK, :], axis=0, keepdims=True
+        )
+    d_taps_ref[4:5, :] += jnp.sum(d_conv, axis=0, keepdims=True)
+    late_ref[CHUNK : CHUNK + 8, :] = d_conv[0:8, :]
+    scale = rows_ref[:, 2:3]
+    d_proj_ref[:, :WIDE] = (d_gate * scale).astype(bf)
+    d_proj_ref[:, WIDE : WIDE + CONVW] = (d_feed * scale).astype(bf)
+    d_proj_ref[:, WIDE + CONVW :] = (d_pre * scale).astype(bf)
+
+
+def whole(shape):
+    return pl.BlockSpec(shape, lambda step: (0,) * len(shape))
+
+
+def scan_forward(proj, taps, head, skip):
+    rows, width = proj.shape
+    chunks = rows // CHUNK
+    by_chunk = lambda step: (step, 0)
+    return pl.pallas_call(
+        scan_forward_kernel,
+        grid=(chunks,),
+        in_specs=[
+            pl.BlockSpec((CHUNK, width), by_chunk),
+            pl.BlockSpec((8, width), lambda step: (jnp.maximum(step * (CHUNK // 8) - 1, 0), 0)),
+            whole(taps.shape),
+            whole(head.shape),
+            whole(skip.shape),
+        ],
+        out_specs=[
+            pl.BlockSpec((CHUNK, WIDE), by_chunk),
+            pl.BlockSpec((CHUNK, WIDE), by_chunk),
+            pl.BlockSpec((CHUNK, 1), by_chunk),
+            pl.BlockSpec((1, 128, WIDE), lambda step: (step, 0, 0)),
+        ],
+        out_shape=[
+            jax.ShapeDtypeStruct((rows, WIDE), jnp.bfloat16),
+            jax.ShapeDtypeStruct((rows, WIDE), jnp.bfloat16),
+            jax.ShapeDtypeStruct((rows, 1), jnp.float32),
+            jax.ShapeDtypeStruct((chunks, 128, WIDE), jnp.float32),
+        ],
+        scratch_shapes=[
+            pltpu.VMEM((128, WIDE), jnp.float32),
+            pltpu.VMEM((CHUNK + 8, CONVW), jnp.float32),
+        ],
+        compiler_params=pltpu.CompilerParams(vmem_limit_bytes=32 << 20),
+        cost_estimate=pl.CostEstimate(
+            flops=3 << 30, bytes_accessed=12 << 20, transcendentals=4 << 20
+        ),
+        name="scan_forward",
+    )(proj, proj, taps, head, skip)
+
+
+def scan_backward(proj, mixed, d_gated, row_values, starts, taps, head, skip):
+    rows, width = proj.shape
+    chunks = rows // CHUNK
+    by_chunk = lambda step: (chunks - 1 - step, 0)
+    return pl.pallas_call(
+        scan_backward_kernel,
+        grid=(chunks,),
+        in_specs=[
+            pl.BlockSpec((CHUNK, width), by_chunk),
+            pl.BlockSpec(
+                (8, width),
+                lambda step: (jnp.maximum((chunks - 1 - step) * (CHUNK // 8) - 1, 0), 0),
+            ),
+            pl.BlockSpec((CHUNK, WIDE), by_chunk),
+            pl.BlockSpec((CHUNK, WIDE), by_chunk),
+            pl.BlockSpec((CHUNK, row_values.shape[1]), by_chunk),
+            pl.BlockSpec((1, 128, WIDE), lambda step: (chunks - 1 - step, 0, 0)),
+            whole(taps.shape),
+            whole(head.shape),
+            whole(skip.shape),
+        ],
+        out_specs=[
+            pl.BlockSpec((CHUNK, width), by_chunk),
+            whole((8, CONVW)),
+            whole((8, 128)),
+            whole((8, WIDE)),
+        ],
+        out_shape=[
+            jax.ShapeDtypeStruct((rows, width), jnp.bfloat16),
+            jax.ShapeDtypeStruct((8, CONVW), jnp.float32),
+            jax.ShapeDtypeStruct((8, 128), jnp.float32),
+            jax.ShapeDtypeStruct((8, WIDE), jnp.float32),
+        ],
+        scratch_shapes=[
+            pltpu.VMEM((128, WIDE), jnp.float32),
+            pltpu.VMEM((CHUNK + 8, CONVW), jnp.float32),
+            pltpu.VMEM((CHUNK + 8, CONVW), jnp.float32),
+        ],
+        compiler_params=pltpu.CompilerParams(vmem_limit_bytes=48 << 20),
+        cost_estimate=pl.CostEstimate(
+            flops=10 << 30, bytes_accessed=20 << 20, transcendentals=8 << 20
+        ),
+        name="scan_backward",
+    )(proj, proj, mixed, d_gated, row_values, starts, taps, head, skip)
 
 
 def on_device(
@@ -173,7 +439,9 @@
     packed = jnp.pad(packed, ((0, 0), (0, total - packed.shape[1])))
 
     w_all = lax.all_gather(packed, "shard", axis=0, tiled=True)
-    x_all = lax.all_gather(x_low, "seq", axis=0, tiled=True)
+    x_all = lax.all_to_all(
+        jnp.broadcast_to(x_low[None], (sq, toks, dim)), "seq", split_axis=0, concat_axis=0, tiled=True
+    ).reshape(seq_rows, dim)
 
     out_scaled = (norm_gain.astype(f32)[:, None] * out_weight.astype(f32)).astype(bf)
     own_out = out_weight.shape[0] // sq
@@ -194,9 +462,6 @@
             forward_pairs.append((j * sh + a, q_to * sh + s_to))
     backward_pairs = [(b, a) for a, b in forward_pairs]
     piece = lax.ppermute(piece, both_axes, forward_pairs)
-    rows_all = lax.all_gather(piece, "shard", axis=0)
-    w_out = rows_all[:, :own_out].reshape(gw, dim)
-    w_down = rows_all[:, own_out:].reshape(gf, dim)
     shared_cols = jnp.concatenate(
         [
             lax.dynamic_slice_in_dim(shared_gate, q * gf, gf, 1),
@@ -204,7 +469,23 @@
         ],
         axis=1,
     )
-    w_shared = lax.all_gather(shared_cols, "shard", axis=0, tiled=True)
+    fold = rows_w * 2 * gf // dim
+    bands = dim // (2 * gf)
+    shared_rows = jnp.concatenate(
+        [shared_cols[fold * band : fold * band + fold] for band in range(bands)], axis=1
+    )
+    piece = jnp.concatenate([piece, shared_rows], axis=0)
+    piece, w_all = lax.optimization_barrier((piece, w_all))
+    rows_all = lax.all_gather(piece, "shard", axis=0)
+    own_rows = own_out + own_down
+    w_out = rows_all[:, :own_out].reshape(gw, dim)
+    w_down = rows_all[:, own_out:own_rows].reshape(gf, dim)
+    w_shared = (
+        rows_all[:, own_rows:]
+        .reshape(sh, fold, bands, 2 * gf)
+        .transpose(0, 2, 1, 3)
+        .reshape(dim, 2 * gf)
+    )
 
     route_ids = routes[0]
     expert_ids = jnp.arange(experts, dtype=jnp.int32)
@@ -236,16 +517,10 @@
         [cot_low, named.astype(bf), jnp.zeros((toks, 128 - experts), bf)], axis=1
     )
     cot_rows_ext = to_experts(times(dispatch_flat, cot_ext).astype(bf))
-    cot_rows = cot_rows_ext[:, :, :dim]
-    row_mask = cot_rows_ext[:, :, dim : dim + experts].astype(f32)
-    cot_all = lax.all_gather(cot_low, "seq", axis=0, tiled=True)
 
     x_wide = x_all.astype(f32)
     x_r = row_scale(x_wide)
     proj = times(x_all, w_all) * x_r
-    gate_in = proj[:, :gw]
-    feed_low = proj[:, gw : 2 * gw + keys_w].astype(bf)
-    step_low = proj[:, 2 * gw + keys_w : used].astype(bf)
 
     small_all = w_all.reshape(sh, rows_w, total)[:, :, at_small:at_router].reshape(sh, -1)
     at = taps * conv_own
@@ -269,25 +544,22 @@
     decay_local = group(decay_full, gh).astype(f32)
     skip_local = group(skip_full, gh).astype(f32)
 
-    mixed_out, mixer_back = jax.vjp(
-        mixer,
-        feed_low[:, :gw].astype(f32),
-        step_low.astype(f32),
-        feed_low[:, gw:].astype(f32),
-        conv_local,
-        offset_local,
-        bias_local,
-        decay_local,
-        skip_local,
-    )
-    mixed = mixed_out.astype(bf).astype(f32)
-
-    gate_act = jax.nn.silu(gate_in)
-    q_val = mixed * gate_act
-    square = lax.psum(jnp.sum(q_val * q_val, axis=1).reshape(sq, toks), "seq")
+    per_head = gw // gh
+    taps_in = jnp.concatenate(
+        [conv_local, offset_local[None], jnp.zeros((8 - taps - 1, gw + keys_w), f32)], axis=0
+    )
+    decay_rate = -jnp.exp(decay_local)
+    head_in = jnp.pad(jnp.stack([bias_local, decay_rate]), ((0, 6), (0, 128 - gh)))
+    skip_in = jnp.broadcast_to(jnp.repeat(skip_local, per_head)[None], (8, gw))
+    mixed, q_low, square_part, starts = scan_forward(proj, taps_in, head_in, skip_in)
+
+    out_part = times(q_low, w_out).astype(bf)
+    out_sum = lax.psum_scatter(out_part, "seq", scatter_dimension=0, tiled=True)
+    square = lax.psum(square_part.reshape(sq, toks), "seq")
     q_r = lax.rsqrt(square / inner + epsilon).reshape(seq_rows, 1)
-    out_part = times(q_val.astype(bf), w_out).astype(bf)
-    out_sum = lax.psum_scatter(out_part, "seq", scatter_dimension=0, tiled=True)
+    out_sum, cot_rows_ext = lax.optimization_barrier((out_sum, cot_rows_ext))
+    cot_rows = cot_rows_ext[:, :, :dim]
+    row_mask = cot_rows_ext[:, :, dim : dim + experts].astype(f32)
     tok_r = lax.dynamic_slice_in_dim(q_r, q * toks, toks, 0)
     x_tok = x_low.astype(f32)
     added = out_sum.astype(f32) * tok_r
@@ -297,6 +569,8 @@
     resid_n = resid * resid_r
     moe_in = (resid_n * moe_gain_full[None, :]).astype(bf)
     moe_all = lax.all_gather(moe_in, "seq", axis=0, tiled=True)
+    cot_late, moe_all = lax.optimization_barrier((cot_low, moe_all))
+    cot_all = lax.all_gather(cot_late, "seq", axis=0, tiled=True)
     logits = times(moe_in, router_full)
 
     def masked_softmax(values, mask):
@@ -400,23 +674,42 @@
     block_output = ((resid + shared_sum.astype(f32) + combined) * live[:, None]).astype(bf)[None]
 
     d_gated = times_transposed(d_o_all, w_out)
-    d_q = q_r * d_gated - q_val * (q_r * q_r * kappa_all)
-    d_mixed = (d_q * gate_act).astype(bf)
-    d_gate_in = d_q * mixed * silu_slope(gate_in)
-    gated_low = (q_val * q_r).astype(bf)
-    grad_out_part = transposed_times(gated_low, d_o_all)
+    grad_out_part = transposed_times(q_low, (q_r * d_o_all.astype(f32)).astype(bf))
     grad_down_part = transposed_times(s_act, cot_all)
     grad_shared_part = transposed_times(moe_all, d_both)
 
-    def sum_over_shard(values):
-        moved = lax.all_to_all(values.astype(bf), "shard", split_axis=0, concat_axis=0, tiled=True)
-        return jnp.sum(moved.astype(f32), axis=0)
+    def to_shards(values):
+        return lax.all_to_all(values.astype(bf), "shard", split_axis=0, concat_axis=0, tiled=True)
 
     rows_part = jnp.concatenate(
         [grad_out_part.reshape(sh, own_out, dim), grad_down_part.reshape(sh, own_down, dim)],
         axis=1,
     )
-    rows_sum = sum_over_shard(rows_part)
+    mid_part = jnp.concatenate(
+        [
+            grad_shared_part,
+            grad_router,
+            grad_moe[:, None],
+            jnp.zeros((dim, 128 - experts - 1), f32),
+        ],
+        axis=1,
+    )
+    moved_rows = to_shards(rows_part)
+    moved_mid = to_shards(mid_part.reshape(sh, rows_w, 2 * gf + 128))
+
+    row_values = jnp.concatenate(
+        [q_r, kappa_all, x_r, jnp.zeros((seq_rows, 5), f32)], axis=1
+    )
+    d_proj, d_taps, d_head, d_skip = scan_backward(
+        proj, mixed, d_gated, row_values, starts, taps_in, head_in, skip_in
+    )
+    grad_conv_local = d_taps[:taps]
+    grad_offset_local = d_taps[taps]
+    grad_bias_local = d_head[0, :gh]
+    grad_decay_local = d_head[1, :gh] * decay_rate
+    grad_skip_local = jnp.sum(d_skip[0].reshape(gh, per_head), axis=1)
+    d_proj, moved_rows, moved_mid = lax.optimization_barrier((d_proj, moved_rows, moved_mid))
+    rows_sum = jnp.sum(moved_rows.astype(f32), axis=0)
     rows_sum = lax.ppermute(rows_sum.astype(bf), both_axes, backward_pairs)
     rows_grad = lax.all_gather(rows_sum, "seq", axis=0)
     grad_out_raw = rows_grad[:, :own_out].reshape(sq * own_out, dim).astype(f32)
@@ -424,16 +717,7 @@
     grad_out = norm_gain.astype(f32)[:, None] * grad_out_raw
     grad_norm = jnp.sum(out_weight.astype(f32) * grad_out_raw, axis=1)
 
-    mid_part = jnp.concatenate(
-        [
-            grad_shared_part,
-            grad_router,
-            grad_moe[:, None],
-            jnp.zeros((dim, 128 - experts - 1), f32),
-        ],
-        axis=1,
-    )
-    mid_sum = sum_over_shard(mid_part.reshape(sh, rows_w, 2 * gf + 128))
+    mid_sum = jnp.sum(moved_mid.astype(f32), axis=0)
     mid_all = lax.all_gather(mid_sum.astype(bf), "seq", axis=0).astype(f32)
     grad_shared_gate = mid_all[:, :, :gf].transpose(1, 0, 2).reshape(rows_w, fs)
     grad_shared_up = mid_all[:, :, gf : 2 * gf].transpose(1, 0, 2).reshape(rows_w, fs)
@@ -441,19 +725,6 @@
     grad_router_weight = mid_rest[:, :experts]
     grad_moe_gain = mid_rest[:, experts]
 
-    (
-        d_mixer_raw,
-        d_step_raw,
-        d_keys_raw,
-        grad_conv_local,
-        grad_offset_local,
-        grad_bias_local,
-        grad_decay_local,
-        grad_skip_local,
-    ) = mixer_back(d_mixed.astype(f32))
-    d_proj = jnp.concatenate([d_gate_in, d_mixer_raw, d_keys_raw, d_step_raw], axis=1)
-    d_proj = (d_proj * x_r).astype(bf)
-    d_proj = jnp.pad(d_proj, ((0, 0), (0, total - used)))
     back_part = times_transposed(d_proj, w_all).astype(bf)
     back_sum = lax.psum_scatter(back_part, "seq", scatter_dimension=0, tiled=True).astype(f32)
     tok_x_r = row_scale(x_tok)
@@ -490,7 +761,7 @@
         ],
         axis=2,
     )
-    last_sum = sum_over_shard(last_part)
+    last_sum = jnp.sum(to_shards(last_part).astype(f32), axis=0)
     last_all = lax.all_gather(last_sum.astype(bf), "seq", axis=0).astype(f32)
 
     def side_by_side(start, width):

time: 1050 us -> 712 us (0.68)
  local copies, waits for them, and re-layouts: 245 us -> 126 us
  waiting for transfers between devices: 251 us -> 167 us
  other arithmetic: 138 us -> 62.8 us
  matrix products: 184 us -> 115 us
  blocking collectives: 138 us -> 103 us
  Pallas kernels: 0 us -> 34.3 us
  starting transfers between devices: 61 us -> 75.9 us
    dynamic_update_slice x16 -> x0, local copies, waits for them, and re-layouts: 82.7 us -> none  [mixer(): final_state, outputs = lax.scan(jax.checkpoint(one_block), initial, pieces)]
    dot_general x56 -> x0, matrix products: 67.2 us -> none  [the longest x12 26.7 us: block_scan(): jnp.einsum('hij,jhp->ihp', decay_table * intersection[None], scaled, prec...]
    all_gather x1 -> x0, blocking collectives: 52.8 us -> none  [on_device(): w_shared = lax.all_gather(shared_cols, 'shard', axis=0, tiled=True)]
    another operation x41 -> x3, other arithmetic: 46.2 us -> 0.17 us  [on_device(): jnp.stack([bias_local, decay_rate])]
    all_to_all x0 -> x1, blocking collectives: none -> 44.1 us  [to_experts(): lax.all_to_all(rows.reshape(experts, CAP, rows.shape[-1]), 'shard', split...]
    pallas_call x0 -> x2, Pallas kernels: none -> 34.3 us  [the longest x1 23.4 us: scan_backward(): pl.pallas_call(scan_backward_kernel, grid=(chunks,), in_specs=[pl.BlockSp...]
    all_gather x1, waiting for transfers between devices: 42 us -> 13.6 us  [on_device(): rows_all = lax.all_gather(piece, 'shard', axis=0)]
    all_gather x2 -> x1, waiting for transfers between devices: 28.1 us -> 0.01 us  [on_device(): cot_all = lax.all_gather(cot_late, 'seq', axis=0, tiled=True)]
  transfers between devices with their start and end apart: 21 -> 20, of which waited for: 10 -> 8; matrix products, arithmetic and copies ran while one was open for 37% -> 34% of each run, Pallas kernels for 0% -> 5%
where the time goes in v2:
time: 712 us; the launch traced here: 701 us
  waiting for transfers between devices  167 us (23%)
  local copies, waits for them, and re-layouts  126 us (18%)
  matrix products  115 us (16%)
  blocking collectives  103 us (14%)
  starting transfers between devices  75.9 us (11%)
  other arithmetic  62.8 us (9%)
  Pallas kernels  34.3 us (5%)
  between operations  16.1 us (2%)
    all_to_all x2, waiting for transfers between devices, from_experts(): lax.all_to_all(values, 'shard', split_axis=1, concat_axis=0, tiled=True)  58.5 us
    all_to_all x1, blocking collectives, to_experts(): lax.all_to_all(rows.reshape(experts, CAP, rows.shape[-1]), 'shard', split...  44.1 us
    all_gather x1, waiting for transfers between devices, on_device(): w_all = lax.all_gather(packed, 'shard', axis=0, tiled=True)  32.7 us
    dot_general x7, matrix products, times(): return jnp.dot(left, right, preferred_element_type=jnp.float32)  24.4 us
    pallas_call x1, Pallas kernels, scan_backward(): pl.pallas_call(scan_backward_kernel, grid=(chunks,), in_specs=[pl.BlockSp...  23.4 us
    all_to_all x1, waiting for transfers between devices, to_experts(): lax.all_to_all(rows.reshape(experts, CAP, rows.shape[-1]), 'shard', split...  22.1 us
    all_to_all x3, waiting for transfers between devices, to_shards(): lax.all_to_all(values.astype(bf), 'shard', split_axis=0, concat_axis=0, t...  22 us
    dot_general x5, matrix products, transposed_times(): lax.dot_general(left, right, (((0,), (0,)), ((), ())), preferred_element_...  21.6 us
  transfers between devices with their start and end apart: 20, of which 8 were waited for; matrix products, arithmetic and copies ran while one was open for 34% of the time, Pallas kernels for 5%

profile of v2, /device:TPU:1, one launch (start us, length us, event | category | flops | bytes accessed | tf_op | source)
XLA Modules:
  0.0 700.5 jit_solution(7106078069607499852)
XLA Ops:
  21.7 6.9 all-to-all-start
  41.2 32.7 %all-gather.13.cloned.1.call-done = bf16[1536,1152]{1,0:T(8,128)(2,1)} async-done(((bf16[96,1152]{1,0:T(8,128)(2,1)}), bf16[1536,1152]{1,0:T(8,128)(2,1)}) %all-gather.13.cloned.1.call-update) | async-done | bytes 3538960 | tf_op jit(solution)/shard_map/all_gather | solution.py:441
  83.1 7.2 %fusion.1.proj_ref.prev_ref = f32[1024,1152]{1,0:T(8,128)S(1)} fusion(bf16[1024,1536]{1,0:T(8,128)(2,1)} %bitcast.2, bf16[1536,1152]{1,0:T(8,128)(2,1)} %all-gather.13.cloned.1.call-done, f32[1024]{0:T(1024)S(1)} %get-tuple-element.165), kind=kOutput, calls=%fused_computation.6 | convolution fusion | flops 3625058304 | bytes 11407360 | tf_op jit(solution)/shard_map/dot_general | solution.py:17
  90.4 10.9 %scan_forward.1 = (bf16[1024,384]{1,0:T(8,128)(2,1)S(1)}, bf16[1024,384]{1,0:T(8,128)(2,1)S(1)}, f32[1024,1]{1,0:T(8,128)S(1)}, f32[8,128,384]{2,1,0:T(8,128)S(1)}) custom-call(f32[1024,1152]{1,0:T(8,128)S(1)} %fusion.1.proj_ref.prev_ref, f32[1024,1152]{1,0:T(8,128)S(1)} %fusion.1.proj_ref.prev_ref, f32[8,640]{1,0:T(8,128)S(1)} %maximum_maximum_fusion.2.taps_ref, ...), custom_call_target="tpu_custom_call" | custom-call | flops 3221225472 | bytes 12582912 | tf_op jit(solution)/shard_map/scan_forward/pallas_call | solution.py:285
  107.1 13.6 %all-gather.21.cloned.1.call-done = bf16[768,1536]{1,0:T(8,128)(2,1)} async-done(((bf16[48,1536]{1,0:T(8,128)(2,1)}), bf16[768,1536]{1,0:T(8,128)(2,1)}) %all-gather.21.cloned.1.call-update) | async-done | bytes 2359312 | tf_op jit(solution)/shard_map/all_gather | solution.py:479
  134.9 44.1 %all_to_all.86 = bf16[32,32,1664]{2,1,0:T(8,128)(2,1)S(1)} all-to-all(bf16[32,32,1664]{2,1,0:T(8,128)(2,1)S(1)} %bitcast.231), channel_id=1, replica_groups=mesh['seq'=8,'shard'=16] {'shard'}, dimensions={0} | all-to-all | bytes 6815744 | tf_op jit(solution)/shard_map/all_to_all | solution.py:508
  182.3 15.2 %psum.28 = f32[8,128]{1,0:T(8,128)S(1)} all-reduce(f32[8,128]{1,0:T(8,128)S(1)} %bitcast.271), channel_id=1, replica_groups=mesh['seq'=8,'shard'=16] {'seq'}, use_global_device_ids=true, to_apply=%region_3.4 | all-reduce | flops 1024 | bytes 8192 | tf_op jit(solution)/shard_map/psum | solution.py:558
  203.1 10.7 %all-gather.17.cloned.1.call-start = ((), (), s32[]{:S(2)}) async-start(), calls=%async_computation.16 | async-start | bytes 3538944 | tf_op jit(solution)/shard_map/all_gather | solution.py:573
  213.8 13.5 %all-gather.15.cloned.1.call-done = bf16[1024,1536]{1,0:T(8,128)(2,1)} async-done(((bf16[128,1536]{1,0:T(8,128)(2,1)}), bf16[1024,1536]{1,0:T(8,128)(2,1)}) %all-gather.15.cloned.1.call-update) | async-done | bytes 3145744 | tf_op jit(solution)/shard_map/all_gather | solution.py:571
  231.0 6.6 all-to-all-start.2
  237.7 5.8 copy.289
  256.3 22.1 %all-to-all-done.2 = bf16[32,32,1536]{2,1,0:T(8,128)(2,1)} async-done(((bf16[32,32,1536]{2,1,0:T(8,128)(2,1)}), bf16[32,32,1536]{2,1,0:T(8,128)(2,1)}, u32[]{:S(2)}, u32[]{:S(2)}) %all-to-all-start.2) | async-done | bytes 3145760 | tf_op jit(solution)/shard_map/all_to_all | solution.py:508
  301.1 7.5 %fusion.20 = (f32[2,512]{1,0:T(2,128)S(1)}, bf16[2,512,512]{1,2,0:T(8,128)(2,1)}, bf16[2,512,512]{1,2,0:T(8,128)(2,1)}, bf16[2,512,512]{1,2,0:T(8,128)(2,1)}) fusion(f32[2,512,512]{1,2,0:T(8,128)} %fusion.86, f32[2,512,512]{1,2,0:T(8,128)} %fusion.85, f32[2,512]{1,0:T(2,128)S(1)} %multiply_reduce_fusion.6, bf16[2,512,1536]{2,1,0:T(8,128)(2,1)S(1)} %copy-done, ...), kind=kOutput, calls=%fused_computation.39 | convolution fusion | flops 1620573184 | bytes 13639680 | tf_op jit(solution)/shard_map/ecd,efd->ecf/dot_general | solution.py:592
  319.4 6.6 concatenate.97
  326.0 7.3 %copy.302 = bf16[2,512,1664]{2,0,1:T(2,128)(2,1)} copy(bf16[2,512,1664]{2,1,0:T(8,128)(2,1)} %concatenate.97) | data formatting | bytes 6815744 | tf_op jit(solution)/shard_map/concatenate | solution.py:607
  333.4 11.2 %all-to-all-start.4 = ((bf16[2,512,1664]{2,0,1:T(2,128)(2,1)}), bf16[2,512,1664]{2,0,1:T(2,128)(2,1)}, u32[]{:S(2)}, u32[]{:S(2)}) async-start(bf16[2,512,1664]{2,0,1:T(2,128)(2,1)} %copy.302), calls=%async_computation.6 | async-start | bytes 6815744 | tf_op jit(solution)/shard_map/all_to_all | solution.py:612
  346.0 41.6 %all-to-all-done.4 = bf16[2,512,1664]{2,0,1:T(2,128)(2,1)} async-done(((bf16[2,512,1664]{2,0,1:T(2,128)(2,1)}), bf16[2,512,1664]{2,0,1:T(2,128)(2,1)}, u32[]{:S(2)}, u32[]{:S(2)}) %all-to-all-start.4) | async-done | bytes 3407904 | tf_op jit(solution)/shard_map/all_to_all | solution.py:612
  401.1 6.4 convolution_convert_fusion.5
  439.6 14.4 %all-gather.5 = f32[8,1,128]{2,1,0:T(1,128)S(1)} all-gather(f32[1,1,128]{2,1,0:T(1,128)S(1)} %multiply_bitcast_fusion), channel_id=3, replica_groups=mesh['seq'=8,'shard'=16] {'seq'}, dimensions={0}, use_global_device_ids=true | all-gather | bytes 4608 | tf_op jit(solution)/shard_map/all_gather | solution.py:664
  459.2 7.0 all-to-all-start.5
  471.7 23.4 %scan_backward.1 = (bf16[1024,1152]{1,0:T(8,128)(2,1)}, f32[8,640]{1,0:T(8,128)S(1)}, f32[8,128]{1,0:T(8,128)S(1)}, f32[8,384]{1,0:T(8,128)S(1)}) custom-call(f32[1024,1152]{1,0:T(8,128)} %copy-done.4, f32[1024,1152]{1,0:T(8,128)} %copy-done.4, bf16[1024,384]{1,0:T(8,128)(2,1)S(1)} %copy-done.8, f32[1024,384]{1,0:T(8,128)S(1)} %fusion.88.d_gated_ref, ...), custom_call_target="tpu_custom_call" | custom-call | flops 10737418240 | bytes 20971520 | tf_op jit(solution)/shard_map/scan_backward/pallas_call | solution.py:323
  495.2 8.6 %convolution_convert_fusion.10 = bf16[1024,1536]{1,0:T(8,128)(2,1)} fusion(bf16[1024,1152]{1,0:T(8,128)(2,1)} %get-tuple-element.47, bf16[1536,1152]{1,0:T(8,128)(2,1)} %all-gather.13.cloned.1.call-done), kind=kOutput, calls=%fused_computation.16 | convolution fusion | flops 3625451520 | bytes 9043968 | tf_op jit(solution)/shard_map/dot_general | solution.py:21
  511.8 7.0 %all-to-all-start.3 = ((bf16[2,512,1536]{2,0,1:T(2,128)(2,1)}), bf16[2,512,1536]{2,0,1:T(2,128)(2,1)}, u32[]{:S(2)}, u32[]{:S(2)}) async-start(bf16[2,512,1536]{2,0,1:T(2,128)(2,1)} %copy.294), calls=%async_computation.5 | async-start | bytes 6291456 | tf_op jit(solution)/shard_map/all_to_all | solution.py:612
  521.7 6.6 fusion
  535.5 6.6 concatenate.107
  542.2 16.9 %all-to-all-done.3 = bf16[2,512,1536]{2,0,1:T(2,128)(2,1)} async-done(((bf16[2,512,1536]{2,0,1:T(2,128)(2,1)}), bf16[2,512,1536]{2,0,1:T(2,128)(2,1)}, u32[]{:S(2)}, u32[]{:S(2)}) %all-to-all-start.3) | async-done | bytes 3145760 | tf_op jit(solution)/shard_map/all_to_all | solution.py:612
  559.1 8.2 %all-to-all-start.7 = ((bf16[16,96,1152]{2,1,0:T(8,128)(2,1)}), bf16[16,96,1152]{2,1,0:T(8,128)(2,1)}, u32[]{:S(2)}, u32[]{:S(2)}) async-start(bf16[16,96,1152]{2,1,0:T(8,128)(2,1)} %concatenate.107), calls=%async_computation.11 | async-start | bytes 7077888 | tf_op jit(solution)/shard_map/all_to_all | solution.py:682
  573.2 5.7 convert_element_type.355
  586.1 22.0 %all-to-all-done.7 = bf16[16,96,1152]{2,1,0:T(8,128)(2,1)} async-done(((bf16[16,96,1152]{2,1,0:T(8,128)(2,1)}), bf16[16,96,1152]{2,1,0:T(8,128)(2,1)}, u32[]{:S(2)}, u32[]{:S(2)}) %all-to-all-start.7) | async-done | bytes 3538976 | tf_op jit(solution)/shard_map/all_to_all | solution.py:682
  619.6 9.7 %collective-permute-start.1 = (bf16[32,1536]{1,0:T(8,128)(2,1)}, bf16[32,1536]{1,0:T(8,128)(2,1)}, u32[]{:S(2)}, u32[]{:S(2)}) collective-permute-start(bf16[32,1536]{1,0:T(8,128)(2,1)} %reduce_sum.238), channel_id=1, source_target_pairs={{0,0},{1,16},{2,32},{3,48},{4,64},{5,80},{6,96},{7,112},{8,1},{9,1... | collective-permute-start | bytes 294920 | tf_op jit(solution)/shard_map/ppermute | solution.py:713
  629.4 15.4 %all-gather.4 = bf16[768,384]{1,0:T(8,128)(2,1)S(1)} all-gather(bf16[96,384]{1,0:T(8,128)(2,1)} %reduce_sum.240), channel_id=6, replica_groups=mesh['seq'=8,'shard'=16] {'seq'}, dimensions={0}, use_global_device_ids=true | all-gather | bytes 663552 | tf_op jit(solution)/shard_map/all_gather | solution.py:721
  651.9 14.0 %all-gather.3 = bf16[256,1536]{1,0:T(8,128)(2,1)S(1)} all-gather(bf16[32,1536]{1,0:T(8,128)(2,1)} %collective-permute-done.1), channel_id=5, replica_groups=mesh['seq'=8,'shard'=16] {'seq'}, dimensions={0}, use_global_device_ids=true | all-gather | bytes 884736 | tf_op jit(solution)/shard_map/all_gather | solution.py:714
  (377 shorter events, 248.7 us)
Async XLA Ops:
  7.2 293.9 %copy-start = (bf16[2,512,1536]{2,1,0:T(8,128)(2,1)S(1)}, bf16[2,512,1536]{2,1,0:T(8,128)(2,1)}, u32[]{:S(2)}) copy-start(bf16[2,512,1536]{2,1,0:T(8,128)(2,1)} %param.41) | copy-start | bytes 9437188
  7.2 66.7 %all-gather.13.cloned.1.call-start = ((), (), s32[]{:S(2)}) async-start(), calls=%async_computation.12 | async-start | bytes 3760128 | tf_op jit(solution)/shard_map/all_gather | solution.py:441
  21.7 52.4 %all-to-all-start = ((bf16[8,128,1536]{2,1,0:T(8,128)(2,1)}), bf16[8,128,1536]{2,1,0:T(8,128)(2,1)}, u32[]{:S(2)}, u32[]{:S(2)}) async-start(bf16[8,128,1536]{2,1,0:T(8,128)(2,1)} %broadcast_in_dim.51), calls=%async_computation | async-start | bytes 6291456 | tf_op jit(solution)/shard_map/all_to_all | solution.py:442
  28.6 92.2 %all-gather.21.cloned.1.call-start = ((), (), s32[]{:S(2)}) async-start(), calls=%async_computation.20 | async-start | bytes 2506752 | tf_op jit(solution)/shard_map/all_gather | solution.py:479
  32.6 7.8 %collective-permute-start = (bf16[32,1536]{1,0:T(8,128)(2,1)S(1)}, bf16[32,1536]{1,0:T(8,128)(2,1)S(1)}, u32[]{:S(2)}, u32[]{:S(2)}) collective-permute-start(bf16[32,1536]{1,0:T(8,128)(2,1)S(1)} %pad_maximum_fusion.6), channel_id=1, source_target_pairs={{0,0},{16,1},{32,2},{48,3},{64,4},{80,5},{96,6},{112,7},{1,8},{17,... | collective-permute-start | bytes 294920 | tf_op jit(solution)/shard_map/ppermute | solution.py:464
  73.9 125.6 %reduce-scatter.5.cloned.1.call-start = ((), (), s32[]{:S(2)}) async-start(), calls=%async_computation.13 | async-start | bytes 3538944 | tf_op jit(solution)/shard_map/reduce_scatter | solution.py:557
  127.7 99.6 %all-gather.15.cloned.1.call-start = ((), (), s32[]{:S(2)}) async-start(), calls=%async_computation.14 | async-start | bytes 3538944 | tf_op jit(solution)/shard_map/all_gather | solution.py:571
  128.6 291.3 %copy-start.33 = (pred[128,32]{0,1:T(8,128)(4,1)}, pred[128,32]{0,1:T(8,128)(4,1)S(1)}, u32[]{:S(2)}) copy-start(pred[128,32]{0,1:T(8,128)(4,1)S(1)} %fusion.45) | copy-start | bytes 12292
  128.6 263.8 %copy-start.39 = (pred[32,128]{1,0:T(8,128)(4,1)}, pred[32,128]{1,0:T(8,128)(4,1)S(1)}, u32[]{:S(2)}) copy-start(pred[32,128]{1,0:T(8,128)(4,1)S(1)} %get-tuple-element.167) | copy-start | bytes 12292
  128.9 263.6 %copy-start.37 = (f32[32,128]{1,0:T(8,128)}, f32[32,128]{1,0:T(8,128)S(1)}, u32[]{:S(2)}) copy-start(f32[32,128]{1,0:T(8,128)S(1)} %fusion.54) | copy-start | bytes 49156
  129.1 270.0 %copy-start.48 = (f32[128]{0:T(128)}, f32[128]{0:T(128)S(1)}, u32[]{:S(2)}) copy-start(f32[128]{0:T(128)S(1)} %compare_convert_fusion.1) | copy-start | bytes 1540
  198.1 201.0 %copy-start.46 = (f32[128]{0:T(128)}, f32[128]{0:T(128)S(1)}, u32[]{:S(2)}) copy-start(f32[128]{0:T(128)S(1)} %fusion.72) | copy-start | bytes 1540
  200.9 30.1 %copy-start.61 = (f32[128]{0:T(128)}, f32[128]{0:T(128)S(1)}, u32[]{:S(2)}) copy-start(f32[128]{0:T(128)S(1)} %multiply_reduce_fusion.5) | copy-start | bytes 1540
  200.9 30.1 %copy-start.54 = (f32[128]{0:T(128)}, f32[128]{0:T(128)S(1)}, u32[]{:S(2)}) copy-start(f32[128]{0:T(128)S(1)} %add_rsqrt_fusion.3) | copy-start | bytes 1540
  203.1 89.2 %all-gather.17.cloned.1.call-start = ((), (), s32[]{:S(2)}) async-start(), calls=%async_computation.16 | async-start | bytes 3538944 | tf_op jit(solution)/shard_map/all_gather | solution.py:573
  231.0 47.4 %all-to-all-start.2 = ((bf16[32,32,1536]{2,1,0:T(8,128)(2,1)}), bf16[32,32,1536]{2,1,0:T(8,128)(2,1)}, u32[]{:S(2)}, u32[]{:S(2)}) async-start(bf16[32,32,1536]{2,1,0:T(8,128)(2,1)} %bitcast.239), calls=%async_computation.4 | async-start | bytes 6291456 | tf_op jit(solution)/shard_map/all_to_all | solution.py:508
  237.6 157.4 %reduce-scatter.9.cloned.1.call-start = ((), (), s32[]{:S(2)}) async-start(), calls=%async_computation.17 | async-start | bytes 3538944 | tf_op jit(solution)/shard_map/reduce_scatter | solution.py:638
  333.4 54.2 %all-to-all-start.4 = ((bf16[2,512,1664]{2,0,1:T(2,128)(2,1)}), bf16[2,512,1664]{2,0,1:T(2,128)(2,1)}, u32[]{:S(2)}, u32[]{:S(2)}) async-start(bf16[2,512,1664]{2,0,1:T(2,128)(2,1)} %copy.302), calls=%async_computation.6 | async-start | bytes 6815744 | tf_op jit(solution)/shard_map/all_to_all | solution.py:612
  344.6 109.5 %all-gather.19.cloned.1.call-start = ((), (), s32[]{:S(2)}) async-start(), calls=%async_computation.18 | async-start | bytes 3538944 | tf_op jit(solution)/shard_map/all_gather | solution.py:663
  345.9 74.0 %copy-start.42 = (f32[128]{0:T(128)}, f32[128]{0:T(128)S(1)}, u32[]{:S(2)}) copy-start(f32[128]{0:T(128)S(1)} %compare_select_fusion.1) | copy-start | bytes 1540
  345.9 74.0 %copy-start.44 = (f32[128]{0:T(128)}, f32[128]{0:T(128)S(1)}, u32[]{:S(2)}) copy-start(f32[128]{0:T(128)S(1)} %broadcast_maximum_fusion.1) | copy-start | bytes 1540
  400.6 172.6 %all-reduce.7.cloned.1.call-start = ((), (), s32[]{:S(2)}) async-start(), calls=%async_computation.22 | async-start | bytes 18874368 | tf_op jit(solution)/shard_map/psum | solution.py:620
  415.1 196.4 %reduce-scatter.7.cloned.1.call-start = ((), (), s32[]{:S(2)}) async-start(), calls=%async_computation.15 | async-start | bytes 3538944 | tf_op jit(solution)/shard_map/reduce_scatter | solution.py:640
  431.9 27.3 %all-to-all-start.6 = ((bf16[16,96,384]{2,1,0:T(8,128)(2,1)}), bf16[16,96,384]{2,1,0:T(8,128)(2,1)}, u32[]{:S(2)}, u32[]{:S(2)}) async-start(bf16[16,96,384]{2,1,0:T(8,128)(2,1)} %maximum_maximum_fusion), calls=%async_computation.9 | async-start | bytes 2359296 | tf_op jit(solution)/shard_map/all_to_all | solution.py:682
  459.2 36.0 %all-to-all-start.5 = ((bf16[16,32,1536]{2,1,0:T(8,128)(2,1)}), bf16[16,32,1536]{2,1,0:T(8,128)(2,1)}, u32[]{:S(2)}, u32[]{:S(2)}) async-start(bf16[16,32,1536]{2,1,0:T(8,128)(2,1)} %pad_maximum_fusion.1), calls=%async_computation.8 | async-start | bytes 3145728 | tf_op jit(solution)/shard_map/all_to_all | solution.py:682
  466.1 202.6 %reduce-scatter.11.cloned.1.call-start = ((), (), s32[]{:S(2)}) async-start(), calls=%async_computation.19 | async-start | bytes 3538944 | tf_op jit(solution)/shard_map/reduce_scatter | solution.py:729
  511.8 47.4 %all-to-all-start.3 = ((bf16[2,512,1536]{2,0,1:T(2,128)(2,1)}), bf16[2,512,1536]{2,0,1:T(2,128)(2,1)}, u32[]{:S(2)}, u32[]{:S(2)}) async-start(bf16[2,512,1536]{2,0,1:T(2,128)(2,1)} %copy.294), calls=%async_computation.5 | async-start | bytes 6291456 | tf_op jit(solution)/shard_map/all_to_all | solution.py:612
  542.2 25.8 %copy-start.38 = (f32[32,128]{1,0:T(8,128)S(1)}, f32[32,128]{1,0:T(8,128)}, u32[]{:S(2)}) copy-start(f32[32,128]{1,0:T(8,128)} %copy-done.37) | copy-start | bytes 49156
  542.2 25.8 %copy-start.40 = (pred[32,128]{1,0:T(8,128)(4,1)S(1)}, pred[32,128]{1,0:T(8,128)(4,1)}, u32[]{:S(2)}) copy-start(pred[32,128]{1,0:T(8,128)(4,1)} %copy-done.39) | copy-start | bytes 12292
  559.1 49.0 %all-to-all-start.7 = ((bf16[16,96,1152]{2,1,0:T(8,128)(2,1)}), bf16[16,96,1152]{2,1,0:T(8,128)(2,1)}, u32[]{:S(2)}, u32[]{:S(2)}) async-start(bf16[16,96,1152]{2,1,0:T(8,128)(2,1)} %concatenate.107), calls=%async_computation.11 | async-start | bytes 7077888 | tf_op jit(solution)/shard_map/all_to_all | solution.py:682
  567.3 105.0 %all-gather.23.cloned.1.call-start = ((), (), s32[]{:S(2)}) async-start(), calls=%async_computation.21 | async-start | bytes 1990656 | tf_op jit(solution)/shard_map/all_gather | solution.py:765
  619.6 32.3 %collective-permute-start.1 = (bf16[32,1536]{1,0:T(8,128)(2,1)}, bf16[32,1536]{1,0:T(8,128)(2,1)}, u32[]{:S(2)}, u32[]{:S(2)}) collective-permute-start(bf16[32,1536]{1,0:T(8,128)(2,1)} %reduce_sum.238), channel_id=1, source_target_pairs={{0,0},{1,16},{2,32},{3,48},{4,64},{5,80},{6,96},{7,112},{8,1},{9,1... | collective-permute-start | bytes 294920 | tf_op jit(solution)/shard_map/ppermute | solution.py:713
  (56 other events, 443.6 us)
Sparse Core Ops, SparseCore 0:
  18.8 54.9 all-gather.12
  76.6 44.0 all-gather.20
  127.9 33.4 reduce-scatter.4
  203.2 24.0 all-gather.14
  229.5 27.8 all-gather.16
  300.3 37.5 reduce-scatter.8
  400.7 30.7 all-gather.18
  434.1 113.5 all-reduce.6
  550.2 33.4 reduce-scatter.6
  585.9 35.3 reduce-scatter.10
  623.6 27.1 all-gather.22

commit v3 on v2

--- a/solution.py
+++ b/solution.py
@@ -360,6 +360,228 @@
         ),
         name="scan_backward",
     )(proj, proj, mixed, d_gated, row_values, starts, taps, head, skip)
+
+
+def expert_early_kernel(cot_ref, down_ref, raw_ref):
+    cot = cot_ref[...].reshape(-1, cot_ref.shape[-1])
+    raw_ref[0] = times_transposed(cot, down_ref[0])
+
+
+def expert_main_kernel(
+    rows_ref, routed_ref, raw_ref, gate_ref, up_ref, router_ref, marks_ref,
+    back_ref, act_ref, scaled_ref, d_g_ref, d_v_ref,
+):
+    f32, bf = jnp.float32, jnp.bfloat16
+    dim = rows_ref.shape[-1]
+    rows = rows_ref[...].reshape(-1, dim)
+    routed = routed_ref[...].reshape(-1, 128).astype(f32) > 0.0
+    logits = times(rows, router_ref[...])
+    top = jnp.max(jnp.where(routed, logits, -1e30), axis=1, keepdims=True)
+    powers = jnp.where(routed, jnp.exp(jnp.where(routed, logits - top, 0.0)), 0.0)
+    own = jnp.sum(powers * marks_ref[0, 0:1, :], axis=1, keepdims=True)
+    gate = own / jnp.maximum(jnp.sum(powers, axis=1, keepdims=True), 1e-30)
+    g = times(rows, gate_ref[0])
+    v = times(rows, up_ref[0])
+    sig = jax.nn.sigmoid(g)
+    silu = g * sig
+    act = (silu * v).astype(bf)
+    act_wide = act.astype(f32)
+    raw = raw_ref[0]
+    d_gate = jnp.sum(act_wide * raw, axis=1, keepdims=True)
+    d_act = gate * raw
+    d_g = (d_act * v * (sig * (1.0 + g * (1.0 - sig)))).astype(bf)
+    d_v = (d_act * silu).astype(bf)
+    d_row = times_transposed(d_g, gate_ref[0]) + times_transposed(d_v, up_ref[0])
+    high = d_gate.astype(bf).astype(f32)
+    scalars = high * marks_ref[0, 1:2, :] + (d_gate - high) * marks_ref[0, 2:3, :]
+    lead = back_ref.shape[:-1]
+    back_ref[:, :, :, :dim] = d_row.astype(bf).reshape(*lead, dim)
+    back_ref[:, :, :, dim:] = scalars.astype(bf).reshape(*lead, 128)
+    act_ref[0] = act
+    scaled_ref[0] = (gate * act_wide).astype(bf)
+    d_g_ref[0] = d_g
+    d_v_ref[0] = d_v
+
+
+def expert_late_kernel(
+    rows_ref, cot_ref, act_ref, scaled_ref, d_g_ref, d_v_ref, down_ref,
+    out_ref, grads_ref,
+):
+    bf = jnp.bfloat16
+    dim = rows_ref.shape[-1]
+    rows = rows_ref[...].reshape(-1, dim)
+    cot = cot_ref[...].reshape(-1, dim)
+    out_ref[...] = times(act_ref[0], down_ref[0]).astype(bf).reshape(out_ref.shape)
+    units = act_ref.shape[-1]
+    grads_ref[0, :dim] = transposed_times(rows, d_g_ref[0]).astype(bf)
+    grads_ref[0, dim : 2 * dim] = transposed_times(rows, d_v_ref[0]).astype(bf)
+    for block in range(dim // units):
+        at = 2 * dim + block * units
+        grads_ref[0, at : at + units] = transposed_times(
+            scaled_ref[0], cot[:, block * units : block * units + units]
+        ).astype(bf)
+
+
+def expert_slots(shape, start=0):
+    return pl.BlockSpec(
+        (shape[0], 1) + tuple(shape[2:]), lambda e: (0, e) + (0,) * (len(shape) - 3) + (start,)
+    )
+
+
+def per_expert(shape):
+    return pl.BlockSpec((1,) + tuple(shape[1:]), lambda e: (e,) + (0,) * (len(shape) - 1))
+
+
+def expert_params(flops, moved):
+    return dict(
+        compiler_params=pltpu.CompilerParams(vmem_limit_bytes=56 << 20),
+        cost_estimate=pl.CostEstimate(flops=flops, bytes_accessed=moved, transcendentals=1 << 19),
+    )
+
+
+def expert_early(cot_rows, down):
+    sources, local, cap, _ = cot_rows.shape
+    units, dim = down.shape[1:]
+    return pl.pallas_call(
+        expert_early_kernel,
+        grid=(local,),
+        in_specs=[expert_slots((sources, local, cap, dim)), per_expert(down.shape)],
+        out_specs=per_expert((local, sources * cap, units)),
+        out_shape=jax.ShapeDtypeStruct((local, sources * cap, units), jnp.float32),
+        name="expert_early",
+        **expert_params(2 << 30, 8 << 20),
+    )(cot_rows, down)
+
+
+def expert_main(rows, cot_rows, raw, gate, up, w_all, marks):
+    sources, local, cap, dim = rows.shape
+    units = gate.shape[2]
+    count = sources * cap
+    hidden = jax.ShapeDtypeStruct((local, count, units), jnp.bfloat16)
+    back = (sources, local, cap, dim + 128)
+    return pl.pallas_call(
+        expert_main_kernel,
+        grid=(local,),
+        in_specs=[
+            expert_slots(rows.shape),
+            expert_slots((sources, local, cap, 128), dim // 128),
+            per_expert(raw.shape),
+            per_expert(gate.shape),
+            per_expert(up.shape),
+            pl.BlockSpec((dim, 128), lambda e: (0, w_all.shape[1] // 128 - 1)),
+            per_expert(marks.shape),
+        ],
+        out_specs=[expert_slots(back)] + [per_expert(hidden.shape)] * 4,
+        out_shape=[jax.ShapeDtypeStruct(back, jnp.bfloat16)] + [hidden] * 4,
+        name="expert_main",
+        **expert_params(8 << 30, 20 << 20),
+    )(rows, cot_rows, raw, gate, up, w_all, marks)
+
+
+def expert_late(rows, cot_rows, act, scaled, d_g, d_v, down):
+    sources, local, cap, dim = rows.shape
+    units = down.shape[1]
+    grads = (local, 3 * dim, units)
+    return pl.pallas_call(
+        expert_late_kernel,
+        grid=(local,),
+        in_specs=[expert_slots(rows.shape), expert_slots(rows.shape)]
+        + [per_expert(act.shape)] * 4
+        + [per_expert(down.shape)],
+        out_specs=[
+            expert_slots(rows.shape),
+            per_expert(grads),
+        ],
+        out_shape=[
+            jax.ShapeDtypeStruct(rows.shape, jnp.bfloat16),
+            jax.ShapeDtypeStruct(grads, jnp.bfloat16),
+        ],
+        name="expert_late",
+        **expert_params(7 << 30, 24 << 20),
+    )(rows, cot_rows, act, scaled, d_g, d_v, down)
+
+
+def assemble_kernel(gate_ref, rest_ref, weight_ref, gain_ref, grad_ref, small_ref):
+    f32, bf = jnp.float32, jnp.bfloat16
+    groups = gate_ref.shape[0]
+    inner = groups * WIDE
+    gain = gain_ref[...]
+    grad_gain = jnp.zeros(gain.shape, f32)
+    keys = jnp.zeros((gain.shape[0], 256), f32)
+    tail = jnp.zeros((gain.shape[0], 128), f32)
+    steps = jnp.zeros((gain.shape[0], 128), f32)
+    rows, columns = grid_of((128, 128))
+
+    def put(start, values):
+        nonlocal grad_gain
+        stop = start + values.shape[1]
+        weight = weight_ref[:, start:stop].astype(f32)
+        grad_gain = grad_gain + jnp.sum(weight * values, axis=1, keepdims=True)
+        grad_ref[:, start:stop] = values * gain
+
+    for group in range(groups):
+        put(group * WIDE, gate_ref[group, :, :WIDE].astype(f32))
+        put(inner + group * WIDE, rest_ref[group, :, :WIDE].astype(f32))
+        keys = keys + rest_ref[group, :, WIDE:CONVW].astype(f32)
+        last = rest_ref[group, :, CONVW:]
+        tail = tail + last.astype(f32)
+        moved = mark((rows < HEADS_HERE) & (columns == rows + HEADS_HERE * group))
+        steps = steps + times(last, moved)
+    put(2 * inner, keys)
+    put(2 * inner + 256, steps[:, : groups * HEADS_HERE])
+    lane = lax.broadcasted_iota(jnp.int32, tail.shape, 1)
+    small_ref[...] = jnp.where(lane == 0, grad_gain, tail)
+
+
+def assemble(gate_sums, rest_sums, in_weight, gain):
+    rows, width = in_weight.shape
+    return pl.pallas_call(
+        assemble_kernel,
+        in_specs=[pl.BlockSpec(memory_space=pltpu.VMEM)] * 4,
+        out_specs=[pl.BlockSpec(memory_space=pltpu.VMEM)] * 2,
+        out_shape=[
+            jax.ShapeDtypeStruct((rows, width), jnp.float32),
+            jax.ShapeDtypeStruct((rows, 128), jnp.float32),
+        ],
+        compiler_params=pltpu.CompilerParams(vmem_limit_bytes=32 << 20),
+        cost_estimate=pl.CostEstimate(flops=4 << 20, bytes_accessed=8 << 20, transcendentals=0),
+        name="assemble",
+    )(gate_sums, rest_sums, in_weight, gain)
+
+
+def sum_expert_grads(grads, q):
+    f32, bf = jnp.float32, jnp.bfloat16
+    size = lax.axis_size("seq")
+    core, z = q % 2, q // 2
+    mates = [(i, i ^ 1) for i in range(size)]
+    near = [(i, 2 * ((i // 2) ^ 1) + i % 2) for i in range(size)]
+    far = [(i, 2 * (size // 2 - 1 - i // 2) + i % 2) for i in range(size)]
+    inner = ((z == 1) | (z == 2)).astype(jnp.int32)
+    high = (z >= 2).astype(jnp.int32)
+
+    def add(left, right):
+        return (left.astype(f32) + right.astype(f32)).astype(bf)
+
+    def halve(values, bit, pairs):
+        parts = values.reshape(2, values.shape[0] // 2, values.shape[1])
+        sent = lax.dynamic_index_in_dim(parts, 1 - bit, 0, keepdims=False)
+        kept = lax.dynamic_index_in_dim(parts, bit, 0, keepdims=False)
+        return add(kept, lax.ppermute(sent, "seq", pairs))
+
+    def double(values, bit, pairs):
+        other = lax.ppermute(values, "seq", pairs)
+        both = jnp.stack([values, other])
+        return jnp.where(bit == 0, both, both[::-1]).reshape(-1, values.shape[-1])
+
+    flat = grads.reshape(2 * grads.shape[1], grads.shape[2])
+    mine = halve(flat, core, mates)
+    cutoff = mine.shape[0] // 2
+    first, second = mine[:cutoff], mine[cutoff:]
+    first, second = halve(first, inner, near), halve(second, high, far)
+    first, second = halve(first, high, far), halve(second, inner, near)
+    first, second = double(first, high, far), double(second, inner, near)
+    first, second = double(first, inner, near), double(second, high, far)
+    return double(jnp.concatenate([first, second], axis=0), core, mates).reshape(grads.shape)
 
 
 def on_device(
@@ -438,10 +660,11 @@
     total = -(-(at_moe + 1) // 128) * 128
     packed = jnp.pad(packed, ((0, 0), (0, total - packed.shape[1])))
 
-    w_all = lax.all_gather(packed, "shard", axis=0, tiled=True)
-    x_all = lax.all_to_all(
-        jnp.broadcast_to(x_low[None], (sq, toks, dim)), "seq", split_axis=0, concat_axis=0, tiled=True
-    ).reshape(seq_rows, dim)
+    def to_shards(values):
+        return lax.all_to_all(values, "shard", split_axis=0, concat_axis=0, tiled=True)
+
+    x_all = lax.all_gather(x_low, "seq", axis=0, tiled=True)
+    w_all = to_shards(jnp.broadcast_to(packed[None], (sh, rows_w, total))).reshape(dim, total)
 
     out_scaled = (norm_gain.astype(f32)[:, None] * out_weight.astype(f32)).astype(bf)
     own_out = out_weight.shape[0] // sq
@@ -475,7 +698,6 @@
         [shared_cols[fold * band : fold * band + fold] for band in range(bands)], axis=1
     )
     piece = jnp.concatenate([piece, shared_rows], axis=0)
-    piece, w_all = lax.optimization_barrier((piece, w_all))
     rows_all = lax.all_gather(piece, "shard", axis=0)
     own_rows = own_out + own_down
     w_out = rows_all[:, :own_out].reshape(gw, dim)
@@ -504,25 +726,22 @@
     cot = out_cotangent[0].astype(f32) * live[:, None]
     cot_low = cot.astype(bf)
 
-    def to_experts(rows):
-        return lax.all_to_all(
-            rows.reshape(experts, CAP, rows.shape[-1]),
-            "shard",
-            split_axis=0,
-            concat_axis=1,
-            tiled=True,
-        )
-
-    cot_ext = jnp.concatenate(
-        [cot_low, named.astype(bf), jnp.zeros((toks, 128 - experts), bf)], axis=1
-    )
-    cot_rows_ext = to_experts(times(dispatch_flat, cot_ext).astype(bf))
+    local_slots = (sh, local_e, CAP)
+
+    def dispatched(values):
+        sent = times(dispatch_flat, values).astype(bf)
+        return to_shards(sent.reshape(sh, local_e * CAP, -1)).reshape(*local_slots, -1)
+
+    router_lane = at_router - (total - 128)
+    lanes = jnp.arange(128, dtype=jnp.int32)
+    named_lanes = jnp.pad(named, ((0, 0), (router_lane, 128 - router_lane - experts)))
+    cot_rows = dispatched(jnp.concatenate([cot_low, named_lanes.astype(bf)], axis=1))
 
     x_wide = x_all.astype(f32)
     x_r = row_scale(x_wide)
     proj = times(x_all, w_all) * x_r
 
-    small_all = w_all.reshape(sh, rows_w, total)[:, :, at_small:at_router].reshape(sh, -1)
+    small_all = w_all[:, at_small:at_router].reshape(sh, -1)
     at = taps * conv_own
     conv_full = (
         small_all[:, :at].reshape(sh, taps, conv_own).transpose(1, 0, 2).reshape(taps, conv_all)
@@ -553,13 +772,14 @@
     skip_in = jnp.broadcast_to(jnp.repeat(skip_local, per_head)[None], (8, gw))
     mixed, q_low, square_part, starts = scan_forward(proj, taps_in, head_in, skip_in)
 
+    w_out, cot_rows = lax.optimization_barrier((w_out, cot_rows))
     out_part = times(q_low, w_out).astype(bf)
     out_sum = lax.psum_scatter(out_part, "seq", scatter_dimension=0, tiled=True)
     square = lax.psum(square_part.reshape(sq, toks), "seq")
     q_r = lax.rsqrt(square / inner + epsilon).reshape(seq_rows, 1)
-    out_sum, cot_rows_ext = lax.optimization_barrier((out_sum, cot_rows_ext))
-    cot_rows = cot_rows_ext[:, :, :dim]
-    row_mask = cot_rows_ext[:, :, dim : dim + experts].astype(f32)
+    d_raw = expert_early(cot_rows, expert_down)
+    cot_late, _ = lax.optimization_barrier((cot_low, out_sum[:16, :128]))
+    cot_all = lax.all_gather(cot_late, "seq", axis=0, tiled=True)
     tok_r = lax.dynamic_slice_in_dim(q_r, q * toks, toks, 0)
     x_tok = x_low.astype(f32)
     added = out_sum.astype(f32) * tok_r
@@ -569,57 +789,27 @@
     resid_n = resid * resid_r
     moe_in = (resid_n * moe_gain_full[None, :]).astype(bf)
     moe_all = lax.all_gather(moe_in, "seq", axis=0, tiled=True)
-    cot_late, moe_all = lax.optimization_barrier((cot_low, moe_all))
-    cot_all = lax.all_gather(cot_late, "seq", axis=0, tiled=True)
-    logits = times(moe_in, router_full)
-
-    def masked_softmax(values, mask):
-        top = jnp.max(jnp.where(mask > 0.0, values, -jnp.inf), axis=-1, keepdims=True)
-        top = jnp.where(top > -jnp.inf, top, 0.0)
-        powers = jnp.where(mask > 0.0, jnp.exp(jnp.where(mask > 0.0, values - top, 0.0)), 0.0)
-        return powers / jnp.maximum(jnp.sum(powers, axis=-1, keepdims=True), 1e-30)
-
-    gates = masked_softmax(logits, named)
-    rows = to_experts(times(dispatch_flat, moe_in).astype(bf))
-    row_logits = lax.dot_general(
-        rows, router_full, (((2,), (0,)), ((), ())), preferred_element_type=f32
-    )
-    row_gates = masked_softmax(row_logits, row_mask)
+
+    logits = times(moe_in, w_all[:, total - 128 :])
+    top = jnp.max(jnp.where(named_lanes > 0.0, logits, -1e30), axis=1, keepdims=True)
+    powers = jnp.where(
+        named_lanes > 0.0, jnp.exp(jnp.where(named_lanes > 0.0, logits - top, 0.0)), 0.0
+    )
+    gates = (powers / jnp.sum(powers, axis=1, keepdims=True))[
+        :, router_lane : router_lane + experts
+    ]
+    rows = dispatched(moe_in)
     own_ids = lax.axis_index("shard") * local_e + jnp.arange(local_e, dtype=jnp.int32)
-    own_pick = (own_ids[:, None] == expert_ids[None, :]).astype(f32)
-    row_gate = jnp.sum(row_gates * own_pick[:, None, :], axis=2, keepdims=True)
-
-    d_raw = jnp.einsum("ecd,efd->ecf", cot_rows, expert_down, preferred_element_type=f32)
-    e_gate = jnp.einsum("ecd,edf->ecf", rows, expert_gate, preferred_element_type=f32)
-    e_up = jnp.einsum("ecd,edf->ecf", rows, expert_up, preferred_element_type=f32)
-    e_sig = jax.nn.sigmoid(e_gate)
-    e_silu = e_gate * e_sig
-    e_act = (e_silu * e_up).astype(bf)
-    d_gate_row = jnp.sum(e_act.astype(f32) * d_raw, axis=2, keepdims=True)
-    d_act = row_gate * d_raw
-    d_g = (d_act * e_up * (e_sig * (1.0 + e_gate * (1.0 - e_sig)))).astype(bf)
-    d_v = (d_act * e_silu).astype(bf)
-    d_row = jnp.einsum("ecf,edf->ecd", d_g, expert_gate, preferred_element_type=f32) + jnp.einsum(
-        "ecf,edf->ecd", d_v, expert_up, preferred_element_type=f32
-    )
-    hi = d_gate_row.astype(bf)
-    lo = (d_gate_row - hi.astype(f32)).astype(bf)
-    back_rows = jnp.concatenate(
-        [d_row.astype(bf), hi, lo, jnp.zeros(hi.shape[:2] + (126,), bf)], axis=2
-    )
-
-    def from_experts(values):
-        return lax.all_to_all(values, "shard", split_axis=1, concat_axis=0, tiled=True)
-
-    d_returned = from_experts(back_rows)
-    e_out = jnp.einsum("ecf,efd->ecd", e_act, expert_down, preferred_element_type=f32).astype(bf)
-    scaled_act = (row_gate * e_act.astype(f32)).astype(bf)
-    grad_e_down = jnp.einsum("ecf,ecd->efd", scaled_act, cot_rows, preferred_element_type=f32)
-    grad_e_gate = jnp.einsum("ecd,ecf->edf", rows, d_g, preferred_element_type=f32)
-    grad_e_up = jnp.einsum("ecd,ecf->edf", rows, d_v, preferred_element_type=f32)
-    e_sum = lax.psum(
-        (grad_e_gate.astype(bf), grad_e_up.astype(bf), grad_e_down.astype(bf)), "seq"
-    )
+    marks = jnp.stack(
+        [own_ids + router_lane, own_ids, own_ids + 64] + [jnp.full_like(own_ids, -1)] * 5, axis=1
+    )
+    marks = (marks[:, :, None] == lanes[None, None, :]).astype(f32)
+    back_rows, e_act, e_scaled, d_g, d_v = expert_main(
+        rows, cot_rows, d_raw, expert_gate, expert_up, w_all, marks
+    )
+    d_returned = to_shards(back_rows.reshape(sh, local_e * CAP, dim + 128))
+    e_out, e_grads = expert_late(rows, cot_rows, e_act, e_scaled, d_g, d_v, expert_down)
+    returned = to_shards(e_out.reshape(sh, local_e * CAP, dim))
 
     s_both = times(moe_all, w_shared)
     s_gate, s_up = s_both[:, :gf], s_both[:, gf:]
@@ -636,17 +826,12 @@
     )
     d_moe_part = times_transposed(d_both, w_shared).astype(bf)
     d_moe_shared = lax.psum_scatter(d_moe_part, "seq", scatter_dimension=0, tiled=True)
-    shared_part = times(s_act, w_down).astype(bf)
-    shared_sum = lax.psum_scatter(shared_part, "seq", scatter_dimension=0, tiled=True)
-
-    d_flat = d_returned.reshape(slots, dim + 128)
-    gate_back = jnp.sum(
-        d_flat[:, dim : dim + 2].astype(f32), axis=1
-    ).reshape(experts, CAP)
-    d_gates = jnp.sum(dispatch.astype(f32) * gate_back[:, :, None], axis=1).T
+
+    d_flat = transposed_times(dispatch_flat, d_returned.reshape(slots, dim + 128))
+    d_gates = d_flat[:, dim : dim + experts] + d_flat[:, dim + 64 : dim + 64 + experts]
     d_logits = gates * (d_gates - jnp.sum(gates * d_gates, axis=1, keepdims=True))
     d_moe = (
-        transposed_times(dispatch_flat, d_flat[:, :dim])
+        d_flat[:, :dim]
         + d_moe_shared.astype(f32)
         + jnp.dot(d_logits, router_full.astype(f32).T, precision=highest)
     )
@@ -663,14 +848,11 @@
     d_o_all = lax.all_gather(d_o, "seq", axis=0, tiled=True)
     kappa_all = lax.all_gather(kappa.reshape(1, toks), "seq", axis=0).reshape(seq_rows, 1)
 
-    returned = from_experts(e_out)
+    s_late, _ = lax.optimization_barrier((s_act, d_o_all[:16, :128]))
+    shared_part = times(s_late, w_down).astype(bf)
+    shared_sum = lax.psum_scatter(shared_part, "seq", scatter_dimension=0, tiled=True)
     weighted = (gates.T[:, None, :] * dispatch.astype(f32)).reshape(slots, toks)
-    combined = lax.dot_general(
-        weighted,
-        returned.reshape(slots, dim).astype(f32),
-        (((0,), (0,)), ((), ())),
-        preferred_element_type=f32,
-    )
+    combined = transposed_times(weighted.astype(bf), returned.reshape(slots, dim))
     block_output = ((resid + shared_sum.astype(f32) + combined) * live[:, None]).astype(bf)[None]
 
     d_gated = times_transposed(d_o_all, w_out)
@@ -678,24 +860,11 @@
     grad_down_part = transposed_times(s_act, cot_all)
     grad_shared_part = transposed_times(moe_all, d_both)
 
-    def to_shards(values):
-        return lax.all_to_all(values.astype(bf), "shard", split_axis=0, concat_axis=0, tiled=True)
-
     rows_part = jnp.concatenate(
         [grad_out_part.reshape(sh, own_out, dim), grad_down_part.reshape(sh, own_down, dim)],
         axis=1,
     )
-    mid_part = jnp.concatenate(
-        [
-            grad_shared_part,
-            grad_router,
-            grad_moe[:, None],
-            jnp.zeros((dim, 128 - experts - 1), f32),
-        ],
-        axis=1,
-    )
-    moved_rows = to_shards(rows_part)
-    moved_mid = to_shards(mid_part.reshape(sh, rows_w, 2 * gf + 128))
+    moved_rows = to_shards(rows_part.astype(bf))
 
     row_values = jnp.concatenate(
         [q_r, kappa_all, x_r, jnp.zeros((seq_rows, 5), f32)], axis=1
@@ -708,23 +877,34 @@
     grad_bias_local = d_head[0, :gh]
     grad_decay_local = d_head[1, :gh] * decay_rate
     grad_skip_local = jnp.sum(d_skip[0].reshape(gh, per_head), axis=1)
-    d_proj, moved_rows, moved_mid = lax.optimization_barrier((d_proj, moved_rows, moved_mid))
-    rows_sum = jnp.sum(moved_rows.astype(f32), axis=0)
-    rows_sum = lax.ppermute(rows_sum.astype(bf), both_axes, backward_pairs)
-    rows_grad = lax.all_gather(rows_sum, "seq", axis=0)
-    grad_out_raw = rows_grad[:, :own_out].reshape(sq * own_out, dim).astype(f32)
-    grad_down = rows_grad[:, own_out:].reshape(sq * own_down, dim).astype(f32)
-    grad_out = norm_gain.astype(f32)[:, None] * grad_out_raw
-    grad_norm = jnp.sum(out_weight.astype(f32) * grad_out_raw, axis=1)
-
-    mid_sum = jnp.sum(moved_mid.astype(f32), axis=0)
-    mid_all = lax.all_gather(mid_sum.astype(bf), "seq", axis=0).astype(f32)
-    grad_shared_gate = mid_all[:, :, :gf].transpose(1, 0, 2).reshape(rows_w, fs)
-    grad_shared_up = mid_all[:, :, gf : 2 * gf].transpose(1, 0, 2).reshape(rows_w, fs)
-    mid_rest = jnp.sum(mid_all[:, :, 2 * gf :], axis=0)
-    grad_router_weight = mid_rest[:, :experts]
-    grad_moe_gain = mid_rest[:, experts]
-
+    d_proj, moved_rows = lax.optimization_barrier((d_proj, moved_rows))
+    d_gate_low = d_proj[:, :gw]
+    mid_part = jnp.concatenate(
+        [
+            transposed_times(x_all, d_gate_low),
+            grad_shared_part,
+            grad_router,
+            grad_moe[:, None],
+            jnp.zeros((dim, 128 - experts - 1), f32),
+        ],
+        axis=1,
+    )
+    mid_width = mid_part.shape[1]
+    moved_mid = to_shards(mid_part.astype(bf).reshape(sh, rows_w, mid_width))
+    rows_sum = jnp.sum(moved_rows.astype(f32), axis=0).astype(bf)
+    rows_sum = lax.ppermute(rows_sum, both_axes, backward_pairs)
+
+    e_all = sum_expert_grads(e_grads, q)
+    grad_e_gate = e_all[:, :dim].astype(f32)
+    grad_e_up = e_all[:, dim : 2 * dim].astype(f32)
+    units = expert_gate.shape[2]
+    grad_e_down = (
+        e_all[:, 2 * dim :]
+        .reshape(local_e, dim // units, units, units)
+        .transpose(0, 2, 1, 3)
+        .reshape(local_e, units, dim)
+        .astype(f32)
+    )
     back_part = times_transposed(d_proj, w_all).astype(bf)
     back_sum = lax.psum_scatter(back_part, "seq", scatter_dimension=0, tiled=True).astype(f32)
     tok_x_r = row_scale(x_tok)
@@ -733,7 +913,8 @@
         d_resid + back_sum - x_n * (tok_x_r * jnp.mean(back_sum * x_tok, axis=1, keepdims=True))
     )[None]
 
-    grad_in_part = transposed_times(x_all, d_proj)[:, :used]
+    rest = total - gw
+    grad_in_part = transposed_times(x_all, d_proj[:, gw:])
 
     def spread(local, count):
         wide = jnp.zeros(local.shape[:-1] + (count,), f32)
@@ -753,32 +934,37 @@
     small_part = jnp.pad(
         small_part, ((0, 0), (0, rows_w * small_cols - small_count))
     ).reshape(sh, rows_w, small_cols)
-    last_part = jnp.concatenate(
-        [
-            grad_in_part.reshape(sh, rows_w, used),
-            small_part,
-            jnp.zeros((sh, rows_w, total - used - small_cols), f32),
-        ],
-        axis=2,
-    )
-    last_sum = jnp.sum(to_shards(last_part).astype(f32), axis=0)
-    last_all = lax.all_gather(last_sum.astype(bf), "seq", axis=0).astype(f32)
-
-    def side_by_side(start, width):
-        return last_all[:, :, start : start + width].transpose(1, 0, 2).reshape(rows_w, sq * width)
-
-    grad_in_raw = jnp.concatenate(
-        [
-            side_by_side(0, gw),
-            side_by_side(gw, gw),
-            jnp.sum(last_all[:, :, 2 * gw : 2 * gw + keys_w], axis=0),
-            side_by_side(2 * gw + keys_w, gh),
-        ],
-        axis=1,
-    )
-    grad_in = gain_col * grad_in_raw
-    grad_mixer_gain = jnp.sum(in_weight.astype(f32) * grad_in_raw, axis=1)
-    small_sum = jnp.sum(last_all[:, :, used : used + small_cols], axis=0).reshape(-1)
+    small_at = used - gw
+    last_part = grad_in_part + jnp.pad(
+        small_part.reshape(dim, small_cols), ((0, 0), (small_at, rest - small_at - small_cols))
+    )
+    last_part, moved_mid = lax.optimization_barrier((last_part.astype(bf), moved_mid))
+    moved_last = to_shards(last_part.reshape(sh, rows_w, rest))
+    mid_sum = jnp.sum(moved_mid.astype(f32), axis=0).astype(bf)
+    side = lax.all_gather(
+        jnp.concatenate([rows_sum, mid_sum.reshape(rows_w * mid_width // dim, dim)], axis=0),
+        "seq",
+        axis=0,
+    )
+    rows_grad = side[:, :own_rows]
+    mid_all = side[:, own_rows:].reshape(sq, rows_w, mid_width)
+    last_sum = jnp.sum(moved_last.astype(f32), axis=0).astype(bf)
+    last_all = lax.all_gather(last_sum, "seq", axis=0)
+
+    grad_out_raw = rows_grad[:, :own_out].reshape(sq * own_out, dim).astype(f32)
+    grad_down = rows_grad[:, own_out:].reshape(sq * own_down, dim).astype(f32)
+    grad_out = norm_gain.astype(f32)[:, None] * grad_out_raw
+    grad_norm = jnp.sum(out_weight.astype(f32) * grad_out_raw, axis=1)
+    mid_all_f = mid_all[:, :, gw:].astype(f32)
+    grad_shared_gate = mid_all_f[:, :, :gf].transpose(1, 0, 2).reshape(rows_w, fs)
+    grad_shared_up = mid_all_f[:, :, gf : 2 * gf].transpose(1, 0, 2).reshape(rows_w, fs)
+    mid_rest = jnp.sum(mid_all_f[:, :, 2 * gf :], axis=0)
+    grad_router_weight = mid_rest[:, :experts]
+    grad_moe_gain = mid_rest[:, experts]
+    grad_in, tail_sums = assemble(mid_all, last_all, in_weight, gain_col)
+    grad_mixer_gain = tail_sums[:, 0]
+    lane_at = used - (total - 128)
+    small_sum = tail_sums[:, lane_at : lane_at + small_cols].reshape(-1)
     at = taps * conv_own
     grad_conv = small_sum[:at].reshape(taps, conv_own)
     grad_offset = small_sum[at : at + conv_own]
@@ -803,9 +989,9 @@
         grad_shared_gate,
         grad_shared_up,
         grad_down,
-        e_sum[0].astype(f32),
-        e_sum[1].astype(f32),
-        e_sum[2].astype(f32),
+        grad_e_gate,
+        grad_e_up,
+        grad_e_down,
     )
 
 

time: 712 us -> 819 us (1.15)
  waiting for transfers between devices: 167 us -> 356 us
  blocking collectives: 103 us -> 27.8 us
  local copies, waits for them, and re-layouts: 126 us -> 76.6 us
  matrix products: 115 us -> 72.8 us
  other arithmetic: 62.8 us -> 99.6 us
  Pallas kernels: 34.3 us -> 67 us
  starting transfers between devices: 75.9 us -> 92.2 us
    ppermute x1 -> x11, waiting for transfers between devices: 0.01 us -> 77.9 us  [the longest x5 43.5 us: halve(): return add(kept, lax.ppermute(sent, 'seq', pairs))]
    dot_general x11 -> x0, matrix products: 45.1 us -> none  [the longest x1 7.53 us: on_device(): jnp.einsum('ecd,efd->ecf', cot_rows, expert_down, preferred_element_type=...]
    all_to_all x1 -> x0, blocking collectives: 44.1 us -> none  [to_experts(): lax.all_to_all(rows.reshape(experts, CAP, rows.shape[-1]), 'shard', split...]
    all_gather x1, waiting for transfers between devices: 13.6 us -> 47.7 us  [on_device(): rows_all = lax.all_gather(piece, 'shard', axis=0)]
    pallas_call x0 -> x4, Pallas kernels: none -> 32.7 us  [the longest x1 13 us: expert_main(): pl.pallas_call(expert_main_kernel, grid=(local,), in_specs=[expert_slots(...]
    all_gather x2 -> x0, blocking collectives: 29.4 us -> none  [the longest x1 15.4 us: on_device(): mid_all = lax.all_gather(mid_sum.astype(bf), 'seq', axis=0).astype(f32)]
    all_gather x1, waiting for transfers between devices: 0.01 us -> 25.9 us  [on_device(): cot_all = lax.all_gather(cot_late, 'seq', axis=0, tiled=True)]
    another operation x0 -> x6, other arithmetic: none -> 20.9 us  [double(): both = jnp.stack([values, other])]
  transfers between devices with their start and end apart: 20 -> 31, of which waited for: 8 -> 15; matrix products, arithmetic and copies ran while one was open for 34% -> 27% of each run, Pallas kernels for 5% -> 7%
where the time goes in v3:
time: 819 us; the launch traced here: 808 us
  waiting for transfers between devices  356 us (43%)
  other arithmetic  99.6 us (12%)
  starting transfers between devices  92.2 us (11%)
  local copies, waits for them, and re-layouts  76.6 us (9%)
  matrix products  72.8 us (9%)
  Pallas kernels  67 us (8%)
  blocking collectives  27.8 us (3%)
  between operations  15.8 us (2%)
    all_to_all x8, waiting for transfers between devices, to_shards(): lax.all_to_all(values, 'shard', split_axis=0, concat_axis=0, tiled=True)  122 us
    all_to_all x8, starting transfers between devices, to_shards(): lax.all_to_all(values, 'shard', split_axis=0, concat_axis=0, tiled=True)  64.7 us
    all_gather x1, waiting for transfers between devices, on_device(): rows_all = lax.all_gather(piece, 'shard', axis=0)  47.7 us
    ppermute x5, waiting for transfers between devices, halve(): return add(kept, lax.ppermute(sent, 'seq', pairs))  43.5 us
    ppermute x5, waiting for transfers between devices, double(): other = lax.ppermute(values, 'seq', pairs)  34.4 us
    all_gather x1, waiting for transfers between devices, on_device(): x_all = lax.all_gather(x_low, 'seq', axis=0, tiled=True)  34.2 us
    dot_general x7, matrix products, times(): return jnp.dot(left, right, preferred_element_type=jnp.float32)  26.3 us
    all_gather x1, waiting for transfers between devices, on_device(): cot_all = lax.all_gather(cot_late, 'seq', axis=0, tiled=True)  25.9 us
  transfers between devices with their start and end apart: 31, of which 15 were waited for; matrix products, arithmetic and copies ran while one was open for 27% of the time, Pallas kernels for 7%

profile of v3, /device:TPU:1, one launch (start us, length us, event | category | flops | bytes accessed | tf_op | source)
XLA Modules:
  0.0 807.9 jit_solution(14931622791664124994)
XLA Ops:
  22.5 11.8 %all-to-all-start = ((bf16[16,96,1152]{2,1,0:T(8,128)(2,1)}), bf16[16,96,1152]{2,1,0:T(8,128)(2,1)S(1)}, u32[]{:S(2)}, u32[]{:S(2)}) async-start(bf16[16,96,1152]{2,1,0:T(8,128)(2,1)} %broadcast_in_dim.33), calls=%async_computation | async-start | bytes 7077888 | tf_op jit(solution)/shard_map/all_to_all | solution.py:664
  48.0 33.2 %all-to-all-done = bf16[16,96,1152]{2,1,0:T(8,128)(2,1)S(1)} async-done(((bf16[16,96,1152]{2,1,0:T(8,128)(2,1)}), bf16[16,96,1152]{2,1,0:T(8,128)(2,1)S(1)}, u32[]{:S(2)}, u32[]{:S(2)}) %all-to-all-start) | async-done | bytes 3538976 | tf_op jit(solution)/shard_map/all_to_all | solution.py:664
  90.8 47.7 %all-gather.22.cloned.1.call-done = bf16[768,1536]{1,0:T(8,128)(2,1)} async-done(((bf16[48,1536]{1,0:T(8,128)(2,1)}), bf16[768,1536]{1,0:T(8,128)(2,1)}) %all-gather.22.cloned.1.call-update) | async-done | bytes 2359312 | tf_op jit(solution)/shard_map/all_gather | solution.py:701
  140.8 34.2 %all-gather.20.cloned.1.call-done = bf16[1,1024,1536]{2,1,0:T(8,128)(2,1)} async-done(((bf16[1,128,1536]{2,1,0:T(8,128)(2,1)}), bf16[1,1024,1536]{2,1,0:T(8,128)(2,1)}) %all-gather.20.cloned.1.call-update) | async-done | bytes 3145744 | tf_op jit(solution)/shard_map/all_gather | solution.py:666
  184.1 10.9 %scan_forward.1 = (bf16[1024,384]{1,0:T(8,128)(2,1)S(1)}, bf16[1024,384]{1,0:T(8,128)(2,1)S(1)}, f32[1024,1]{1,0:T(8,128)S(1)}, f32[8,128,384]{2,1,0:T(8,128)S(1)}) custom-call(f32[1024,1152]{1,0:T(8,128)S(1)} %fusion.2.proj_ref.prev_ref, f32[1024,1152]{1,0:T(8,128)S(1)} %fusion.2.proj_ref.prev_ref, f32[8,640]{1,0:T(8,128)S(1)} %maximum_maximum_fusion.1.taps_ref, ...), custom_call_target="tpu_custom_call" | custom-call | flops 3221225472 | bytes 12582912 | tf_op jit(solution)/shard_map/scan_forward/pallas_call | solution.py:285
  201.1 12.1 %psum.7 = f32[8,128]{1,0:T(8,128)S(1)} all-reduce(f32[8,128]{1,0:T(8,128)S(1)} %bitcast.272), channel_id=1, replica_groups=mesh['seq'=8,'shard'=16] {'seq'}, use_global_device_ids=true, to_apply=%region_3.4 | all-reduce | flops 1024 | bytes 8192 | tf_op jit(solution)/shard_map/psum | solution.py:778
  213.1 18.6 %reduce-scatter.5.cloned.1.call-done = bf16[128,1536]{1,0:T(8,128)(2,1)} async-done(((bf16[1024,1536]{1,0:T(8,128)(2,1)}), bf16[128,1536]{1,0:T(8,128)(2,1)}) %reduce-scatter.5.cloned.1.call-update) | async-done | bytes 393232 | tf_op jit(solution)/shard_map/reduce_scatter | solution.py:777
  239.4 6.6 all-to-all-start.2
  253.7 11.9 %all-gather.14.cloned.1.call-done = bf16[1024,1536]{1,0:T(8,128)(2,1)} async-done(((bf16[128,1536]{1,0:T(8,128)(2,1)}), bf16[1024,1536]{1,0:T(8,128)(2,1)}) %all-gather.14.cloned.1.call-update) | async-done | bytes 3145744 | tf_op jit(solution)/shard_map/all_gather | solution.py:791
  269.7 25.9 %all-gather.16.cloned.1.call-done = bf16[1024,1536]{1,0:T(8,128)(2,1)} async-done(((bf16[128,1536]{1,0:T(8,128)(2,1)}), bf16[1024,1536]{1,0:T(8,128)(2,1)}) %all-gather.16.cloned.1.call-update) | async-done | bytes 3145744 | tf_op jit(solution)/shard_map/all_gather | solution.py:782
  309.0 13.0 %expert_main.1 = (bf16[16,2,32,1664]{3,2,1,0:T(8,128)(2,1)}, bf16[2,512,512]{2,1,0:T(8,128)(2,1)}, bf16[2,512,512]{2,1,0:T(8,128)(2,1)}, bf16[2,512,512]{2,1,0:T(8,128)(2,1)}, bf16[2,512,512]{2,1,0:T(8,128)(2,1)}) custom-call(bf16[16,2,32,1536]{3,2,1,0:T(8,128)(2,1)} %bitcast.25.rows_ref, bf16[16,2,32,1664]{3,2,1,0:T(8,128)(2,1)} %bitcast.16.cot_ref.routed_ref, ...), custom_call_target="tpu_custom_call" | custom-call | flops 8589934592 | bytes 20971520 | tf_op jit(solution)/shard_map/expert_main/pallas_call | solution.py:462
  322.1 12.8 %expert_late.1 = (bf16[16,2,32,1536]{3,2,1,0:T(8,128)(2,1)}, bf16[2,4608,512]{2,1,0:T(8,128)(2,1)}) custom-call(bf16[16,2,32,1536]{3,2,1,0:T(8,128)(2,1)} %bitcast.25.rows_ref, bf16[16,2,32,1664]{3,2,1,0:T(8,128)(2,1)} %bitcast.16.cot_ref.routed_ref, bf16[2,512,512]{2,1,0:T(8,128)(2,1)} %get-tuple-element.46.act_ref, ...), custom_call_target="tpu_custom_call" | custom-call | flops 7516192768 | bytes 25165824 | tf_op jit(solution)/shard_map/expert_late/pallas_call | solution.py:485
  339.9 6.7 all-to-all-start.4
  348.5 44.0 %all-to-all-done.4 = bf16[16,64,1664]{2,1,0:T(8,128)(2,1)} async-done(((bf16[16,64,1664]{2,1,0:T(8,128)(2,1)}), bf16[16,64,1664]{2,1,0:T(8,128)(2,1)}, u32[]{:S(2)}, u32[]{:S(2)}) %all-to-all-start.4) | async-done | bytes 3407904 | tf_op jit(solution)/shard_map/all_to_all | solution.py:664
  414.0 35.0 %collective-permute-done.3 = bf16[1152,512]{1,0:T(8,128)(2,1)} collective-permute-done((bf16[1152,512]{1,0:T(8,128)(2,1)}, bf16[1152,512]{1,0:T(8,128)(2,1)}, u32[]{:S(2)}, u32[]{:S(2)}) %collective-permute-start.3) | collective-permute-done | bytes 1179680 | tf_op jit(solution)/shard_map/ppermute | solution.py:569
  456.5 8.5 %collective-permute-done.4 = bf16[576,512]{1,0:T(8,128)(2,1)S(1)} collective-permute-done((bf16[576,512]{1,0:T(8,128)(2,1)S(1)}, bf16[576,512]{1,0:T(8,128)(2,1)S(1)}, u32[]{:S(2)}, u32[]{:S(2)}) %collective-permute-start.4) | collective-permute-done | bytes 589856 | tf_op jit(solution)/shard_map/ppermute | solution.py:569
  492.7 29.1 %collective-permute-done.6 = bf16[1152,512]{1,0:T(8,128)(2,1)} collective-permute-done((bf16[1152,512]{1,0:T(8,128)(2,1)}, bf16[1152,512]{1,0:T(8,128)(2,1)}, u32[]{:S(2)}, u32[]{:S(2)}) %collective-permute-start.6) | collective-permute-done | bytes 1179680 | tf_op jit(solution)/shard_map/ppermute | solution.py:572
  525.6 15.7 %all-gather.5 = f32[8,1,128]{2,1,0:T(1,128)S(1)} all-gather(f32[1,1,128]{2,1,0:T(1,128)S(1)} %multiply_bitcast_fusion), channel_id=4, replica_groups=mesh['seq'=8,'shard'=16] {'seq'}, dimensions={0}, use_global_device_ids=true | all-gather | bytes 4608 | tf_op jit(solution)/shard_map/all_gather | solution.py:849
  546.1 13.3 %all-to-all-start.5 = ((bf16[16,32,1536]{2,1,0:T(8,128)(2,1)}), bf16[16,32,1536]{2,1,0:T(8,128)(2,1)}, u32[]{:S(2)}, u32[]{:S(2)}) async-start(bf16[16,32,1536]{2,1,0:T(8,128)(2,1)} %pad_maximum_fusion.4), calls=%async_computation.8 | async-start | bytes 3145728 | tf_op jit(solution)/shard_map/all_to_all | solution.py:664
  565.3 23.4 %scan_backward.1 = (bf16[1024,1152]{1,0:T(8,128)(2,1)}, f32[8,640]{1,0:T(8,128)S(1)}, f32[8,128]{1,0:T(8,128)S(1)}, f32[8,384]{1,0:T(8,128)S(1)}) custom-call(f32[1024,1152]{1,0:T(8,128)} %copy-done.5, f32[1024,1152]{1,0:T(8,128)} %copy-done.5, bf16[1024,384]{1,0:T(8,128)(2,1)S(1)} %copy-done.7, f32[1024,384]{1,0:T(8,128)S(1)} %fusion.75.d_gated_ref, ...), custom_call_target="tpu_custom_call" | custom-call | flops 10737418240 | bytes 20971520 | tf_op jit(solution)/shard_map/scan_backward/pallas_call | solution.py:323
  600.0 6.7 all-to-all-start.6
  626.7 10.9 %all-to-all-done.6 = bf16[16,96,768]{2,1,0:T(8,128)(2,1)} async-done(((bf16[16,96,768]{2,1,0:T(8,128)(2,1)}), bf16[16,96,768]{2,1,0:T(8,128)(2,1)}, u32[]{:S(2)}, u32[]{:S(2)}) %all-to-all-start.6) | async-done | bytes 2359328 | tf_op jit(solution)/shard_map/all_to_all | solution.py:664
  647.4 6.9 collective-permute-start.11
  659.0 7.7 convolution_convert_fusion.5
  667.7 34.0 %all-to-all-done.3 = bf16[16,64,1536]{2,1,0:T(8,128)(2,1)} async-done(((bf16[16,64,1536]{2,1,0:T(8,128)(2,1)}), bf16[16,64,1536]{2,1,0:T(8,128)(2,1)}, u32[]{:S(2)}, u32[]{:S(2)}) %all-to-all-start.3) | async-done | bytes 3145760 | tf_op jit(solution)/shard_map/all_to_all | solution.py:664
  705.1 8.4 %pad_maximum_fusion = bf16[2,4608,512]{2,1,0:T(8,128)(2,1)} fusion(bf16[1,4608,512]{2,1,0:T(8,128)(2,1)} %bitcast.86, bf16[1,4608,512]{2,1,0:T(8,128)(2,1)} %get-tuple-element.171), kind=kLoop, calls=%fused_computation.1 | loop fusion | flops 4718592 | bytes 18874368 | tf_op jit(solution)/shard_map/stack | solution.py:573
  716.0 10.5 %all-to-all-start.7 = ((bf16[16,96,768]{2,1,0:T(8,128)(2,1)}), bf16[16,96,768]{2,1,0:T(8,128)(2,1)S(1)}, u32[]{:S(2)}, u32[]{:S(2)}) async-start(bf16[16,96,768]{2,1,0:T(8,128)(2,1)} %bitcast.229), calls=%async_computation.11 | async-start | bytes 4718592 | tf_op jit(solution)/shard_map/all_to_all | solution.py:664
  726.6 13.0 %reverse_select_fusion = bf16[2,4608,512]{2,1,0:T(8,128)(2,1)} fusion(bf16[2,4608,512]{2,1,0:T(8,128)(2,1)} %pad_maximum_fusion, pred[]{:T(512)S(6)} %eq.101), kind=kLoop, calls=%fused_computation | loop fusion | flops 4718592 | bytes 18874368 | tf_op jit(solution)/shard_map/jit(_where)/select_n | solution.py:574
  739.6 8.0 fusion.69
  751.2 6.6 copy.172
  757.8 6.6 copy.174
  781.8 13.3 %all-gather.26.cloned.1.call-done = bf16[768,768]{1,0:T(8,128)(2,1)} async-done(((bf16[96,768]{1,0:T(8,128)(2,1)}), bf16[768,768]{1,0:T(8,128)(2,1)}) %all-gather.26.cloned.1.call-update) | async-done | bytes 1179664 | tf_op jit(solution)/shard_map/all_gather | solution.py:952
  (364 shorter events, 245.1 us)
Async XLA Ops:
  7.3 131.1 %all-gather.22.cloned.1.call-start = ((), (), s32[]{:S(2)}) async-start(), calls=%async_computation.20 | async-start | bytes 2506752 | tf_op jit(solution)/shard_map/all_gather | solution.py:701
  9.6 8.5 %collective-permute-start = (bf16[32,1536]{1,0:T(8,128)(2,1)S(1)}, bf16[32,1536]{1,0:T(8,128)(2,1)S(1)}, u32[]{:S(2)}, u32[]{:S(2)}) collective-permute-start(bf16[32,1536]{1,0:T(8,128)(2,1)S(1)} %pad_maximum_fusion.13), channel_id=1, source_target_pairs={{0,0},{16,1},{32,2},{48,3},{64,4},{80,5},{96,6},{112,7},{1,8},{17,... | collective-permute-start | bytes 294920 | tf_op jit(solution)/shard_map/ppermute | solution.py:687
  22.5 58.7 %all-to-all-start = ((bf16[16,96,1152]{2,1,0:T(8,128)(2,1)}), bf16[16,96,1152]{2,1,0:T(8,128)(2,1)S(1)}, u32[]{:S(2)}, u32[]{:S(2)}) async-start(bf16[16,96,1152]{2,1,0:T(8,128)(2,1)} %broadcast_in_dim.33), calls=%async_computation | async-start | bytes 7077888 | tf_op jit(solution)/shard_map/all_to_all | solution.py:664
  34.3 140.7 %all-gather.20.cloned.1.call-start = ((), (), s32[]{:S(2)}) async-start(), calls=%async_computation.19 | async-start | bytes 3538944 | tf_op jit(solution)/shard_map/all_gather | solution.py:666
  81.2 59.7 %all-to-all-start.1 = ((bf16[16,64,1664]{2,1,0:T(8,128)(2,1)}), bf16[16,64,1664]{2,1,0:T(8,128)(2,1)}, u32[]{:S(2)}, u32[]{:S(2)}) async-start(bf16[16,64,1664]{2,1,0:T(8,128)(2,1)} %bitcast.15), calls=%async_computation.1 | async-start | bytes 6815744 | tf_op jit(solution)/shard_map/all_to_all | solution.py:664
  85.7 146.1 %reduce-scatter.5.cloned.1.call-start = ((), (), s32[]{:S(2)}) async-start(), calls=%async_computation.12 | async-start | bytes 3538944 | tf_op jit(solution)/shard_map/reduce_scatter | solution.py:777
  199.4 66.2 %all-gather.14.cloned.1.call-start = ((), (), s32[]{:S(2)}) async-start(), calls=%async_computation.13 | async-start | bytes 3538944 | tf_op jit(solution)/shard_map/all_gather | solution.py:791
  235.1 60.5 %all-gather.16.cloned.1.call-start = ((), (), s32[]{:S(2)}) async-start(), calls=%async_computation.15 | async-start | bytes 3538944 | tf_op jit(solution)/shard_map/all_gather | solution.py:782
  239.4 69.7 %all-to-all-start.2 = ((bf16[16,64,1536]{2,1,0:T(8,128)(2,1)}), bf16[16,64,1536]{2,1,0:T(8,128)(2,1)}, u32[]{:S(2)}, u32[]{:S(2)}) async-start(bf16[16,64,1536]{2,1,0:T(8,128)(2,1)} %bitcast.225), calls=%async_computation.4 | async-start | bytes 6291456 | tf_op jit(solution)/shard_map/all_to_all | solution.py:664
  246.0 150.2 %reduce-scatter.9.cloned.1.call-start = ((), (), s32[]{:S(2)}) async-start(), calls=%async_computation.16 | async-start | bytes 3538944 | tf_op jit(solution)/shard_map/reduce_scatter | solution.py:828
  339.7 60.7 %collective-permute-start.2 = (bf16[4608,512]{1,0:T(8,128)(2,1)}, bf16[4608,512]{1,0:T(8,128)(2,1)}, u32[]{:S(2)}, u32[]{:S(2)}) collective-permute-start(bf16[4608,512]{1,0:T(8,128)(2,1)} %dynamic-slice_bitcast_fusion), channel_id=1, source_target_pairs={{0,16},{16,0},{32,48},{48,32},{64,80},{80,64},{96,112},{112,96},{1... | collective-permute-start | bytes 14155784 | tf_op jit(solution)/shard_map/ppermute | solution.py:569
  339.9 52.6 %all-to-all-start.4 = ((bf16[16,64,1664]{2,1,0:T(8,128)(2,1)}), bf16[16,64,1664]{2,1,0:T(8,128)(2,1)}, u32[]{:S(2)}, u32[]{:S(2)}) async-start(bf16[16,64,1664]{2,1,0:T(8,128)(2,1)} %bitcast.248), calls=%async_computation.6 | async-start | bytes 6815744 | tf_op jit(solution)/shard_map/all_to_all | solution.py:664
  346.6 194.7 %all-gather.18.cloned.1.call-start = ((), (), s32[]{:S(2)}) async-start(), calls=%async_computation.17 | async-start | bytes 3538944 | tf_op jit(solution)/shard_map/all_gather | solution.py:848
  400.3 301.3 %reduce-scatter.7.cloned.1.call-start = ((), (), s32[]{:S(2)}) async-start(), calls=%async_computation.14 | async-start | bytes 3538944 | tf_op jit(solution)/shard_map/reduce_scatter | solution.py:853
  409.8 39.3 %collective-permute-start.3 = (bf16[1152,512]{1,0:T(8,128)(2,1)}, bf16[1152,512]{1,0:T(8,128)(2,1)}, u32[]{:S(2)}, u32[]{:S(2)}) collective-permute-start(bf16[1152,512]{1,0:T(8,128)(2,1)} %dynamic-slice_bitcast_fusion.2), channel_id=1, source_target_pairs={{0,32},{16,48},{32,0},{48,16},{64,96},{80,112},{96,64},{112,80},{1... | collective-permute-start | bytes 3538952 | tf_op jit(solution)/shard_map/ppermute | solution.py:569
  412.3 40.8 %collective-permute-start.7 = (bf16[1152,512]{1,0:T(8,128)(2,1)}, bf16[1152,512]{1,0:T(8,128)(2,1)}, u32[]{:S(2)}, u32[]{:S(2)}) collective-permute-start(bf16[1152,512]{1,0:T(8,128)(2,1)} %dynamic-slice_bitcast_fusion.1), channel_id=1, source_target_pairs={{0,96},{16,112},{32,64},{48,80},{64,32},{80,48},{96,0},{112,16},{1... | collective-permute-start | bytes 3538952 | tf_op jit(solution)/shard_map/ppermute | solution.py:569
  414.0 39.0 %copy-start.11 = (bf16[2304,512]{1,0:T(8,128)(2,1)S(1)}, bf16[2304,512]{1,0:T(8,128)(2,1)}, u32[]{:S(2)}) copy-start(bf16[2304,512]{1,0:T(8,128)(2,1)} %get-tuple-element.174) | copy-start | bytes 7077892
  451.0 14.0 %collective-permute-start.4 = (bf16[576,512]{1,0:T(8,128)(2,1)S(1)}, bf16[576,512]{1,0:T(8,128)(2,1)S(1)}, u32[]{:S(2)}, u32[]{:S(2)}) collective-permute-start(bf16[576,512]{1,0:T(8,128)(2,1)S(1)} %dynamic-slice_bitcast_fusion.4), channel_id=1, source_target_pairs={{0,96},{16,112},{32,64},{48,80},{64,32},{80,48},{96,0},{112,16},{1... | collective-permute-start | bytes 1769480 | tf_op jit(solution)/shard_map/ppermute | solution.py:569
  456.5 15.4 %collective-permute-start.8 = (bf16[576,512]{1,0:T(8,128)(2,1)}, bf16[576,512]{1,0:T(8,128)(2,1)}, u32[]{:S(2)}, u32[]{:S(2)}) collective-permute-start(bf16[576,512]{1,0:T(8,128)(2,1)} %dynamic-slice_bitcast_fusion.3), channel_id=1, source_target_pairs={{0,32},{16,48},{32,0},{48,16},{64,96},{80,112},{96,64},{112,80},{1... | collective-permute-start | bytes 1769480 | tf_op jit(solution)/shard_map/ppermute | solution.py:569
  466.1 13.4 %collective-permute-start.5 = (bf16[576,512]{1,0:T(8,128)(2,1)}, bf16[576,512]{1,0:T(8,128)(2,1)}, u32[]{:S(2)}, u32[]{:S(2)}) collective-permute-start(bf16[576,512]{1,0:T(8,128)(2,1)} %fusion.25), channel_id=1, source_target_pairs={{0,96},{16,112},{32,64},{48,80},{64,32},{80,48},{96,0},{112,16},{1... | collective-permute-start | bytes 1769480 | tf_op jit(solution)/shard_map/ppermute | solution.py:572
  474.2 13.5 %collective-permute-start.9 = (bf16[576,512]{1,0:T(8,128)(2,1)}, bf16[576,512]{1,0:T(8,128)(2,1)}, u32[]{:S(2)}, u32[]{:S(2)}) collective-permute-start(bf16[576,512]{1,0:T(8,128)(2,1)} %fusion.24), channel_id=1, source_target_pairs={{0,32},{16,48},{32,0},{48,16},{64,96},{80,112},{96,64},{112,80},{1... | collective-permute-start | bytes 1769480 | tf_op jit(solution)/shard_map/ppermute | solution.py:572
  482.2 39.6 %collective-permute-start.6 = (bf16[1152,512]{1,0:T(8,128)(2,1)}, bf16[1152,512]{1,0:T(8,128)(2,1)}, u32[]{:S(2)}, u32[]{:S(2)}) collective-permute-start(bf16[1152,512]{1,0:T(8,128)(2,1)} %bitcast.70), channel_id=1, source_target_pairs={{0,32},{16,48},{32,0},{48,16},{64,96},{80,112},{96,64},{112,80},{1... | collective-permute-start | bytes 3538952 | tf_op jit(solution)/shard_map/ppermute | solution.py:572
  490.3 116.4 %collective-permute-start.10 = (bf16[1152,512]{1,0:T(8,128)(2,1)}, bf16[1152,512]{1,0:T(8,128)(2,1)}, u32[]{:S(2)}, u32[]{:S(2)}) collective-permute-start(bf16[1152,512]{1,0:T(8,128)(2,1)} %bitcast.82), channel_id=1, source_target_pairs={{0,96},{16,112},{32,64},{48,80},{64,32},{80,48},{96,0},{112,16},{1... | collective-permute-start | bytes 3538952 | tf_op jit(solution)/shard_map/ppermute | solution.py:572
  546.1 42.6 %all-to-all-start.5 = ((bf16[16,32,1536]{2,1,0:T(8,128)(2,1)}), bf16[16,32,1536]{2,1,0:T(8,128)(2,1)}, u32[]{:S(2)}, u32[]{:S(2)}) async-start(bf16[16,32,1536]{2,1,0:T(8,128)(2,1)} %pad_maximum_fusion.4), calls=%async_computation.8 | async-start | bytes 3145728 | tf_op jit(solution)/shard_map/all_to_all | solution.py:664
  600.0 37.6 %all-to-all-start.6 = ((bf16[16,96,768]{2,1,0:T(8,128)(2,1)}), bf16[16,96,768]{2,1,0:T(8,128)(2,1)}, u32[]{:S(2)}, u32[]{:S(2)}) async-start(bf16[16,96,768]{2,1,0:T(8,128)(2,1)} %concatenate.102), calls=%async_computation.10 | async-start | bytes 4718592 | tf_op jit(solution)/shard_map/all_to_all | solution.py:664
  606.7 158.8 %all-gather.24.cloned.1.call-start = ((), (), s32[]{:S(2)}) async-start(), calls=%async_computation.21 | async-start | bytes 2211840 | tf_op jit(solution)/shard_map/all_gather | solution.py:944
  613.9 25.8 %collective-permute-start.1 = (bf16[32,1536]{1,0:T(8,128)(2,1)S(1)}, bf16[32,1536]{1,0:T(8,128)(2,1)}, u32[]{:S(2)}, u32[]{:S(2)}) collective-permute-start(bf16[32,1536]{1,0:T(8,128)(2,1)S(1)} %reduce_sum.152), channel_id=1, source_target_pairs={{0,0},{1,16},{2,32},{3,48},{4,64},{5,80},{6,96},{7,112},{8,1},{9,1... | collective-permute-start | bytes 294920 | tf_op jit(solution)/shard_map/ppermute | solution.py:895
  647.4 57.7 %collective-permute-start.11 = (bf16[4608,512]{1,0:T(8,128)(2,1)}, bf16[4608,512]{1,0:T(8,128)(2,1)}, u32[]{:S(2)}, u32[]{:S(2)}) collective-permute-start(bf16[4608,512]{1,0:T(8,128)(2,1)} %get-tuple-element.172), channel_id=1, source_target_pairs={{0,16},{16,0},{32,48},{48,32},{64,80},{80,64},{96,112},{112,96},{1... | collective-permute-start | bytes 14155784 | tf_op jit(solution)/shard_map/ppermute | solution.py:572
  654.3 47.4 %all-to-all-start.3 = ((bf16[16,64,1536]{2,1,0:T(8,128)(2,1)}), bf16[16,64,1536]{2,1,0:T(8,128)(2,1)}, u32[]{:S(2)}, u32[]{:S(2)}) async-start(bf16[16,64,1536]{2,1,0:T(8,128)(2,1)} %bitcast.249), calls=%async_computation.5 | async-start | bytes 6291456 | tf_op jit(solution)/shard_map/all_to_all | solution.py:664
  658.9 119.2 %reduce-scatter.11.cloned.1.call-start = ((), (), s32[]{:S(2)}) async-start(), calls=%async_computation.18 | async-start | bytes 3538944 | tf_op jit(solution)/shard_map/reduce_scatter | solution.py:909
  716.0 48.4 %all-to-all-start.7 = ((bf16[16,96,768]{2,1,0:T(8,128)(2,1)}), bf16[16,96,768]{2,1,0:T(8,128)(2,1)S(1)}, u32[]{:S(2)}, u32[]{:S(2)}) async-start(bf16[16,96,768]{2,1,0:T(8,128)(2,1)} %bitcast.229), calls=%async_computation.11 | async-start | bytes 4718592 | tf_op jit(solution)/shard_map/all_to_all | solution.py:664
  726.4 68.7 %all-gather.26.cloned.1.call-start = ((), (), s32[]{:S(2)}) async-start(), calls=%async_computation.22 | async-start | bytes 1327104 | tf_op jit(solution)/shard_map/all_gather | solution.py:952
  (55 other events, 417.2 us)
Sparse Core Ops, SparseCore 0:
  18.9 119.5 all-gather.21
  140.1 34.8 all-gather.19
  199.5 32.1 reduce-scatter.4
  235.3 30.3 all-gather.13
  267.7 27.8 all-gather.15
  303.6 32.1 reduce-scatter.8
  400.4 47.0 all-gather.17
  472.1 58.6 reduce-scatter.6
  641.4 27.6 all-gather.23
  671.3 33.2 reduce-scatter.10
  765.5 29.5 all-gather.25

commit v4 on v3

--- a/solution.py
+++ b/solution.py
@@ -1,3 +1,5 @@
+import functools
+
 import jax
 import jax.numpy as jnp
 from jax import lax
@@ -27,6 +29,11 @@
     return lax.dot_general(
         left, right, (((0,), (0,)), ((), ())), preferred_element_type=jnp.float32
     )
+
+
+def after(value, other):
+    corner = other[(0,) * (other.ndim - 1)][:1].astype(jnp.float32)
+    return (value.astype(jnp.float32) + 0.0 * corner).astype(value.dtype)
 
 
 def silu_slope(values):
@@ -171,7 +178,7 @@
 
 def scan_backward_kernel(
     proj_ref, prev_ref, mixed_ref, d_gated_ref, rows_ref, start_ref, taps_ref, head_ref, skip_ref,
-    d_proj_ref, d_taps_ref, d_head_ref, d_skip_ref,
+    earlier_0, earlier_1, earlier_2, d_proj_ref, d_taps_ref, d_head_ref, d_skip_ref,
     state_ref, pad_ref, late_ref,
 ):
     f32, bf = jnp.float32, jnp.bfloat16
@@ -274,6 +281,12 @@
     d_proj_ref[:, WIDE + CONVW :] = (d_pre * scale).astype(bf)
 
 
+def corner_of(array):
+    return pl.BlockSpec(
+        (1,) * (array.ndim - 2) + (16, 128), lambda *step: (0,) * array.ndim
+    )
+
+
 def whole(shape):
     return pl.BlockSpec(shape, lambda step: (0,) * len(shape))
 
@@ -316,7 +329,7 @@
     )(proj, proj, taps, head, skip)
 
 
-def scan_backward(proj, mixed, d_gated, row_values, starts, taps, head, skip):
+def scan_backward(proj, mixed, d_gated, row_values, starts, taps, head, skip, earlier):
     rows, width = proj.shape
     chunks = rows // CHUNK
     by_chunk = lambda step: (chunks - 1 - step, 0)
@@ -336,6 +349,7 @@
             whole(taps.shape),
             whole(head.shape),
             whole(skip.shape),
+            *map(corner_of, earlier),
         ],
         out_specs=[
             pl.BlockSpec((CHUNK, width), by_chunk),
@@ -359,7 +373,7 @@
             flops=10 << 30, bytes_accessed=20 << 20, transcendentals=8 << 20
         ),
         name="scan_backward",
-    )(proj, proj, mixed, d_gated, row_values, starts, taps, head, skip)
+    )(proj, proj, mixed, d_gated, row_values, starts, taps, head, skip, *earlier)
 
 
 def expert_early_kernel(cot_ref, down_ref, raw_ref):
@@ -368,7 +382,7 @@
 
 
 def expert_main_kernel(
-    rows_ref, routed_ref, raw_ref, gate_ref, up_ref, router_ref, marks_ref,
+    rows_ref, routed_ref, raw_ref, gate_ref, up_ref, router_ref, marks_ref, earlier_ref,
     back_ref, act_ref, scaled_ref, d_g_ref, d_v_ref,
 ):
     f32, bf = jnp.float32, jnp.bfloat16
@@ -453,7 +467,7 @@
     )(cot_rows, down)
 
 
-def expert_main(rows, cot_rows, raw, gate, up, w_all, marks):
+def expert_main(rows, cot_rows, raw, gate, up, w_all, marks, earlier):
     sources, local, cap, dim = rows.shape
     units = gate.shape[2]
     count = sources * cap
@@ -470,12 +484,13 @@
             per_expert(up.shape),
             pl.BlockSpec((dim, 128), lambda e: (0, w_all.shape[1] // 128 - 1)),
             per_expert(marks.shape),
+            corner_of(earlier),
         ],
         out_specs=[expert_slots(back)] + [per_expert(hidden.shape)] * 4,
         out_shape=[jax.ShapeDtypeStruct(back, jnp.bfloat16)] + [hidden] * 4,
         name="expert_main",
         **expert_params(8 << 30, 20 << 20),
-    )(rows, cot_rows, raw, gate, up, w_all, marks)
+    )(rows, cot_rows, raw, gate, up, w_all, marks, earlier)
 
 
 def expert_late(rows, cot_rows, act, scaled, d_g, d_v, down):
@@ -501,87 +516,157 @@
     )(rows, cot_rows, act, scaled, d_g, d_v, down)
 
 
-def assemble_kernel(gate_ref, rest_ref, weight_ref, gain_ref, grad_ref, small_ref):
-    f32, bf = jnp.float32, jnp.bfloat16
-    groups = gate_ref.shape[0]
+def assemble_kernel(
+    own_out, own_down, side_ref, in_ref, in_gain_ref, out_ref, out_gain_ref,
+    grad_in_ref, tail_ref, grad_out_ref, norm_ref, grad_down_ref, gate_ref, up_ref, mid_ref,
+):
+    f32 = jnp.float32
+    groups = side_ref.shape[0]
     inner = groups * WIDE
-    gain = gain_ref[...]
-    grad_gain = jnp.zeros(gain.shape, f32)
-    keys = jnp.zeros((gain.shape[0], 256), f32)
-    tail = jnp.zeros((gain.shape[0], 128), f32)
-    steps = jnp.zeros((gain.shape[0], 128), f32)
+    bands = out_ref.shape[1] // WIDE
+    rows_w = in_ref.shape[0]
+    gain = in_gain_ref[...]
+    at_down = bands * own_out
+    at_mid = at_down + bands * own_down
+    at_in = at_mid + rows_w
+    units = gate_ref.shape[1] // groups
+
+    def block(group, start, rows):
+        return side_ref[group, start : start + rows, :].astype(f32)
+
+    grad_gain = jnp.zeros((rows_w, 1), f32)
+    keys = jnp.zeros((rows_w, 256), f32)
+    tail = jnp.zeros((rows_w, 128), f32)
+    steps = jnp.zeros((rows_w, 128), f32)
+    mid = jnp.zeros((rows_w, 128), f32)
     rows, columns = grid_of((128, 128))
 
     def put(start, values):
-        nonlocal grad_gain
         stop = start + values.shape[1]
-        weight = weight_ref[:, start:stop].astype(f32)
-        grad_gain = grad_gain + jnp.sum(weight * values, axis=1, keepdims=True)
-        grad_ref[:, start:stop] = values * gain
+        grad_in_ref[:, start:stop] = values * gain
+        weight = in_ref[:, start:stop].astype(f32)
+        return jnp.sum(weight * values, axis=1, keepdims=True)
 
     for group in range(groups):
-        put(group * WIDE, gate_ref[group, :, :WIDE].astype(f32))
-        put(inner + group * WIDE, rest_ref[group, :, :WIDE].astype(f32))
-        keys = keys + rest_ref[group, :, WIDE:CONVW].astype(f32)
-        last = rest_ref[group, :, CONVW:]
-        tail = tail + last.astype(f32)
+        grad_gain += put(group * WIDE, block(group, at_in, rows_w))
+        grad_gain += put(inner + group * WIDE, block(group, at_in + rows_w, rows_w))
+        last = block(group, at_in + 2 * rows_w, rows_w)
+        keys = keys + last[:, :256]
+        tail = tail + last[:, 256:]
         moved = mark((rows < HEADS_HERE) & (columns == rows + HEADS_HERE * group))
-        steps = steps + times(last, moved)
-    put(2 * inner, keys)
-    put(2 * inner + 256, steps[:, : groups * HEADS_HERE])
+        steps = steps + times(last[:, 256:].astype(jnp.bfloat16), moved)
+        shared = block(group, at_mid, rows_w)
+        gate_ref[:, units * group : units * group + units] = shared[:, :units]
+        up_ref[:, units * group : units * group + units] = shared[:, units : 2 * units]
+        mid = mid + shared[:, 2 * units :]
+    grad_gain += put(2 * inner, keys)
+    grad_gain += put(2 * inner + 256, steps[:, : groups * HEADS_HERE])
     lane = lax.broadcasted_iota(jnp.int32, tail.shape, 1)
-    small_ref[...] = jnp.where(lane == 0, grad_gain, tail)
-
-
-def assemble(gate_sums, rest_sums, in_weight, gain):
+    tail_ref[...] = jnp.where(lane == 0, grad_gain, tail)
+    mid_ref[...] = mid
+
+    for group in range(groups):
+        sums = jnp.zeros((own_out, 1), f32)
+        mine = slice(own_out * group, own_out * group + own_out)
+        for band in range(bands):
+            wide = slice(WIDE * band, WIDE * band + WIDE)
+            values = block(group, own_out * band, own_out)
+            grad_out_ref[mine, wide] = values * out_gain_ref[mine, :]
+            sums += jnp.sum(out_ref[mine, wide].astype(f32) * values, axis=1, keepdims=True)
+            grad_down_ref[own_down * group : own_down * group + own_down, wide] = block(
+                group, at_down + own_down * band, own_down
+            )
+        norm_ref[mine, :] = sums
+
+
+def assemble(side, in_weight, in_gain, out_weight, out_gain, own_out, own_down):
+    groups = side.shape[0]
     rows, width = in_weight.shape
+    out_rows, dim = out_weight.shape
+    shapes = [
+        (rows, width),
+        (rows, 128),
+        (out_rows, dim),
+        (out_rows, 1),
+        (groups * own_down, dim),
+        (rows, groups * 128),
+        (rows, groups * 128),
+        (rows, 128),
+    ]
     return pl.pallas_call(
-        assemble_kernel,
-        in_specs=[pl.BlockSpec(memory_space=pltpu.VMEM)] * 4,
-        out_specs=[pl.BlockSpec(memory_space=pltpu.VMEM)] * 2,
+        functools.partial(assemble_kernel, own_out, own_down),
+        in_specs=[pl.BlockSpec(memory_space=pltpu.VMEM)] * 5,
+        out_specs=[pl.BlockSpec(memory_space=pltpu.VMEM)] * len(shapes),
+        out_shape=[jax.ShapeDtypeStruct(shape, jnp.float32) for shape in shapes],
+        compiler_params=pltpu.CompilerParams(vmem_limit_bytes=40 << 20),
+        cost_estimate=pl.CostEstimate(flops=8 << 20, bytes_accessed=12 << 20, transcendentals=0),
+        name="assemble",
+    )(side, in_weight, in_gain, out_weight, out_gain)
+
+
+def halve(values, bit, pairs):
+    f32 = jnp.float32
+    parts = values.reshape(2, values.shape[0] // 2, values.shape[1])
+    sent = lax.dynamic_index_in_dim(parts, 1 - bit, 0, keepdims=False)
+    kept = lax.dynamic_index_in_dim(parts, bit, 0, keepdims=False)
+    other = lax.ppermute(sent, "seq", pairs)
+    return (kept.astype(f32) + other.astype(f32)).astype(jnp.bfloat16)
+
+
+def double(values, bit, pairs):
+    other = lax.ppermute(values, "seq", pairs)
+    first = jnp.where(bit == 0, values, other)
+    second = jnp.where(bit == 0, other, values)
+    return jnp.concatenate([first, second], axis=0)
+
+
+def unpack_kernel(core_ref, own_ref, other_ref, gate_ref, up_ref, down_ref):
+    part = pl.program_id(1)
+    block = jnp.where(pl.program_id(0) == 0, own_ref[...], other_ref[...]).astype(jnp.float32)
+    units = block.shape[1]
+
+    @pl.when(part == 0)
+    def _():
+        gate_ref[0] = block
+
+    @pl.when(part == 1)
+    def _():
+        up_ref[0] = block
+
+    @pl.when(part == 2)
+    def _():
+        for at in range(0, block.shape[0], units):
+            down_ref[0, :, at : at + units] = block[at : at + units]
+
+
+def unpack_expert_grads(own, other, core):
+    rows, units = own.shape
+    dim = rows // 3
+    to_expert = lambda who, part, core: (jnp.where(who == 0, core[0], 1 - core[0]), 0, 0)
+    return pl.pallas_call(
+        unpack_kernel,
+        grid_spec=pltpu.PrefetchScalarGridSpec(
+            num_scalar_prefetch=1,
+            grid=(2, 3),
+            in_specs=[
+                pl.BlockSpec((dim, units), lambda who, part, core: (jnp.where(who == 0, part, 2), 0)),
+                pl.BlockSpec((dim, units), lambda who, part, core: (jnp.where(who == 0, 0, part), 0)),
+            ],
+            out_specs=[
+                pl.BlockSpec((1, dim, units), to_expert),
+                pl.BlockSpec((1, dim, units), to_expert),
+                pl.BlockSpec((1, units, dim), to_expert),
+            ],
+        ),
         out_shape=[
-            jax.ShapeDtypeStruct((rows, width), jnp.float32),
-            jax.ShapeDtypeStruct((rows, 128), jnp.float32),
-        ],
-        compiler_params=pltpu.CompilerParams(vmem_limit_bytes=32 << 20),
-        cost_estimate=pl.CostEstimate(flops=4 << 20, bytes_accessed=8 << 20, transcendentals=0),
-        name="assemble",
-    )(gate_sums, rest_sums, in_weight, gain)
-
-
-def sum_expert_grads(grads, q):
-    f32, bf = jnp.float32, jnp.bfloat16
-    size = lax.axis_size("seq")
-    core, z = q % 2, q // 2
-    mates = [(i, i ^ 1) for i in range(size)]
-    near = [(i, 2 * ((i // 2) ^ 1) + i % 2) for i in range(size)]
-    far = [(i, 2 * (size // 2 - 1 - i // 2) + i % 2) for i in range(size)]
-    inner = ((z == 1) | (z == 2)).astype(jnp.int32)
-    high = (z >= 2).astype(jnp.int32)
-
-    def add(left, right):
-        return (left.astype(f32) + right.astype(f32)).astype(bf)
-
-    def halve(values, bit, pairs):
-        parts = values.reshape(2, values.shape[0] // 2, values.shape[1])
-        sent = lax.dynamic_index_in_dim(parts, 1 - bit, 0, keepdims=False)
-        kept = lax.dynamic_index_in_dim(parts, bit, 0, keepdims=False)
-        return add(kept, lax.ppermute(sent, "seq", pairs))
-
-    def double(values, bit, pairs):
-        other = lax.ppermute(values, "seq", pairs)
-        both = jnp.stack([values, other])
-        return jnp.where(bit == 0, both, both[::-1]).reshape(-1, values.shape[-1])
-
-    flat = grads.reshape(2 * grads.shape[1], grads.shape[2])
-    mine = halve(flat, core, mates)
-    cutoff = mine.shape[0] // 2
-    first, second = mine[:cutoff], mine[cutoff:]
-    first, second = halve(first, inner, near), halve(second, high, far)
-    first, second = halve(first, high, far), halve(second, inner, near)
-    first, second = double(first, high, far), double(second, inner, near)
-    first, second = double(first, inner, near), double(second, high, far)
-    return double(jnp.concatenate([first, second], axis=0), core, mates).reshape(grads.shape)
+            jax.ShapeDtypeStruct((2, dim, units), jnp.float32),
+            jax.ShapeDtypeStruct((2, dim, units), jnp.float32),
+            jax.ShapeDtypeStruct((2, units, dim), jnp.float32),
+        ],
+        compiler_params=pltpu.CompilerParams(vmem_limit_bytes=40 << 20),
+        cost_estimate=pl.CostEstimate(flops=1 << 20, bytes_accessed=28 << 20, transcendentals=0),
+        name="unpack_expert_grads",
+    )(core.reshape(1), own, other)
 
 
 def on_device(
@@ -698,7 +783,7 @@
         [shared_cols[fold * band : fold * band + fold] for band in range(bands)], axis=1
     )
     piece = jnp.concatenate([piece, shared_rows], axis=0)
-    rows_all = lax.all_gather(piece, "shard", axis=0)
+    rows_all = to_shards(jnp.broadcast_to(piece[None], (sh,) + piece.shape))
     own_rows = own_out + own_down
     w_out = rows_all[:, :own_out].reshape(gw, dim)
     w_down = rows_all[:, own_out:own_rows].reshape(gf, dim)
@@ -772,15 +857,14 @@
     skip_in = jnp.broadcast_to(jnp.repeat(skip_local, per_head)[None], (8, gw))
     mixed, q_low, square_part, starts = scan_forward(proj, taps_in, head_in, skip_in)
 
-    w_out, cot_rows = lax.optimization_barrier((w_out, cot_rows))
+    cot_all = lax.all_gather(after(cot_low, w_all), "seq", axis=0, tiled=True)
+    w_out, cot_rows, cot_all = lax.optimization_barrier((w_out, cot_rows, cot_all))
     out_part = times(q_low, w_out).astype(bf)
     out_sum = lax.psum_scatter(out_part, "seq", scatter_dimension=0, tiled=True)
     square = lax.psum(square_part.reshape(sq, toks), "seq")
     q_r = lax.rsqrt(square / inner + epsilon).reshape(seq_rows, 1)
     d_raw = expert_early(cot_rows, expert_down)
-    cot_late, _ = lax.optimization_barrier((cot_low, out_sum[:16, :128]))
-    cot_all = lax.all_gather(cot_late, "seq", axis=0, tiled=True)
-    tok_r = lax.dynamic_slice_in_dim(q_r, q * toks, toks, 0)
+    tok_r = after(lax.dynamic_slice_in_dim(q_r, q * toks, toks, 0), d_raw)
     x_tok = x_low.astype(f32)
     added = out_sum.astype(f32) * tok_r
     resid = x_tok + added
@@ -804,12 +888,6 @@
         [own_ids + router_lane, own_ids, own_ids + 64] + [jnp.full_like(own_ids, -1)] * 5, axis=1
     )
     marks = (marks[:, :, None] == lanes[None, None, :]).astype(f32)
-    back_rows, e_act, e_scaled, d_g, d_v = expert_main(
-        rows, cot_rows, d_raw, expert_gate, expert_up, w_all, marks
-    )
-    d_returned = to_shards(back_rows.reshape(sh, local_e * CAP, dim + 128))
-    e_out, e_grads = expert_late(rows, cot_rows, e_act, e_scaled, d_g, d_v, expert_down)
-    returned = to_shards(e_out.reshape(sh, local_e * CAP, dim))
 
     s_both = times(moe_all, w_shared)
     s_gate, s_up = s_both[:, :gf], s_both[:, gf:]
@@ -827,6 +905,26 @@
     d_moe_part = times_transposed(d_both, w_shared).astype(bf)
     d_moe_shared = lax.psum_scatter(d_moe_part, "seq", scatter_dimension=0, tiled=True)
 
+    back_rows, e_act, e_scaled, d_g, d_v = expert_main(
+        rows, cot_rows, d_raw, expert_gate, expert_up, w_all, marks, d_moe_part
+    )
+    d_returned = to_shards(back_rows.reshape(sh, local_e * CAP, dim + 128))
+    e_out, e_grads = expert_late(rows, cot_rows, e_act, e_scaled, d_g, d_v, expert_down)
+    d_returned, e_out = lax.optimization_barrier((d_returned, e_out))
+    returned = to_shards(e_out.reshape(sh, local_e * CAP, dim))
+
+    core, z_at = q % 2, q // 2
+    mates = [(i, i ^ 1) for i in range(sq)]
+    near = [(i, 2 * ((i // 2) ^ 1) + i % 2) for i in range(sq)]
+    far = [(i, 2 * (sq // 2 - 1 - i // 2) + i % 2) for i in range(sq)]
+    is_inner = ((z_at == 1) | (z_at == 2)).astype(jnp.int32)
+    is_high = (z_at >= 2).astype(jnp.int32)
+    e_mine = halve(e_grads.reshape(-1, e_grads.shape[2]), core, mates)
+    cutoff = e_mine.shape[0] // 2
+    e_one = halve(e_mine[:cutoff], is_inner, near)
+    e_two = halve(e_mine[cutoff:], is_high, far)
+    e_one, e_two = halve(e_one, is_high, far), halve(e_two, is_inner, near)
+
     d_flat = transposed_times(dispatch_flat, d_returned.reshape(slots, dim + 128))
     d_gates = d_flat[:, dim : dim + experts] + d_flat[:, dim + 64 : dim + 64 + experts]
     d_logits = gates * (d_gates - jnp.sum(gates * d_gates, axis=1, keepdims=True))
@@ -846,75 +944,71 @@
     d_o = d_resid.astype(bf)
     kappa = jnp.sum(d_o.astype(f32) * added, axis=1) / inner
     d_o_all = lax.all_gather(d_o, "seq", axis=0, tiled=True)
-    kappa_all = lax.all_gather(kappa.reshape(1, toks), "seq", axis=0).reshape(seq_rows, 1)
-
-    s_late, _ = lax.optimization_barrier((s_act, d_o_all[:16, :128]))
-    shared_part = times(s_late, w_down).astype(bf)
-    shared_sum = lax.psum_scatter(shared_part, "seq", scatter_dimension=0, tiled=True)
-    weighted = (gates.T[:, None, :] * dispatch.astype(f32)).reshape(slots, toks)
-    combined = transposed_times(weighted.astype(bf), returned.reshape(slots, dim))
-    block_output = ((resid + shared_sum.astype(f32) + combined) * live[:, None]).astype(bf)[None]
+    kappa_all = lax.all_gather(after(kappa, e_mine).reshape(1, toks), "seq", axis=0)
+    kappa_all = kappa_all.reshape(seq_rows, 1)
+
 
     d_gated = times_transposed(d_o_all, w_out)
-    grad_out_part = transposed_times(q_low, (q_r * d_o_all.astype(f32)).astype(bf))
+    grad_out_part = transposed_times(
+        q_low, (after(q_r, kappa_all) * d_o_all.astype(f32)).astype(bf)
+    )
     grad_down_part = transposed_times(s_act, cot_all)
     grad_shared_part = transposed_times(moe_all, d_both)
 
-    rows_part = jnp.concatenate(
-        [grad_out_part.reshape(sh, own_out, dim), grad_down_part.reshape(sh, own_down, dim)],
+    mid_part = jnp.concatenate(
+        [
+            grad_shared_part,
+            grad_router,
+            grad_moe[:, None],
+            jnp.zeros((dim, 128 - experts - 1), f32),
+        ],
         axis=1,
     )
-    moved_rows = to_shards(rows_part.astype(bf))
+    lane_w = mid_part.shape[1]
+    bands = dim // lane_w
+
+    def to_bands(values):
+        return jnp.concatenate(
+            [values[:, :, band * lane_w : band * lane_w + lane_w] for band in range(bands)], axis=1
+        )
+
+    early_part = jnp.concatenate(
+        [
+            to_bands(grad_out_part.astype(bf).reshape(sh, own_out, dim)),
+            to_bands(grad_down_part.astype(bf).reshape(sh, own_down, dim)),
+            mid_part.astype(bf).reshape(sh, rows_w, lane_w),
+        ],
+        axis=1,
+    )
+    moved_early = to_shards(early_part)
 
     row_values = jnp.concatenate(
         [q_r, kappa_all, x_r, jnp.zeros((seq_rows, 5), f32)], axis=1
     )
     d_proj, d_taps, d_head, d_skip = scan_backward(
-        proj, mixed, d_gated, row_values, starts, taps_in, head_in, skip_in
+        proj, mixed, d_gated, row_values, starts, taps_in, head_in, skip_in, (returned, e_one, e_two)
     )
     grad_conv_local = d_taps[:taps]
     grad_offset_local = d_taps[taps]
     grad_bias_local = d_head[0, :gh]
     grad_decay_local = d_head[1, :gh] * decay_rate
     grad_skip_local = jnp.sum(d_skip[0].reshape(gh, per_head), axis=1)
-    d_proj, moved_rows = lax.optimization_barrier((d_proj, moved_rows))
-    d_gate_low = d_proj[:, :gw]
-    mid_part = jnp.concatenate(
-        [
-            transposed_times(x_all, d_gate_low),
-            grad_shared_part,
-            grad_router,
-            grad_moe[:, None],
-            jnp.zeros((dim, 128 - experts - 1), f32),
-        ],
-        axis=1,
-    )
-    mid_width = mid_part.shape[1]
-    moved_mid = to_shards(mid_part.astype(bf).reshape(sh, rows_w, mid_width))
-    rows_sum = jnp.sum(moved_rows.astype(f32), axis=0).astype(bf)
-    rows_sum = lax.ppermute(rows_sum, both_axes, backward_pairs)
-
-    e_all = sum_expert_grads(e_grads, q)
-    grad_e_gate = e_all[:, :dim].astype(f32)
-    grad_e_up = e_all[:, dim : 2 * dim].astype(f32)
-    units = expert_gate.shape[2]
-    grad_e_down = (
-        e_all[:, 2 * dim :]
-        .reshape(local_e, dim // units, units, units)
-        .transpose(0, 2, 1, 3)
-        .reshape(local_e, units, dim)
-        .astype(f32)
-    )
     back_part = times_transposed(d_proj, w_all).astype(bf)
-    back_sum = lax.psum_scatter(back_part, "seq", scatter_dimension=0, tiled=True).astype(f32)
+    shared_part = times(s_act, w_down).astype(bf)
+    both_sum = lax.psum_scatter(
+        jnp.concatenate([back_part, shared_part], axis=1), "seq", scatter_dimension=0, tiled=True
+    ).astype(f32)
+    back_sum, shared_sum = both_sum[:, :dim], both_sum[:, dim:]
+    weighted = (gates.T[:, None, :] * dispatch.astype(f32)).reshape(slots, toks)
+    combined = transposed_times(weighted.astype(bf), returned.reshape(slots, dim))
+    block_output = ((resid + shared_sum + combined) * live[:, None]).astype(bf)[None]
     tok_x_r = row_scale(x_tok)
     x_n = x_tok * tok_x_r
     input_grad = (
         d_resid + back_sum - x_n * (tok_x_r * jnp.mean(back_sum * x_tok, axis=1, keepdims=True))
     )[None]
 
-    rest = total - gw
-    grad_in_part = transposed_times(x_all, d_proj[:, gw:])
+    grad_in_part = transposed_times(x_all, d_proj)
 
     def spread(local, count):
         wide = jnp.zeros(local.shape[:-1] + (count,), f32)
@@ -934,34 +1028,44 @@
     small_part = jnp.pad(
         small_part, ((0, 0), (0, rows_w * small_cols - small_count))
     ).reshape(sh, rows_w, small_cols)
-    small_at = used - gw
     last_part = grad_in_part + jnp.pad(
-        small_part.reshape(dim, small_cols), ((0, 0), (small_at, rest - small_at - small_cols))
-    )
-    last_part, moved_mid = lax.optimization_barrier((last_part.astype(bf), moved_mid))
-    moved_last = to_shards(last_part.reshape(sh, rows_w, rest))
-    mid_sum = jnp.sum(moved_mid.astype(f32), axis=0).astype(bf)
+        small_part.reshape(dim, small_cols), ((0, 0), (used, total - used - small_cols))
+    )
+    last_part, moved_early = lax.optimization_barrier((last_part.astype(bf), moved_early))
+    early_sum = jnp.sum(moved_early.astype(f32), axis=0).astype(bf)
+    rows_sum = lax.ppermute(early_sum[: bands * own_rows], both_axes, backward_pairs)
+    e_one, e_two = after(e_one, last_part), after(e_two, last_part)
+    e_one, e_two = double(e_one, is_high, far), double(e_two, is_inner, near)
+    e_one, e_two = double(e_one, is_inner, near), double(e_two, is_high, far)
+    moved_last = to_shards(last_part.reshape(sh, rows_w, total))
+    last_sum = jnp.sum(moved_last.astype(f32), axis=0)
+    last_sum = after(after(after(last_sum, e_one), e_two), both_sum).astype(bf)
+    e_mine = jnp.concatenate([e_one, e_two], axis=0)
+    e_other = lax.ppermute(e_mine, "seq", mates)
+    grad_e_gate, grad_e_up, grad_e_down = unpack_expert_grads(e_mine, e_other, core)
     side = lax.all_gather(
-        jnp.concatenate([rows_sum, mid_sum.reshape(rows_w * mid_width // dim, dim)], axis=0),
+        jnp.concatenate(
+            [rows_sum, early_sum[bands * own_rows :]]
+            + [last_sum[:, lane_w * i : lane_w * i + lane_w] for i in range(total // lane_w)],
+            axis=0,
+        ),
         "seq",
         axis=0,
     )
-    rows_grad = side[:, :own_rows]
-    mid_all = side[:, own_rows:].reshape(sq, rows_w, mid_width)
-    last_sum = jnp.sum(moved_last.astype(f32), axis=0).astype(bf)
-    last_all = lax.all_gather(last_sum, "seq", axis=0)
-
-    grad_out_raw = rows_grad[:, :own_out].reshape(sq * own_out, dim).astype(f32)
-    grad_down = rows_grad[:, own_out:].reshape(sq * own_down, dim).astype(f32)
-    grad_out = norm_gain.astype(f32)[:, None] * grad_out_raw
-    grad_norm = jnp.sum(out_weight.astype(f32) * grad_out_raw, axis=1)
-    mid_all_f = mid_all[:, :, gw:].astype(f32)
-    grad_shared_gate = mid_all_f[:, :, :gf].transpose(1, 0, 2).reshape(rows_w, fs)
-    grad_shared_up = mid_all_f[:, :, gf : 2 * gf].transpose(1, 0, 2).reshape(rows_w, fs)
-    mid_rest = jnp.sum(mid_all_f[:, :, 2 * gf :], axis=0)
-    grad_router_weight = mid_rest[:, :experts]
-    grad_moe_gain = mid_rest[:, experts]
-    grad_in, tail_sums = assemble(mid_all, last_all, in_weight, gain_col)
+    gain_out = norm_gain.astype(f32)[:, None]
+    (
+        grad_in,
+        tail_sums,
+        grad_out,
+        norm_sums,
+        grad_down,
+        grad_shared_gate,
+        grad_shared_up,
+        mid_sums,
+    ) = assemble(side, in_weight, gain_col, out_weight, gain_out, own_out, own_down)
+    grad_norm = norm_sums[:, 0]
+    grad_router_weight = mid_sums[:, :experts]
+    grad_moe_gain = mid_sums[:, experts]
     grad_mixer_gain = tail_sums[:, 0]
     lane_at = used - (total - 128)
     small_sum = tail_sums[:, lane_at : lane_at + small_cols].reshape(-1)

time: 819 us -> 682 us (0.83)
  waiting for transfers between devices: 356 us -> 229 us
  other arithmetic: 99.6 us -> 50.1 us
  Pallas kernels: 67 us -> 82.4 us
  starting transfers between devices: 92.2 us -> 106 us
  blocking collectives: 27.8 us -> 40.8 us
    all_gather x4 -> x2, waiting for transfers between devices: 86.9 us -> 12.4 us  [the longest x1 12.4 us: on_device(): lax.all_gather(jnp.concatenate([rows_sum, early_sum[bands * own_rows:]] +...]
    all_gather x1, waiting for transfers between devices: 34.2 us -> 0.01 us  [on_device(): x_all = lax.all_gather(x_low, 'seq', axis=0, tiled=True)]
    ppermute x5 -> x4, waiting for transfers between devices: 34.4 us -> 10.3 us  [double(): other = lax.ppermute(values, 'seq', pairs)]
    all_to_all x8, waiting for transfers between devices: 122 us -> 145 us  [to_shards(): lax.all_to_all(values, 'shard', split_axis=0, concat_axis=0, tiled=True)]
    another operation x6 -> x0, other arithmetic: 20.9 us -> none  [double(): both = jnp.stack([values, other])]
    ppermute x6 -> x7, starting transfers between devices: 10.3 us -> 28.8 us  [the longest x5 17.9 us: halve(): other = lax.ppermute(sent, 'seq', pairs)]
    pallas_call x1 -> x2, Pallas kernels: 1.99 us -> 17 us  [the longest x1 13.9 us: unpack_expert_grads(): pl.pallas_call(unpack_kernel, grid_spec=pltpu.PrefetchScalarGridSpec(num_...]
    select_n x5 -> x4, other arithmetic: 17.9 us -> 6.03 us  [the longest x2 3.43 us: double(): second = jnp.where(bit == 0, other, values)]
  transfers between devices with their start and end apart: 31 -> 28, of which waited for: 15 -> 15; matrix products, arithmetic and copies ran while one was open for 27% -> 22% of each run, Pallas kernels for 7% -> 8%
where the time goes in v4:
time: 682 us; the launch traced here: 672 us
  waiting for transfers between devices  229 us (34%)
  starting transfers between devices  106 us (16%)
  Pallas kernels  82.4 us (12%)
  local copies, waits for them, and re-layouts  70.9 us (10%)
  matrix products  70.4 us (10%)
  other arithmetic  50.1 us (7%)
  blocking collectives  40.8 us (6%)
  between operations  21.9 us (3%)
    all_to_all x8, waiting for transfers between devices, to_shards(): lax.all_to_all(values, 'shard', split_axis=0, concat_axis=0, tiled=True)  145 us
    all_to_all x8, starting transfers between devices, to_shards(): lax.all_to_all(values, 'shard', split_axis=0, concat_axis=0, tiled=True)  69.2 us
    dot_general x7, matrix products, times(): return jnp.dot(left, right, preferred_element_type=jnp.float32)  26.6 us
    unnamed x153, local copies, waits for them, and re-layouts  26.2 us
    pallas_call x1, Pallas kernels, scan_backward(): pl.pallas_call(scan_backward_kernel, grid=(chunks,), in_specs=[pl.BlockSp...  23.4 us
    dot_general x6, matrix products, transposed_times(): lax.dot_general(left, right, (((0,), (0,)), ((), ())), preferred_element_...  22.9 us
    psum x1, blocking collectives, on_device(): square = lax.psum(square_part.reshape(sq, toks), 'seq')  21.3 us
    ppermute x5, waiting for transfers between devices, halve(): other = lax.ppermute(sent, 'seq', pairs)  19.9 us
  transfers between devices with their start and end apart: 28, of which 15 were waited for; matrix products, arithmetic and copies ran while one was open for 22% of the time, Pallas kernels for 8%

profile of v4, /device:TPU:1, one launch (start us, length us, event | category | flops | bytes accessed | tf_op | source)
XLA Modules:
  0.0 671.9 jit_solution(4011661600800419505)
XLA Ops:
  19.4 7.8 %all-to-all-start = ((bf16[16,96,1152]{2,1,0:T(8,128)(2,1)}), bf16[16,96,1152]{2,1,0:T(8,128)(2,1)}, u32[]{:S(2)}, u32[]{:S(2)}) async-start(bf16[16,96,1152]{2,1,0:T(8,128)(2,1)} %broadcast_in_dim.37), calls=%async_computation | async-start | bytes 7077888 | tf_op jit(solution)/shard_map/all_to_all | solution.py:749
  33.3 38.9 %all-to-all-done = bf16[16,96,1152]{2,1,0:T(8,128)(2,1)} async-done(((bf16[16,96,1152]{2,1,0:T(8,128)(2,1)}), bf16[16,96,1152]{2,1,0:T(8,128)(2,1)}, u32[]{:S(2)}, u32[]{:S(2)}) %all-to-all-start) | async-done | bytes 3538976 | tf_op jit(solution)/shard_map/all_to_all | solution.py:749
  76.8 11.8 %all-to-all-start.1 = ((bf16[16,48,1536]{2,1,0:T(8,128)(2,1)}), bf16[16,48,1536]{2,1,0:T(8,128)(2,1)S(1)}, u32[]{:S(2)}, u32[]{:S(2)}) async-start(bf16[16,48,1536]{2,1,0:T(8,128)(2,1)} %broadcast_in_dim.42), calls=%async_computation.1 | async-start | bytes 4718592 | tf_op jit(solution)/shard_map/all_to_all | solution.py:749
  93.1 23.5 %all-to-all-done.1 = bf16[16,48,1536]{2,1,0:T(8,128)(2,1)S(1)} async-done(((bf16[16,48,1536]{2,1,0:T(8,128)(2,1)}), bf16[16,48,1536]{2,1,0:T(8,128)(2,1)S(1)}, u32[]{:S(2)}, u32[]{:S(2)}) %all-to-all-start.1) | async-done | bytes 2359328 | tf_op jit(solution)/shard_map/all_to_all | solution.py:749
  116.6 6.0 all-to-all-start.2
  130.9 6.3 fusion.3.proj_ref.prev_ref
  137.2 10.9 %scan_forward.1 = (bf16[1024,384]{1,0:T(8,128)(2,1)S(1)}, bf16[1024,384]{1,0:T(8,128)(2,1)S(1)}, f32[1024,1]{1,0:T(8,128)S(1)}, f32[8,128,384]{2,1,0:T(8,128)S(1)}) custom-call(f32[1024,1152]{1,0:T(8,128)S(1)} %fusion.3.proj_ref.prev_ref, f32[1024,1152]{1,0:T(8,128)S(1)} %fusion.3.proj_ref.prev_ref, f32[8,640]{1,0:T(8,128)S(1)} %maximum_maximum_fusion.1.taps_ref, ...), custom_call_target="tpu_custom_call" | custom-call | flops 3221225472 | bytes 12582912 | tf_op jit(solution)/shard_map/scan_forward/pallas_call | solution.py:298
  152.3 8.9 %all-to-all-done.2 = bf16[16,64,1664]{2,1,0:T(8,128)(2,1)} async-done(((bf16[16,64,1664]{2,1,0:T(8,128)(2,1)}), bf16[16,64,1664]{2,1,0:T(8,128)(2,1)}, u32[]{:S(2)}, u32[]{:S(2)}) %all-to-all-start.2) | async-done | bytes 3407904 | tf_op jit(solution)/shard_map/all_to_all | solution.py:749
  167.4 21.3 %psum.7 = f32[8,128]{1,0:T(8,128)S(1)} all-reduce(f32[8,128]{1,0:T(8,128)S(1)} %bitcast.220), channel_id=1, replica_groups=mesh['seq'=8,'shard'=16] {'seq'}, use_global_device_ids=true, to_apply=%region_3.4 | all-reduce | flops 1024 | bytes 8192 | tf_op jit(solution)/shard_map/psum | solution.py:864
  196.3 11.2 %reduce-scatter.4.cloned.1.call-done = bf16[128,1536]{1,0:T(8,128)(2,1)} async-done(((bf16[1024,1536]{1,0:T(8,128)(2,1)}), bf16[128,1536]{1,0:T(8,128)(2,1)}) %reduce-scatter.4.cloned.1.call-update) | async-done | bytes 393232 | tf_op jit(solution)/shard_map/reduce_scatter | solution.py:863
  214.5 6.5 all-to-all-start.3
  224.5 16.6 %all-gather.12.cloned.1.call-done = bf16[1024,1536]{1,0:T(8,128)(2,1)} async-done(((bf16[128,1536]{1,0:T(8,128)(2,1)}), bf16[1024,1536]{1,0:T(8,128)(2,1)}) %all-gather.12.cloned.1.call-update) | async-done | bytes 3145744 | tf_op jit(solution)/shard_map/all_gather | solution.py:875
  251.4 5.4 all-to-all-done.3
  256.8 13.3 %expert_main.1 = (bf16[16,2,32,1664]{3,2,1,0:T(8,128)(2,1)}, bf16[2,512,512]{2,1,0:T(8,128)(2,1)}, bf16[2,512,512]{2,1,0:T(8,128)(2,1)}, bf16[2,512,512]{2,1,0:T(8,128)(2,1)}, bf16[2,512,512]{2,1,0:T(8,128)(2,1)}) custom-call(bf16[16,2,32,1536]{3,2,1,0:T(8,128)(2,1)} %bitcast.22.rows_ref, bf16[16,2,32,1664]{3,2,1,0:T(8,128)(2,1)} %bitcast.15.cot_ref.routed_ref, ...), custom_call_target="tpu_custom_call" | custom-call | flops 8589934592 | bytes 20971520 | tf_op jit(solution)/shard_map/expert_main/pallas_call | solution.py:476
  270.1 12.7 %expert_late.1 = (bf16[16,2,32,1536]{3,2,1,0:T(8,128)(2,1)}, bf16[2,4608,512]{2,1,0:T(8,128)(2,1)}) custom-call(bf16[16,2,32,1536]{3,2,1,0:T(8,128)(2,1)} %bitcast.22.rows_ref, bf16[16,2,32,1664]{3,2,1,0:T(8,128)(2,1)} %bitcast.15.cot_ref.routed_ref, bf16[2,512,512]{2,1,0:T(8,128)(2,1)} %get-tuple-element.59.act_ref, ...), custom_call_target="tpu_custom_call" | custom-call | flops 7516192768 | bytes 25165824 | tf_op jit(solution)/shard_map/expert_late/pallas_call | solution.py:500
  287.6 6.1 collective-permute-start.1
  301.1 42.9 %all-to-all-done.4 = bf16[16,64,1664]{2,1,0:T(8,128)(2,1)} async-done(((bf16[16,64,1664]{2,1,0:T(8,128)(2,1)}), bf16[16,64,1664]{2,1,0:T(8,128)(2,1)}, u32[]{:S(2)}, u32[]{:S(2)}) %all-to-all-start.4) | async-done | bytes 3407904 | tf_op jit(solution)/shard_map/all_to_all | solution.py:749
  361.7 10.7 %collective-permute-start.4 = (bf16[1152,512]{1,0:T(8,128)(2,1)S(1)}, bf16[1152,512]{1,0:T(8,128)(2,1)}, u32[]{:S(2)}, u32[]{:S(2)}) collective-permute-start(bf16[1152,512]{1,0:T(8,128)(2,1)S(1)} %dynamic-slice_bitcast_fusion.1), channel_id=1, source_target_pairs={{0,96},{16,112},{32,64},{48,80},{64,32},{80,48},{96,0},{112,16},{1... | collective-permute-start | bytes 3538952 | tf_op jit(solution)/shard_map/ppermute | solution.py:612
  374.8 11.5 %all-to-all-start.5 = ((bf16[16,64,1536]{2,1,0:T(8,128)(2,1)}), bf16[16,64,1536]{2,1,0:T(8,128)(2,1)}, u32[]{:S(2)}, u32[]{:S(2)}) async-start(bf16[16,64,1536]{2,1,0:T(8,128)(2,1)} %bitcast.202), calls=%async_computation.7 | async-start | bytes 6291456 | tf_op jit(solution)/shard_map/all_to_all | solution.py:749
  392.3 18.2 %collective-permute-done.4 = bf16[1152,512]{1,0:T(8,128)(2,1)} collective-permute-done((bf16[1152,512]{1,0:T(8,128)(2,1)S(1)}, bf16[1152,512]{1,0:T(8,128)(2,1)}, u32[]{:S(2)}, u32[]{:S(2)}) %collective-permute-start.4) | collective-permute-done | bytes 1179680 | tf_op jit(solution)/shard_map/ppermute | solution.py:612
  416.7 19.5 %all-gather.3 = f32[8,1,128]{2,1,0:T(1,128)S(1)} all-gather(f32[1,1,128]{2,1,0:T(1,128)S(1)} %add_bitcast_fusion.1), channel_id=3, replica_groups=mesh['seq'=8,'shard'=16] {'seq'}, dimensions={0}, use_global_device_ids=true | all-gather | bytes 4608 | tf_op jit(solution)/shard_map/all_gather | solution.py:947
  448.4 23.4 %scan_backward.1 = (bf16[1024,1152]{1,0:T(8,128)(2,1)}, f32[8,640]{1,0:T(8,128)S(1)}, f32[8,128]{1,0:T(8,128)S(1)}, f32[8,384]{1,0:T(8,128)S(1)}) custom-call(f32[1024,1152]{1,0:T(8,128)} %copy-done.5, f32[1024,1152]{1,0:T(8,128)} %copy-done.5, bf16[1024,384]{1,0:T(8,128)(2,1)S(1)} %copy-done.10, f32[1024,384]{1,0:T(8,128)S(1)} %copy-done.8, ...), custom_call_target="tpu_custom_call" | custom-call | flops 10737418240 | bytes 20971520 | tf_op jit(solution)/shard_map/scan_backward/pallas_call | solution.py:336
  471.9 7.1 %convolution_convert_fusion.5 = bf16[1024,1536]{1,0:T(8,128)(2,1)S(1)} fusion(bf16[1024,1152]{1,0:T(8,128)(2,1)} %get-tuple-element.68, bf16[1536,1152]{1,0:T(8,128)(2,1)} %bitcast.2.router_ref), kind=kOutput, calls=%fused_computation.18 | convolution fusion | flops 3625451520 | bytes 9043968 | tf_op jit(solution)/shard_map/dot_general | solution.py:23
  501.9 12.3 %all-to-all-start.6 = ((bf16[16,224,384]{2,1,0:T(8,128)(2,1)}), bf16[16,224,384]{2,1,0:T(8,128)(2,1)}, u32[]{:S(2)}, u32[]{:S(2)}) async-start(bf16[16,224,384]{2,1,0:T(8,128)(2,1)} %maximum_dynamic-update-slice_fusion), calls=%async_computation.9 | async-start | bytes 5505024 | tf_op jit(solution)/shard_map/all_to_all | solution.py:749
  516.3 8.8 %fusion.2 = bf16[1536,1152]{1,0:T(8,128)(2,1)} fusion(bf16[1024,1152]{1,0:T(8,128)(2,1)} %get-tuple-element.68, f32[1536,11]{1,0:T(8,128)S(1)} %reshape_reshape.3, bf16[1,1024,1536]{2,1,0:T(8,128)(2,1)} %all-gather.16.cloned.1.call-done), kind=kOutput, calls=%fused_computation.4 | convolution fusion | flops 3627417600 | bytes 9111552 | tf_op jit(solution)/shard_map/dot_general | solution.py:29
  525.1 25.6 %all-to-all-done.6 = bf16[16,224,384]{2,1,0:T(8,128)(2,1)} async-done(((bf16[16,224,384]{2,1,0:T(8,128)(2,1)}), bf16[16,224,384]{2,1,0:T(8,128)(2,1)}, u32[]{:S(2)}, u32[]{:S(2)}) %all-to-all-start.6) | async-done | bytes 2752544 | tf_op jit(solution)/shard_map/all_to_all | solution.py:749
  553.2 8.2 %all-to-all-start.7 = ((bf16[16,96,1152]{2,1,0:T(8,128)(2,1)}), bf16[16,96,1152]{2,1,0:T(8,128)(2,1)}, u32[]{:S(2)}, u32[]{:S(2)}) async-start(bf16[16,96,1152]{2,1,0:T(8,128)(2,1)} %bitcast.200), calls=%async_computation.10 | async-start | bytes 7077888 | tf_op jit(solution)/shard_map/all_to_all | solution.py:749
  569.0 6.7 collective-permute-done.9
  583.1 10.5 %collective-permute-start.6 = (bf16[128,384]{1,0:T(8,128)(2,1)S(1)}, bf16[128,384]{1,0:T(8,128)(2,1)S(1)}, u32[]{:S(2)}, u32[]{:S(2)}) collective-permute-start(bf16[128,384]{1,0:T(8,128)(2,1)S(1)} %slice.338), channel_id=1, source_target_pairs={{0,0},{1,16},{2,32},{3,48},{4,64},{5,80},{6,96},{7,112},{8,1},{9,1... | collective-permute-start | bytes 294920 | tf_op jit(solution)/shard_map/ppermute | solution.py:1036
  593.6 11.7 %collective-permute-done.6 = bf16[128,384]{1,0:T(8,128)(2,1)S(1)} collective-permute-done((bf16[128,384]{1,0:T(8,128)(2,1)S(1)}, bf16[128,384]{1,0:T(8,128)(2,1)S(1)}, u32[]{:S(2)}, u32[]{:S(2)}) %collective-permute-start.6) | collective-permute-done | bytes 98336 | tf_op jit(solution)/shard_map/ppermute | solution.py:1036
  622.8 13.9 %unpack_expert_grads.1 = (f32[2,1536,512]{2,1,0:T(8,128)}, f32[2,1536,512]{2,1,0:T(8,128)}, f32[2,512,1536]{2,1,0:T(8,128)}) custom-call(s32[1]{0:T(128)} %bitcast.74.core_ref, bf16[4608,512]{1,0:T(8,128)(2,1)} %pad_maximum_fusion.1.own_ref, bf16[4608,512]{1,0:T(8,128)(2,1)} %collective-permute-done.11.other_ref), custom_call_target="tpu_custom_call" | custom-call | flops 1048576 | bytes 29360128 | tf_op jit(solution)/shard_map/unpack_expert_grads/pallas_call | solution.py:646
  642.4 12.4 %all-gather.18.cloned.1.call-done = bf16[4096,384]{1,0:T(8,128)(2,1)} async-done(((bf16[512,384]{1,0:T(8,128)(2,1)}), bf16[4096,384]{1,0:T(8,128)(2,1)}) %all-gather.18.cloned.1.call-update) | async-done | bytes 3145744 | tf_op jit(solution)/shard_map/all_gather | solution.py:1046
  (389 shorter events, 199.7 us)
Async XLA Ops:
  7.2 120.8 %all-gather.16.cloned.1.call-start = ((), (), s32[]{:S(2)}) async-start(), calls=%async_computation.17 | async-start | bytes 3538944 | tf_op jit(solution)/shard_map/all_gather | solution.py:751
  19.4 54.6 %copy-start.30 = (bf16[1,128,1536]{2,1,0:T(8,128)(2,1)S(1)}, bf16[1,128,1536]{2,1,0:T(8,128)(2,1)}, u32[]{:S(2)}) copy-start(bf16[1,128,1536]{2,1,0:T(8,128)(2,1)} %param.24) | copy-start | bytes 1179652
  19.4 52.8 %all-to-all-start = ((bf16[16,96,1152]{2,1,0:T(8,128)(2,1)}), bf16[16,96,1152]{2,1,0:T(8,128)(2,1)}, u32[]{:S(2)}, u32[]{:S(2)}) async-start(bf16[16,96,1152]{2,1,0:T(8,128)(2,1)} %broadcast_in_dim.37), calls=%async_computation | async-start | bytes 7077888 | tf_op jit(solution)/shard_map/all_to_all | solution.py:749
  27.2 134.0 %all-gather.10.cloned.1.call-start = ((), (), s32[]{:S(2)}) async-start(), calls=%async_computation.11 | async-start | bytes 3538944 | tf_op jit(solution)/shard_map/all_gather | solution.py:860
  27.4 47.7 %collective-permute-start = (bf16[32,1536]{1,0:T(8,128)(2,1)S(1)}, bf16[32,1536]{1,0:T(8,128)(2,1)S(1)}, u32[]{:S(2)}, u32[]{:S(2)}) collective-permute-start(bf16[32,1536]{1,0:T(8,128)(2,1)S(1)} %pad_maximum_fusion.9), channel_id=1, source_target_pairs={{0,0},{16,1},{32,2},{48,3},{64,4},{80,5},{96,6},{112,7},{1,8},{17,... | collective-permute-start | bytes 294920 | tf_op jit(solution)/shard_map/ppermute | solution.py:772
  76.8 39.8 %all-to-all-start.1 = ((bf16[16,48,1536]{2,1,0:T(8,128)(2,1)}), bf16[16,48,1536]{2,1,0:T(8,128)(2,1)S(1)}, u32[]{:S(2)}, u32[]{:S(2)}) async-start(bf16[16,48,1536]{2,1,0:T(8,128)(2,1)} %broadcast_in_dim.42), calls=%async_computation.1 | async-start | bytes 4718592 | tf_op jit(solution)/shard_map/all_to_all | solution.py:749
  88.8 210.6 %copy-start.45 = (pred[32,128]{1,0:T(8,128)(4,1)}, pred[32,128]{1,0:T(8,128)(4,1)S(1)}, u32[]{:S(2)}) copy-start(pred[32,128]{1,0:T(8,128)(4,1)S(1)} %fusion.37) | copy-start | bytes 12292
  116.6 44.5 %all-to-all-start.2 = ((bf16[16,64,1664]{2,1,0:T(8,128)(2,1)}), bf16[16,64,1664]{2,1,0:T(8,128)(2,1)}, u32[]{:S(2)}, u32[]{:S(2)}) async-start(bf16[16,64,1664]{2,1,0:T(8,128)(2,1)} %bitcast.189), calls=%async_computation.2 | async-start | bytes 6815744 | tf_op jit(solution)/shard_map/all_to_all | solution.py:749
  122.6 84.9 %reduce-scatter.4.cloned.1.call-start = ((), (), s32[]{:S(2)}) async-start(), calls=%async_computation.12 | async-start | bytes 3538944 | tf_op jit(solution)/shard_map/reduce_scatter | solution.py:863
  165.9 75.2 %all-gather.12.cloned.1.call-start = ((), (), s32[]{:S(2)}) async-start(), calls=%async_computation.13 | async-start | bytes 3538944 | tf_op jit(solution)/shard_map/all_gather | solution.py:875
  214.5 42.3 %all-to-all-start.3 = ((bf16[16,64,1536]{2,1,0:T(8,128)(2,1)}), bf16[16,64,1536]{2,1,0:T(8,128)(2,1)}, u32[]{:S(2)}, u32[]{:S(2)}) async-start(bf16[16,64,1536]{2,1,0:T(8,128)(2,1)} %bitcast.190), calls=%async_computation.4 | async-start | bytes 6291456 | tf_op jit(solution)/shard_map/all_to_all | solution.py:749
  221.0 127.3 %reduce-scatter.6.cloned.1.call-start = ((), (), s32[]{:S(2)}) async-start(), calls=%async_computation.14 | async-start | bytes 3538944 | tf_op jit(solution)/shard_map/reduce_scatter | solution.py:906
  247.3 139.1 %copy-start.33 = (bf16[1024,128]{0,1:T(8,128)(2,1)}, bf16[1024,128]{0,1:T(8,128)(2,1)S(1)}, u32[]{:S(2)}) copy-start(bf16[1024,128]{0,1:T(8,128)(2,1)S(1)} %get-tuple-element.185) | copy-start | bytes 786436
  287.6 64.6 %collective-permute-start.1 = (bf16[4608,512]{1,0:T(8,128)(2,1)}, bf16[4608,512]{1,0:T(8,128)(2,1)}, u32[]{:S(2)}, u32[]{:S(2)}) collective-permute-start(bf16[4608,512]{1,0:T(8,128)(2,1)} %dynamic-slice_bitcast_fusion), channel_id=1, source_target_pairs={{0,16},{16,0},{32,48},{48,32},{64,80},{80,64},{96,112},{112,96},{1... | collective-permute-start | bytes 14155784 | tf_op jit(solution)/shard_map/ppermute | solution.py:612
  293.7 50.2 %all-to-all-start.4 = ((bf16[16,64,1664]{2,1,0:T(8,128)(2,1)}), bf16[16,64,1664]{2,1,0:T(8,128)(2,1)}, u32[]{:S(2)}, u32[]{:S(2)}) async-start(bf16[16,64,1664]{2,1,0:T(8,128)(2,1)} %bitcast.201), calls=%async_computation.5 | async-start | bytes 6815744 | tf_op jit(solution)/shard_map/all_to_all | solution.py:749
  298.9 140.4 %all-gather.14.cloned.1.call-start = ((), (), s32[]{:S(2)}) async-start(), calls=%async_computation.15 | async-start | bytes 3538944 | tf_op jit(solution)/shard_map/all_gather | solution.py:946
  300.8 47.5 %copy-start.20 = (bf16[128,1536]{1,0:T(8,128)(2,1)S(1)}, bf16[128,1536]{1,0:T(8,128)(2,1)}, u32[]{:S(2)}) copy-start(bf16[128,1536]{1,0:T(8,128)(2,1)} %reduce-scatter.4.cloned.1.call-done) | copy-start | bytes 1179652
  361.7 48.8 %collective-permute-start.4 = (bf16[1152,512]{1,0:T(8,128)(2,1)S(1)}, bf16[1152,512]{1,0:T(8,128)(2,1)}, u32[]{:S(2)}, u32[]{:S(2)}) collective-permute-start(bf16[1152,512]{1,0:T(8,128)(2,1)S(1)} %dynamic-slice_bitcast_fusion.1), channel_id=1, source_target_pairs={{0,96},{16,112},{32,64},{48,80},{64,32},{80,48},{96,0},{112,16},{1... | collective-permute-start | bytes 3538952 | tf_op jit(solution)/shard_map/ppermute | solution.py:612
  374.7 39.2 %collective-permute-start.2 = (bf16[1152,512]{1,0:T(8,128)(2,1)}, bf16[1152,512]{1,0:T(8,128)(2,1)}, u32[]{:S(2)}, u32[]{:S(2)}) collective-permute-start(bf16[1152,512]{1,0:T(8,128)(2,1)} %dynamic-slice_bitcast_fusion.2), channel_id=1, source_target_pairs={{0,32},{16,48},{32,0},{48,16},{64,96},{80,112},{96,64},{112,80},{1... | collective-permute-start | bytes 3538952 | tf_op jit(solution)/shard_map/ppermute | solution.py:612
  374.8 69.6 %all-to-all-start.5 = ((bf16[16,64,1536]{2,1,0:T(8,128)(2,1)}), bf16[16,64,1536]{2,1,0:T(8,128)(2,1)}, u32[]{:S(2)}, u32[]{:S(2)}) async-start(bf16[16,64,1536]{2,1,0:T(8,128)(2,1)} %bitcast.202), calls=%async_computation.7 | async-start | bytes 6291456 | tf_op jit(solution)/shard_map/all_to_all | solution.py:749
  386.4 230.8 %reduce-scatter.8.cloned.1.call-start = ((), (), s32[]{:S(2)}) async-start(), calls=%async_computation.16 | async-start | bytes 7077888 | tf_op jit(solution)/shard_map/reduce_scatter | solution.py:998
  412.2 24.2 %collective-permute-start.5 = (bf16[576,512]{1,0:T(8,128)(2,1)S(1)}, bf16[576,512]{1,0:T(8,128)(2,1)}, u32[]{:S(2)}, u32[]{:S(2)}) collective-permute-start(bf16[576,512]{1,0:T(8,128)(2,1)S(1)} %dynamic-slice_bitcast_fusion.3), channel_id=1, source_target_pairs={{0,32},{16,48},{32,0},{48,16},{64,96},{80,112},{96,64},{112,80},{1... | collective-permute-start | bytes 1769480 | tf_op jit(solution)/shard_map/ppermute | solution.py:612
  415.6 22.2 %collective-permute-start.3 = (bf16[576,512]{1,0:T(8,128)(2,1)S(1)}, bf16[576,512]{1,0:T(8,128)(2,1)}, u32[]{:S(2)}, u32[]{:S(2)}) collective-permute-start(bf16[576,512]{1,0:T(8,128)(2,1)S(1)} %dynamic-slice_bitcast_fusion.4), channel_id=1, source_target_pairs={{0,96},{16,112},{32,64},{48,80},{64,32},{80,48},{96,0},{112,16},{1... | collective-permute-start | bytes 1769480 | tf_op jit(solution)/shard_map/ppermute | solution.py:612
  501.9 48.7 %all-to-all-start.6 = ((bf16[16,224,384]{2,1,0:T(8,128)(2,1)}), bf16[16,224,384]{2,1,0:T(8,128)(2,1)}, u32[]{:S(2)}, u32[]{:S(2)}) async-start(bf16[16,224,384]{2,1,0:T(8,128)(2,1)} %maximum_dynamic-update-slice_fusion), calls=%async_computation.9 | async-start | bytes 5505024 | tf_op jit(solution)/shard_map/all_to_all | solution.py:749
  552.6 14.0 %collective-permute-start.7 = (bf16[576,512]{1,0:T(8,128)(2,1)S(1)}, bf16[576,512]{1,0:T(8,128)(2,1)}, u32[]{:S(2)}, u32[]{:S(2)}) collective-permute-start(bf16[576,512]{1,0:T(8,128)(2,1)S(1)} %add_convert_fusion.1), channel_id=1, source_target_pairs={{0,96},{16,112},{32,64},{48,80},{64,32},{80,48},{96,0},{112,16},{1... | collective-permute-start | bytes 1769480 | tf_op jit(solution)/shard_map/ppermute | solution.py:617
  553.2 61.3 %all-to-all-start.7 = ((bf16[16,96,1152]{2,1,0:T(8,128)(2,1)}), bf16[16,96,1152]{2,1,0:T(8,128)(2,1)}, u32[]{:S(2)}, u32[]{:S(2)}) async-start(bf16[16,96,1152]{2,1,0:T(8,128)(2,1)} %bitcast.200), calls=%async_computation.10 | async-start | bytes 7077888 | tf_op jit(solution)/shard_map/all_to_all | solution.py:749
  561.4 93.3 %all-gather.18.cloned.1.call-start = ((), (), s32[]{:S(2)}) async-start(), calls=%async_computation.18 | async-start | bytes 3538944 | tf_op jit(solution)/shard_map/all_gather | solution.py:1046
  562.4 13.3 %collective-permute-start.9 = (bf16[576,512]{1,0:T(8,128)(2,1)}, bf16[576,512]{1,0:T(8,128)(2,1)}, u32[]{:S(2)}, u32[]{:S(2)}) collective-permute-start(bf16[576,512]{1,0:T(8,128)(2,1)} %add_convert_fusion), channel_id=1, source_target_pairs={{0,32},{16,48},{32,0},{48,16},{64,96},{80,112},{96,64},{112,80},{1... | collective-permute-start | bytes 1769480 | tf_op jit(solution)/shard_map/ppermute | solution.py:617
  569.0 37.0 %collective-permute-start.8 = (bf16[1152,512]{1,0:T(8,128)(2,1)}, bf16[1152,512]{1,0:T(8,128)(2,1)}, u32[]{:S(2)}, u32[]{:S(2)}) collective-permute-start(bf16[1152,512]{1,0:T(8,128)(2,1)} %pad_maximum_fusion.2), channel_id=1, source_target_pairs={{0,32},{16,48},{32,0},{48,16},{64,96},{80,112},{96,64},{112,80},{1... | collective-permute-start | bytes 3538952 | tf_op jit(solution)/shard_map/ppermute | solution.py:617
  578.9 30.1 %collective-permute-start.10 = (bf16[1152,512]{1,0:T(8,128)(2,1)}, bf16[1152,512]{1,0:T(8,128)(2,1)}, u32[]{:S(2)}, u32[]{:S(2)}) collective-permute-start(bf16[1152,512]{1,0:T(8,128)(2,1)} %pad_maximum_fusion.3), channel_id=1, source_target_pairs={{0,96},{16,112},{32,64},{48,80},{64,32},{80,48},{96,0},{112,16},{1... | collective-permute-start | bytes 3538952 | tf_op jit(solution)/shard_map/ppermute | solution.py:617
  583.1 22.2 %collective-permute-start.6 = (bf16[128,384]{1,0:T(8,128)(2,1)S(1)}, bf16[128,384]{1,0:T(8,128)(2,1)S(1)}, u32[]{:S(2)}, u32[]{:S(2)}) collective-permute-start(bf16[128,384]{1,0:T(8,128)(2,1)S(1)} %slice.338), channel_id=1, source_target_pairs={{0,0},{1,16},{2,32},{3,48},{4,64},{5,80},{6,96},{7,112},{8,1},{9,1... | collective-permute-start | bytes 294920 | tf_op jit(solution)/shard_map/ppermute | solution.py:1036
  614.2 8.6 %collective-permute-start.11 = (bf16[4608,512]{1,0:T(8,128)(2,1)}, bf16[4608,512]{1,0:T(8,128)(2,1)}, u32[]{:S(2)}, u32[]{:S(2)}) collective-permute-start(bf16[4608,512]{1,0:T(8,128)(2,1)} %pad_maximum_fusion.1.own_ref), channel_id=1, source_target_pairs={{0,16},{16,0},{32,48},{48,32},{64,80},{80,64},{96,112},{112,96},{1... | collective-permute-start | bytes 14155784 | tf_op jit(solution)/shard_map/ppermute | solution.py:1044
  (66 other events, 589.6 us)
Sparse Core Ops, SparseCore 0:
  9.7 31.5 all-gather.15
  75.2 37.8 all-gather.9
  166.0 41.4 reduce-scatter.3
  211.0 30.0 all-gather.11
  250.9 32.4 reduce-scatter.5
  352.3 55.6 all-gather.13
  482.8 45.5 reduce-scatter.7
  621.1 33.5 all-gather.17

commit v5 on v4

--- a/solution.py
+++ b/solution.py
@@ -382,8 +382,9 @@
 
 
 def expert_main_kernel(
-    rows_ref, routed_ref, raw_ref, gate_ref, up_ref, router_ref, marks_ref, earlier_ref,
-    back_ref, act_ref, scaled_ref, d_g_ref, d_v_ref,
+    rows_ref, routed_ref, raw_ref, gate_ref, up_ref, router_ref, marks_ref,
+    moe_ref, cot_ref, shared_ref, down_ref,
+    back_ref, act_ref, scaled_ref, d_g_ref, d_v_ref, both_ref, s_act_ref, d_both_ref,
 ):
     f32, bf = jnp.float32, jnp.bfloat16
     dim = rows_ref.shape[-1]
@@ -416,6 +417,20 @@
     d_g_ref[0] = d_g
     d_v_ref[0] = d_v
 
+    units = down_ref.shape[0]
+    s_both = times(moe_ref[...], shared_ref[...])
+    s_gate, s_up = s_both[:, :units], s_both[:, units:]
+    s_sig = jax.nn.sigmoid(s_gate)
+    s_silu = s_gate * s_sig
+    s_act = (s_silu * s_up).astype(bf)
+    d_sh = times_transposed(cot_ref[...], down_ref[...])
+    d_gs = (d_sh * s_up * (s_sig * (1.0 + s_gate * (1.0 - s_sig)))).astype(bf)
+    d_both = jnp.concatenate([d_gs, (d_sh * s_silu).astype(bf)], axis=1)
+    both_ref[:, :dim] = times_transposed(d_both, shared_ref[...]).astype(bf)
+    both_ref[:, dim:] = times(s_act, down_ref[...]).astype(bf)
+    s_act_ref[...] = s_act
+    d_both_ref[...] = d_both
+
 
 def expert_late_kernel(
     rows_ref, cot_ref, act_ref, scaled_ref, d_g_ref, d_v_ref, down_ref,
@@ -467,12 +482,15 @@
     )(cot_rows, down)
 
 
-def expert_main(rows, cot_rows, raw, gate, up, w_all, marks, earlier):
+def expert_main(rows, cot_rows, raw, gate, up, w_all, marks, moe_all, cot_all, w_shared, w_down):
     sources, local, cap, dim = rows.shape
     units = gate.shape[2]
     count = sources * cap
     hidden = jax.ShapeDtypeStruct((local, count, units), jnp.bfloat16)
     back = (sources, local, cap, dim + 128)
+    seq_rows = moe_all.shape[0]
+    shared_units = w_down.shape[0]
+    share = lambda width: pl.BlockSpec((seq_rows // local, width), lambda e: (e, 0))
     return pl.pallas_call(
         expert_main_kernel,
         grid=(local,),
@@ -484,13 +502,23 @@
             per_expert(up.shape),
             pl.BlockSpec((dim, 128), lambda e: (0, w_all.shape[1] // 128 - 1)),
             per_expert(marks.shape),
-            corner_of(earlier),
-        ],
-        out_specs=[expert_slots(back)] + [per_expert(hidden.shape)] * 4,
-        out_shape=[jax.ShapeDtypeStruct(back, jnp.bfloat16)] + [hidden] * 4,
+            share(dim),
+            share(dim),
+            whole(w_shared.shape),
+            whole(w_down.shape),
+        ],
+        out_specs=[expert_slots(back)]
+        + [per_expert(hidden.shape)] * 4
+        + [share(2 * dim), share(shared_units), share(2 * shared_units)],
+        out_shape=[jax.ShapeDtypeStruct(back, jnp.bfloat16)]
+        + [hidden] * 4
+        + [
+            jax.ShapeDtypeStruct((seq_rows, width), jnp.bfloat16)
+            for width in (2 * dim, shared_units, 2 * shared_units)
+        ],
         name="expert_main",
         **expert_params(8 << 30, 20 << 20),
-    )(rows, cot_rows, raw, gate, up, w_all, marks, earlier)
+    )(rows, cot_rows, raw, gate, up, w_all, marks, moe_all, cot_all, w_shared, w_down)
 
 
 def expert_late(rows, cot_rows, act, scaled, d_g, d_v, down):
@@ -602,6 +630,26 @@
         cost_estimate=pl.CostEstimate(flops=8 << 20, bytes_accessed=12 << 20, transcendentals=0),
         name="assemble",
     )(side, in_weight, in_gain, out_weight, out_gain)
+
+
+def gather_rows(values, core, z_at, mates):
+    cores = 2
+    chips = len(mates) // cores
+    column = [values]
+    for hop in range(1, chips):
+        pairs = [
+            (i, (i // cores + hop) % chips * cores + i % cores) for i in range(len(mates))
+        ]
+        column.append(lax.ppermute(values, "seq", pairs))
+    column = jnp.stack(column)
+    both = jnp.stack([column, lax.ppermute(column, "seq", mates)], axis=1)
+    both = both.reshape((len(mates),) + values.shape)
+    ordered = [
+        lax.dynamic_index_in_dim(both, (z_at - z) % chips * cores + (c ^ core), 0, keepdims=False)
+        for z in range(chips)
+        for c in range(cores)
+    ]
+    return jnp.concatenate(ordered, axis=0)
 
 
 def halve(values, bit, pairs):
@@ -748,8 +796,10 @@
     def to_shards(values):
         return lax.all_to_all(values, "shard", split_axis=0, concat_axis=0, tiled=True)
 
-    x_all = lax.all_gather(x_low, "seq", axis=0, tiled=True)
-    w_all = to_shards(jnp.broadcast_to(packed[None], (sh, rows_w, total))).reshape(dim, total)
+    w_all = lax.all_gather(packed, "shard", axis=0, tiled=True)
+    core, z_at = q % 2, q // 2
+    mates = [(i, i ^ 1) for i in range(sq)]
+    x_all = gather_rows(x_low, core, z_at, mates)
 
     out_scaled = (norm_gain.astype(f32)[:, None] * out_weight.astype(f32)).astype(bf)
     own_out = out_weight.shape[0] // sq
@@ -783,17 +833,6 @@
         [shared_cols[fold * band : fold * band + fold] for band in range(bands)], axis=1
     )
     piece = jnp.concatenate([piece, shared_rows], axis=0)
-    rows_all = to_shards(jnp.broadcast_to(piece[None], (sh,) + piece.shape))
-    own_rows = own_out + own_down
-    w_out = rows_all[:, :own_out].reshape(gw, dim)
-    w_down = rows_all[:, own_out:own_rows].reshape(gf, dim)
-    w_shared = (
-        rows_all[:, own_rows:]
-        .reshape(sh, fold, bands, 2 * gf)
-        .transpose(0, 2, 1, 3)
-        .reshape(dim, 2 * gf)
-    )
-
     route_ids = routes[0]
     expert_ids = jnp.arange(experts, dtype=jnp.int32)
     named = jnp.any(route_ids[:, :, None] == expert_ids[None, None, :], axis=1).astype(f32)
@@ -822,6 +861,19 @@
     named_lanes = jnp.pad(named, ((0, 0), (router_lane, 128 - router_lane - experts)))
     cot_rows = dispatched(jnp.concatenate([cot_low, named_lanes.astype(bf)], axis=1))
 
+    w_all, cot_rows = lax.optimization_barrier((w_all, cot_rows))
+    piece = after(piece, cot_rows)
+    rows_all = to_shards(jnp.broadcast_to(piece[None], (sh,) + piece.shape))
+    own_rows = own_out + own_down
+    w_out = rows_all[:, :own_out].reshape(gw, dim)
+    w_down = rows_all[:, own_out:own_rows].reshape(gf, dim)
+    w_shared = (
+        rows_all[:, own_rows:]
+        .reshape(sh, fold, bands, 2 * gf)
+        .transpose(0, 2, 1, 3)
+        .reshape(dim, 2 * gf)
+    )
+
     x_wide = x_all.astype(f32)
     x_r = row_scale(x_wide)
     proj = times(x_all, w_all) * x_r
@@ -858,7 +910,7 @@
     mixed, q_low, square_part, starts = scan_forward(proj, taps_in, head_in, skip_in)
 
     cot_all = lax.all_gather(after(cot_low, w_all), "seq", axis=0, tiled=True)
-    w_out, cot_rows, cot_all = lax.optimization_barrier((w_out, cot_rows, cot_all))
+    w_out, cot_all = lax.optimization_barrier((w_out, cot_all))
     out_part = times(q_low, w_out).astype(bf)
     out_sum = lax.psum_scatter(out_part, "seq", scatter_dimension=0, tiled=True)
     square = lax.psum(square_part.reshape(sq, toks), "seq")
@@ -889,41 +941,33 @@
     )
     marks = (marks[:, :, None] == lanes[None, None, :]).astype(f32)
 
-    s_both = times(moe_all, w_shared)
-    s_gate, s_up = s_both[:, :gf], s_both[:, gf:]
-    s_sig = jax.nn.sigmoid(s_gate)
-    s_silu = s_gate * s_sig
-    s_act = (s_silu * s_up).astype(bf)
-    d_sh = times_transposed(cot_all, w_down)
-    d_both = jnp.concatenate(
-        [
-            (d_sh * s_up * (s_sig * (1.0 + s_gate * (1.0 - s_sig)))).astype(bf),
-            (d_sh * s_silu).astype(bf),
-        ],
-        axis=1,
-    )
-    d_moe_part = times_transposed(d_both, w_shared).astype(bf)
-    d_moe_shared = lax.psum_scatter(d_moe_part, "seq", scatter_dimension=0, tiled=True)
-
-    back_rows, e_act, e_scaled, d_g, d_v = expert_main(
-        rows, cot_rows, d_raw, expert_gate, expert_up, w_all, marks, d_moe_part
-    )
+    back_rows, e_act, e_scaled, d_g, d_v, both_part, s_act, d_both = expert_main(
+        rows,
+        cot_rows,
+        d_raw,
+        expert_gate,
+        expert_up,
+        w_all,
+        marks,
+        moe_all,
+        cot_all,
+        w_shared,
+        w_down,
+    )
+    shared_both = lax.psum_scatter(both_part, "seq", scatter_dimension=0, tiled=True)
+    d_moe_shared = shared_both[:, :dim]
+    shared_sum = shared_both[:, dim:]
     d_returned = to_shards(back_rows.reshape(sh, local_e * CAP, dim + 128))
     e_out, e_grads = expert_late(rows, cot_rows, e_act, e_scaled, d_g, d_v, expert_down)
     d_returned, e_out = lax.optimization_barrier((d_returned, e_out))
     returned = to_shards(e_out.reshape(sh, local_e * CAP, dim))
 
-    core, z_at = q % 2, q // 2
-    mates = [(i, i ^ 1) for i in range(sq)]
     near = [(i, 2 * ((i // 2) ^ 1) + i % 2) for i in range(sq)]
     far = [(i, 2 * (sq // 2 - 1 - i // 2) + i % 2) for i in range(sq)]
     is_inner = ((z_at == 1) | (z_at == 2)).astype(jnp.int32)
     is_high = (z_at >= 2).astype(jnp.int32)
     e_mine = halve(e_grads.reshape(-1, e_grads.shape[2]), core, mates)
     cutoff = e_mine.shape[0] // 2
-    e_one = halve(e_mine[:cutoff], is_inner, near)
-    e_two = halve(e_mine[cutoff:], is_high, far)
-    e_one, e_two = halve(e_one, is_high, far), halve(e_two, is_inner, near)
 
     d_flat = transposed_times(dispatch_flat, d_returned.reshape(slots, dim + 128))
     d_gates = d_flat[:, dim : dim + experts] + d_flat[:, dim + 64 : dim + 64 + experts]
@@ -943,15 +987,16 @@
     )
     d_o = d_resid.astype(bf)
     kappa = jnp.sum(d_o.astype(f32) * added, axis=1) / inner
-    d_o_all = lax.all_gather(d_o, "seq", axis=0, tiled=True)
-    kappa_all = lax.all_gather(after(kappa, e_mine).reshape(1, toks), "seq", axis=0)
-    kappa_all = kappa_all.reshape(seq_rows, 1)
-
-
-    d_gated = times_transposed(d_o_all, w_out)
-    grad_out_part = transposed_times(
-        q_low, (after(q_r, kappa_all) * d_o_all.astype(f32)).astype(bf)
-    )
+    kappa_high = kappa.astype(bf)
+    kappa_low = (kappa - kappa_high.astype(f32)).astype(bf)
+    d_o_ext = jnp.concatenate(
+        [d_o, kappa_high[:, None], kappa_low[:, None], jnp.zeros((toks, 126), bf)], axis=1
+    )
+    d_o_all = lax.all_gather(d_o_ext, "seq", axis=0, tiled=True)
+    kappa_all = jnp.sum(d_o_all[:, dim : dim + 2].astype(f32), axis=1, keepdims=True)
+
+    d_gated = times_transposed(d_o_all, jnp.pad(w_out, ((0, 0), (0, 128))))
+    grad_out_part = transposed_times(q_low, (q_r * d_o_all[:, :dim].astype(f32)).astype(bf))
     grad_down_part = transposed_times(s_act, cot_all)
     grad_shared_part = transposed_times(moe_all, d_both)
 
@@ -982,6 +1027,9 @@
     )
     moved_early = to_shards(early_part)
 
+    e_late = after(e_mine, d_o_all)
+    e_one = halve(e_late[:cutoff], is_inner, near)
+    e_two = halve(e_late[cutoff:], is_high, far)
     row_values = jnp.concatenate(
         [q_r, kappa_all, x_r, jnp.zeros((seq_rows, 5), f32)], axis=1
     )
@@ -993,15 +1041,12 @@
     grad_bias_local = d_head[0, :gh]
     grad_decay_local = d_head[1, :gh] * decay_rate
     grad_skip_local = jnp.sum(d_skip[0].reshape(gh, per_head), axis=1)
+    d_proj, moved_early = lax.optimization_barrier((d_proj, moved_early))
     back_part = times_transposed(d_proj, w_all).astype(bf)
-    shared_part = times(s_act, w_down).astype(bf)
-    both_sum = lax.psum_scatter(
-        jnp.concatenate([back_part, shared_part], axis=1), "seq", scatter_dimension=0, tiled=True
-    ).astype(f32)
-    back_sum, shared_sum = both_sum[:, :dim], both_sum[:, dim:]
+    back_sum = lax.psum_scatter(back_part, "seq", scatter_dimension=0, tiled=True).astype(f32)
     weighted = (gates.T[:, None, :] * dispatch.astype(f32)).reshape(slots, toks)
     combined = transposed_times(weighted.astype(bf), returned.reshape(slots, dim))
-    block_output = ((resid + shared_sum + combined) * live[:, None]).astype(bf)[None]
+    block_output = ((resid + shared_sum.astype(f32) + combined) * live[:, None]).astype(bf)[None]
     tok_x_r = row_scale(x_tok)
     x_n = x_tok * tok_x_r
     input_grad = (
@@ -1031,15 +1076,16 @@
     last_part = grad_in_part + jnp.pad(
         small_part.reshape(dim, small_cols), ((0, 0), (used, total - used - small_cols))
     )
-    last_part, moved_early = lax.optimization_barrier((last_part.astype(bf), moved_early))
+    last_part = last_part.astype(bf)
     early_sum = jnp.sum(moved_early.astype(f32), axis=0).astype(bf)
     rows_sum = lax.ppermute(early_sum[: bands * own_rows], both_axes, backward_pairs)
+    e_one, e_two = halve(e_one, is_high, far), halve(e_two, is_inner, near)
     e_one, e_two = after(e_one, last_part), after(e_two, last_part)
     e_one, e_two = double(e_one, is_high, far), double(e_two, is_inner, near)
     e_one, e_two = double(e_one, is_inner, near), double(e_two, is_high, far)
     moved_last = to_shards(last_part.reshape(sh, rows_w, total))
     last_sum = jnp.sum(moved_last.astype(f32), axis=0)
-    last_sum = after(after(after(last_sum, e_one), e_two), both_sum).astype(bf)
+    last_sum = after(after(after(last_sum, e_one), e_two), back_sum).astype(bf)
     e_mine = jnp.concatenate([e_one, e_two], axis=0)
     e_other = lax.ppermute(e_mine, "seq", mates)
     grad_e_gate, grad_e_up, grad_e_down = unpack_expert_grads(e_mine, e_other, core)

time: 682 us -> 607 us (0.89)
  waiting for transfers between devices: 229 us -> 201 us
  blocking collectives: 40.8 us -> 15 us
  matrix products: 70.4 us -> 55.2 us
    all_to_all x8 -> x7, waiting for transfers between devices: 145 us -> 82.1 us  [to_shards(): lax.all_to_all(values, 'shard', split_axis=0, concat_axis=0, tiled=True)]
    all_gather x2, waiting for transfers between devices: 0.02 us -> 60.1 us  [the longest x1 31.5 us: on_device(): w_all = lax.all_gather(packed, 'shard', axis=0, tiled=True)]
    all_to_all x8 -> x7, starting transfers between devices: 69.2 us -> 46.6 us  [to_shards(): lax.all_to_all(values, 'shard', split_axis=0, concat_axis=0, tiled=True)]
    all_gather x1 -> x0, blocking collectives: 19.5 us -> none  [on_device(): lax.all_gather(after(kappa, e_mine).reshape(1, toks), 'seq', axis=0)]
    all_gather x1, waiting for transfers between devices: 16.6 us -> 0.01 us  [on_device(): moe_all = lax.all_gather(moe_in, 'seq', axis=0, tiled=True)]
    ppermute x0 -> x4, waiting for transfers between devices: none -> 15.3 us  [the longest x3 15.3 us: gather_rows(): column.append(lax.ppermute(values, 'seq', pairs))]
    ppermute x5, waiting for transfers between devices: 19.9 us -> 9.87 us  [halve(): other = lax.ppermute(sent, 'seq', pairs)]
    all_gather x1, waiting for transfers between devices: 12.4 us -> 2.52 us  [on_device(): lax.all_gather(jnp.concatenate([rows_sum, early_sum[bands * own_rows:]] +...]
  transfers between devices with their start and end apart: 28 -> 31, of which waited for: 15 -> 15; matrix products, arithmetic and copies ran while one was open for 22% -> 21% of each run, Pallas kernels for 8% -> 11%
where the time goes in v5:
time: 607 us; the launch traced here: 599 us
  waiting for transfers between devices  201 us (33%)
  starting transfers between devices  101 us (17%)
  Pallas kernels  88.2 us (15%)
  local copies, waits for them, and re-layouts  66 us (11%)
  matrix products  55.2 us (9%)
  other arithmetic  51.3 us (8%)
  between operations  21.9 us (4%)
  blocking collectives  15 us (2%)
    all_to_all x7, waiting for transfers between devices, to_shards(): lax.all_to_all(values, 'shard', split_axis=0, concat_axis=0, tiled=True)  82.1 us
    all_to_all x7, starting transfers between devices, to_shards(): lax.all_to_all(values, 'shard', split_axis=0, concat_axis=0, tiled=True)  46.6 us
    all_gather x1, waiting for transfers between devices, on_device(): w_all = lax.all_gather(packed, 'shard', axis=0, tiled=True)  31.5 us
    all_gather x1, waiting for transfers between devices, on_device(): d_o_all = lax.all_gather(d_o_ext, 'seq', axis=0, tiled=True)  28.6 us
    pallas_call x1, Pallas kernels, scan_backward(): pl.pallas_call(scan_backward_kernel, grid=(chunks,), in_specs=[pl.BlockSp...  23.6 us
    dot_general x5, matrix products, times(): return jnp.dot(left, right, preferred_element_type=jnp.float32)  20 us
    dot_general x6, matrix products, transposed_times(): lax.dot_general(left, right, (((0,), (0,)), ((), ())), preferred_element_...  19.5 us
    pallas_call x1, Pallas kernels, expert_main(): pl.pallas_call(expert_main_kernel, grid=(local,), in_specs=[expert_slots(...  19.2 us
  transfers between devices with their start and end apart: 31, of which 15 were waited for; matrix products, arithmetic and copies ran while one was open for 21% of the time, Pallas kernels for 11%

profile of v5, /device:TPU:1, one launch (start us, length us, event | category | flops | bytes accessed | tf_op | source)
XLA Modules:
  0.0 599.2 jit_solution(14746230171435491043)
XLA Ops:
  22.5 7.8 %all-to-all-start = ((bf16[16,64,1664]{2,1,0:T(8,128)(2,1)}), bf16[16,64,1664]{2,1,0:T(8,128)(2,1)}, u32[]{:S(2)}, u32[]{:S(2)}) async-start(bf16[16,64,1664]{2,1,0:T(8,128)(2,1)} %bitcast.200), calls=%async_computation | async-start | bytes 6815744 | tf_op jit(solution)/shard_map/all_to_all | solution.py:797
  36.8 5.7 collective-permute-done.1
  42.5 9.5 %collective-permute-done = bf16[128,1536]{1,0:T(8,128)(2,1)S(1)} collective-permute-done((bf16[128,1536]{1,0:T(8,128)(2,1)S(1)}, bf16[128,1536]{1,0:T(8,128)(2,1)S(1)}, u32[]{:S(2)}, u32[]{:S(2)}) %collective-permute-start) | collective-permute-done | bytes 393248 | tf_op jit(solution)/shard_map/ppermute | solution.py:643
  60.8 16.9 %all-to-all-done = bf16[16,64,1664]{2,1,0:T(8,128)(2,1)} async-done(((bf16[16,64,1664]{2,1,0:T(8,128)(2,1)}), bf16[16,64,1664]{2,1,0:T(8,128)(2,1)}, u32[]{:S(2)}, u32[]{:S(2)}) %all-to-all-start) | async-done | bytes 3407904 | tf_op jit(solution)/shard_map/all_to_all | solution.py:797
  77.7 31.5 %all-gather.7.cloned.1.call-done.router_ref = bf16[1536,1152]{1,0:T(8,128)(2,1)} async-done(((bf16[96,1152]{1,0:T(8,128)(2,1)}), bf16[1536,1152]{1,0:T(8,128)(2,1)}) %all-gather.7.cloned.1.call-update) | async-done | bytes 3538960 | tf_op jit(solution)/shard_map/all_gather | solution.py:799
  129.0 7.3 %convolution_multiply_fusion.proj_ref.prev_ref = f32[1024,1152]{1,0:T(8,128)S(1)} fusion(bf16[1024,1536]{1,0:T(8,128)(2,1)} %copy-done.23, bf16[1536,1152]{1,0:T(8,128)(2,1)} %all-gather.7.cloned.1.call-done.router_ref, f32[1024]{0:T(1024)S(1)} %add_rsqrt_fusion.1), kind=kOutput, calls=%fused_computation.8 | convolution fusion | flops 3625058304 | bytes 11407360 | tf_op jit(solution)/shard_map/dot_general | solution.py:19
  136.3 10.9 %scan_forward.1 = (bf16[1024,384]{1,0:T(8,128)(2,1)S(1)}, bf16[1024,384]{1,0:T(8,128)(2,1)S(1)}, f32[1024,1]{1,0:T(8,128)S(1)}, f32[8,128,384]{2,1,0:T(8,128)S(1)}) custom-call(f32[1024,1152]{1,0:T(8,128)S(1)} %convolution_multiply_fusion.proj_ref.prev_ref, f32[1024,1152]{1,0:T(8,128)S(1)} %convolution_multiply_fusion.proj_ref.prev_ref, ...), custom_call_target="tpu_custom_call" | custom-call | flops 3221225472 | bytes 12582912 | tf_op jit(solution)/shard_map/scan_forward/pallas_call | solution.py:298
  151.2 8.6 %all-to-all-done.1 = bf16[16,48,1536]{2,1,0:T(8,128)(2,1)} async-done(((bf16[16,48,1536]{2,1,0:T(8,128)(2,1)}), bf16[16,48,1536]{2,1,0:T(8,128)(2,1)}, u32[]{:S(2)}, u32[]{:S(2)}) %all-to-all-start.1) | async-done | bytes 2359328 | tf_op jit(solution)/shard_map/all_to_all | solution.py:797
  162.1 5.0 convolution_convert_fusion.1
  167.2 4.9 expert_early.1.raw_ref
  174.1 15.0 %psum.7 = f32[8,128]{1,0:T(8,128)S(1)} all-reduce(f32[8,128]{1,0:T(8,128)S(1)} %bitcast.238), channel_id=1, replica_groups=mesh['seq'=8,'shard'=16] {'seq'}, use_global_device_ids=true, to_apply=%region_3.4 | all-reduce | flops 1024 | bytes 8192 | tf_op jit(solution)/shard_map/psum | solution.py:916
  191.0 9.4 %reduce-scatter.4.cloned.1.call-done = bf16[128,1536]{1,0:T(8,128)(2,1)} async-done(((bf16[1024,1536]{1,0:T(8,128)(2,1)}), bf16[128,1536]{1,0:T(8,128)(2,1)}) %reduce-scatter.4.cloned.1.call-update) | async-done | bytes 393232 | tf_op jit(solution)/shard_map/reduce_scatter | solution.py:915
  207.4 6.3 %all-to-all-start.2 = ((bf16[16,64,1536]{2,1,0:T(8,128)(2,1)}), bf16[16,64,1536]{2,1,0:T(8,128)(2,1)}, u32[]{:S(2)}, u32[]{:S(2)}) async-start(bf16[16,64,1536]{2,1,0:T(8,128)(2,1)} %bitcast.209), calls=%async_computation.3 | async-start | bytes 6291456 | tf_op jit(solution)/shard_map/all_to_all | solution.py:797
  219.7 29.8 %all-to-all-done.2 = bf16[16,64,1536]{2,1,0:T(8,128)(2,1)} async-done(((bf16[16,64,1536]{2,1,0:T(8,128)(2,1)}), bf16[16,64,1536]{2,1,0:T(8,128)(2,1)}, u32[]{:S(2)}, u32[]{:S(2)}) %all-to-all-start.2) | async-done | bytes 3145760 | tf_op jit(solution)/shard_map/all_to_all | solution.py:797
  249.6 19.2 %expert_main.1 = (bf16[16,2,32,1664]{3,2,1,0:T(8,128)(2,1)}, bf16[2,512,512]{2,1,0:T(8,128)(2,1)}, bf16[2,512,512]{2,1,0:T(8,128)(2,1)}, bf16[2,512,512]{2,1,0:T...) custom-call(bf16[16,2,32,1536]{3,2,1,0:T(8,128)(2,1)} %bitcast.33.ro, ...), custom_call_target="tpu_custom_call" | custom-call | flops 8589934592 | bytes 20971520 | tf_op jit(solution)/shard_map/expert_main/pallas_call | solution.py:494
  268.8 9.8 %all-to-all-start.3 = ((bf16[16,64,1664]{2,1,0:T(8,128)(2,1)}), bf16[16,64,1664]{2,1,0:T(8,128)(2,1)}, u32[]{:S(2)}, u32[]{:S(2)}) async-start(bf16[16,64,1664]{2,1,0:T(8,128)(2,1)} %bitcast.216), calls=%async_computation.5 | async-start | bytes 6815744 | tf_op jit(solution)/shard_map/all_to_all | solution.py:797
  280.7 12.6 %expert_late.1 = (bf16[16,2,32,1536]{3,2,1,0:T(8,128)(2,1)}, bf16[2,4608,512]{2,1,0:T(8,128)(2,1)}) custom-call(bf16[16,2,32,1536]{3,2,1,0:T(8,128)(2,1)} %bitcast.33.rows_ref, bf16[16,2,32,1664]{3,2,1,0:T(8,128)(2,1)} %bitcast.22.cot_ref.routed_ref, bf16[2,512,512]{2,1,0:T(8,128)(2,1)} %get-tuple-element.64.act_ref, ...), custom_call_target="tpu_custom_call" | custom-call | flops 7516192768 | bytes 25165824 | tf_op jit(solution)/shard_map/expert_late/pallas_call | solution.py:528
  293.3 26.9 %all-to-all-done.3 = bf16[16,64,1664]{2,1,0:T(8,128)(2,1)} async-done(((bf16[16,64,1664]{2,1,0:T(8,128)(2,1)}), bf16[16,64,1664]{2,1,0:T(8,128)(2,1)}, u32[]{:S(2)}, u32[]{:S(2)}) %all-to-all-start.3) | async-done | bytes 3407904 | tf_op jit(solution)/shard_map/all_to_all | solution.py:797
  334.1 5.4 collective-permute-start.5
  350.1 28.6 %all-gather.13.cloned.1.call-done = bf16[1024,1664]{1,0:T(8,128)(2,1)} async-done(((bf16[128,1664]{1,0:T(8,128)(2,1)}), bf16[1024,1664]{1,0:T(8,128)(2,1)}) %all-gather.13.cloned.1.call-update) | async-done | bytes 3407888 | tf_op jit(solution)/shard_map/all_gather | solution.py:995
  380.6 5.2 add_convert_fusion
  395.4 6.7 %all-to-all-start.5 = ((bf16[16,224,384]{2,1,0:T(8,128)(2,1)}), bf16[16,224,384]{2,1,0:T(8,128)(2,1)}, u32[]{:S(2)}, u32[]{:S(2)}) async-start(bf16[16,224,384]{2,1,0:T(8,128)(2,1)} %copy-done.27), calls=%async_computation.7 | async-start | bytes 5505024 | tf_op jit(solution)/shard_map/all_to_all | solution.py:797
  406.3 9.9 %collective-permute-done.7 = bf16[1152,512]{1,0:T(8,128)(2,1)} collective-permute-done((bf16[1152,512]{1,0:T(8,128)(2,1)}, bf16[1152,512]{1,0:T(8,128)(2,1)}, u32[]{:S(2)}, u32[]{:S(2)}) %collective-permute-start.7) | collective-permute-done | bytes 1179680 | tf_op jit(solution)/shard_map/ppermute | solution.py:660
  420.3 23.6 %scan_backward.1 = (bf16[1024,1152]{1,0:T(8,128)(2,1)}, f32[8,640]{1,0:T(8,128)S(1)}, f32[8,128]{1,0:T(8,128)S(1)}, f32[8,384]{1,0:T(8,128)S(1)}) custom-call(f32[1024,1152]{1,0:T(8,128)} %copy-done.5, f32[1024,1152]{1,0:T(8,128)} %copy-done.5, bf16[1024,384]{1,0:T(8,128)(2,1)S(1)} %copy-done.10, f32[1024,384]{1,0:T(8,128)S(1)} %fusion.12.d_gated_ref, ...), custom_call_target="tpu_custom_call" | custom-call | flops 10737418240 | bytes 20971520 | tf_op jit(solution)/shard_map/scan_backward/pallas_call | solution.py:336
  444.1 8.6 %convolution_convert_fusion.3 = bf16[1024,1536]{1,0:T(8,128)(2,1)} fusion(bf16[1024,1152]{1,0:T(8,128)(2,1)} %get-tuple-element.77, bf16[1536,1152]{1,0:T(8,128)(2,1)} %all-gather.7.cloned.1.call-done.router_ref), kind=kOutput, calls=%fused_computation.14 | convolution fusion | flops 3625451520 | bytes 9043968 | tf_op jit(solution)/shard_map/dot_general | solution.py:23
  456.3 11.6 %collective-permute-start.9 = (bf16[576,512]{1,0:T(8,128)(2,1)}, bf16[576,512]{1,0:T(8,128)(2,1)S(1)}, u32[]{:S(2)}, u32[]{:S(2)}) collective-permute-start(bf16[576,512]{1,0:T(8,128)(2,1)} %dynamic-slice_bitcast_fusion.4), channel_id=1, source_target_pairs={{0,96},{16,112},{32,64},{48,80},{64,32},{80,48},{96,0},{112,16},{1... | collective-permute-start | bytes 1769480 | tf_op jit(solution)/shard_map/ppermute | solution.py:660
  472.0 7.2 %fusion.1 = bf16[1536,1152]{1,0:T(8,128)(2,1)S(1)} fusion(bf16[1024,1536]{1,0:T(8,128)(2,1)} %copy-done.23, bf16[1024,1152]{1,0:T(8,128)(2,1)} %get-tuple-element.77, f32[1536,11]{1,0:T(8,128)} %reshape_reshape.3), kind=kOutput, calls=%fused_computation.4 | convolution fusion | flops 3627417600 | bytes 9111552 | tf_op jit(solution)/shard_map/dot_general | solution.py:29
  484.5 6.8 %all-to-all-start.6 = ((bf16[16,96,1152]{2,1,0:T(8,128)(2,1)}), bf16[16,96,1152]{2,1,0:T(8,128)(2,1)}, u32[]{:S(2)}, u32[]{:S(2)}) async-start(bf16[16,96,1152]{2,1,0:T(8,128)(2,1)} %bitcast.215), calls=%async_computation.9 | async-start | bytes 7077888 | tf_op jit(solution)/shard_map/all_to_all | solution.py:797
  492.7 7.8 %collective-permute-done.10 = bf16[576,512]{1,0:T(8,128)(2,1)S(1)} collective-permute-done((bf16[576,512]{1,0:T(8,128)(2,1)S(1)}, bf16[576,512]{1,0:T(8,128)(2,1)S(1)}, u32[]{:S(2)}, u32[]{:S(2)}) %collective-permute-start.10) | collective-permute-done | bytes 589856 | tf_op jit(solution)/shard_map/ppermute | solution.py:665
  510.6 17.1 %collective-permute-start.8 = (bf16[128,384]{1,0:T(8,128)(2,1)S(1)}, bf16[128,384]{1,0:T(8,128)(2,1)S(1)}, u32[]{:S(2)}, u32[]{:S(2)}) collective-permute-start(bf16[128,384]{1,0:T(8,128)(2,1)S(1)} %slice.335), channel_id=1, source_target_pairs={{0,0},{1,16},{2,32},{3,48},{4,64},{5,80},{6,96},{7,112},{8,1},{9,1... | collective-permute-start | bytes 294920 | tf_op jit(solution)/shard_map/ppermute | solution.py:1081
  527.8 8.4 %collective-permute-done.8 = bf16[128,384]{1,0:T(8,128)(2,1)S(1)} collective-permute-done((bf16[128,384]{1,0:T(8,128)(2,1)S(1)}, bf16[128,384]{1,0:T(8,128)(2,1)S(1)}, u32[]{:S(2)}, u32[]{:S(2)}) %collective-permute-start.8) | collective-permute-done | bytes 98336 | tf_op jit(solution)/shard_map/ppermute | solution.py:1081
  565.8 14.0 %unpack_expert_grads.1 = (f32[2,1536,512]{2,1,0:T(8,128)}, f32[2,1536,512]{2,1,0:T(8,128)}, f32[2,512,1536]{2,1,0:T(8,128)}) custom-call(s32[1]{0:T(128)} %bitcast.82.core_ref, bf16[4608,512]{1,0:T(8,128)(2,1)} %pad_maximum_fusion.own_ref, bf16[4608,512]{1,0:T(8,128)(2,1)} %collective-permute-done.15.other_ref), custom_call_target="tpu_custom_call" | custom-call | flops 1048576 | bytes 29360128 | tf_op jit(solution)/shard_map/unpack_expert_grads/pallas_call | solution.py:694
  (389 shorter events, 179.4 us)
Async XLA Ops:
  7.2 101.9 %all-gather.7.cloned.1.call-start = ((), (), s32[]{:S(2)}) async-start(), calls=%async_computation.10 | async-start | bytes 3760128 | tf_op jit(solution)/shard_map/all_gather | solution.py:799
  22.5 55.2 %all-to-all-start = ((bf16[16,64,1664]{2,1,0:T(8,128)(2,1)}), bf16[16,64,1664]{2,1,0:T(8,128)(2,1)}, u32[]{:S(2)}, u32[]{:S(2)}) async-start(bf16[16,64,1664]{2,1,0:T(8,128)(2,1)} %bitcast.200), calls=%async_computation | async-start | bytes 6815744 | tf_op jit(solution)/shard_map/all_to_all | solution.py:797
  30.2 131.9 %all-gather.9.cloned.1.call-start = ((), (), s32[]{:S(2)}) async-start(), calls=%async_computation.11 | async-start | bytes 3538944 | tf_op jit(solution)/shard_map/all_gather | solution.py:912
  30.3 12.2 %collective-permute-start.1 = (bf16[128,1536]{1,0:T(8,128)(2,1)S(1)}, bf16[128,1536]{1,0:T(8,128)(2,1)S(1)}, u32[]{:S(2)}, u32[]{:S(2)}) collective-permute-start(bf16[128,1536]{1,0:T(8,128)(2,1)S(1)} %bitcast.197), channel_id=1, source_target_pairs={{0,64},{16,80},{32,96},{48,112},{64,0},{80,16},{96,32},{112,48},{1... | collective-permute-start | bytes 1179656 | tf_op jit(solution)/shard_map/ppermute | solution.py:643
  34.0 18.1 %collective-permute-start = (bf16[128,1536]{1,0:T(8,128)(2,1)S(1)}, bf16[128,1536]{1,0:T(8,128)(2,1)S(1)}, u32[]{:S(2)}, u32[]{:S(2)}) collective-permute-start(bf16[128,1536]{1,0:T(8,128)(2,1)S(1)} %bitcast.198), channel_id=1, source_target_pairs={{0,32},{16,48},{32,64},{48,80},{64,96},{80,112},{96,0},{112,16},{1... | collective-permute-start | bytes 1179656 | tf_op jit(solution)/shard_map/ppermute | solution.py:643
  34.7 17.4 %collective-permute-start.2 = (bf16[128,1536]{1,0:T(8,128)(2,1)S(1)}, bf16[128,1536]{1,0:T(8,128)(2,1)S(1)}, u32[]{:S(2)}, u32[]{:S(2)}) collective-permute-start(bf16[128,1536]{1,0:T(8,128)(2,1)S(1)} %bitcast.199), channel_id=1, source_target_pairs={{0,96},{16,112},{32,0},{48,16},{64,32},{80,48},{96,64},{112,80},{1... | collective-permute-start | bytes 1179656 | tf_op jit(solution)/shard_map/ppermute | solution.py:643
  55.6 56.4 %collective-permute-start.3 = (bf16[4,128,1536]{2,1,0:T(8,128)(2,1)}, bf16[4,128,1536]{2,1,0:T(8,128)(2,1)}, u32[]{:S(2)}, u32[]{:S(2)}) collective-permute-start(bf16[4,128,1536]{2,1,0:T(8,128)(2,1)} %get-tuple-element.203), channel_id=1, source_target_pairs={{0,16},{16,0},{32,48},{48,32},{64,80},{80,64},{96,112},{112,96},{1... | collective-permute-start | bytes 4718600 | tf_op jit(solution)/shard_map/ppermute | solution.py:645
  56.6 64.0 %collective-permute-start.4 = (bf16[32,1536]{1,0:T(8,128)(2,1)S(1)}, bf16[32,1536]{1,0:T(8,128)(2,1)}, u32[]{:S(2)}, u32[]{:S(2)}) collective-permute-start(bf16[32,1536]{1,0:T(8,128)(2,1)S(1)} %pad_maximum_fusion.6), channel_id=1, source_target_pairs={{0,0},{16,1},{32,2},{48,3},{64,4},{80,5},{96,6},{112,7},{1,8},{17,... | collective-permute-start | bytes 294920 | tf_op jit(solution)/shard_map/ppermute | solution.py:822
  123.2 36.5 %all-to-all-start.1 = ((bf16[16,48,1536]{2,1,0:T(8,128)(2,1)}), bf16[16,48,1536]{2,1,0:T(8,128)(2,1)}, u32[]{:S(2)}, u32[]{:S(2)}) async-start(bf16[16,48,1536]{2,1,0:T(8,128)(2,1)} %broadcast_in_dim.43), calls=%async_computation.1 | async-start | bytes 4718592 | tf_op jit(solution)/shard_map/all_to_all | solution.py:797
  128.0 72.4 %reduce-scatter.4.cloned.1.call-start = ((), (), s32[]{:S(2)}) async-start(), calls=%async_computation.12 | async-start | bytes 3538944 | tf_op jit(solution)/shard_map/reduce_scatter | solution.py:915
  167.1 82.5 %all-gather.11.cloned.1.call-start = ((), (), s32[]{:S(2)}) async-start(), calls=%async_computation.13 | async-start | bytes 3538944 | tf_op jit(solution)/shard_map/all_gather | solution.py:927
  189.7 136.9 %copy-start.48 = (f32[128]{0:T(128)}, f32[128]{0:T(128)S(1)}, u32[]{:S(2)}) copy-start(f32[128]{0:T(128)S(1)} %fusion.44) | copy-start | bytes 1540
  207.4 42.1 %all-to-all-start.2 = ((bf16[16,64,1536]{2,1,0:T(8,128)(2,1)}), bf16[16,64,1536]{2,1,0:T(8,128)(2,1)}, u32[]{:S(2)}, u32[]{:S(2)}) async-start(bf16[16,64,1536]{2,1,0:T(8,128)(2,1)} %bitcast.209), calls=%async_computation.3 | async-start | bytes 6291456 | tf_op jit(solution)/shard_map/all_to_all | solution.py:797
  213.7 110.2 %reduce-scatter.6.cloned.1.call-start = ((), (), s32[]{:S(2)}) async-start(), calls=%async_computation.14 | async-start | bytes 7077888 | tf_op jit(solution)/shard_map/reduce_scatter | solution.py:957
  268.8 51.4 %all-to-all-start.3 = ((bf16[16,64,1664]{2,1,0:T(8,128)(2,1)}), bf16[16,64,1664]{2,1,0:T(8,128)(2,1)}, u32[]{:S(2)}, u32[]{:S(2)}) async-start(bf16[16,64,1664]{2,1,0:T(8,128)(2,1)} %bitcast.216), calls=%async_computation.5 | async-start | bytes 6815744 | tf_op jit(solution)/shard_map/all_to_all | solution.py:797
  278.6 100.1 %all-gather.13.cloned.1.call-start = ((), (), s32[]{:S(2)}) async-start(), calls=%async_computation.15 | async-start | bytes 3833856 | tf_op jit(solution)/shard_map/all_gather | solution.py:995
  334.1 46.5 %collective-permute-start.5 = (bf16[4608,512]{1,0:T(8,128)(2,1)}, bf16[4608,512]{1,0:T(8,128)(2,1)}, u32[]{:S(2)}, u32[]{:S(2)}) collective-permute-start(bf16[4608,512]{1,0:T(8,128)(2,1)} %dynamic-slice_bitcast_fusion), channel_id=1, source_target_pairs={{0,16},{16,0},{32,48},{48,32},{64,80},{80,64},{96,112},{112,96},{1... | collective-permute-start | bytes 14155784 | tf_op jit(solution)/shard_map/ppermute | solution.py:660
  344.3 51.2 %all-to-all-start.4 = ((bf16[16,64,1536]{2,1,0:T(8,128)(2,1)}), bf16[16,64,1536]{2,1,0:T(8,128)(2,1)}, u32[]{:S(2)}, u32[]{:S(2)}) async-start(bf16[16,64,1536]{2,1,0:T(8,128)(2,1)} %bitcast.217), calls=%async_computation.6 | async-start | bytes 6291456 | tf_op jit(solution)/shard_map/all_to_all | solution.py:797
  387.3 28.8 %collective-permute-start.7 = (bf16[1152,512]{1,0:T(8,128)(2,1)}, bf16[1152,512]{1,0:T(8,128)(2,1)}, u32[]{:S(2)}, u32[]{:S(2)}) collective-permute-start(bf16[1152,512]{1,0:T(8,128)(2,1)} %dynamic-slice_bitcast_fusion.1), channel_id=1, source_target_pairs={{0,96},{16,112},{32,64},{48,80},{64,32},{80,48},{96,0},{112,16},{1... | collective-permute-start | bytes 3538952 | tf_op jit(solution)/shard_map/ppermute | solution.py:660
  388.4 30.3 %collective-permute-start.6 = (bf16[1152,512]{1,0:T(8,128)(2,1)S(1)}, bf16[1152,512]{1,0:T(8,128)(2,1)}, u32[]{:S(2)}, u32[]{:S(2)}) collective-permute-start(bf16[1152,512]{1,0:T(8,128)(2,1)S(1)} %dynamic-slice_bitcast_fusion.2), channel_id=1, source_target_pairs={{0,32},{16,48},{32,0},{48,16},{64,96},{80,112},{96,64},{112,80},{1... | collective-permute-start | bytes 3538952 | tf_op jit(solution)/shard_map/ppermute | solution.py:660
  395.4 48.6 %all-to-all-start.5 = ((bf16[16,224,384]{2,1,0:T(8,128)(2,1)}), bf16[16,224,384]{2,1,0:T(8,128)(2,1)}, u32[]{:S(2)}, u32[]{:S(2)}) async-start(bf16[16,224,384]{2,1,0:T(8,128)(2,1)} %copy-done.27), calls=%async_computation.7 | async-start | bytes 5505024 | tf_op jit(solution)/shard_map/all_to_all | solution.py:797
  402.2 145.4 %reduce-scatter.8.cloned.1.call-start = ((), (), s32[]{:S(2)}) async-start(), calls=%async_computation.16 | async-start | bytes 3538944 | tf_op jit(solution)/shard_map/reduce_scatter | solution.py:1046
  418.6 72.7 %collective-permute-start.12 = (bf16[576,512]{1,0:T(8,128)(2,1)}, bf16[576,512]{1,0:T(8,128)(2,1)}, u32[]{:S(2)}, u32[]{:S(2)}) collective-permute-start(bf16[576,512]{1,0:T(8,128)(2,1)} %dynamic-slice_bitcast_fusion.3), channel_id=1, source_target_pairs={{0,32},{16,48},{32,0},{48,16},{64,96},{80,112},{96,64},{112,80},{1... | collective-permute-start | bytes 1769480 | tf_op jit(solution)/shard_map/ppermute | solution.py:660
  456.3 24.2 %collective-permute-start.9 = (bf16[576,512]{1,0:T(8,128)(2,1)}, bf16[576,512]{1,0:T(8,128)(2,1)S(1)}, u32[]{:S(2)}, u32[]{:S(2)}) collective-permute-start(bf16[576,512]{1,0:T(8,128)(2,1)} %dynamic-slice_bitcast_fusion.4), channel_id=1, source_target_pairs={{0,96},{16,112},{32,64},{48,80},{64,32},{80,48},{96,0},{112,16},{1... | collective-permute-start | bytes 1769480 | tf_op jit(solution)/shard_map/ppermute | solution.py:660
  482.5 18.0 %collective-permute-start.10 = (bf16[576,512]{1,0:T(8,128)(2,1)S(1)}, bf16[576,512]{1,0:T(8,128)(2,1)S(1)}, u32[]{:S(2)}, u32[]{:S(2)}) collective-permute-start(bf16[576,512]{1,0:T(8,128)(2,1)S(1)} %add_convert_fusion.2), channel_id=1, source_target_pairs={{0,96},{16,112},{32,64},{48,80},{64,32},{80,48},{96,0},{112,16},{1... | collective-permute-start | bytes 1769480 | tf_op jit(solution)/shard_map/ppermute | solution.py:665
  484.5 60.5 %all-to-all-start.6 = ((bf16[16,96,1152]{2,1,0:T(8,128)(2,1)}), bf16[16,96,1152]{2,1,0:T(8,128)(2,1)}, u32[]{:S(2)}, u32[]{:S(2)}) async-start(bf16[16,96,1152]{2,1,0:T(8,128)(2,1)} %bitcast.215), calls=%async_computation.9 | async-start | bytes 7077888 | tf_op jit(solution)/shard_map/all_to_all | solution.py:797
  491.3 91.0 %all-gather.15.cloned.1.call-start = ((), (), s32[]{:S(2)}) async-start(), calls=%async_computation.17 | async-start | bytes 3538944 | tf_op jit(solution)/shard_map/all_gather | solution.py:1092
  492.6 12.1 %collective-permute-start.13 = (bf16[576,512]{1,0:T(8,128)(2,1)S(1)}, bf16[576,512]{1,0:T(8,128)(2,1)}, u32[]{:S(2)}, u32[]{:S(2)}) collective-permute-start(bf16[576,512]{1,0:T(8,128)(2,1)S(1)} %add_convert_fusion.1), channel_id=1, source_target_pairs={{0,32},{16,48},{32,0},{48,16},{64,96},{80,112},{96,64},{112,80},{1... | collective-permute-start | bytes 1769480 | tf_op jit(solution)/shard_map/ppermute | solution.py:665
  501.7 34.4 %collective-permute-start.11 = (bf16[1152,512]{1,0:T(8,128)(2,1)}, bf16[1152,512]{1,0:T(8,128)(2,1)}, u32[]{:S(2)}, u32[]{:S(2)}) collective-permute-start(bf16[1152,512]{1,0:T(8,128)(2,1)} %pad_maximum_fusion.3), channel_id=1, source_target_pairs={{0,32},{16,48},{32,0},{48,16},{64,96},{80,112},{96,64},{112,80},{1... | collective-permute-start | bytes 3538952 | tf_op jit(solution)/shard_map/ppermute | solution.py:665
  507.2 32.9 %collective-permute-start.14 = (bf16[1152,512]{1,0:T(8,128)(2,1)}, bf16[1152,512]{1,0:T(8,128)(2,1)}, u32[]{:S(2)}, u32[]{:S(2)}) collective-permute-start(bf16[1152,512]{1,0:T(8,128)(2,1)} %pad_maximum_fusion.4), channel_id=1, source_target_pairs={{0,96},{16,112},{32,64},{48,80},{64,32},{80,48},{96,0},{112,16},{1... | collective-permute-start | bytes 3538952 | tf_op jit(solution)/shard_map/ppermute | solution.py:665
  510.6 25.5 %collective-permute-start.8 = (bf16[128,384]{1,0:T(8,128)(2,1)S(1)}, bf16[128,384]{1,0:T(8,128)(2,1)S(1)}, u32[]{:S(2)}, u32[]{:S(2)}) collective-permute-start(bf16[128,384]{1,0:T(8,128)(2,1)S(1)} %slice.335), channel_id=1, source_target_pairs={{0,0},{1,16},{2,32},{3,48},{4,64},{5,80},{6,96},{7,112},{8,1},{9,1... | collective-permute-start | bytes 294920 | tf_op jit(solution)/shard_map/ppermute | solution.py:1081
  554.3 11.5 %collective-permute-start.15 = (bf16[4608,512]{1,0:T(8,128)(2,1)}, bf16[4608,512]{1,0:T(8,128)(2,1)}, u32[]{:S(2)}, u32[]{:S(2)}) collective-permute-start(bf16[4608,512]{1,0:T(8,128)(2,1)} %pad_maximum_fusion.own_ref), channel_id=1, source_target_pairs={{0,16},{16,0},{32,48},{48,32},{64,80},{80,64},{96,112},{112,96},{1... | collective-permute-start | bytes 14155784 | tf_op jit(solution)/shard_map/ppermute | solution.py:1090
  (61 other events, 544.0 us)
Sparse Core Ops, SparseCore 0:
  17.6 91.5 all-gather.6
  112.1 27.8 all-gather.8
  167.2 33.1 reduce-scatter.3
  203.9 29.9 all-gather.10
  268.9 53.9 reduce-scatter.5
  329.3 49.3 all-gather.12
  452.9 54.1 reduce-scatter.7
  550.4 31.7 all-gather.14

commit v6 on v5

--- a/solution.py
+++ b/solution.py
@@ -139,7 +139,7 @@
 
 
 def scan_forward_kernel(
-    proj_ref, prev_ref, taps_ref, head_ref, skip_ref,
+    proj_ref, prev_ref, taps_ref, head_ref, skip_ref, earlier_ref,
     mixed_ref, q_ref, square_ref, start_ref, state_ref, pad_ref,
 ):
     f32, bf = jnp.float32, jnp.bfloat16
@@ -177,24 +177,26 @@
 
 
 def scan_backward_kernel(
-    proj_ref, prev_ref, mixed_ref, d_gated_ref, rows_ref, start_ref, taps_ref, head_ref, skip_ref,
-    earlier_0, earlier_1, earlier_2, d_proj_ref, d_taps_ref, d_head_ref, d_skip_ref,
+    chunks, proj_ref, prev_ref, mixed_ref, d_gated_ref, rows_ref, start_ref, taps_ref, head_ref,
+    skip_ref, held_ref, carry_in_ref, sums_in_ref, earlier_0, earlier_1,
+    d_proj_ref, carry_ref, sums_ref,
     state_ref, pad_ref, late_ref,
 ):
     f32, bf = jnp.float32, jnp.bfloat16
     step = pl.program_id(0)
-    last = pl.num_programs(0) - 1
+    chunk = chunks[1] - 1 - step
+    d_taps_ref = sums_ref.at[0:8, :]
+    d_head_ref = sums_ref.at[8:16, 0:128]
+    d_skip_ref = sums_ref.at[16:24, 0:WIDE]
 
     @pl.when(step == 0)
     def _():
-        state_ref[...] = jnp.zeros(state_ref.shape, f32)
-        late_ref[CHUNK : CHUNK + 8, :] = jnp.zeros((8, CONVW), f32)
-        d_taps_ref[...] = jnp.zeros(d_taps_ref.shape, f32)
-        d_head_ref[...] = jnp.zeros(d_head_ref.shape, f32)
-        d_skip_ref[...] = jnp.zeros(d_skip_ref.shape, f32)
+        state_ref[...] = carry_in_ref[0:128, 0:WIDE]
+        late_ref[CHUNK : CHUNK + 8, :] = carry_in_ref[128:136, :]
+        sums_ref[...] = sums_in_ref[...]
 
     parts = chunk_parts(
-        proj_ref[...], prev_ref[...], step < last, taps_ref, head_ref, pad_ref
+        proj_ref[...], prev_ref[...], chunk > 0, taps_ref, head_ref, pad_ref
     )
     u, key, query, xs = parts["u"], parts["key"], parts["query"], parts["xs"]
     e_w, w_w, dt_w = parts["e_w"], parts["w_w"], parts["dt_w"]
@@ -275,6 +277,8 @@
         )
     d_taps_ref[4:5, :] += jnp.sum(d_conv, axis=0, keepdims=True)
     late_ref[CHUNK : CHUNK + 8, :] = d_conv[0:8, :]
+    carry_ref[0:128, 0:WIDE] = state_ref[...]
+    carry_ref[128:136, :] = d_conv[0:8, :]
     scale = rows_ref[:, 2:3]
     d_proj_ref[:, :WIDE] = (d_gate * scale).astype(bf)
     d_proj_ref[:, WIDE : WIDE + CONVW] = (d_feed * scale).astype(bf)
@@ -291,7 +295,7 @@
     return pl.BlockSpec(shape, lambda step: (0,) * len(shape))
 
 
-def scan_forward(proj, taps, head, skip):
+def scan_forward(proj, taps, head, skip, earlier):
     rows, width = proj.shape
     chunks = rows // CHUNK
     by_chunk = lambda step: (step, 0)
@@ -304,6 +308,7 @@
             whole(taps.shape),
             whole(head.shape),
             whole(skip.shape),
+            corner_of(earlier),
         ],
         out_specs=[
             pl.BlockSpec((CHUNK, WIDE), by_chunk),
@@ -326,54 +331,56 @@
             flops=3 << 30, bytes_accessed=12 << 20, transcendentals=4 << 20
         ),
         name="scan_forward",
-    )(proj, proj, taps, head, skip)
-
-
-def scan_backward(proj, mixed, d_gated, row_values, starts, taps, head, skip, earlier):
-    rows, width = proj.shape
-    chunks = rows // CHUNK
-    by_chunk = lambda step: (chunks - 1 - step, 0)
+    )(proj, proj, taps, head, skip, earlier)
+
+
+def scan_backward(chunks, inputs, held, carry, sums, earlier):
+    proj, mixed, d_gated, row_values, starts, taps, head, skip = inputs
+    width = proj.shape[1]
+    at = lambda step: chunks[1] - 1 - step
+    by_chunk = lambda step: (at(step), 0)
     return pl.pallas_call(
-        scan_backward_kernel,
-        grid=(chunks,),
+        functools.partial(scan_backward_kernel, chunks),
+        grid=(chunks[1] - chunks[0],),
         in_specs=[
             pl.BlockSpec((CHUNK, width), by_chunk),
             pl.BlockSpec(
-                (8, width),
-                lambda step: (jnp.maximum((chunks - 1 - step) * (CHUNK // 8) - 1, 0), 0),
+                (8, width), lambda step: (jnp.maximum(at(step) * (CHUNK // 8) - 1, 0), 0)
             ),
             pl.BlockSpec((CHUNK, WIDE), by_chunk),
             pl.BlockSpec((CHUNK, WIDE), by_chunk),
             pl.BlockSpec((CHUNK, row_values.shape[1]), by_chunk),
-            pl.BlockSpec((1, 128, WIDE), lambda step: (chunks - 1 - step, 0, 0)),
+            pl.BlockSpec((1, 128, WIDE), lambda step: (at(step), 0, 0)),
             whole(taps.shape),
             whole(head.shape),
             whole(skip.shape),
+            pl.BlockSpec(memory_space=pl.ANY),
+            whole(carry.shape),
+            whole(sums.shape),
             *map(corner_of, earlier),
         ],
         out_specs=[
             pl.BlockSpec((CHUNK, width), by_chunk),
-            whole((8, CONVW)),
-            whole((8, 128)),
-            whole((8, WIDE)),
+            whole(carry.shape),
+            whole(sums.shape),
         ],
         out_shape=[
-            jax.ShapeDtypeStruct((rows, width), jnp.bfloat16),
-            jax.ShapeDtypeStruct((8, CONVW), jnp.float32),
-            jax.ShapeDtypeStruct((8, 128), jnp.float32),
-            jax.ShapeDtypeStruct((8, WIDE), jnp.float32),
+            jax.ShapeDtypeStruct(held.shape, held.dtype),
+            jax.ShapeDtypeStruct(carry.shape, jnp.float32),
+            jax.ShapeDtypeStruct(sums.shape, jnp.float32),
         ],
         scratch_shapes=[
             pltpu.VMEM((128, WIDE), jnp.float32),
             pltpu.VMEM((CHUNK + 8, CONVW), jnp.float32),
             pltpu.VMEM((CHUNK + 8, CONVW), jnp.float32),
         ],
+        input_output_aliases={9: 0},
         compiler_params=pltpu.CompilerParams(vmem_limit_bytes=48 << 20),
         cost_estimate=pl.CostEstimate(
             flops=10 << 30, bytes_accessed=20 << 20, transcendentals=8 << 20
         ),
         name="scan_backward",
-    )(proj, proj, mixed, d_gated, row_values, starts, taps, head, skip, *earlier)
+    )(proj, proj, mixed, d_gated, row_values, starts, taps, head, skip, held, carry, sums, *earlier)
 
 
 def expert_early_kernel(cot_ref, down_ref, raw_ref):
@@ -833,6 +840,18 @@
         [shared_cols[fold * band : fold * band + fold] for band in range(bands)], axis=1
     )
     piece = jnp.concatenate([piece, shared_rows], axis=0)
+    piece = after(piece, w_all)
+    rows_all = to_shards(jnp.broadcast_to(piece[None], (sh,) + piece.shape))
+    own_rows = own_out + own_down
+    w_out = rows_all[:, :own_out].reshape(gw, dim)
+    w_down = rows_all[:, own_out:own_rows].reshape(gf, dim)
+    w_shared = (
+        rows_all[:, own_rows:]
+        .reshape(sh, fold, bands, 2 * gf)
+        .transpose(0, 2, 1, 3)
+        .reshape(dim, 2 * gf)
+    )
+
     route_ids = routes[0]
     expert_ids = jnp.arange(experts, dtype=jnp.int32)
     named = jnp.any(route_ids[:, :, None] == expert_ids[None, None, :], axis=1).astype(f32)
@@ -852,27 +871,17 @@
 
     local_slots = (sh, local_e, CAP)
 
-    def dispatched(values):
-        sent = times(dispatch_flat, values).astype(bf)
-        return to_shards(sent.reshape(sh, local_e * CAP, -1)).reshape(*local_slots, -1)
+    def in_slots(values):
+        return times(dispatch_flat, values).astype(bf).reshape(sh, local_e * CAP, -1)
+
+    def dispatched(sent):
+        return to_shards(sent).reshape(*local_slots, -1)
 
     router_lane = at_router - (total - 128)
     lanes = jnp.arange(128, dtype=jnp.int32)
     named_lanes = jnp.pad(named, ((0, 0), (router_lane, 128 - router_lane - experts)))
-    cot_rows = dispatched(jnp.concatenate([cot_low, named_lanes.astype(bf)], axis=1))
-
-    w_all, cot_rows = lax.optimization_barrier((w_all, cot_rows))
-    piece = after(piece, cot_rows)
-    rows_all = to_shards(jnp.broadcast_to(piece[None], (sh,) + piece.shape))
-    own_rows = own_out + own_down
-    w_out = rows_all[:, :own_out].reshape(gw, dim)
-    w_down = rows_all[:, own_out:own_rows].reshape(gf, dim)
-    w_shared = (
-        rows_all[:, own_rows:]
-        .reshape(sh, fold, bands, 2 * gf)
-        .transpose(0, 2, 1, 3)
-        .reshape(dim, 2 * gf)
-    )
+    cot_sent = in_slots(jnp.concatenate([cot_low, named_lanes.astype(bf)], axis=1))
+    cot_rows = dispatched(cot_sent)
 
     x_wide = x_all.astype(f32)
     x_r = row_scale(x_wide)
@@ -907,7 +916,9 @@
     decay_rate = -jnp.exp(decay_local)
     head_in = jnp.pad(jnp.stack([bias_local, decay_rate]), ((0, 6), (0, 128 - gh)))
     skip_in = jnp.broadcast_to(jnp.repeat(skip_local, per_head)[None], (8, gw))
-    mixed, q_low, square_part, starts = scan_forward(proj, taps_in, head_in, skip_in)
+    mixed, q_low, square_part, starts = scan_forward(
+        proj, taps_in, head_in, skip_in, cot_sent
+    )
 
     cot_all = lax.all_gather(after(cot_low, w_all), "seq", axis=0, tiled=True)
     w_out, cot_all = lax.optimization_barrier((w_out, cot_all))
@@ -916,7 +927,7 @@
     square = lax.psum(square_part.reshape(sq, toks), "seq")
     q_r = lax.rsqrt(square / inner + epsilon).reshape(seq_rows, 1)
     d_raw = expert_early(cot_rows, expert_down)
-    tok_r = after(lax.dynamic_slice_in_dim(q_r, q * toks, toks, 0), d_raw)
+    tok_r = after(lax.dynamic_slice_in_dim(q_r, q * toks, toks, 0), cot_rows)
     x_tok = x_low.astype(f32)
     added = out_sum.astype(f32) * tok_r
     resid = x_tok + added
@@ -934,7 +945,7 @@
     gates = (powers / jnp.sum(powers, axis=1, keepdims=True))[
         :, router_lane : router_lane + experts
     ]
-    rows = dispatched(moe_in)
+    rows = dispatched(in_slots(moe_in))
     own_ids = lax.axis_index("shard") * local_e + jnp.arange(local_e, dtype=jnp.int32)
     marks = jnp.stack(
         [own_ids + router_lane, own_ids, own_ids + 64] + [jnp.full_like(own_ids, -1)] * 5, axis=1
@@ -966,9 +977,18 @@
     far = [(i, 2 * (sq // 2 - 1 - i // 2) + i % 2) for i in range(sq)]
     is_inner = ((z_at == 1) | (z_at == 2)).astype(jnp.int32)
     is_high = (z_at >= 2).astype(jnp.int32)
-    e_mine = halve(e_grads.reshape(-1, e_grads.shape[2]), core, mates)
+    e_mine = jnp.concatenate(
+        [
+            halve(e_grads[:, dim * part : dim * part + dim].reshape(local_e * dim, -1), core, mates)
+            for part in range(3)
+        ],
+        axis=0,
+    )
     cutoff = e_mine.shape[0] // 2
 
+    grad_down_part = transposed_times(s_act, cot_all).astype(bf)
+    grad_shared_part = transposed_times(moe_all, d_both).astype(bf)
+    gates = after(after(gates, grad_down_part), grad_shared_part)
     d_flat = transposed_times(dispatch_flat, d_returned.reshape(slots, dim + 128))
     d_gates = d_flat[:, dim : dim + experts] + d_flat[:, dim + 64 : dim + 64 + experts]
     d_logits = gates * (d_gates - jnp.sum(gates * d_gates, axis=1, keepdims=True))
@@ -987,6 +1007,8 @@
     )
     d_o = d_resid.astype(bf)
     kappa = jnp.sum(d_o.astype(f32) * added, axis=1) / inner
+    for start in range(0, e_mine.shape[0], dim):
+        kappa = after(kappa, e_mine[start:])
     kappa_high = kappa.astype(bf)
     kappa_low = (kappa - kappa_high.astype(f32)).astype(bf)
     d_o_ext = jnp.concatenate(
@@ -997,15 +1019,13 @@
 
     d_gated = times_transposed(d_o_all, jnp.pad(w_out, ((0, 0), (0, 128))))
     grad_out_part = transposed_times(q_low, (q_r * d_o_all[:, :dim].astype(f32)).astype(bf))
-    grad_down_part = transposed_times(s_act, cot_all)
-    grad_shared_part = transposed_times(moe_all, d_both)
 
     mid_part = jnp.concatenate(
         [
             grad_shared_part,
-            grad_router,
-            grad_moe[:, None],
-            jnp.zeros((dim, 128 - experts - 1), f32),
+            grad_router.astype(bf),
+            grad_moe[:, None].astype(bf),
+            jnp.zeros((dim, 128 - experts - 1), bf),
         ],
         axis=1,
     )
@@ -1020,8 +1040,8 @@
     early_part = jnp.concatenate(
         [
             to_bands(grad_out_part.astype(bf).reshape(sh, own_out, dim)),
-            to_bands(grad_down_part.astype(bf).reshape(sh, own_down, dim)),
-            mid_part.astype(bf).reshape(sh, rows_w, lane_w),
+            to_bands(grad_down_part.reshape(sh, own_down, dim)),
+            mid_part.reshape(sh, rows_w, lane_w),
         ],
         axis=1,
     )
@@ -1033,14 +1053,27 @@
     row_values = jnp.concatenate(
         [q_r, kappa_all, x_r, jnp.zeros((seq_rows, 5), f32)], axis=1
     )
-    d_proj, d_taps, d_head, d_skip = scan_backward(
-        proj, mixed, d_gated, row_values, starts, taps_in, head_in, skip_in, (returned, e_one, e_two)
-    )
+    scan_inputs = (proj, mixed, d_gated, row_values, starts, taps_in, head_in, skip_in)
+    chunks = seq_rows // CHUNK
+    middle = chunks // 2
+    d_proj, carry, sums = scan_backward(
+        (middle, chunks),
+        scan_inputs,
+        jnp.zeros((seq_rows, total), bf),
+        jnp.zeros((136, gw + keys_w), f32),
+        jnp.zeros((24, gw + keys_w), f32),
+        (returned, early_part),
+    )
+    d_proj, carry, sums = scan_backward(
+        (0, middle), scan_inputs, d_proj, carry, sums, (e_one, e_two)
+    )
+    d_taps, d_head, d_skip = sums[0:8], sums[8:16, :128], sums[16:24, :gw]
     grad_conv_local = d_taps[:taps]
     grad_offset_local = d_taps[taps]
     grad_bias_local = d_head[0, :gh]
     grad_decay_local = d_head[1, :gh] * decay_rate
     grad_skip_local = jnp.sum(d_skip[0].reshape(gh, per_head), axis=1)
+    e_one, e_two = halve(e_one, is_high, far), halve(e_two, is_inner, near)
     d_proj, moved_early = lax.optimization_barrier((d_proj, moved_early))
     back_part = times_transposed(d_proj, w_all).astype(bf)
     back_sum = lax.psum_scatter(back_part, "seq", scatter_dimension=0, tiled=True).astype(f32)
@@ -1079,7 +1112,6 @@
     last_part = last_part.astype(bf)
     early_sum = jnp.sum(moved_early.astype(f32), axis=0).astype(bf)
     rows_sum = lax.ppermute(early_sum[: bands * own_rows], both_axes, backward_pairs)
-    e_one, e_two = halve(e_one, is_high, far), halve(e_two, is_inner, near)
     e_one, e_two = after(e_one, last_part), after(e_two, last_part)
     e_one, e_two = double(e_one, is_high, far), double(e_two, is_inner, near)
     e_one, e_two = double(e_one, is_inner, near), double(e_two, is_high, far)

time: 607 us -> 566 us (0.932)
  waiting for transfers between devices: 201 us -> 145 us
  local copies, waits for them, and re-layouts: 66 us -> 83.6 us
  starting transfers between devices: 101 us -> 83.6 us
  other arithmetic: 51.3 us -> 59.3 us
    all_to_all x7, waiting for transfers between devices: 82.1 us -> 58 us  [to_shards(): lax.all_to_all(values, 'shard', split_axis=0, concat_axis=0, tiled=True)]
    all_gather x1, waiting for transfers between devices: 31.5 us -> 20.7 us  [on_device(): w_all = lax.all_gather(packed, 'shard', axis=0, tiled=True)]
    ppermute x5 -> x7, waiting for transfers between devices: 9.87 us -> 0.02 us  [halve(): other = lax.ppermute(sent, 'seq', pairs)]
    ppermute x5 -> x7, starting transfers between devices: 18.3 us -> 8.51 us  [halve(): other = lax.ppermute(sent, 'seq', pairs)]
    reduce_scatter x1, waiting for transfers between devices: 9.44 us -> 0.02 us  [on_device(): out_sum = lax.psum_scatter(out_part, 'seq', scatter_dimension=0, tiled=True)]
    concatenate x1, other arithmetic: 3.84 us -> 10.7 us  [on_device(): e_mine = jnp.concatenate([e_one, e_two], axis=0)]
    ppermute x1, starting transfers between devices: 17.1 us -> 10.9 us  [on_device(): lax.ppermute(early_sum[:bands * own_rows], both_axes, backward_pairs)]
    unnamed x146 -> x152, local copies, waits for them, and re-layouts: 18.4 us -> 22.9 us
  transfers between devices with their start and end apart: 31 -> 33, of which waited for: 15 -> 11; matrix products, arithmetic and copies ran while one was open for 21% -> 27% of each run, Pallas kernels for 11% -> 12%
where the time goes in v6:
time: 566 us; the launch traced here: 555 us
  waiting for transfers between devices  145 us (26%)
  Pallas kernels  90.9 us (16%)
  local copies, waits for them, and re-layouts  83.6 us (15%)
  starting transfers between devices  83.6 us (15%)
  other arithmetic  59.3 us (10%)
  matrix products  52.3 us (9%)
  between operations  24.6 us (4%)
  blocking collectives  15.2 us (3%)
    all_to_all x7, waiting for transfers between devices, to_shards(): lax.all_to_all(values, 'shard', split_axis=0, concat_axis=0, tiled=True)  58 us
    all_to_all x7, starting transfers between devices, to_shards(): lax.all_to_all(values, 'shard', split_axis=0, concat_axis=0, tiled=True)  48.1 us
    pallas_call x2, Pallas kernels, scan_backward(): pl.pallas_call(functools.partial(scan_backward_kernel, chunks), grid=(chu...  25.5 us
    all_gather x1, waiting for transfers between devices, on_device(): d_o_all = lax.all_gather(d_o_ext, 'seq', axis=0, tiled=True)  24.8 us
    unnamed x152, local copies, waits for them, and re-layouts  22.9 us
    all_gather x1, waiting for transfers between devices, on_device(): w_all = lax.all_gather(packed, 'shard', axis=0, tiled=True)  20.7 us
    pallas_call x1, Pallas kernels, expert_main(): pl.pallas_call(expert_main_kernel, grid=(local,), in_specs=[expert_slots(...  19.2 us
    dot_general x5, matrix products, times(): return jnp.dot(left, right, preferred_element_type=jnp.float32)  18.7 us
  transfers between devices with their start and end apart: 33, of which 11 were waited for; matrix products, arithmetic and copies ran while one was open for 27% of the time, Pallas kernels for 12%

profile of v6, /device:TPU:1, one launch (start us, length us, event | category | flops | bytes accessed | tf_op | source)
XLA Modules:
  0.0 554.8 jit_solution(17481812546667631830)
XLA Ops:
  17.5 4.5 collective-permute-start.1
  26.4 4.6 collective-permute-start.4
  31.9 11.0 %collective-permute-done = bf16[128,1536]{1,0:T(8,128)(2,1)S(1)} collective-permute-done((bf16[128,1536]{1,0:T(8,128)(2,1)}, bf16[128,1536]{1,0:T(8,128)(2,1)S(1)}, u32[]{:S(2)}, u32[]{:S(2)}) %collective-permute-start) | collective-permute-done | bytes 393248 | tf_op jit(solution)/shard_map/ppermute | solution.py:650
  49.8 20.7 %all-gather.7.cloned.1.call-done.router_ref = bf16[1536,1152]{1,0:T(8,128)(2,1)} async-done(((bf16[96,1152]{1,0:T(8,128)(2,1)}), bf16[1536,1152]{1,0:T(8,128)(2,1)}) %all-gather.7.cloned.1.call-update) | async-done | bytes 3538960 | tf_op jit(solution)/shard_map/all_gather | solution.py:806
  81.4 4.7 all-to-all-start
  90.3 6.2 %convolution_multiply_fusion.proj_ref.prev_ref = f32[1024,1152]{1,0:T(8,128)S(1)} fusion(bf16[1024,1536]{1,0:T(8,128)(2,1)} %copy-done.26, bf16[1536,1152]{1,0:T(8,128)(2,1)S(1)} %copy-done.46, f32[1024]{0:T(1024)S(1)} %add_rsqrt_fusion.1), kind=kOutput, calls=%fused_computation.6 | convolution fusion | flops 3625058304 | bytes 11407360 | tf_op jit(solution)/shard_map/dot_general | solution.py:19
  96.6 11.6 %scan_forward.1 = (bf16[1024,384]{1,0:T(8,128)(2,1)S(1)}, bf16[1024,384]{1,0:T(8,128)(2,1)S(1)}, f32[1024,1]{1,0:T(8,128)S(1)}, f32[8,128,384]{2,1,0:T(8,128)S(1)}) custom-call(f32[1024,1152]{1,0:T(8,128)S(1)} %convolution_multiply_fusion.proj_ref.prev_ref, f32[1024,1152]{1,0:T(8,128)S(1)} %convolution_multiply_fusion.proj_ref.prev_ref, ...), custom_call_target="tpu_custom_call" | custom-call | flops 3221225472 | bytes 12582912 | tf_op jit(solution)/shard_map/scan_forward/pallas_call | solution.py:302
  111.3 6.7 %all-to-all-done = bf16[16,48,1536]{2,1,0:T(8,128)(2,1)} async-done(((bf16[16,48,1536]{2,1,0:T(8,128)(2,1)}), bf16[16,48,1536]{2,1,0:T(8,128)(2,1)}, u32[]{:S(2)}, u32[]{:S(2)}) %all-to-all-start) | async-done | bytes 2359328 | tf_op jit(solution)/shard_map/all_to_all | solution.py:804
  120.3 4.7 convolution_convert_fusion.1
  125.1 4.5 all-to-all-start.1
  129.8 15.2 %psum.7 = f32[8,128]{1,0:T(8,128)S(1)} all-reduce(f32[8,128]{1,0:T(8,128)S(1)} %bitcast.250), channel_id=1, replica_groups=mesh['seq'=8,'shard'=16] {'seq'}, use_global_device_ids=true, to_apply=%region_3.4 | all-reduce | flops 1024 | bytes 8192 | tf_op jit(solution)/shard_map/psum | solution.py:927
  146.4 21.6 %all-to-all-done.1 = bf16[16,64,1664]{2,1,0:T(8,128)(2,1)} async-done(((bf16[16,64,1664]{2,1,0:T(8,128)(2,1)}), bf16[16,64,1664]{2,1,0:T(8,128)(2,1)}, u32[]{:S(2)}, u32[]{:S(2)}) %all-to-all-start.1) | async-done | bytes 3407904 | tf_op jit(solution)/shard_map/all_to_all | solution.py:804
  176.9 7.9 %all-to-all-start.2 = ((bf16[16,64,1536]{2,1,0:T(8,128)(2,1)}), bf16[16,64,1536]{2,1,0:T(8,128)(2,1)}, u32[]{:S(2)}, u32[]{:S(2)}) async-start(bf16[16,64,1536]{2,1,0:T(8,128)(2,1)} %bitcast.217), calls=%async_computation.3 | async-start | bytes 6291456 | tf_op jit(solution)/shard_map/all_to_all | solution.py:804
  192.8 4.9 expert_early.1.raw_ref
  197.7 23.2 %all-to-all-done.2 = bf16[16,64,1536]{2,1,0:T(8,128)(2,1)} async-done(((bf16[16,64,1536]{2,1,0:T(8,128)(2,1)}), bf16[16,64,1536]{2,1,0:T(8,128)(2,1)}, u32[]{:S(2)}, u32[]{:S(2)}) %all-to-all-start.2) | async-done | bytes 3145760 | tf_op jit(solution)/shard_map/all_to_all | solution.py:804
  220.9 19.2 %expert_main.1 = (bf16[16,2,32,1664]{3,2,1,0:T(8,128)(2,1)}, bf16[2,512,512]{2,1,0:T(8,128)(2,1)}, bf16[2,512,512]{2,1,0:T(8,128)(2,1)}, bf16[2,512,512]{2,1,0:T...) custom-call(bf16[16,2,32,1536]{3,2,1,0:T(8,128)(2,1)} %bitcast.32.ro, ...), custom_call_target="tpu_custom_call" | custom-call | flops 8589934592 | bytes 20971520 | tf_op jit(solution)/shard_map/expert_main/pallas_call | solution.py:501
  240.9 10.5 %all-to-all-start.3 = ((bf16[16,64,1664]{2,1,0:T(8,128)(2,1)}), bf16[16,64,1664]{2,1,0:T(8,128)(2,1)}, u32[]{:S(2)}, u32[]{:S(2)}) async-start(bf16[16,64,1664]{2,1,0:T(8,128)(2,1)} %bitcast.224), calls=%async_computation.5 | async-start | bytes 6815744 | tf_op jit(solution)/shard_map/all_to_all | solution.py:804
  251.4 12.6 %expert_late.1 = (bf16[16,2,32,1536]{3,2,1,0:T(8,128)(2,1)}, bf16[2,4608,512]{2,1,0:T(8,128)(2,1)}) custom-call(bf16[16,2,32,1536]{3,2,1,0:T(8,128)(2,1)} %bitcast.32.rows_ref, bf16[16,2,32,1664]{3,2,1,0:T(8,128)(2,1)} %bitcast.28.cot_ref.routed_ref, bf16[2,512,512]{2,1,0:T(8,128)(2,1)} %get-tuple-element.63.act_ref, ...), custom_call_target="tpu_custom_call" | custom-call | flops 7516192768 | bytes 25165824 | tf_op jit(solution)/shard_map/expert_late/pallas_call | solution.py:535
  284.6 6.5 %all-to-all-done.3 = bf16[16,64,1664]{2,1,0:T(8,128)(2,1)} async-done(((bf16[16,64,1664]{2,1,0:T(8,128)(2,1)}), bf16[16,64,1664]{2,1,0:T(8,128)(2,1)}, u32[]{:S(2)}, u32[]{:S(2)}) %all-to-all-start.3) | async-done | bytes 3407904 | tf_op jit(solution)/shard_map/all_to_all | solution.py:804
  302.1 6.7 %all-to-all-start.4 = ((bf16[16,64,1536]{2,1,0:T(8,128)(2,1)}), bf16[16,64,1536]{2,1,0:T(8,128)(2,1)}, u32[]{:S(2)}, u32[]{:S(2)}) async-start(bf16[16,64,1536]{2,1,0:T(8,128)(2,1)} %bitcast.225), calls=%async_computation.6 | async-start | bytes 6291456 | tf_op jit(solution)/shard_map/all_to_all | solution.py:804
  311.6 24.8 %all-gather.13.cloned.1.call-done = bf16[1024,1664]{1,0:T(8,128)(2,1)} async-done(((bf16[128,1664]{1,0:T(8,128)(2,1)}), bf16[1024,1664]{1,0:T(8,128)(2,1)}) %all-gather.13.cloned.1.call-update) | async-done | bytes 3407888 | tf_op jit(solution)/shard_map/all_gather | solution.py:1017
  363.4 6.6 %all-to-all-start.5 = ((bf16[16,224,384]{2,1,0:T(8,128)(2,1)}), bf16[16,224,384]{2,1,0:T(8,128)(2,1)}, u32[]{:S(2)}, u32[]{:S(2)}) async-start(bf16[16,224,384]{2,1,0:T(8,128)(2,1)} %maximum_dynamic-update-slice_fusion.earlier_1), calls=%async_computation.7 | async-start | bytes 5505024 | tf_op jit(solution)/shard_map/all_to_all | solution.py:804
  372.5 12.8 %scan_backward.2 = (bf16[1024,1152]{1,0:T(8,128)(2,1)}, f32[136,640]{1,0:T(8,128)S(1)}, f32[24,640]{1,0:T(8,128)S(1)}) custom-call(f32[1024,1152]{1,0:T(8,128)} %copy-done.2, f32[1024,1152]{1,0:T(8,128)} %copy-done.2, bf16[1024,384]{1,0:T(8,128)(2,1)S(1)} %copy-done.8, f32[1024,384]{1,0:T(8,128)S(1)} %copy-done.11, ...), custom_call_target="tpu_custom_call", output_to_operand_aliasing={{0}: (9, {})} | custom-call | flops 10737418240 | bytes 20971520 | tf_op jit(solution)/shard_map/scan_backward/pallas_call | solution.py:342
  388.9 12.7 %scan_backward.3 = (bf16[1024,1152]{1,0:T(8,128)(2,1)}, f32[136,640]{1,0:T(8,128)}, f32[24,640]{1,0:T(8,128)S(1)}) custom-call(f32[1024,1152]{1,0:T(8,128)} %copy-done.2, f32[1024,1152]{1,0:T(8,128)} %copy-done.2, bf16[1024,384]{1,0:T(8,128)(2,1)S(1)} %copy-done.8, f32[1024,384]{1,0:T(8,128)S(1)} %copy-done.11, ...), custom_call_target="tpu_custom_call", output_to_operand_aliasing={{0}: (9, {})} | custom-call | flops 10737418240 | bytes 20971520 | tf_op jit(solution)/shard_map/scan_backward/pallas_call | solution.py:342
  406.7 8.6 %convolution_convert_fusion.3 = bf16[1024,1536]{1,0:T(8,128)(2,1)} fusion(bf16[1024,1152]{1,0:T(8,128)(2,1)} %get-tuple-element.77, bf16[1536,1152]{1,0:T(8,128)(2,1)} %all-gather.7.cloned.1.call-done.router_ref), kind=kOutput, calls=%fused_computation.11 | convolution fusion | flops 3625451520 | bytes 9043968 | tf_op jit(solution)/shard_map/dot_general | solution.py:23
  422.8 7.1 %fusion = bf16[1536,1152]{1,0:T(8,128)(2,1)S(1)} fusion(bf16[1024,1536]{1,0:T(8,128)(2,1)} %copy-done.26, bf16[1024,1152]{1,0:T(8,128)(2,1)} %get-tuple-element.77, f32[1536,11]{1,0:T(8,128)} %reshape_reshape.3), kind=kOutput, calls=%fused_computation.2 | convolution fusion | flops 3627417600 | bytes 9111552 | tf_op jit(solution)/shard_map/dot_general | solution.py:29
  434.3 7.1 %all-to-all-start.6 = ((bf16[16,96,1152]{2,1,0:T(8,128)(2,1)}), bf16[16,96,1152]{2,1,0:T(8,128)(2,1)}, u32[]{:S(2)}, u32[]{:S(2)}) async-start(bf16[16,96,1152]{2,1,0:T(8,128)(2,1)} %bitcast.223), calls=%async_computation.9 | async-start | bytes 7077888 | tf_op jit(solution)/shard_map/all_to_all | solution.py:804
  442.8 11.5 %collective-permute-done.12 = bf16[576,512]{1,0:T(8,128)(2,1)S(1)} collective-permute-done((bf16[576,512]{1,0:T(8,128)(2,1)S(1)}, bf16[576,512]{1,0:T(8,128)(2,1)S(1)}, u32[]{:S(2)}, u32[]{:S(2)}) %collective-permute-start.12) | collective-permute-done | bytes 589856 | tf_op jit(solution)/shard_map/ppermute | solution.py:672
  464.2 10.9 %collective-permute-start.10 = (bf16[128,384]{1,0:T(8,128)(2,1)S(1)}, bf16[128,384]{1,0:T(8,128)(2,1)S(1)}, u32[]{:S(2)}, u32[]{:S(2)}) collective-permute-start(bf16[128,384]{1,0:T(8,128)(2,1)S(1)} %slice.399), channel_id=1, source_target_pairs={{0,0},{1,16},{2,32},{3,48},{4,64},{5,80},{6,96},{7,112},{8,1},{9,1... | collective-permute-start | bytes 294920 | tf_op jit(solution)/shard_map/ppermute | solution.py:1114
  475.1 13.4 %collective-permute-done.10 = bf16[128,384]{1,0:T(8,128)(2,1)S(1)} collective-permute-done((bf16[128,384]{1,0:T(8,128)(2,1)S(1)}, bf16[128,384]{1,0:T(8,128)(2,1)S(1)}, u32[]{:S(2)}, u32[]{:S(2)}) %collective-permute-start.10) | collective-permute-done | bytes 98336 | tf_op jit(solution)/shard_map/ppermute | solution.py:1114
  504.8 10.7 %pad_maximum_fusion.own_ref = bf16[4608,512]{1,0:T(8,128)(2,1)} fusion(bf16[1152,512]{1,0:T(8,128)(2,1)} %get-tuple-element.205, bf16[1152,512]{1,0:T(8,128)(2,1)} %copy-done.25, bf16[1152,512]{1,0:T(8,128)(2,1)S(1)} %copy-done.22, bf16[1152,512]{1,0:T(8,128)(2,1)S(1)} %copy-done.24), kind=kLoop, calls=%fused_computation.7 | loop fusion | flops 18874368 | bytes 9437184 | tf_op jit(solution)/shard_map/concatenate | solution.py:1121
  523.7 14.1 %unpack_expert_grads.1 = (f32[2,1536,512]{2,1,0:T(8,128)}, f32[2,1536,512]{2,1,0:T(8,128)}, f32[2,512,1536]{2,1,0:T(8,128)}) custom-call(s32[1]{0:T(128)} %bitcast.90.core_ref, bf16[4608,512]{1,0:T(8,128)(2,1)} %pad_maximum_fusion.own_ref, bf16[4608,512]{1,0:T(8,128)(2,1)} %collective-permute-done.17.other_ref), custom_call_target="tpu_custom_call" | custom-call | flops 1048576 | bytes 29360128 | tf_op jit(solution)/shard_map/unpack_expert_grads/pallas_call | solution.py:701
  (413 shorter events, 182.3 us)
Async XLA Ops:
  7.2 63.2 %all-gather.7.cloned.1.call-start = ((), (), s32[]{:S(2)}) async-start(), calls=%async_computation.10 | async-start | bytes 3760128 | tf_op jit(solution)/shard_map/all_gather | solution.py:806
  17.5 102.8 %all-gather.9.cloned.1.call-start = ((), (), s32[]{:S(2)}) async-start(), calls=%async_computation.11 | async-start | bytes 3538944 | tf_op jit(solution)/shard_map/all_gather | solution.py:923
  17.5 14.4 %collective-permute-start.1 = (bf16[128,1536]{1,0:T(8,128)(2,1)}, bf16[128,1536]{1,0:T(8,128)(2,1)S(1)}, u32[]{:S(2)}, u32[]{:S(2)}) collective-permute-start(bf16[128,1536]{1,0:T(8,128)(2,1)} %bitcast.206), channel_id=1, source_target_pairs={{0,64},{16,80},{32,96},{48,112},{64,0},{80,16},{96,32},{112,48},{1... | collective-permute-start | bytes 1179656 | tf_op jit(solution)/shard_map/ppermute | solution.py:650
  22.0 20.8 %collective-permute-start = (bf16[128,1536]{1,0:T(8,128)(2,1)}, bf16[128,1536]{1,0:T(8,128)(2,1)S(1)}, u32[]{:S(2)}, u32[]{:S(2)}) collective-permute-start(bf16[128,1536]{1,0:T(8,128)(2,1)} %bitcast.207), channel_id=1, source_target_pairs={{0,32},{16,48},{32,64},{48,80},{64,96},{80,112},{96,0},{112,16},{1... | collective-permute-start | bytes 1179656 | tf_op jit(solution)/shard_map/ppermute | solution.py:650
  22.8 20.1 %collective-permute-start.2 = (bf16[128,1536]{1,0:T(8,128)(2,1)}, bf16[128,1536]{1,0:T(8,128)(2,1)S(1)}, u32[]{:S(2)}, u32[]{:S(2)}) collective-permute-start(bf16[128,1536]{1,0:T(8,128)(2,1)} %bitcast.208), channel_id=1, source_target_pairs={{0,96},{16,112},{32,0},{48,16},{64,32},{80,48},{96,64},{112,80},{1... | collective-permute-start | bytes 1179656 | tf_op jit(solution)/shard_map/ppermute | solution.py:650
  26.4 53.3 %collective-permute-start.4 = (bf16[32,1536]{1,0:T(8,128)(2,1)S(1)}, bf16[32,1536]{1,0:T(8,128)(2,1)S(1)}, u32[]{:S(2)}, u32[]{:S(2)}) collective-permute-start(bf16[32,1536]{1,0:T(8,128)(2,1)S(1)} %pad_maximum_fusion.6), channel_id=1, source_target_pairs={{0,0},{16,1},{32,2},{48,3},{64,4},{80,5},{96,6},{112,7},{1,8},{17,... | collective-permute-start | bytes 294920 | tf_op jit(solution)/shard_map/ppermute | solution.py:829
  46.0 27.1 %collective-permute-start.3 = (bf16[4,128,1536]{2,1,0:T(8,128)(2,1)}, bf16[4,128,1536]{2,1,0:T(8,128)(2,1)}, u32[]{:S(2)}, u32[]{:S(2)}) collective-permute-start(bf16[4,128,1536]{2,1,0:T(8,128)(2,1)} %get-tuple-element.208), channel_id=1, source_target_pairs={{0,16},{16,0},{32,48},{48,32},{64,80},{80,64},{96,112},{112,96},{1... | collective-permute-start | bytes 4718600 | tf_op jit(solution)/shard_map/ppermute | solution.py:652
  81.4 36.5 %all-to-all-start = ((bf16[16,48,1536]{2,1,0:T(8,128)(2,1)}), bf16[16,48,1536]{2,1,0:T(8,128)(2,1)}, u32[]{:S(2)}, u32[]{:S(2)}) async-start(bf16[16,48,1536]{2,1,0:T(8,128)(2,1)} %broadcast_in_dim.49), calls=%async_computation | async-start | bytes 4718592 | tf_op jit(solution)/shard_map/all_to_all | solution.py:804
  86.2 83.7 %reduce-scatter.4.cloned.1.call-start = ((), (), s32[]{:S(2)}) async-start(), calls=%async_computation.12 | async-start | bytes 3538944 | tf_op jit(solution)/shard_map/reduce_scatter | solution.py:926
  125.1 42.9 %all-to-all-start.1 = ((bf16[16,64,1664]{2,1,0:T(8,128)(2,1)}), bf16[16,64,1664]{2,1,0:T(8,128)(2,1)}, u32[]{:S(2)}, u32[]{:S(2)}) async-start(bf16[16,64,1664]{2,1,0:T(8,128)(2,1)} %bitcast.24.earlier_ref), calls=%async_computation.2 | async-start | bytes 6815744 | tf_op jit(solution)/shard_map/all_to_all | solution.py:804
  129.6 91.3 %all-gather.11.cloned.1.call-start = ((), (), s32[]{:S(2)}) async-start(), calls=%async_computation.13 | async-start | bytes 3538944 | tf_op jit(solution)/shard_map/all_gather | solution.py:938
  176.9 44.0 %all-to-all-start.2 = ((bf16[16,64,1536]{2,1,0:T(8,128)(2,1)}), bf16[16,64,1536]{2,1,0:T(8,128)(2,1)}, u32[]{:S(2)}, u32[]{:S(2)}) async-start(bf16[16,64,1536]{2,1,0:T(8,128)(2,1)} %bitcast.217), calls=%async_computation.3 | async-start | bytes 6291456 | tf_op jit(solution)/shard_map/all_to_all | solution.py:804
  184.8 110.6 %reduce-scatter.6.cloned.1.call-start = ((), (), s32[]{:S(2)}) async-start(), calls=%async_computation.14 | async-start | bytes 7077888 | tf_op jit(solution)/shard_map/reduce_scatter | solution.py:968
  240.9 50.2 %all-to-all-start.3 = ((bf16[16,64,1664]{2,1,0:T(8,128)(2,1)}), bf16[16,64,1664]{2,1,0:T(8,128)(2,1)}, u32[]{:S(2)}, u32[]{:S(2)}) async-start(bf16[16,64,1664]{2,1,0:T(8,128)(2,1)} %bitcast.224), calls=%async_computation.5 | async-start | bytes 6815744 | tf_op jit(solution)/shard_map/all_to_all | solution.py:804
  251.4 85.0 %all-gather.13.cloned.1.call-start = ((), (), s32[]{:S(2)}) async-start(), calls=%async_computation.15 | async-start | bytes 3833856 | tf_op jit(solution)/shard_map/all_gather | solution.py:1017
  268.5 10.3 %collective-permute-start.6 = (bf16[1536,512]{1,0:T(8,128)(2,1)S(1)}, bf16[1536,512]{1,0:T(8,128)(2,1)S(1)}, u32[]{:S(2)}, u32[]{:S(2)}) collective-permute-start(bf16[1536,512]{1,0:T(8,128)(2,1)S(1)} %dynamic-slice_bitcast_fusion.1), channel_id=1, source_target_pairs={{0,16},{16,0},{32,48},{48,32},{64,80},{80,64},{96,112},{112,96},{1... | collective-permute-start | bytes 4718600 | tf_op jit(solution)/shard_map/ppermute | solution.py:667
  274.0 8.3 %collective-permute-start.5 = (bf16[1536,512]{1,0:T(8,128)(2,1)S(1)}, bf16[1536,512]{1,0:T(8,128)(2,1)S(1)}, u32[]{:S(2)}, u32[]{:S(2)}) collective-permute-start(bf16[1536,512]{1,0:T(8,128)(2,1)S(1)} %dynamic-slice_bitcast_fusion.2), channel_id=1, source_target_pairs={{0,16},{16,0},{32,48},{48,32},{64,80},{80,64},{96,112},{112,96},{1... | collective-permute-start | bytes 4718600 | tf_op jit(solution)/shard_map/ppermute | solution.py:667
  302.1 61.3 %all-to-all-start.4 = ((bf16[16,64,1536]{2,1,0:T(8,128)(2,1)}), bf16[16,64,1536]{2,1,0:T(8,128)(2,1)}, u32[]{:S(2)}, u32[]{:S(2)}) async-start(bf16[16,64,1536]{2,1,0:T(8,128)(2,1)} %bitcast.225), calls=%async_computation.6 | async-start | bytes 6291456 | tf_op jit(solution)/shard_map/all_to_all | solution.py:804
  347.6 37.7 %collective-permute-start.9 = (bf16[1152,512]{1,0:T(8,128)(2,1)}, bf16[1152,512]{1,0:T(8,128)(2,1)}, u32[]{:S(2)}, u32[]{:S(2)}) collective-permute-start(bf16[1152,512]{1,0:T(8,128)(2,1)} %dynamic-slice_bitcast_fusion.3), channel_id=1, source_target_pairs={{0,96},{16,112},{32,64},{48,80},{64,32},{80,48},{96,0},{112,16},{1... | collective-permute-start | bytes 3538952 | tf_op jit(solution)/shard_map/ppermute | solution.py:667
  349.7 37.4 %collective-permute-start.8 = (bf16[1152,512]{1,0:T(8,128)(2,1)}, bf16[1152,512]{1,0:T(8,128)(2,1)}, u32[]{:S(2)}, u32[]{:S(2)}) collective-permute-start(bf16[1152,512]{1,0:T(8,128)(2,1)} %dynamic-slice_bitcast_fusion.4), channel_id=1, source_target_pairs={{0,32},{16,48},{32,0},{48,16},{64,96},{80,112},{96,64},{112,80},{1... | collective-permute-start | bytes 3538952 | tf_op jit(solution)/shard_map/ppermute | solution.py:667
  363.4 43.3 %all-to-all-start.5 = ((bf16[16,224,384]{2,1,0:T(8,128)(2,1)}), bf16[16,224,384]{2,1,0:T(8,128)(2,1)}, u32[]{:S(2)}, u32[]{:S(2)}) async-start(bf16[16,224,384]{2,1,0:T(8,128)(2,1)} %maximum_dynamic-update-slice_fusion.earlier_1), calls=%async_computation.7 | async-start | bytes 5505024 | tf_op jit(solution)/shard_map/all_to_all | solution.py:804
  370.0 130.8 %reduce-scatter.8.cloned.1.call-start = ((), (), s32[]{:S(2)}) async-start(), calls=%async_computation.16 | async-start | bytes 3538944 | tf_op jit(solution)/shard_map/reduce_scatter | solution.py:1079
  402.5 39.0 %collective-permute-start.14 = (bf16[576,512]{1,0:T(8,128)(2,1)}, bf16[576,512]{1,0:T(8,128)(2,1)}, u32[]{:S(2)}, u32[]{:S(2)}) collective-permute-start(bf16[576,512]{1,0:T(8,128)(2,1)} %dynamic-slice_bitcast_fusion.5), channel_id=1, source_target_pairs={{0,32},{16,48},{32,0},{48,16},{64,96},{80,112},{96,64},{112,80},{1... | collective-permute-start | bytes 1769480 | tf_op jit(solution)/shard_map/ppermute | solution.py:667
  404.8 26.3 %collective-permute-start.11 = (bf16[576,512]{1,0:T(8,128)(2,1)}, bf16[576,512]{1,0:T(8,128)(2,1)S(1)}, u32[]{:S(2)}, u32[]{:S(2)}) collective-permute-start(bf16[576,512]{1,0:T(8,128)(2,1)} %dynamic-slice_bitcast_fusion.6), channel_id=1, source_target_pairs={{0,96},{16,112},{32,64},{48,80},{64,32},{80,48},{96,0},{112,16},{1... | collective-permute-start | bytes 1769480 | tf_op jit(solution)/shard_map/ppermute | solution.py:667
  433.2 21.2 %collective-permute-start.12 = (bf16[576,512]{1,0:T(8,128)(2,1)S(1)}, bf16[576,512]{1,0:T(8,128)(2,1)S(1)}, u32[]{:S(2)}, u32[]{:S(2)}) collective-permute-start(bf16[576,512]{1,0:T(8,128)(2,1)S(1)} %add_convert_fusion.2), channel_id=1, source_target_pairs={{0,96},{16,112},{32,64},{48,80},{64,32},{80,48},{96,0},{112,16},{1... | collective-permute-start | bytes 1769480 | tf_op jit(solution)/shard_map/ppermute | solution.py:672
  434.3 63.8 %all-to-all-start.6 = ((bf16[16,96,1152]{2,1,0:T(8,128)(2,1)}), bf16[16,96,1152]{2,1,0:T(8,128)(2,1)}, u32[]{:S(2)}, u32[]{:S(2)}) async-start(bf16[16,96,1152]{2,1,0:T(8,128)(2,1)} %bitcast.223), calls=%async_computation.9 | async-start | bytes 7077888 | tf_op jit(solution)/shard_map/all_to_all | solution.py:804
  441.4 96.4 %all-gather.15.cloned.1.call-start = ((), (), s32[]{:S(2)}) async-start(), calls=%async_computation.17 | async-start | bytes 3538944 | tf_op jit(solution)/shard_map/all_gather | solution.py:1124
  442.7 15.9 %collective-permute-start.15 = (bf16[576,512]{1,0:T(8,128)(2,1)S(1)}, bf16[576,512]{1,0:T(8,128)(2,1)}, u32[]{:S(2)}, u32[]{:S(2)}) collective-permute-start(bf16[576,512]{1,0:T(8,128)(2,1)S(1)} %add_convert_fusion.1), channel_id=1, source_target_pairs={{0,32},{16,48},{32,0},{48,16},{64,96},{80,112},{96,64},{112,80},{1... | collective-permute-start | bytes 1769480 | tf_op jit(solution)/shard_map/ppermute | solution.py:672
  455.5 33.8 %collective-permute-start.13 = (bf16[1152,512]{1,0:T(8,128)(2,1)}, bf16[1152,512]{1,0:T(8,128)(2,1)}, u32[]{:S(2)}, u32[]{:S(2)}) collective-permute-start(bf16[1152,512]{1,0:T(8,128)(2,1)} %pad_maximum_fusion.3), channel_id=1, source_target_pairs={{0,32},{16,48},{32,0},{48,16},{64,96},{80,112},{96,64},{112,80},{1... | collective-permute-start | bytes 3538952 | tf_op jit(solution)/shard_map/ppermute | solution.py:672
  461.1 32.2 %collective-permute-start.16 = (bf16[1152,512]{1,0:T(8,128)(2,1)}, bf16[1152,512]{1,0:T(8,128)(2,1)}, u32[]{:S(2)}, u32[]{:S(2)}) collective-permute-start(bf16[1152,512]{1,0:T(8,128)(2,1)} %pad_maximum_fusion.4), channel_id=1, source_target_pairs={{0,96},{16,112},{32,64},{48,80},{64,32},{80,48},{96,0},{112,16},{1... | collective-permute-start | bytes 3538952 | tf_op jit(solution)/shard_map/ppermute | solution.py:672
  464.2 24.4 %collective-permute-start.10 = (bf16[128,384]{1,0:T(8,128)(2,1)S(1)}, bf16[128,384]{1,0:T(8,128)(2,1)S(1)}, u32[]{:S(2)}, u32[]{:S(2)}) collective-permute-start(bf16[128,384]{1,0:T(8,128)(2,1)S(1)} %slice.399), channel_id=1, source_target_pairs={{0,0},{1,16},{2,32},{3,48},{4,64},{5,80},{6,96},{7,112},{8,1},{9,1... | collective-permute-start | bytes 294920 | tf_op jit(solution)/shard_map/ppermute | solution.py:1114
  515.5 8.3 %collective-permute-start.17 = (bf16[4608,512]{1,0:T(8,128)(2,1)}, bf16[4608,512]{1,0:T(8,128)(2,1)}, u32[]{:S(2)}, u32[]{:S(2)}) collective-permute-start(bf16[4608,512]{1,0:T(8,128)(2,1)} %pad_maximum_fusion.own_ref), channel_id=1, source_target_pairs={{0,16},{16,0},{32,48},{48,32},{64,80},{80,64},{96,112},{112,96},{1... | collective-permute-start | bytes 14155784 | tf_op jit(solution)/shard_map/ppermute | solution.py:1122
  (66 other events, 825.4 us)
Sparse Core Ops, SparseCore 0:
  17.6 52.8 all-gather.6
  73.3 27.8 all-gather.8
  125.2 33.9 reduce-scatter.3
  173.4 34.8 all-gather.10
  240.2 48.3 reduce-scatter.5
  302.0 34.3 all-gather.12
  415.5 43.0 reduce-scatter.7
  504.8 29.8 all-gather.14

commit v7 on v6

--- a/solution.py
+++ b/solution.py
@@ -139,7 +139,7 @@
 
 
 def scan_forward_kernel(
-    proj_ref, prev_ref, taps_ref, head_ref, skip_ref, earlier_ref,
+    proj_ref, prev_ref, taps_ref, head_ref, skip_ref,
     mixed_ref, q_ref, square_ref, start_ref, state_ref, pad_ref,
 ):
     f32, bf = jnp.float32, jnp.bfloat16
@@ -177,12 +177,11 @@
 
 
 def scan_backward_kernel(
-    chunks, proj_ref, prev_ref, mixed_ref, d_gated_ref, rows_ref, start_ref, taps_ref, head_ref,
-    skip_ref, held_ref, carry_in_ref, sums_in_ref, earlier_0, earlier_1,
-    d_proj_ref, carry_ref, sums_ref,
-    state_ref, pad_ref, late_ref,
+    chunks, held_count, proj_ref, prev_ref, mixed_ref, d_gated_ref, rows_ref, start_ref, taps_ref,
+    head_ref, skip_ref, w_ref, carry_in_ref, sums_in_ref, *refs,
 ):
     f32, bf = jnp.float32, jnp.bfloat16
+    d_proj_ref, back_ref, carry_ref, sums_ref, state_ref, pad_ref, late_ref = refs[held_count:]
     step = pl.program_id(0)
     chunk = chunks[1] - 1 - step
     d_taps_ref = sums_ref.at[0:8, :]
@@ -280,14 +279,16 @@
     carry_ref[0:128, 0:WIDE] = state_ref[...]
     carry_ref[128:136, :] = d_conv[0:8, :]
     scale = rows_ref[:, 2:3]
-    d_proj_ref[:, :WIDE] = (d_gate * scale).astype(bf)
-    d_proj_ref[:, WIDE : WIDE + CONVW] = (d_feed * scale).astype(bf)
-    d_proj_ref[:, WIDE + CONVW :] = (d_pre * scale).astype(bf)
+    d_proj = jnp.concatenate([d_gate, d_feed, d_pre], axis=1) * scale
+    d_proj = d_proj.astype(bf)
+    d_proj_ref[...] = d_proj
+    back_ref[...] = times_transposed(d_proj, w_ref[...]).astype(bf)
 
 
 def corner_of(array):
     return pl.BlockSpec(
-        (1,) * (array.ndim - 2) + (16, 128), lambda *step: (0,) * array.ndim
+        (1,) * (array.ndim - 2) + (min(16, array.shape[-2]), 128),
+        lambda *step: (0,) * array.ndim,
     )
 
 
@@ -295,7 +296,51 @@
     return pl.BlockSpec(shape, lambda step: (0,) * len(shape))
 
 
-def scan_forward(proj, taps, head, skip, earlier):
+def project_kernel(x_ref, weights_ref, earlier_ref, proj_ref, scale_ref, w_ref):
+    width = weights_ref.shape[2]
+
+    @pl.when(pl.program_id(0) == 0)
+    def _():
+        w_ref[...] = weights_ref[...].reshape(-1, width)
+
+    x = x_ref[...]
+    wide = x.astype(jnp.float32)
+    scale = row_scale(wide)
+    proj_ref[...] = times(x, w_ref[...]) * scale
+    scale_ref[...] = scale
+
+
+def project(x_all, weights, rows_w, earlier):
+    rows, dim = x_all.shape
+    sources, _, width = weights.shape
+    tile = rows // 4
+    return pl.pallas_call(
+        project_kernel,
+        grid=(4,),
+        in_specs=[
+            pl.BlockSpec((tile, dim), lambda step: (step, 0)),
+            pl.BlockSpec((sources, rows_w, width), lambda step: (0, 0, 0)),
+            corner_of(earlier),
+        ],
+        out_specs=[
+            pl.BlockSpec((tile, width), lambda step: (step, 0)),
+            pl.BlockSpec((tile, 1), lambda step: (step, 0)),
+            pl.BlockSpec((dim, width), lambda step: (0, 0)),
+        ],
+        out_shape=[
+            jax.ShapeDtypeStruct((rows, width), jnp.float32),
+            jax.ShapeDtypeStruct((rows, 1), jnp.float32),
+            jax.ShapeDtypeStruct((dim, width), jnp.bfloat16),
+        ],
+        compiler_params=pltpu.CompilerParams(vmem_limit_bytes=40 << 20),
+        cost_estimate=pl.CostEstimate(
+            flops=2 * rows * dim * width, bytes_accessed=16 << 20, transcendentals=0
+        ),
+        name="project",
+    )(x_all, weights, earlier)
+
+
+def scan_forward(proj, taps, head, skip):
     rows, width = proj.shape
     chunks = rows // CHUNK
     by_chunk = lambda step: (step, 0)
@@ -308,7 +353,6 @@
             whole(taps.shape),
             whole(head.shape),
             whole(skip.shape),
-            corner_of(earlier),
         ],
         out_specs=[
             pl.BlockSpec((CHUNK, WIDE), by_chunk),
@@ -331,16 +375,18 @@
             flops=3 << 30, bytes_accessed=12 << 20, transcendentals=4 << 20
         ),
         name="scan_forward",
-    )(proj, proj, taps, head, skip, earlier)
+    )(proj, proj, taps, head, skip)
 
 
 def scan_backward(chunks, inputs, held, carry, sums, earlier):
-    proj, mixed, d_gated, row_values, starts, taps, head, skip = inputs
-    width = proj.shape[1]
+    proj, mixed, d_gated, row_values, starts, taps, head, skip, w_all = inputs
+    rows, width = proj.shape
+    dim = w_all.shape[0]
     at = lambda step: chunks[1] - 1 - step
     by_chunk = lambda step: (at(step), 0)
+    given = (proj, proj, mixed, d_gated, row_values, starts, taps, head, skip, w_all, carry, sums)
     return pl.pallas_call(
-        functools.partial(scan_backward_kernel, chunks),
+        functools.partial(scan_backward_kernel, chunks, len(held) + len(earlier)),
         grid=(chunks[1] - chunks[0],),
         in_specs=[
             pl.BlockSpec((CHUNK, width), by_chunk),
@@ -354,18 +400,21 @@
             whole(taps.shape),
             whole(head.shape),
             whole(skip.shape),
-            pl.BlockSpec(memory_space=pl.ANY),
+            whole(w_all.shape),
             whole(carry.shape),
             whole(sums.shape),
+            *[pl.BlockSpec(memory_space=pl.ANY) for _ in held],
             *map(corner_of, earlier),
         ],
         out_specs=[
             pl.BlockSpec((CHUNK, width), by_chunk),
+            pl.BlockSpec((CHUNK, dim), by_chunk),
             whole(carry.shape),
             whole(sums.shape),
         ],
         out_shape=[
-            jax.ShapeDtypeStruct(held.shape, held.dtype),
+            jax.ShapeDtypeStruct((rows, width), jnp.bfloat16),
+            jax.ShapeDtypeStruct((rows, dim), jnp.bfloat16),
             jax.ShapeDtypeStruct(carry.shape, jnp.float32),
             jax.ShapeDtypeStruct(sums.shape, jnp.float32),
         ],
@@ -374,16 +423,16 @@
             pltpu.VMEM((CHUNK + 8, CONVW), jnp.float32),
             pltpu.VMEM((CHUNK + 8, CONVW), jnp.float32),
         ],
-        input_output_aliases={9: 0},
+        input_output_aliases={len(given) + i: i for i in range(len(held))},
         compiler_params=pltpu.CompilerParams(vmem_limit_bytes=48 << 20),
         cost_estimate=pl.CostEstimate(
             flops=10 << 30, bytes_accessed=20 << 20, transcendentals=8 << 20
         ),
         name="scan_backward",
-    )(proj, proj, mixed, d_gated, row_values, starts, taps, head, skip, held, carry, sums, *earlier)
-
-
-def expert_early_kernel(cot_ref, down_ref, raw_ref):
+    )(*given, *held, *earlier)
+
+
+def expert_early_kernel(cot_ref, down_ref, earlier_ref, raw_ref):
     cot = cot_ref[...].reshape(-1, cot_ref.shape[-1])
     raw_ref[0] = times_transposed(cot, down_ref[0])
 
@@ -475,18 +524,22 @@
     )
 
 
-def expert_early(cot_rows, down):
+def expert_early(cot_rows, down, earlier):
     sources, local, cap, _ = cot_rows.shape
     units, dim = down.shape[1:]
     return pl.pallas_call(
         expert_early_kernel,
         grid=(local,),
-        in_specs=[expert_slots((sources, local, cap, dim)), per_expert(down.shape)],
+        in_specs=[
+            expert_slots((sources, local, cap, dim)),
+            per_expert(down.shape),
+            corner_of(earlier),
+        ],
         out_specs=per_expert((local, sources * cap, units)),
         out_shape=jax.ShapeDtypeStruct((local, sources * cap, units), jnp.float32),
         name="expert_early",
-        **expert_params(2 << 30, 8 << 20),
-    )(cot_rows, down)
+        **expert_params(64 << 30, 256 << 20),
+    )(cot_rows, down, earlier)
 
 
 def expert_main(rows, cot_rows, raw, gate, up, w_all, marks, moe_all, cot_all, w_shared, w_down):
@@ -639,6 +692,21 @@
     )(side, in_weight, in_gain, out_weight, out_gain)
 
 
+def fold_rows(values, width):
+    rest = values[:, width:]
+    count = rest.shape[1] * values.shape[0] // width
+    parts = [rest[at : at + count] for at in range(0, values.shape[0], count)]
+    return jnp.concatenate([values[:, :width], jnp.concatenate(parts, axis=1)], axis=0)
+
+
+def unfold_rows(values, dim):
+    sources, rows, width = values.shape
+    count = rows * width // dim
+    rest = dim - width
+    parts = [values[:, count:, at : at + rest] for at in range(0, width, rest)]
+    return jnp.concatenate([values[:, :count], jnp.concatenate(parts, axis=1)], axis=2)
+
+
 def gather_rows(values, core, z_at, mates):
     cores = 2
     chips = len(mates) // cores
@@ -659,11 +727,13 @@
     return jnp.concatenate(ordered, axis=0)
 
 
-def halve(values, bit, pairs):
+def halve(values, bit, pairs, start=None):
     f32 = jnp.float32
     parts = values.reshape(2, values.shape[0] // 2, values.shape[1])
     sent = lax.dynamic_index_in_dim(parts, 1 - bit, 0, keepdims=False)
     kept = lax.dynamic_index_in_dim(parts, bit, 0, keepdims=False)
+    if start is not None:
+        sent = after(sent, start)
     other = lax.ppermute(sent, "seq", pairs)
     return (kept.astype(f32) + other.astype(f32)).astype(jnp.bfloat16)
 
@@ -803,7 +873,6 @@
     def to_shards(values):
         return lax.all_to_all(values, "shard", split_axis=0, concat_axis=0, tiled=True)
 
-    w_all = lax.all_gather(packed, "shard", axis=0, tiled=True)
     core, z_at = q % 2, q // 2
     mates = [(i, i ^ 1) for i in range(sq)]
     x_all = gather_rows(x_low, core, z_at, mates)
@@ -839,14 +908,25 @@
     shared_rows = jnp.concatenate(
         [shared_cols[fold * band : fold * band + fold] for band in range(bands)], axis=1
     )
-    piece = jnp.concatenate([piece, shared_rows], axis=0)
-    piece = after(piece, w_all)
-    rows_all = to_shards(jnp.broadcast_to(piece[None], (sh,) + piece.shape))
     own_rows = own_out + own_down
-    w_out = rows_all[:, :own_out].reshape(gw, dim)
-    w_down = rows_all[:, own_out:own_rows].reshape(gf, dim)
+    weights = lax.all_gather(
+        jnp.concatenate(
+            [
+                packed,
+                fold_rows(piece[:own_out], total),
+                fold_rows(jnp.concatenate([piece[own_out:], shared_rows], axis=0), total),
+            ],
+            axis=0,
+        ),
+        "shard",
+        axis=0,
+    )
+    folded = rows_w + own_out * dim // total
+    w_out = unfold_rows(weights[:, rows_w:folded], dim).reshape(gw, dim)
+    second = unfold_rows(weights[:, folded:], dim)
+    w_down = second[:, :own_down].reshape(gf, dim)
     w_shared = (
-        rows_all[:, own_rows:]
+        second[:, own_down:]
         .reshape(sh, fold, bands, 2 * gf)
         .transpose(0, 2, 1, 3)
         .reshape(dim, 2 * gf)
@@ -883,11 +963,9 @@
     cot_sent = in_slots(jnp.concatenate([cot_low, named_lanes.astype(bf)], axis=1))
     cot_rows = dispatched(cot_sent)
 
-    x_wide = x_all.astype(f32)
-    x_r = row_scale(x_wide)
-    proj = times(x_all, w_all) * x_r
-
-    small_all = w_all[:, at_small:at_router].reshape(sh, -1)
+    proj, x_r, w_all = project(x_all, weights, rows_w, cot_sent)
+
+    small_all = weights[:, :rows_w, at_small:at_router].reshape(sh, -1)
     at = taps * conv_own
     conv_full = (
         small_all[:, :at].reshape(sh, taps, conv_own).transpose(1, 0, 2).reshape(taps, conv_all)
@@ -897,8 +975,8 @@
     bias_full = small_all[:, at : at + head_own].reshape(heads)
     decay_full = small_all[:, at + head_own : at + 2 * head_own].reshape(heads)
     skip_full = small_all[:, at + 2 * head_own : at + 3 * head_own].reshape(heads)
-    router_full = w_all[:, at_router:at_moe]
-    moe_gain_full = w_all[:, at_moe].astype(f32)
+    router_full = weights[:, :rows_w, at_router:at_moe].reshape(dim, experts)
+    moe_gain_full = weights[:, :rows_w, at_moe].reshape(dim).astype(f32)
 
     def group(values, width):
         return lax.dynamic_slice_in_dim(values, q * width, width, values.ndim - 1)
@@ -916,18 +994,16 @@
     decay_rate = -jnp.exp(decay_local)
     head_in = jnp.pad(jnp.stack([bias_local, decay_rate]), ((0, 6), (0, 128 - gh)))
     skip_in = jnp.broadcast_to(jnp.repeat(skip_local, per_head)[None], (8, gw))
-    mixed, q_low, square_part, starts = scan_forward(
-        proj, taps_in, head_in, skip_in, cot_sent
-    )
+    mixed, q_low, square_part, starts = scan_forward(proj, taps_in, head_in, skip_in)
 
     cot_all = lax.all_gather(after(cot_low, w_all), "seq", axis=0, tiled=True)
     w_out, cot_all = lax.optimization_barrier((w_out, cot_all))
     out_part = times(q_low, w_out).astype(bf)
     out_sum = lax.psum_scatter(out_part, "seq", scatter_dimension=0, tiled=True)
-    square = lax.psum(square_part.reshape(sq, toks), "seq")
+    square = lax.psum(after(square_part.reshape(sq, toks), out_part), "seq")
     q_r = lax.rsqrt(square / inner + epsilon).reshape(seq_rows, 1)
-    d_raw = expert_early(cot_rows, expert_down)
-    tok_r = after(lax.dynamic_slice_in_dim(q_r, q * toks, toks, 0), cot_rows)
+    d_raw = expert_early(cot_rows, expert_down, square)
+    tok_r = after(lax.dynamic_slice_in_dim(q_r, q * toks, toks, 0), d_raw)
     x_tok = x_low.astype(f32)
     added = out_sum.astype(f32) * tok_r
     resid = x_tok + added
@@ -1047,25 +1123,24 @@
     )
     moved_early = to_shards(early_part)
 
-    e_late = after(e_mine, d_o_all)
-    e_one = halve(e_late[:cutoff], is_inner, near)
-    e_two = halve(e_late[cutoff:], is_high, far)
+    e_one = halve(e_mine[:cutoff], is_inner, near, d_o_all)
+    e_two = halve(e_mine[cutoff:], is_high, far, d_o_all)
     row_values = jnp.concatenate(
         [q_r, kappa_all, x_r, jnp.zeros((seq_rows, 5), f32)], axis=1
     )
-    scan_inputs = (proj, mixed, d_gated, row_values, starts, taps_in, head_in, skip_in)
+    scan_inputs = (proj, mixed, d_gated, row_values, starts, taps_in, head_in, skip_in, w_all)
     chunks = seq_rows // CHUNK
     middle = chunks // 2
-    d_proj, carry, sums = scan_backward(
+    *held, carry, sums = scan_backward(
         (middle, chunks),
         scan_inputs,
-        jnp.zeros((seq_rows, total), bf),
+        (),
         jnp.zeros((136, gw + keys_w), f32),
         jnp.zeros((24, gw + keys_w), f32),
-        (returned, early_part),
-    )
-    d_proj, carry, sums = scan_backward(
-        (0, middle), scan_inputs, d_proj, carry, sums, (e_one, e_two)
+        (),
+    )
+    d_proj, back_part, carry, sums = scan_backward(
+        (0, middle), scan_inputs, held, carry, sums, (returned, early_part, e_one, e_two)
     )
     d_taps, d_head, d_skip = sums[0:8], sums[8:16, :128], sums[16:24, :gw]
     grad_conv_local = d_taps[:taps]
@@ -1074,8 +1149,6 @@
     grad_decay_local = d_head[1, :gh] * decay_rate
     grad_skip_local = jnp.sum(d_skip[0].reshape(gh, per_head), axis=1)
     e_one, e_two = halve(e_one, is_high, far), halve(e_two, is_inner, near)
-    d_proj, moved_early = lax.optimization_barrier((d_proj, moved_early))
-    back_part = times_transposed(d_proj, w_all).astype(bf)
     back_sum = lax.psum_scatter(back_part, "seq", scatter_dimension=0, tiled=True).astype(f32)
     weighted = (gates.T[:, None, :] * dispatch.astype(f32)).reshape(slots, toks)
     combined = transposed_times(weighted.astype(bf), returned.reshape(slots, dim))
@@ -1086,7 +1159,8 @@
         d_resid + back_sum - x_n * (tok_x_r * jnp.mean(back_sum * x_tok, axis=1, keepdims=True))
     )[None]
 
-    grad_in_part = transposed_times(x_all, d_proj)
+    grad_in_part = transposed_times(x_all, d_proj).astype(bf)
+    grad_in_part, moved_early = lax.optimization_barrier((grad_in_part, moved_early))
 
     def spread(local, count):
         wide = jnp.zeros(local.shape[:-1] + (count,), f32)

time: 566 us -> 569 us (level)
  waiting for transfers between devices: 145 us -> 170 us
  Pallas kernels: 90.9 us -> 108 us
  matrix products: 52.3 us -> 38.1 us
  starting transfers between devices: 83.6 us -> 71.2 us
  local copies, waits for them, and re-layouts: 83.6 us -> 77.1 us
    all_to_all x7 -> x6, waiting for transfers between devices: 58 us -> 37.5 us  [to_shards(): lax.all_to_all(values, 'shard', split_axis=0, concat_axis=0, tiled=True)]
    pallas_call x2 -> x3, Pallas kernels: 25.5 us -> 43 us  [the longest x2 34.9 us: scan_backward(): pl.pallas_call(functools.partial(scan_backward_kernel, chunks, len(held)...]
    all_gather x1, waiting for transfers between devices: 24.8 us -> 39 us  [on_device(): d_o_all = lax.all_gather(d_o_ext, 'seq', axis=0, tiled=True)]
    reduce_scatter x1, waiting for transfers between devices: 0.02 us -> 12.1 us  [on_device(): out_sum = lax.psum_scatter(out_part, 'seq', scatter_dimension=0, tiled=True)]
    dot_general x2 -> x1, matrix products: 11.7 us -> 1.91 us  [times_transposed(): lax.dot_general(left, right, (((1,), (1,)), ((), ())), preferred_element_...]
    all_to_all x7 -> x6, starting transfers between devices: 48.1 us -> 40.2 us  [to_shards(): lax.all_to_all(values, 'shard', split_axis=0, concat_axis=0, tiled=True)]
    all_gather x1, waiting for transfers between devices: 20.7 us -> 27.6 us  [on_device(): lax.all_gather(jnp.concatenate([packed, fold_rows(piece[:own_out], total)...]
    concatenate x1, other arithmetic: 10.7 us -> 3.92 us  [on_device(): e_mine = jnp.concatenate([e_one, e_two], axis=0)]
  transfers between devices with their start and end apart: 33 -> 32, of which waited for: 11 -> 14; matrix products, arithmetic and copies ran while one was open for 27% -> 23% of each run, Pallas kernels for 12% -> 14%
where the time goes in v7:
time: 569 us; the launch traced here: 558 us
  waiting for transfers between devices  170 us (30%)
  Pallas kernels  108 us (19%)
  local copies, waits for them, and re-layouts  77.1 us (14%)
  starting transfers between devices  71.2 us (13%)
  other arithmetic  54.6 us (10%)
  matrix products  38.1 us (7%)
  between operations  25.5 us (4%)
  blocking collectives  14 us (2%)
    all_to_all x6, starting transfers between devices, to_shards(): lax.all_to_all(values, 'shard', split_axis=0, concat_axis=0, tiled=True)  40.2 us
    all_gather x1, waiting for transfers between devices, on_device(): d_o_all = lax.all_gather(d_o_ext, 'seq', axis=0, tiled=True)  39 us
    all_to_all x6, waiting for transfers between devices, to_shards(): lax.all_to_all(values, 'shard', split_axis=0, concat_axis=0, tiled=True)  37.5 us
    pallas_call x2, Pallas kernels, scan_backward(): pl.pallas_call(functools.partial(scan_backward_kernel, chunks, len(held)...  34.9 us
    all_gather x1, waiting for transfers between devices, on_device(): lax.all_gather(jnp.concatenate([packed, fold_rows(piece[:own_out], total)...  27.6 us
    unnamed x164, local copies, waits for them, and re-layouts  26.9 us
    dot_general x6, matrix products, transposed_times(): lax.dot_general(left, right, (((0,), (0,)), ((), ())), preferred_element_...  20.1 us
    pallas_call x1, Pallas kernels, expert_main(): pl.pallas_call(expert_main_kernel, grid=(local,), in_specs=[expert_slots(...  19.2 us
  transfers between devices with their start and end apart: 32, of which 14 were waited for; matrix products, arithmetic and copies ran while one was open for 23% of the time, Pallas kernels for 14%

profile of v7, /device:TPU:1, one launch (start us, length us, event | category | flops | bytes accessed | tf_op | source)
XLA Modules:
  0.0 558.5 jit_solution(5161402442145072217)
XLA Ops:
  9.1 4.6 collective-permute-start.4
  31.3 6.7 %collective-permute-done.1 = bf16[128,1536]{1,0:T(8,128)(2,1)S(1)} collective-permute-done((bf16[128,1536]{1,0:T(8,128)(2,1)S(1)}, bf16[128,1536]{1,0:T(8,128)(2,1)S(1)}, u32[]{:S(2)}, u32[]{:S(2)}) %collective-permute-start.1) | collective-permute-done | bytes 393248 | tf_op jit(solution)/shard_map/ppermute | solution.py:718
  37.9 8.3 %collective-permute-done = bf16[128,1536]{1,0:T(8,128)(2,1)S(1)} collective-permute-done((bf16[128,1536]{1,0:T(8,128)(2,1)S(1)}, bf16[128,1536]{1,0:T(8,128)(2,1)S(1)}, u32[]{:S(2)}, u32[]{:S(2)}) %collective-permute-start) | collective-permute-done | bytes 393248 | tf_op jit(solution)/shard_map/ppermute | solution.py:718
  58.5 27.6 %all-gather.14.cloned.1.call-done = bf16[2560,1152]{1,0:T(8,128)(2,1)} async-done(((bf16[160,1152]{1,0:T(8,128)(2,1)}), bf16[2560,1152]{1,0:T(8,128)(2,1)}) %all-gather.14.cloned.1.call-update) | async-done | bytes 5898256 | tf_op jit(solution)/shard_map/all_gather | solution.py:912
  88.0 8.1 %project.1 = (f32[1024,1152]{1,0:T(8,128)}, f32[1024,1]{1,0:T(8,128)S(1)}, bf16[1536,1152]{1,0:T(8,128)(2,1)S(1)}) custom-call(bf16[1024,1536]{1,0:T(8,128)(2,1)S(1)} %copy-done.6, bf16[16,160,1152]{2,1,0:T(8,128)(2,1)} %bitcast.226, bf16[16,64,1664]{2,1,0:T(8,128)(2,1)} %bitcast.22.earlier_ref), custom_call_target="tpu_custom_call" | custom-call | flops 3623878656 | bytes 16777216 | tf_op jit(solution)/shard_map/project/pallas_call | solution.py:317
  100.0 5.0 all-to-all-start
  116.8 10.9 %scan_forward.1 = (bf16[1024,384]{1,0:T(8,128)(2,1)S(1)}, bf16[1024,384]{1,0:T(8,128)(2,1)S(1)}, f32[1024,1]{1,0:T(8,128)S(1)}, f32[8,128,384]{2,1,0:T(8,128)S(1)}) custom-call(f32[1024,1152]{1,0:T(8,128)S(1)} %copy-done.8, f32[1024,1152]{1,0:T(8,128)S(1)} %copy-done.8, f32[8,640]{1,0:T(8,128)S(1)} %maximum_maximum_fusion.3.taps_ref, ...), custom_call_target="tpu_custom_call" | custom-call | flops 3221225472 | bytes 12582912 | tf_op jit(solution)/shard_map/scan_forward/pallas_call | solution.py:347
  129.7 4.8 convolution_convert_fusion.2
  136.6 14.0 %psum.7.earlier_ref = f32[8,128]{1,0:T(8,128)} all-reduce(f32[8,128]{1,0:T(8,128)S(1)} %bitcast.257), channel_id=1, replica_groups=mesh['seq'=8,'shard'=16] {'seq'}, use_global_device_ids=true, to_apply=%region_2.3 | all-reduce | flops 1024 | bytes 8192 | tf_op jit(solution)/shard_map/psum | solution.py:1003
  150.7 5.5 expert_early.1.raw_ref
  158.6 12.1 %reduce-scatter.4.cloned.1.call-done = bf16[128,1536]{1,0:T(8,128)(2,1)} async-done(((bf16[1024,1536]{1,0:T(8,128)(2,1)}), bf16[128,1536]{1,0:T(8,128)(2,1)}) %reduce-scatter.4.cloned.1.call-update) | async-done | bytes 393232 | tf_op jit(solution)/shard_map/reduce_scatter | solution.py:1002
  177.7 6.7 %all-to-all-start.1 = ((bf16[16,64,1536]{2,1,0:T(8,128)(2,1)}), bf16[16,64,1536]{2,1,0:T(8,128)(2,1)}, u32[]{:S(2)}, u32[]{:S(2)}) async-start(bf16[16,64,1536]{2,1,0:T(8,128)(2,1)} %bitcast.218), calls=%async_computation.2 | async-start | bytes 6291456 | tf_op jit(solution)/shard_map/all_to_all | solution.py:874
  192.2 28.0 %all-to-all-done.1 = bf16[16,64,1536]{2,1,0:T(8,128)(2,1)} async-done(((bf16[16,64,1536]{2,1,0:T(8,128)(2,1)}), bf16[16,64,1536]{2,1,0:T(8,128)(2,1)}, u32[]{:S(2)}, u32[]{:S(2)}) %all-to-all-start.1) | async-done | bytes 3145760 | tf_op jit(solution)/shard_map/all_to_all | solution.py:874
  220.2 19.2 %expert_main.1 = (bf16[16,2,32,1664]{3,2,1,0:T(8,128)(2,1)}, bf16[2,512,512]{2,1,0:T(8,128)(2,1)}, bf16[2,512,512]{2,1,0:T(8,128)(2,1)}, bf16[2,512,512]{2,1,0:T...) custom-call(bf16[16,2,32,1536]{3,2,1,0:T(8,128)(2,1)} %bitcast.34.ro, ...), custom_call_target="tpu_custom_call" | custom-call | flops 8589934592 | bytes 20971520 | tf_op jit(solution)/shard_map/expert_main/pallas_call | solution.py:554
  242.2 9.5 %all-to-all-start.2 = ((bf16[16,64,1664]{2,1,0:T(8,128)(2,1)}), bf16[16,64,1664]{2,1,0:T(8,128)(2,1)}, u32[]{:S(2)}, u32[]{:S(2)}) async-start(bf16[16,64,1664]{2,1,0:T(8,128)(2,1)} %bitcast.224), calls=%async_computation.4 | async-start | bytes 6815744 | tf_op jit(solution)/shard_map/all_to_all | solution.py:874
  252.2 12.7 %expert_late.1 = (bf16[16,2,32,1536]{3,2,1,0:T(8,128)(2,1)}, bf16[2,4608,512]{2,1,0:T(8,128)(2,1)}) custom-call(bf16[16,2,32,1536]{3,2,1,0:T(8,128)(2,1)} %bitcast.34.rows_ref, bf16[16,2,32,1664]{3,2,1,0:T(8,128)(2,1)} %bitcast.30.cot_ref.routed_ref, bf16[2,512,512]{2,1,0:T(8,128)(2,1)} %get-tuple-element.70.act_ref, ...), custom_call_target="tpu_custom_call" | custom-call | flops 7516192768 | bytes 25165824 | tf_op jit(solution)/shard_map/expert_late/pallas_call | solution.py:588
  264.8 4.3 fusion.65
  284.8 8.0 %all-to-all-done.2 = bf16[16,64,1664]{2,1,0:T(8,128)(2,1)} async-done(((bf16[16,64,1664]{2,1,0:T(8,128)(2,1)}), bf16[16,64,1664]{2,1,0:T(8,128)(2,1)}, u32[]{:S(2)}, u32[]{:S(2)}) %all-to-all-start.2) | async-done | bytes 3407904 | tf_op jit(solution)/shard_map/all_to_all | solution.py:874
  304.4 3.7 pad_maximum_fusion.2
  308.2 5.7 %all-to-all-start.3 = ((bf16[16,64,1536]{2,1,0:T(8,128)(2,1)}), bf16[16,64,1536]{2,1,0:T(8,128)(2,1)}, u32[]{:S(2)}, u32[]{:S(2)}) async-start(bf16[16,64,1536]{2,1,0:T(8,128)(2,1)} %bitcast.225), calls=%async_computation.5 | async-start | bytes 6291456 | tf_op jit(solution)/shard_map/all_to_all | solution.py:874
  315.2 39.0 %all-gather.12.cloned.1.call-done = bf16[1024,1664]{1,0:T(8,128)(2,1)} async-done(((bf16[128,1664]{1,0:T(8,128)(2,1)}), bf16[1024,1664]{1,0:T(8,128)(2,1)}) %all-gather.12.cloned.1.call-update) | async-done | bytes 3407888 | tf_op jit(solution)/shard_map/all_gather | solution.py:1093
  367.8 17.7 %scan_backward.2 = (bf16[1024,1152]{1,0:T(8,128)(2,1)}, bf16[1024,1536]{1,0:T(8,128)(2,1)}, f32[136,640]{1,0:T(8,128)S(1)}, f32[24,640]{1,0:T(8,128)S(1)}) custom-call(f32[1024,1152]{1,0:T(8,128)} %get-tuple-element.60.proj_ref.prev_ref, f32[1024,1152]{1,0:T(8,128)} %get-tuple-element.60.proj_ref.prev_ref, bf16[1024,384]{1,0:T(8,128)(2,1)S(1)} %copy-done.12, ...), custom_call_target="tpu_custom_call" | custom-call | flops 10737418240 | bytes 20971520 | tf_op jit(solution)/shard_map/scan_backward/pallas_call | solution.py:388
  393.5 6.6 %all-to-all-start.4 = ((bf16[16,224,384]{2,1,0:T(8,128)(2,1)}), bf16[16,224,384]{2,1,0:T(8,128)(2,1)}, u32[]{:S(2)}, u32[]{:S(2)}) async-start(bf16[16,224,384]{2,1,0:T(8,128)(2,1)} %copy-done.31), calls=%async_computation.7 | async-start | bytes 5505024 | tf_op jit(solution)/shard_map/all_to_all | solution.py:874
  402.9 17.2 %scan_backward.3 = (bf16[1024,1152]{1,0:T(8,128)(2,1)}, bf16[1024,1536]{1,0:T(8,128)(2,1)}, f32[136,640]{1,0:T(8,128)}, f32[24,640]{1,0:T(8,128)S(1)}) custom-call(f32[1024,1152]{1,0:T(8,128)} %get-tuple-element.60.proj_ref.prev_ref, f32[1024,1152]{1,0:T(8,128)} %get-tuple-element.60.proj_ref.prev_ref, ...), custom_call_target="tpu_custom_call", output_to_operand_aliasing={{0}: (12, {}), {1}: (13, {})} | custom-call | flops 10737418240 | bytes 20971520 | tf_op jit(solution)/shard_map/scan_backward/pallas_call | solution.py:388
  426.1 8.7 %convolution_convert_fusion = bf16[1536,1152]{1,0:T(8,128)(2,1)} fusion(bf16[1024,1536]{1,0:T(8,128)(2,1)} %copy-done.5, bf16[1024,1152]{1,0:T(8,128)(2,1)} %get-tuple-element.86), kind=kOutput, calls=%fused_computation | convolution fusion | flops 3625648128 | bytes 9043968 | tf_op jit(solution)/shard_map/dot_general | solution.py:29
  443.0 6.6 %all-to-all-start.5 = ((bf16[16,96,1152]{2,1,0:T(8,128)(2,1)}), bf16[16,96,1152]{2,1,0:T(8,128)(2,1)}, u32[]{:S(2)}, u32[]{:S(2)}) async-start(bf16[16,96,1152]{2,1,0:T(8,128)(2,1)} %bitcast.209), calls=%async_computation.8 | async-start | bytes 7077888 | tf_op jit(solution)/shard_map/all_to_all | solution.py:874
  449.9 12.4 %collective-permute-done.12 = bf16[576,512]{1,0:T(8,128)(2,1)S(1)} collective-permute-done((bf16[576,512]{1,0:T(8,128)(2,1)S(1)}, bf16[576,512]{1,0:T(8,128)(2,1)S(1)}, u32[]{:S(2)}, u32[]{:S(2)}) %collective-permute-start.12) | collective-permute-done | bytes 589856 | tf_op jit(solution)/shard_map/ppermute | solution.py:742
  463.5 4.8 collective-permute-done.15
  473.4 9.4 %collective-permute-start.10 = (bf16[128,384]{1,0:T(8,128)(2,1)S(1)}, bf16[128,384]{1,0:T(8,128)(2,1)S(1)}, u32[]{:S(2)}, u32[]{:S(2)}) collective-permute-start(bf16[128,384]{1,0:T(8,128)(2,1)S(1)} %slice.508), channel_id=1, source_target_pairs={{0,0},{1,16},{2,32},{3,48},{4,64},{5,80},{6,96},{7,112},{8,1},{9,1... | collective-permute-start | bytes 294920 | tf_op jit(solution)/shard_map/ppermute | solution.py:1188
  482.8 13.9 %collective-permute-done.10 = bf16[128,384]{1,0:T(8,128)(2,1)S(1)} collective-permute-done((bf16[128,384]{1,0:T(8,128)(2,1)S(1)}, bf16[128,384]{1,0:T(8,128)(2,1)S(1)}, u32[]{:S(2)}, u32[]{:S(2)}) %collective-permute-start.10) | collective-permute-done | bytes 98336 | tf_op jit(solution)/shard_map/ppermute | solution.py:1188
  511.9 3.9 pad_maximum_fusion.own_ref
  524.1 14.0 %unpack_expert_grads.1 = (f32[2,1536,512]{2,1,0:T(8,128)}, f32[2,1536,512]{2,1,0:T(8,128)}, f32[2,512,1536]{2,1,0:T(8,128)}) custom-call(s32[1]{0:T(128)} %bitcast.92.core_ref, bf16[4608,512]{1,0:T(8,128)(2,1)} %pad_maximum_fusion.own_ref, bf16[4608,512]{1,0:T(8,128)(2,1)} %collective-permute-done.17.other_ref), custom_call_target="tpu_custom_call" | custom-call | flops 1048576 | bytes 29360128 | tf_op jit(solution)/shard_map/unpack_expert_grads/pallas_call | solution.py:771
  (429 shorter events, 173.4 us)
Async XLA Ops:
  7.2 78.9 %all-gather.14.cloned.1.call-start = ((), (), s32[]{:S(2)}) async-start(), calls=%async_computation.15 | async-start | bytes 6266880 | tf_op jit(solution)/shard_map/all_gather | solution.py:912
  9.1 14.9 %collective-permute-start.4 = (bf16[32,1536]{1,0:T(8,128)(2,1)S(1)}, bf16[32,1536]{1,0:T(8,128)(2,1)S(1)}, u32[]{:S(2)}, u32[]{:S(2)}) collective-permute-start(bf16[32,1536]{1,0:T(8,128)(2,1)S(1)} %pad_maximum_fusion.8), channel_id=1, source_target_pairs={{0,0},{16,1},{32,2},{48,3},{64,4},{80,5},{96,6},{112,7},{1,8},{17,... | collective-permute-start | bytes 294920 | tf_op jit(solution)/shard_map/ppermute | solution.py:898
  24.8 104.9 %all-gather.8.cloned.1.call-start = ((), (), s32[]{:S(2)}) async-start(), calls=%async_computation.9 | async-start | bytes 3538944 | tf_op jit(solution)/shard_map/all_gather | solution.py:999
  24.9 13.0 %collective-permute-start.1 = (bf16[128,1536]{1,0:T(8,128)(2,1)S(1)}, bf16[128,1536]{1,0:T(8,128)(2,1)S(1)}, u32[]{:S(2)}, u32[]{:S(2)}) collective-permute-start(bf16[128,1536]{1,0:T(8,128)(2,1)S(1)} %bitcast.206), channel_id=1, source_target_pairs={{0,64},{16,80},{32,96},{48,112},{64,0},{80,16},{96,32},{112,48},{1... | collective-permute-start | bytes 1179656 | tf_op jit(solution)/shard_map/ppermute | solution.py:718
  28.6 17.7 %collective-permute-start = (bf16[128,1536]{1,0:T(8,128)(2,1)S(1)}, bf16[128,1536]{1,0:T(8,128)(2,1)S(1)}, u32[]{:S(2)}, u32[]{:S(2)}) collective-permute-start(bf16[128,1536]{1,0:T(8,128)(2,1)S(1)} %bitcast.207), channel_id=1, source_target_pairs={{0,32},{16,48},{32,64},{48,80},{64,96},{80,112},{96,0},{112,16},{1... | collective-permute-start | bytes 1179656 | tf_op jit(solution)/shard_map/ppermute | solution.py:718
  30.3 17.2 %collective-permute-start.2 = (bf16[128,1536]{1,0:T(8,128)(2,1)S(1)}, bf16[128,1536]{1,0:T(8,128)(2,1)S(1)}, u32[]{:S(2)}, u32[]{:S(2)}) collective-permute-start(bf16[128,1536]{1,0:T(8,128)(2,1)S(1)} %bitcast.208), channel_id=1, source_target_pairs={{0,96},{16,112},{32,0},{48,16},{64,32},{80,48},{96,64},{112,80},{1... | collective-permute-start | bytes 1179656 | tf_op jit(solution)/shard_map/ppermute | solution.py:718
  48.9 5.7 %collective-permute-start.3 = (bf16[4,128,1536]{2,1,0:T(8,128)(2,1)}, bf16[4,128,1536]{2,1,0:T(8,128)(2,1)}, u32[]{:S(2)}, u32[]{:S(2)}) collective-permute-start(bf16[4,128,1536]{2,1,0:T(8,128)(2,1)} %get-tuple-element.228), channel_id=1, source_target_pairs={{0,16},{16,0},{32,48},{48,32},{64,80},{80,64},{96,112},{112,96},{1... | collective-permute-start | bytes 4718600 | tf_op jit(solution)/shard_map/ppermute | solution.py:720
  100.0 50.6 %all-to-all-start = ((bf16[16,64,1664]{2,1,0:T(8,128)(2,1)}), bf16[16,64,1664]{2,1,0:T(8,128)(2,1)}, u32[]{:S(2)}, u32[]{:S(2)}) async-start(bf16[16,64,1664]{2,1,0:T(8,128)(2,1)} %bitcast.22.earlier_ref), calls=%async_computation.1 | async-start | bytes 6815744 | tf_op jit(solution)/shard_map/all_to_all | solution.py:874
  105.1 65.6 %reduce-scatter.4.cloned.1.call-start = ((), (), s32[]{:S(2)}) async-start(), calls=%async_computation.10 | async-start | bytes 3538944 | tf_op jit(solution)/shard_map/reduce_scatter | solution.py:1002
  135.7 84.5 %all-gather.10.cloned.1.call-start = ((), (), s32[]{:S(2)}) async-start(), calls=%async_computation.11 | async-start | bytes 3538944 | tf_op jit(solution)/shard_map/all_gather | solution.py:1014
  177.7 42.5 %all-to-all-start.1 = ((bf16[16,64,1536]{2,1,0:T(8,128)(2,1)}), bf16[16,64,1536]{2,1,0:T(8,128)(2,1)}, u32[]{:S(2)}, u32[]{:S(2)}) async-start(bf16[16,64,1536]{2,1,0:T(8,128)(2,1)} %bitcast.218), calls=%async_computation.2 | async-start | bytes 6291456 | tf_op jit(solution)/shard_map/all_to_all | solution.py:874
  184.5 112.7 %reduce-scatter.6.cloned.1.call-start = ((), (), s32[]{:S(2)}) async-start(), calls=%async_computation.12 | async-start | bytes 7077888 | tf_op jit(solution)/shard_map/reduce_scatter | solution.py:1044
  242.2 50.5 %all-to-all-start.2 = ((bf16[16,64,1664]{2,1,0:T(8,128)(2,1)}), bf16[16,64,1664]{2,1,0:T(8,128)(2,1)}, u32[]{:S(2)}, u32[]{:S(2)}) async-start(bf16[16,64,1664]{2,1,0:T(8,128)(2,1)} %bitcast.224), calls=%async_computation.4 | async-start | bytes 6815744 | tf_op jit(solution)/shard_map/all_to_all | solution.py:874
  251.7 102.5 %all-gather.12.cloned.1.call-start = ((), (), s32[]{:S(2)}) async-start(), calls=%async_computation.13 | async-start | bytes 3833856 | tf_op jit(solution)/shard_map/all_gather | solution.py:1093
  269.3 9.8 %collective-permute-start.6 = (bf16[1536,512]{1,0:T(8,128)(2,1)S(1)}, bf16[1536,512]{1,0:T(8,128)(2,1)S(1)}, u32[]{:S(2)}, u32[]{:S(2)}) collective-permute-start(bf16[1536,512]{1,0:T(8,128)(2,1)S(1)} %dynamic-slice_bitcast_fusion.1), channel_id=1, source_target_pairs={{0,16},{16,0},{32,48},{48,32},{64,80},{80,64},{96,112},{112,96},{1... | collective-permute-start | bytes 4718600 | tf_op jit(solution)/shard_map/ppermute | solution.py:737
  272.9 7.8 %collective-permute-start.7 = (bf16[1536,512]{1,0:T(8,128)(2,1)S(1)}, bf16[1536,512]{1,0:T(8,128)(2,1)S(1)}, u32[]{:S(2)}, u32[]{:S(2)}) collective-permute-start(bf16[1536,512]{1,0:T(8,128)(2,1)S(1)} %dynamic-slice_bitcast_fusion), channel_id=1, source_target_pairs={{0,16},{16,0},{32,48},{48,32},{64,80},{80,64},{96,112},{112,96},{1... | collective-permute-start | bytes 4718600 | tf_op jit(solution)/shard_map/ppermute | solution.py:737
  274.1 8.3 %collective-permute-start.5 = (bf16[1536,512]{1,0:T(8,128)(2,1)S(1)}, bf16[1536,512]{1,0:T(8,128)(2,1)S(1)}, u32[]{:S(2)}, u32[]{:S(2)}) collective-permute-start(bf16[1536,512]{1,0:T(8,128)(2,1)S(1)} %dynamic-slice_bitcast_fusion.2), channel_id=1, source_target_pairs={{0,16},{16,0},{32,48},{48,32},{64,80},{80,64},{96,112},{112,96},{1... | collective-permute-start | bytes 4718600 | tf_op jit(solution)/shard_map/ppermute | solution.py:737
  308.2 85.3 %all-to-all-start.3 = ((bf16[16,64,1536]{2,1,0:T(8,128)(2,1)}), bf16[16,64,1536]{2,1,0:T(8,128)(2,1)}, u32[]{:S(2)}, u32[]{:S(2)}) async-start(bf16[16,64,1536]{2,1,0:T(8,128)(2,1)} %bitcast.225), calls=%async_computation.5 | async-start | bytes 6291456 | tf_op jit(solution)/shard_map/all_to_all | solution.py:874
  359.1 30.3 %collective-permute-start.8 = (bf16[1152,512]{1,0:T(8,128)(2,1)S(1)}, bf16[1152,512]{1,0:T(8,128)(2,1)}, u32[]{:S(2)}, u32[]{:S(2)}) collective-permute-start(bf16[1152,512]{1,0:T(8,128)(2,1)S(1)} %fusion.14), channel_id=1, source_target_pairs={{0,32},{16,48},{32,0},{48,16},{64,96},{80,112},{96,64},{112,80},{1... | collective-permute-start | bytes 3538952 | tf_op jit(solution)/shard_map/ppermute | solution.py:737
  359.7 32.2 %collective-permute-start.9 = (bf16[1152,512]{1,0:T(8,128)(2,1)S(1)}, bf16[1152,512]{1,0:T(8,128)(2,1)}, u32[]{:S(2)}, u32[]{:S(2)}) collective-permute-start(bf16[1152,512]{1,0:T(8,128)(2,1)S(1)} %fusion.15), channel_id=1, source_target_pairs={{0,96},{16,112},{32,64},{48,80},{64,32},{80,48},{96,0},{112,16},{1... | collective-permute-start | bytes 3538952 | tf_op jit(solution)/shard_map/ppermute | solution.py:737
  393.5 42.7 %all-to-all-start.4 = ((bf16[16,224,384]{2,1,0:T(8,128)(2,1)}), bf16[16,224,384]{2,1,0:T(8,128)(2,1)}, u32[]{:S(2)}, u32[]{:S(2)}) async-start(bf16[16,224,384]{2,1,0:T(8,128)(2,1)} %copy-done.31), calls=%async_computation.7 | async-start | bytes 5505024 | tf_op jit(solution)/shard_map/all_to_all | solution.py:874
  400.1 107.9 %reduce-scatter.8.cloned.1.call-start = ((), (), s32[]{:S(2)}) async-start(), calls=%async_computation.14 | async-start | bytes 3538944 | tf_op jit(solution)/shard_map/reduce_scatter | solution.py:1152
  421.0 19.2 %collective-permute-start.11 = (bf16[576,512]{1,0:T(8,128)(2,1)}, bf16[576,512]{1,0:T(8,128)(2,1)}, u32[]{:S(2)}, u32[]{:S(2)}) collective-permute-start(bf16[576,512]{1,0:T(8,128)(2,1)} %dynamic-slice_bitcast_fusion.4), channel_id=1, source_target_pairs={{0,96},{16,112},{32,64},{48,80},{64,32},{80,48},{96,0},{112,16},{1... | collective-permute-start | bytes 1769480 | tf_op jit(solution)/shard_map/ppermute | solution.py:737
  423.2 26.5 %collective-permute-start.14 = (bf16[576,512]{1,0:T(8,128)(2,1)}, bf16[576,512]{1,0:T(8,128)(2,1)S(1)}, u32[]{:S(2)}, u32[]{:S(2)}) collective-permute-start(bf16[576,512]{1,0:T(8,128)(2,1)} %dynamic-slice_bitcast_fusion.3), channel_id=1, source_target_pairs={{0,32},{16,48},{32,0},{48,16},{64,96},{80,112},{96,64},{112,80},{1... | collective-permute-start | bytes 1769480 | tf_op jit(solution)/shard_map/ppermute | solution.py:737
  441.5 20.8 %collective-permute-start.12 = (bf16[576,512]{1,0:T(8,128)(2,1)S(1)}, bf16[576,512]{1,0:T(8,128)(2,1)S(1)}, u32[]{:S(2)}, u32[]{:S(2)}) collective-permute-start(bf16[576,512]{1,0:T(8,128)(2,1)S(1)} %add_convert_fusion.4), channel_id=1, source_target_pairs={{0,96},{16,112},{32,64},{48,80},{64,32},{80,48},{96,0},{112,16},{1... | collective-permute-start | bytes 1769480 | tf_op jit(solution)/shard_map/ppermute | solution.py:742
  443.0 62.4 %all-to-all-start.5 = ((bf16[16,96,1152]{2,1,0:T(8,128)(2,1)}), bf16[16,96,1152]{2,1,0:T(8,128)(2,1)}, u32[]{:S(2)}, u32[]{:S(2)}) async-start(bf16[16,96,1152]{2,1,0:T(8,128)(2,1)} %bitcast.209), calls=%async_computation.8 | async-start | bytes 7077888 | tf_op jit(solution)/shard_map/all_to_all | solution.py:874
  449.6 91.8 %all-gather.16.cloned.1.call-start = ((), (), s32[]{:S(2)}) async-start(), calls=%async_computation.16 | async-start | bytes 3538944 | tf_op jit(solution)/shard_map/all_gather | solution.py:1198
  449.8 18.4 %collective-permute-start.15 = (bf16[576,512]{1,0:T(8,128)(2,1)S(1)}, bf16[576,512]{1,0:T(8,128)(2,1)}, u32[]{:S(2)}, u32[]{:S(2)}) collective-permute-start(bf16[576,512]{1,0:T(8,128)(2,1)S(1)} %add_convert_fusion.3), channel_id=1, source_target_pairs={{0,32},{16,48},{32,0},{48,16},{64,96},{80,112},{96,64},{112,80},{1... | collective-permute-start | bytes 1769480 | tf_op jit(solution)/shard_map/ppermute | solution.py:742
  463.5 34.0 %collective-permute-start.13 = (bf16[1152,512]{1,0:T(8,128)(2,1)}, bf16[1152,512]{1,0:T(8,128)(2,1)}, u32[]{:S(2)}, u32[]{:S(2)}) collective-permute-start(bf16[1152,512]{1,0:T(8,128)(2,1)} %pad_maximum_fusion.5), channel_id=1, source_target_pairs={{0,32},{16,48},{32,0},{48,16},{64,96},{80,112},{96,64},{112,80},{1... | collective-permute-start | bytes 3538952 | tf_op jit(solution)/shard_map/ppermute | solution.py:742
  470.5 29.9 %collective-permute-start.16 = (bf16[1152,512]{1,0:T(8,128)(2,1)}, bf16[1152,512]{1,0:T(8,128)(2,1)}, u32[]{:S(2)}, u32[]{:S(2)}) collective-permute-start(bf16[1152,512]{1,0:T(8,128)(2,1)} %pad_maximum_fusion.6), channel_id=1, source_target_pairs={{0,96},{16,112},{32,64},{48,80},{64,32},{80,48},{96,0},{112,16},{1... | collective-permute-start | bytes 3538952 | tf_op jit(solution)/shard_map/ppermute | solution.py:742
  473.4 23.3 %collective-permute-start.10 = (bf16[128,384]{1,0:T(8,128)(2,1)S(1)}, bf16[128,384]{1,0:T(8,128)(2,1)S(1)}, u32[]{:S(2)}, u32[]{:S(2)}) collective-permute-start(bf16[128,384]{1,0:T(8,128)(2,1)S(1)} %slice.508), channel_id=1, source_target_pairs={{0,0},{1,16},{2,32},{3,48},{4,64},{5,80},{6,96},{7,112},{8,1},{9,1... | collective-permute-start | bytes 294920 | tf_op jit(solution)/shard_map/ppermute | solution.py:1188
  515.9 8.3 %collective-permute-start.17 = (bf16[4608,512]{1,0:T(8,128)(2,1)}, bf16[4608,512]{1,0:T(8,128)(2,1)}, u32[]{:S(2)}, u32[]{:S(2)}) collective-permute-start(bf16[4608,512]{1,0:T(8,128)(2,1)} %pad_maximum_fusion.own_ref), channel_id=1, source_target_pairs={{0,16},{16,0},{32,48},{48,32},{64,80},{80,64},{96,112},{112,96},{1... | collective-permute-start | bytes 14155784 | tf_op jit(solution)/shard_map/ppermute | solution.py:1196
  (70 other events, 925.5 us)
Sparse Core Ops, SparseCore 0:
  24.9 61.1 all-gather.13
  100.1 28.1 all-gather.7
  135.8 34.8 reduce-scatter.3
  174.2 30.1 all-gather.9
  239.6 53.8 reduce-scatter.5
  304.2 49.9 all-gather.11
  423.3 44.2 reduce-scatter.7
  512.0 29.3 all-gather.15

commit v8 on v7

--- a/solution.py
+++ b/solution.py
@@ -82,11 +82,10 @@
     return jnp.where(condition, 1.0, 0.0).astype(jnp.bfloat16)
 
 
-def chunk_parts(proj, prev, has_prev, taps_ref, head_ref, pad_ref):
+def chunk_parts(proj, before, taps_ref, head_ref, pad_ref):
     f32, bf = jnp.float32, jnp.bfloat16
     feed = proj[:, WIDE : WIDE + CONVW].astype(bf).astype(f32)
-    before = prev[:, WIDE : WIDE + CONVW].astype(bf).astype(f32)
-    pad_ref[0:8, :] = jnp.where(has_prev, before, 0.0)
+    pad_ref[0:8, :] = before
     pad_ref[8 : 8 + CHUNK, :] = feed
     conv = taps_ref[4:5, :]
     for tap in range(4):
@@ -138,47 +137,67 @@
     ).astype(jnp.bfloat16)
 
 
-def scan_forward_kernel(
-    proj_ref, prev_ref, taps_ref, head_ref, skip_ref,
-    mixed_ref, q_ref, square_ref, start_ref, state_ref, pad_ref,
+def front_kernel(
+    x_ref, w_in_ref, rows_in_ref, place_ref, taps_ref, head_ref, skip_ref, earlier_0, earlier_1,
+    proj_ref, scale_ref, w_ref, out_w_ref, mixed_ref, q_ref, out_ref, square_ref, start_ref,
+    state_ref, pad_ref,
 ):
     f32, bf = jnp.float32, jnp.bfloat16
-    chunk = pl.program_id(0)
-
-    @pl.when(chunk == 0)
+    width = w_ref.shape[1]
+
+    @pl.when(pl.program_id(0) == 0)
     def _():
         state_ref[...] = jnp.zeros(state_ref.shape, f32)
-
-    parts = chunk_parts(
-        proj_ref[...], prev_ref[...], chunk > 0, taps_ref, head_ref, pad_ref
-    )
-    state = state_ref[...]
-    start_ref[0] = state
-    xs = parts["xs"]
-    inside = []
-    for pair in range(PAIRS):
-        _, table = pair_table(parts, pair)
-        inside.append(times(table.astype(bf), stack_heads(xs, pair)))
-    across = times(parts["query"], state.astype(bf))
-    y = (
-        jnp.concatenate(inside, axis=1)
-        + parts["e_w"] * across
-        + skip_ref[0:1, :] * parts["u"]
-    )
-    mixed = y.astype(bf)
-    mixed_ref[...] = mixed
-    gate = proj_ref[:, :WIDE]
-    q_val = mixed.astype(f32) * (gate * jax.nn.sigmoid(gate))
-    q_ref[...] = q_val.astype(bf)
-    square_ref[...] = jnp.sum(q_val * q_val, axis=1, keepdims=True)
-    state_ref[...] = state * parts["e_w"][CHUNK - 1 : CHUNK, :] + transposed_times(
-        parts["key"], (xs * parts["w_w"]).astype(bf)
-    )
+        pad_ref[CHUNK : CHUNK + 8, :] = jnp.zeros((8, CONVW), f32)
+        w_ref[...] = w_in_ref[...].reshape(-1, width)
+        folded = rows_in_ref[...].reshape(-1, width)
+        out_w_ref[:, :width] = times(place_ref[0], folded).astype(bf)
+        rest = out_w_ref.shape[1] - width
+        tail = jnp.zeros((out_w_ref.shape[0], rest), f32)
+        for part in range(width // rest):
+            tail = tail + times(place_ref[1 + part], folded[:, rest * part : rest * part + rest])
+        out_w_ref[:, width:] = tail.astype(bf)
+
+    x = x_ref[...]
+    scale = row_scale(x.astype(f32))
+    proj = times(x, w_ref[...]) * scale
+    proj_ref[...] = proj
+    scale_ref[...] = scale
+    gated = []
+    for at in range(0, x.shape[0], CHUNK):
+        here = slice(at, at + CHUNK)
+        before = pad_ref[CHUNK : CHUNK + 8, :]
+        parts = chunk_parts(proj[here], before, taps_ref, head_ref, pad_ref)
+        state = state_ref[...]
+        start_ref[at // CHUNK] = state
+        xs = parts["xs"]
+        inside = []
+        for pair in range(PAIRS):
+            _, table = pair_table(parts, pair)
+            inside.append(times(table.astype(bf), stack_heads(xs, pair)))
+        across = times(parts["query"], state.astype(bf))
+        y = (
+            jnp.concatenate(inside, axis=1)
+            + parts["e_w"] * across
+            + skip_ref[0:1, :] * parts["u"]
+        )
+        mixed = y.astype(bf)
+        mixed_ref[here, :] = mixed
+        gate = proj[here, :WIDE]
+        q_val = mixed.astype(f32) * (gate * jax.nn.sigmoid(gate))
+        gated.append(q_val.astype(bf))
+        square_ref[here, :] = jnp.sum(q_val * q_val, axis=1, keepdims=True)
+        state_ref[...] = state * parts["e_w"][CHUNK - 1 : CHUNK, :] + transposed_times(
+            parts["key"], (xs * parts["w_w"]).astype(bf)
+        )
+    gated = jnp.concatenate(gated, axis=0)
+    q_ref[...] = gated
+    out_ref[...] = times(gated, out_w_ref[...]).astype(bf)
 
 
 def scan_backward_kernel(
-    chunks, held_count, proj_ref, prev_ref, mixed_ref, d_gated_ref, rows_ref, start_ref, taps_ref,
-    head_ref, skip_ref, w_ref, carry_in_ref, sums_in_ref, *refs,
+    chunks, held_count, proj_ref, prev_ref, mixed_ref, d_o_ref, rows_ref, start_ref, taps_ref,
+    head_ref, skip_ref, w_ref, out_w_ref, carry_in_ref, sums_in_ref, *refs,
 ):
     f32, bf = jnp.float32, jnp.bfloat16
     d_proj_ref, back_ref, carry_ref, sums_ref, state_ref, pad_ref, late_ref = refs[held_count:]
@@ -194,9 +213,9 @@
         late_ref[CHUNK : CHUNK + 8, :] = carry_in_ref[128:136, :]
         sums_ref[...] = sums_in_ref[...]
 
-    parts = chunk_parts(
-        proj_ref[...], prev_ref[...], chunk > 0, taps_ref, head_ref, pad_ref
-    )
+    before = prev_ref[:, WIDE : WIDE + CONVW].astype(bf).astype(f32)
+    before = jnp.where(chunk > 0, before, 0.0)
+    parts = chunk_parts(proj_ref[...], before, taps_ref, head_ref, pad_ref)
     u, key, query, xs = parts["u"], parts["key"], parts["query"], parts["xs"]
     e_w, w_w, dt_w = parts["e_w"], parts["w_w"], parts["dt_w"]
 
@@ -206,7 +225,10 @@
     mixed = mixed_ref[...].astype(f32)
     q_val = mixed * gate_act
     q_r = rows_ref[:, 0:1]
-    d_q = q_r * d_gated_ref[...] - q_val * (q_r * q_r * rows_ref[:, 1:2])
+    dim = out_w_ref.shape[1]
+    d_gated = times_transposed(d_o_ref[:, :dim], out_w_ref[...])
+    kappa = d_o_ref[:, dim : dim + 1].astype(f32) + d_o_ref[:, dim + 1 : dim + 2].astype(f32)
+    d_q = q_r * d_gated - q_val * (q_r * q_r * kappa)
     d_gate = d_q * mixed * (gate_sig * (1.0 + gate * (1.0 - gate_sig)))
     d_y = (d_q * gate_act).astype(bf).astype(f32)
 
@@ -278,7 +300,7 @@
     late_ref[CHUNK : CHUNK + 8, :] = d_conv[0:8, :]
     carry_ref[0:128, 0:WIDE] = state_ref[...]
     carry_ref[128:136, :] = d_conv[0:8, :]
-    scale = rows_ref[:, 2:3]
+    scale = rows_ref[:, 1:2]
     d_proj = jnp.concatenate([d_gate, d_feed, d_pre], axis=1) * scale
     d_proj = d_proj.astype(bf)
     d_proj_ref[...] = d_proj
@@ -296,95 +318,79 @@
     return pl.BlockSpec(shape, lambda step: (0,) * len(shape))
 
 
-def project_kernel(x_ref, weights_ref, earlier_ref, proj_ref, scale_ref, w_ref):
-    width = weights_ref.shape[2]
-
-    @pl.when(pl.program_id(0) == 0)
-    def _():
-        w_ref[...] = weights_ref[...].reshape(-1, width)
-
-    x = x_ref[...]
-    wide = x.astype(jnp.float32)
-    scale = row_scale(wide)
-    proj_ref[...] = times(x, w_ref[...]) * scale
-    scale_ref[...] = scale
-
-
-def project(x_all, weights, rows_w, earlier):
+def front(x_all, weights, rows_w, taps, head, skip, *earlier):
+    f32, bf = jnp.float32, jnp.bfloat16
     rows, dim = x_all.shape
     sources, _, width = weights.shape
-    tile = rows // 4
+    own = WIDE // sources
+    count = own * dim // width
+    tile = 2 * CHUNK
+    row = jnp.arange(WIDE)[:, None]
+    slot = jnp.arange(sources * count)[None, :]
+    same = row // own == slot // count
+    deep = count - own
+    place = [same & (row % own == slot % count)] + [
+        same & (row % own // deep == part) & (row % deep + own == slot % count)
+        for part in range(own // deep)
+    ]
+    place = jnp.stack(place).astype(bf)
+    by_tile = lambda step: (step, 0)
+    chunks = rows // CHUNK
     return pl.pallas_call(
-        project_kernel,
-        grid=(4,),
+        front_kernel,
+        grid=(rows // tile,),
         in_specs=[
-            pl.BlockSpec((tile, dim), lambda step: (step, 0)),
+            pl.BlockSpec((tile, dim), by_tile),
             pl.BlockSpec((sources, rows_w, width), lambda step: (0, 0, 0)),
-            corner_of(earlier),
-        ],
-        out_specs=[
-            pl.BlockSpec((tile, width), lambda step: (step, 0)),
-            pl.BlockSpec((tile, 1), lambda step: (step, 0)),
-            pl.BlockSpec((dim, width), lambda step: (0, 0)),
-        ],
-        out_shape=[
-            jax.ShapeDtypeStruct((rows, width), jnp.float32),
-            jax.ShapeDtypeStruct((rows, 1), jnp.float32),
-            jax.ShapeDtypeStruct((dim, width), jnp.bfloat16),
-        ],
-        compiler_params=pltpu.CompilerParams(vmem_limit_bytes=40 << 20),
-        cost_estimate=pl.CostEstimate(
-            flops=2 * rows * dim * width, bytes_accessed=16 << 20, transcendentals=0
-        ),
-        name="project",
-    )(x_all, weights, earlier)
-
-
-def scan_forward(proj, taps, head, skip):
-    rows, width = proj.shape
-    chunks = rows // CHUNK
-    by_chunk = lambda step: (step, 0)
-    return pl.pallas_call(
-        scan_forward_kernel,
-        grid=(chunks,),
-        in_specs=[
-            pl.BlockSpec((CHUNK, width), by_chunk),
-            pl.BlockSpec((8, width), lambda step: (jnp.maximum(step * (CHUNK // 8) - 1, 0), 0)),
+            pl.BlockSpec((sources, count, width), lambda step: (0, rows_w // count, 0)),
+            whole(place.shape),
             whole(taps.shape),
             whole(head.shape),
             whole(skip.shape),
+            *map(corner_of, earlier),
         ],
         out_specs=[
-            pl.BlockSpec((CHUNK, WIDE), by_chunk),
-            pl.BlockSpec((CHUNK, WIDE), by_chunk),
-            pl.BlockSpec((CHUNK, 1), by_chunk),
-            pl.BlockSpec((1, 128, WIDE), lambda step: (step, 0, 0)),
+            pl.BlockSpec((tile, width), by_tile),
+            pl.BlockSpec((tile, 1), by_tile),
+            whole((dim, width)),
+            whole((WIDE, dim)),
+            pl.BlockSpec((tile, WIDE), by_tile),
+            pl.BlockSpec((tile, WIDE), by_tile),
+            pl.BlockSpec((tile, dim), by_tile),
+            pl.BlockSpec((tile, 1), by_tile),
+            pl.BlockSpec((tile // CHUNK, 128, WIDE), lambda step: (step, 0, 0)),
         ],
         out_shape=[
-            jax.ShapeDtypeStruct((rows, WIDE), jnp.bfloat16),
-            jax.ShapeDtypeStruct((rows, WIDE), jnp.bfloat16),
-            jax.ShapeDtypeStruct((rows, 1), jnp.float32),
-            jax.ShapeDtypeStruct((chunks, 128, WIDE), jnp.float32),
+            jax.ShapeDtypeStruct((rows, width), f32),
+            jax.ShapeDtypeStruct((rows, 1), f32),
+            jax.ShapeDtypeStruct((dim, width), bf),
+            jax.ShapeDtypeStruct((WIDE, dim), bf),
+            jax.ShapeDtypeStruct((rows, WIDE), bf),
+            jax.ShapeDtypeStruct((rows, WIDE), bf),
+            jax.ShapeDtypeStruct((rows, dim), bf),
+            jax.ShapeDtypeStruct((rows, 1), f32),
+            jax.ShapeDtypeStruct((chunks, 128, WIDE), f32),
         ],
         scratch_shapes=[
-            pltpu.VMEM((128, WIDE), jnp.float32),
-            pltpu.VMEM((CHUNK + 8, CONVW), jnp.float32),
-        ],
-        compiler_params=pltpu.CompilerParams(vmem_limit_bytes=32 << 20),
+            pltpu.VMEM((128, WIDE), f32),
+            pltpu.VMEM((CHUNK + 8, CONVW), f32),
+        ],
+        compiler_params=pltpu.CompilerParams(vmem_limit_bytes=52 << 20),
         cost_estimate=pl.CostEstimate(
-            flops=3 << 30, bytes_accessed=12 << 20, transcendentals=4 << 20
+            flops=16 << 30, bytes_accessed=48 << 20, transcendentals=4 << 20
         ),
-        name="scan_forward",
-    )(proj, proj, taps, head, skip)
+        name="front",
+    )(x_all, weights, weights, place, taps, head, skip, *earlier)
 
 
 def scan_backward(chunks, inputs, held, carry, sums, earlier):
-    proj, mixed, d_gated, row_values, starts, taps, head, skip, w_all = inputs
+    proj, mixed, d_o_all, row_values, starts, taps, head, skip, w_all, w_out = inputs
     rows, width = proj.shape
     dim = w_all.shape[0]
     at = lambda step: chunks[1] - 1 - step
     by_chunk = lambda step: (at(step), 0)
-    given = (proj, proj, mixed, d_gated, row_values, starts, taps, head, skip, w_all, carry, sums)
+    given = (proj, proj, mixed, d_o_all, row_values, starts, taps, head, skip, w_all, w_out)
+    given = given + (carry, sums)
     return pl.pallas_call(
         functools.partial(scan_backward_kernel, chunks, len(held) + len(earlier)),
         grid=(chunks[1] - chunks[0],),
@@ -394,13 +400,14 @@
                 (8, width), lambda step: (jnp.maximum(at(step) * (CHUNK // 8) - 1, 0), 0)
             ),
             pl.BlockSpec((CHUNK, WIDE), by_chunk),
-            pl.BlockSpec((CHUNK, WIDE), by_chunk),
+            pl.BlockSpec((CHUNK, d_o_all.shape[1]), by_chunk),
             pl.BlockSpec((CHUNK, row_values.shape[1]), by_chunk),
             pl.BlockSpec((1, 128, WIDE), lambda step: (at(step), 0, 0)),
             whole(taps.shape),
             whole(head.shape),
             whole(skip.shape),
             whole(w_all.shape),
+            whole(w_out.shape),
             whole(carry.shape),
             whole(sums.shape),
             *[pl.BlockSpec(memory_space=pl.ANY) for _ in held],
@@ -426,10 +433,109 @@
         input_output_aliases={len(given) + i: i for i in range(len(held))},
         compiler_params=pltpu.CompilerParams(vmem_limit_bytes=48 << 20),
         cost_estimate=pl.CostEstimate(
-            flops=10 << 30, bytes_accessed=20 << 20, transcendentals=8 << 20
+            flops=(1 << 20) if held else (10 << 30), bytes_accessed=1 << 20, transcendentals=0
         ),
         name="scan_backward",
     )(*given, *held, *earlier)
+
+
+def token_front_kernel(x_ref, out_ref, scale_ref, gain_ref, slots_ref, resid_ref, moe_ref, sent_ref):
+    f32, bf = jnp.float32, jnp.bfloat16
+    resid = x_ref[...].astype(f32) + out_ref[...].astype(f32) * scale_ref[...]
+    resid_ref[...] = resid
+    moe_in = (resid * row_scale(resid) * gain_ref[0:1, :]).astype(bf)
+    moe_ref[...] = moe_in
+    sent_ref[...] = times(slots_ref[...], moe_in).astype(bf)
+
+
+def token_front(x, out_sum, scale, gain, slots):
+    rows, dim = x.shape
+    return pl.pallas_call(
+        token_front_kernel,
+        out_shape=[
+            jax.ShapeDtypeStruct((rows, dim), jnp.float32),
+            jax.ShapeDtypeStruct((rows, dim), jnp.bfloat16),
+            jax.ShapeDtypeStruct((slots.shape[0], dim), jnp.bfloat16),
+        ],
+        compiler_params=pltpu.CompilerParams(vmem_limit_bytes=24 << 20),
+        cost_estimate=pl.CostEstimate(flops=1 << 28, bytes_accessed=5 << 20, transcendentals=0),
+        name="token_front",
+    )(x, out_sum, scale, gain, slots)
+
+
+def token_back_kernel(
+    back_ref, slots_ref, shared_ref, x_ref, resid_ref, gates_ref, router_ref, gain_ref, cot_ref,
+    *refs,
+):
+    f32, bf = jnp.float32, jnp.bfloat16
+    d_o_ref, d_resid_ref, d_logits_ref, d_gain_ref = refs[-4:]
+    dim = x_ref.shape[1]
+    sums = transposed_times(slots_ref[...], back_ref[...])
+    scalars = sums[:, dim:]
+    gates = gates_ref[...]
+    d_gates = scalars + pltpu.roll(scalars, 64, 1)
+    d_logits = gates * (d_gates - jnp.sum(gates * d_gates, axis=1, keepdims=True))
+    d_logits_ref[...] = d_logits
+    high, low = split_two(d_logits)
+    router = router_ref[...]
+    d_moe = (
+        sums[:, :dim]
+        + shared_ref[...].astype(f32)
+        + times_transposed(high, router)
+        + times_transposed(low, router)
+    )
+    resid = resid_ref[...]
+    scale = row_scale(resid)
+    normed = resid * scale
+    d_gain_ref[0:1, :] = jnp.sum(d_moe * normed, axis=0, keepdims=True)
+    d_gain_ref[1:8, :] = jnp.zeros((7, dim), f32)
+    d_scaled = d_moe * gain_ref[0:1, :]
+    mean = jnp.mean(d_scaled * normed, axis=1, keepdims=True)
+    d_resid = cot_ref[...].astype(f32) + scale * (d_scaled - normed * mean)
+    d_resid_ref[...] = d_resid
+    d_o = d_resid.astype(bf)
+    d_o_ref[:, :dim] = d_o
+    added = resid - x_ref[...].astype(f32)
+    kappa = jnp.sum(d_o.astype(f32) * added, axis=1, keepdims=True) * (1.0 / (2 * dim))
+    kappa_high = kappa.astype(bf).astype(f32)
+    lane = lax.broadcasted_iota(jnp.int32, scalars.shape, 1)
+    both = jnp.where(lane == 0, kappa_high, jnp.where(lane == 1, kappa - kappa_high, 0.0))
+    d_o_ref[:, dim:] = both.astype(bf)
+
+
+def token_back(back, slots, shared_both, x, resid, gates, w_all, gain, cot, earlier):
+    rows, dim = x.shape
+    return pl.pallas_call(
+        token_back_kernel,
+        grid=(1,),
+        in_specs=[
+            whole(back.shape),
+            whole(slots.shape),
+            whole((rows, dim)),
+            whole(x.shape),
+            whole(resid.shape),
+            whole(gates.shape),
+            pl.BlockSpec((dim, 128), lambda step: (0, w_all.shape[1] // 128 - 1)),
+            whole(gain.shape),
+            whole(cot.shape),
+            *map(corner_of, earlier),
+        ],
+        out_specs=[
+            whole((rows, dim + 128)),
+            whole((rows, dim)),
+            whole((rows, 128)),
+            whole((8, dim)),
+        ],
+        out_shape=[
+            jax.ShapeDtypeStruct((rows, dim + 128), jnp.bfloat16),
+            jax.ShapeDtypeStruct((rows, dim), jnp.float32),
+            jax.ShapeDtypeStruct((rows, 128), jnp.float32),
+            jax.ShapeDtypeStruct((8, dim), jnp.float32),
+        ],
+        compiler_params=pltpu.CompilerParams(vmem_limit_bytes=32 << 20),
+        cost_estimate=pl.CostEstimate(flops=1 << 29, bytes_accessed=8 << 20, transcendentals=0),
+        name="token_back",
+    )(back, slots, shared_both, x, resid, gates, w_all, gain, cot, *earlier)
 
 
 def expert_early_kernel(cot_ref, down_ref, earlier_ref, raw_ref):
@@ -490,7 +596,7 @@
 
 def expert_late_kernel(
     rows_ref, cot_ref, act_ref, scaled_ref, d_g_ref, d_v_ref, down_ref,
-    out_ref, grads_ref,
+    out_ref, grad_gate_ref, grad_up_ref, grad_down_ref,
 ):
     bf = jnp.bfloat16
     dim = rows_ref.shape[-1]
@@ -498,11 +604,11 @@
     cot = cot_ref[...].reshape(-1, dim)
     out_ref[...] = times(act_ref[0], down_ref[0]).astype(bf).reshape(out_ref.shape)
     units = act_ref.shape[-1]
-    grads_ref[0, :dim] = transposed_times(rows, d_g_ref[0]).astype(bf)
-    grads_ref[0, dim : 2 * dim] = transposed_times(rows, d_v_ref[0]).astype(bf)
+    grad_gate_ref[0] = transposed_times(rows, d_g_ref[0]).astype(bf)
+    grad_up_ref[0] = transposed_times(rows, d_v_ref[0]).astype(bf)
     for block in range(dim // units):
-        at = 2 * dim + block * units
-        grads_ref[0, at : at + units] = transposed_times(
+        at = block * units
+        grad_down_ref[0, at : at + units] = transposed_times(
             scaled_ref[0], cot[:, block * units : block * units + units]
         ).astype(bf)
 
@@ -584,7 +690,7 @@
 def expert_late(rows, cot_rows, act, scaled, d_g, d_v, down):
     sources, local, cap, dim = rows.shape
     units = down.shape[1]
-    grads = (local, 3 * dim, units)
+    grads = (local, dim, units)
     return pl.pallas_call(
         expert_late_kernel,
         grid=(local,),
@@ -594,9 +700,13 @@
         out_specs=[
             expert_slots(rows.shape),
             per_expert(grads),
+            per_expert(grads),
+            per_expert(grads),
         ],
         out_shape=[
             jax.ShapeDtypeStruct(rows.shape, jnp.bfloat16),
+            jax.ShapeDtypeStruct(grads, jnp.bfloat16),
+            jax.ShapeDtypeStruct(grads, jnp.bfloat16),
             jax.ShapeDtypeStruct(grads, jnp.bfloat16),
         ],
         name="expert_late",
@@ -857,18 +967,21 @@
     w_cols = (w_cols.astype(f32) * gain_col).astype(bf)
     used = 2 * gw + keys_w + gh
     small = jnp.concatenate(
-        [conv_weight.reshape(-1), conv_bias, step_bias, decay_log, skip_gain]
-    )
-    small_cols = -(-small.shape[0] // rows_w)
-    small = jnp.pad(small, (0, small_cols * rows_w - small.shape[0])).reshape(rows_w, small_cols)
+        [conv_weight.reshape(-1), conv_bias, step_bias, decay_log, skip_gain, moe_gain]
+    )
+    small_cols = -(-(small.shape[0] - rows_w) // rows_w)
+    at_router = used + small_cols
+    total = -(-(at_router + experts) // 128) * 128
     packed = jnp.concatenate(
-        [w_cols, small, router_weight, moe_gain[:, None]], axis=1
-    )
-    at_small = used
-    at_router = at_small + small_cols
-    at_moe = at_router + experts
-    total = -(-(at_moe + 1) // 128) * 128
-    packed = jnp.pad(packed, ((0, 0), (0, total - packed.shape[1])))
+        [
+            w_cols,
+            jnp.zeros((rows_w, small_cols), bf),
+            router_weight,
+            jnp.zeros((rows_w, total - at_router - experts), bf),
+        ],
+        axis=1,
+    )
+    small_all = lax.all_gather(jnp.pad(small, (0, total - small.shape[0])), "shard", axis=0)
 
     def to_shards(values):
         return lax.all_to_all(values, "shard", split_axis=0, concat_axis=0, tiled=True)
@@ -922,7 +1035,6 @@
         axis=0,
     )
     folded = rows_w + own_out * dim // total
-    w_out = unfold_rows(weights[:, rows_w:folded], dim).reshape(gw, dim)
     second = unfold_rows(weights[:, folded:], dim)
     w_down = second[:, :own_down].reshape(gf, dim)
     w_shared = (
@@ -960,12 +1072,10 @@
     router_lane = at_router - (total - 128)
     lanes = jnp.arange(128, dtype=jnp.int32)
     named_lanes = jnp.pad(named, ((0, 0), (router_lane, 128 - router_lane - experts)))
+    cot_all = gather_rows(after(cot_low, x_all), core, z_at, mates)
     cot_sent = in_slots(jnp.concatenate([cot_low, named_lanes.astype(bf)], axis=1))
     cot_rows = dispatched(cot_sent)
 
-    proj, x_r, w_all = project(x_all, weights, rows_w, cot_sent)
-
-    small_all = weights[:, :rows_w, at_small:at_router].reshape(sh, -1)
     at = taps * conv_own
     conv_full = (
         small_all[:, :at].reshape(sh, taps, conv_own).transpose(1, 0, 2).reshape(taps, conv_all)
@@ -975,8 +1085,9 @@
     bias_full = small_all[:, at : at + head_own].reshape(heads)
     decay_full = small_all[:, at + head_own : at + 2 * head_own].reshape(heads)
     skip_full = small_all[:, at + 2 * head_own : at + 3 * head_own].reshape(heads)
-    router_full = weights[:, :rows_w, at_router:at_moe].reshape(dim, experts)
-    moe_gain_full = weights[:, :rows_w, at_moe].reshape(dim).astype(f32)
+    gain_at = at + 3 * head_own
+    moe_gain_full = small_all[:, gain_at : gain_at + rows_w].reshape(1, dim).astype(f32)
+    moe_gain_rows = jnp.broadcast_to(moe_gain_full, (8, dim))
 
     def group(values, width):
         return lax.dynamic_slice_in_dim(values, q * width, width, values.ndim - 1)
@@ -994,23 +1105,18 @@
     decay_rate = -jnp.exp(decay_local)
     head_in = jnp.pad(jnp.stack([bias_local, decay_rate]), ((0, 6), (0, 128 - gh)))
     skip_in = jnp.broadcast_to(jnp.repeat(skip_local, per_head)[None], (8, gw))
-    mixed, q_low, square_part, starts = scan_forward(proj, taps_in, head_in, skip_in)
-
-    cot_all = lax.all_gather(after(cot_low, w_all), "seq", axis=0, tiled=True)
-    w_out, cot_all = lax.optimization_barrier((w_out, cot_all))
-    out_part = times(q_low, w_out).astype(bf)
+    proj, x_r, w_all, w_out, mixed, q_low, out_part, square_part, starts = front(
+        x_all, weights, rows_w, taps_in, head_in, skip_in, cot_sent, cot_all
+    )
+
     out_sum = lax.psum_scatter(out_part, "seq", scatter_dimension=0, tiled=True)
-    square = lax.psum(after(square_part.reshape(sq, toks), out_part), "seq")
+    square = lax.psum(square_part.reshape(sq, toks), "seq")
     q_r = lax.rsqrt(square / inner + epsilon).reshape(seq_rows, 1)
     d_raw = expert_early(cot_rows, expert_down, square)
     tok_r = after(lax.dynamic_slice_in_dim(q_r, q * toks, toks, 0), d_raw)
     x_tok = x_low.astype(f32)
-    added = out_sum.astype(f32) * tok_r
-    resid = x_tok + added
-
-    resid_r = row_scale(resid)
-    resid_n = resid * resid_r
-    moe_in = (resid_n * moe_gain_full[None, :]).astype(bf)
+    resid, moe_in, moe_sent = token_front(x_low, out_sum, tok_r, moe_gain_rows, dispatch_flat)
+
     moe_all = lax.all_gather(moe_in, "seq", axis=0, tiled=True)
 
     logits = times(moe_in, w_all[:, total - 128 :])
@@ -1018,13 +1124,11 @@
     powers = jnp.where(
         named_lanes > 0.0, jnp.exp(jnp.where(named_lanes > 0.0, logits - top, 0.0)), 0.0
     )
-    gates = (powers / jnp.sum(powers, axis=1, keepdims=True))[
-        :, router_lane : router_lane + experts
-    ]
-    rows = dispatched(in_slots(moe_in))
+    gates = powers / jnp.sum(powers, axis=1, keepdims=True)
+    rows = dispatched(moe_sent.reshape(sh, local_e * CAP, dim))
     own_ids = lax.axis_index("shard") * local_e + jnp.arange(local_e, dtype=jnp.int32)
     marks = jnp.stack(
-        [own_ids + router_lane, own_ids, own_ids + 64] + [jnp.full_like(own_ids, -1)] * 5, axis=1
+        [own_ids + router_lane, own_ids + router_lane, own_ids + router_lane + 64] + [jnp.full_like(own_ids, -1)] * 5, axis=1
     )
     marks = (marks[:, :, None] == lanes[None, None, :]).astype(f32)
 
@@ -1042,10 +1146,9 @@
         w_down,
     )
     shared_both = lax.psum_scatter(both_part, "seq", scatter_dimension=0, tiled=True)
-    d_moe_shared = shared_both[:, :dim]
     shared_sum = shared_both[:, dim:]
     d_returned = to_shards(back_rows.reshape(sh, local_e * CAP, dim + 128))
-    e_out, e_grads = expert_late(rows, cot_rows, e_act, e_scaled, d_g, d_v, expert_down)
+    e_out, *e_grads = expert_late(rows, cot_rows, e_act, e_scaled, d_g, d_v, expert_down)
     d_returned, e_out = lax.optimization_barrier((d_returned, e_out))
     returned = to_shards(e_out.reshape(sh, local_e * CAP, dim))
 
@@ -1053,55 +1156,34 @@
     far = [(i, 2 * (sq // 2 - 1 - i // 2) + i % 2) for i in range(sq)]
     is_inner = ((z_at == 1) | (z_at == 2)).astype(jnp.int32)
     is_high = (z_at >= 2).astype(jnp.int32)
-    e_mine = jnp.concatenate(
-        [
-            halve(e_grads[:, dim * part : dim * part + dim].reshape(local_e * dim, -1), core, mates)
-            for part in range(3)
-        ],
-        axis=0,
-    )
+    e_parts = [halve(part.reshape(-1, part.shape[2]), core, mates) for part in e_grads]
+    e_mine = jnp.concatenate(e_parts, axis=0)
     cutoff = e_mine.shape[0] // 2
 
     grad_down_part = transposed_times(s_act, cot_all).astype(bf)
     grad_shared_part = transposed_times(moe_all, d_both).astype(bf)
-    gates = after(after(gates, grad_down_part), grad_shared_part)
-    d_flat = transposed_times(dispatch_flat, d_returned.reshape(slots, dim + 128))
-    d_gates = d_flat[:, dim : dim + experts] + d_flat[:, dim + 64 : dim + 64 + experts]
-    d_logits = gates * (d_gates - jnp.sum(gates * d_gates, axis=1, keepdims=True))
-    d_moe = (
-        d_flat[:, :dim]
-        + d_moe_shared.astype(f32)
-        + jnp.dot(d_logits, router_full.astype(f32).T, precision=highest)
+    d_o_ext, d_resid, d_logits, d_moe_gain = token_back(
+        d_returned.reshape(slots, dim + 128),
+        dispatch_flat,
+        shared_both,
+        x_low,
+        resid,
+        gates,
+        w_all,
+        moe_gain_rows,
+        cot_low,
+        (grad_down_part, grad_shared_part, *e_parts),
     )
     grad_router = jnp.dot(moe_in.astype(f32).T, d_logits, precision=highest)
-    grad_moe = jnp.sum(d_moe * resid_n, axis=0)
-    d_scaled = d_moe * moe_gain_full[None, :]
-    d_resid = (
-        cot
-        + d_scaled * resid_r
-        - resid_n * (resid_r * jnp.mean(d_scaled * resid_n, axis=1, keepdims=True))
-    )
-    d_o = d_resid.astype(bf)
-    kappa = jnp.sum(d_o.astype(f32) * added, axis=1) / inner
-    for start in range(0, e_mine.shape[0], dim):
-        kappa = after(kappa, e_mine[start:])
-    kappa_high = kappa.astype(bf)
-    kappa_low = (kappa - kappa_high.astype(f32)).astype(bf)
-    d_o_ext = jnp.concatenate(
-        [d_o, kappa_high[:, None], kappa_low[:, None], jnp.zeros((toks, 126), bf)], axis=1
-    )
+    grad_router = grad_router + jnp.pad(d_moe_gain[0][:, None], ((0, 0), (0, 127)))
     d_o_all = lax.all_gather(d_o_ext, "seq", axis=0, tiled=True)
-    kappa_all = jnp.sum(d_o_all[:, dim : dim + 2].astype(f32), axis=1, keepdims=True)
-
-    d_gated = times_transposed(d_o_all, jnp.pad(w_out, ((0, 0), (0, 128))))
+
     grad_out_part = transposed_times(q_low, (q_r * d_o_all[:, :dim].astype(f32)).astype(bf))
 
     mid_part = jnp.concatenate(
         [
             grad_shared_part,
             grad_router.astype(bf),
-            grad_moe[:, None].astype(bf),
-            jnp.zeros((dim, 128 - experts - 1), bf),
         ],
         axis=1,
     )
@@ -1126,9 +1208,9 @@
     e_one = halve(e_mine[:cutoff], is_inner, near, d_o_all)
     e_two = halve(e_mine[cutoff:], is_high, far, d_o_all)
     row_values = jnp.concatenate(
-        [q_r, kappa_all, x_r, jnp.zeros((seq_rows, 5), f32)], axis=1
-    )
-    scan_inputs = (proj, mixed, d_gated, row_values, starts, taps_in, head_in, skip_in, w_all)
+        [q_r, x_r, jnp.zeros((seq_rows, 6), f32)], axis=1
+    )
+    scan_inputs = (proj, mixed, d_o_all, row_values, starts, taps_in, head_in, skip_in, w_all, w_out)
     chunks = seq_rows // CHUNK
     middle = chunks // 2
     *held, carry, sums = scan_backward(
@@ -1150,7 +1232,8 @@
     grad_skip_local = jnp.sum(d_skip[0].reshape(gh, per_head), axis=1)
     e_one, e_two = halve(e_one, is_high, far), halve(e_two, is_inner, near)
     back_sum = lax.psum_scatter(back_part, "seq", scatter_dimension=0, tiled=True).astype(f32)
-    weighted = (gates.T[:, None, :] * dispatch.astype(f32)).reshape(slots, toks)
+    route_gates = gates[:, router_lane : router_lane + experts]
+    weighted = (route_gates.T[:, None, :] * dispatch.astype(f32)).reshape(slots, toks)
     combined = transposed_times(weighted.astype(bf), returned.reshape(slots, dim))
     block_output = ((resid + shared_sum.astype(f32) + combined) * live[:, None]).astype(bf)[None]
     tok_x_r = row_scale(x_tok)
@@ -1216,8 +1299,8 @@
         mid_sums,
     ) = assemble(side, in_weight, gain_col, out_weight, gain_out, own_out, own_down)
     grad_norm = norm_sums[:, 0]
-    grad_router_weight = mid_sums[:, :experts]
-    grad_moe_gain = mid_sums[:, experts]
+    grad_router_weight = mid_sums[:, router_lane : router_lane + experts]
+    grad_moe_gain = mid_sums[:, 0]
     grad_mixer_gain = tail_sums[:, 0]
     lane_at = used - (total - 128)
     small_sum = tail_sums[:, lane_at : lane_at + small_cols].reshape(-1)

time: 569 us -> 567 us (level)
  waiting for transfers between devices: 170 us -> 144 us
  starting transfers between devices: 71.2 us -> 87 us
  blocking collectives: 14 us -> 29.7 us
  Pallas kernels: 108 us -> 120 us
  matrix products: 38.1 us -> 28 us
    all_gather x1, waiting for transfers between devices: 27.6 us -> 0.01 us  [on_device(): lax.all_gather(jnp.concatenate([packed, fold_rows(piece[:own_out], total)...]
    all_gather x0 -> x1, blocking collectives: none -> 17.9 us  [on_device(): lax.all_gather(jnp.pad(small, (0, total - small.shape[0])), 'shard', axis=0)]
    unnamed x164 -> x215, local copies, waits for them, and re-layouts: 26.9 us -> 43 us
    pallas_call x2 -> x3, Pallas kernels: 19 us -> 28 us  [the longest x1 23.1 us: front(): pl.pallas_call(front_kernel, grid=(rows // tile,), in_specs=[pl.BlockSpec...]
    slice x4 -> x2, local copies, waits for them, and re-layouts: 8.15 us -> 0.71 us  [the longest x1 0.63 us: on_device(): grad_moe_gain = mid_sums[:, 0]]
    dot_general x4 -> x2, matrix products: 12.5 us -> 5.17 us  [times(): return jnp.dot(left, right, preferred_element_type=jnp.float32)]
    ppermute x3 -> x6, starting transfers between devices: 6.37 us -> 13.4 us  [gather_rows(): column.append(lax.ppermute(values, 'seq', pairs))]
    ppermute x3 -> x6, waiting for transfers between devices: 16.2 us -> 19.9 us  [gather_rows(): column.append(lax.ppermute(values, 'seq', pairs))]
  transfers between devices with their start and end apart: 32 -> 35, of which waited for: 14 -> 16; matrix products, arithmetic and copies ran while one was open for 23% -> 20% of each run, Pallas kernels for 14% -> 17%
where the time goes in v8:
time: 567 us; the launch traced here: 559 us
  waiting for transfers between devices  144 us (25%)
  Pallas kernels  120 us (21%)
  starting transfers between devices  87 us (15%)
  local copies, waits for them, and re-layouts  72.6 us (13%)
  other arithmetic  57 us (10%)
  blocking collectives  29.7 us (5%)
  matrix products  28 us (5%)
  between operations  20.8 us (4%)
    unnamed x215, local copies, waits for them, and re-layouts  43 us
    all_to_all x6, starting transfers between devices, to_shards(): lax.all_to_all(values, 'shard', split_axis=0, concat_axis=0, tiled=True)  39.6 us
    all_to_all x6, waiting for transfers between devices, to_shards(): lax.all_to_all(values, 'shard', split_axis=0, concat_axis=0, tiled=True)  38.1 us
    pallas_call x2, Pallas kernels, scan_backward(): pl.pallas_call(functools.partial(scan_backward_kernel, chunks, len(held)...  37.9 us
    all_gather x1, waiting for transfers between devices, on_device(): d_o_all = lax.all_gather(d_o_ext, 'seq', axis=0, tiled=True)  34.2 us
    pallas_call x1, Pallas kernels, front(): pl.pallas_call(front_kernel, grid=(rows // tile,), in_specs=[pl.BlockSpec...  23.1 us
    dot_general x5, matrix products, transposed_times(): lax.dot_general(left, right, (((0,), (0,)), ((), ())), preferred_element_...  21.1 us
    ppermute x6, waiting for transfers between devices, gather_rows(): column.append(lax.ppermute(values, 'seq', pairs))  19.9 us
  transfers between devices with their start and end apart: 35, of which 16 were waited for; matrix products, arithmetic and copies ran while one was open for 20% of the time, Pallas kernels for 17%

profile of v8, /device:TPU:1, one launch (start us, length us, event | category | flops | bytes accessed | tf_op | source)
XLA Modules:
  0.0 558.9 jit_solution(17399983958419508618)
XLA Ops:
  9.2 4.6 collective-permute-start.4
  20.5 8.6 %collective-permute-start.2 = (bf16[128,1536]{1,0:T(8,128)(2,1)S(1)}, bf16[128,1536]{1,0:T(8,128)(2,1)S(1)}, u32[]{:S(2)}, u32[]{:S(2)}) collective-permute-start(bf16[128,1536]{1,0:T(8,128)(2,1)S(1)} %bitcast.195), channel_id=1, source_target_pairs={{0,96},{16,112},{32,0},{48,16},{64,32},{80,48},{96,64},{112,80},{1... | collective-permute-start | bytes 1179656 | tf_op jit(solution)/shard_map/ppermute | solution.py:828
  30.0 17.9 %all-gather.3 = bf16[16,1,1152]{2,1,0:T(2,128)(2,1)S(1)} all-gather(bf16[1,1,1152]{2,1,0:T(2,128)(2,1)S(1)} %reshape.962), channel_id=3, replica_groups=mesh['seq'=8,'shard'=16] {'shard'}, dimensions={0}, use_global_device_ids=true | all-gather | bytes 39168 | tf_op jit(solution)/shard_map/all_gather | solution.py:984
  51.2 4.8 collective-permute-start.3
  67.9 6.7 %collective-permute-done.7 = bf16[128,1536]{1,0:T(8,128)(2,1)S(1)} collective-permute-done((bf16[128,1536]{1,0:T(8,128)(2,1)S(1)}, bf16[128,1536]{1,0:T(8,128)(2,1)S(1)}, u32[]{:S(2)}, u32[]{:S(2)}) %collective-permute-start.7) | collective-permute-done | bytes 393248 | tf_op jit(solution)/shard_map/ppermute | solution.py:828
  76.6 9.4 %collective-permute-done.5 = bf16[128,1536]{1,0:T(8,128)(2,1)S(1)} collective-permute-done((bf16[128,1536]{1,0:T(8,128)(2,1)S(1)}, bf16[128,1536]{1,0:T(8,128)(2,1)S(1)}, u32[]{:S(2)}, u32[]{:S(2)}) %collective-permute-start.5) | collective-permute-done | bytes 393248 | tf_op jit(solution)/shard_map/ppermute | solution.py:828
  94.3 4.5 all-to-all-start
  110.9 23.1 %front.1 = (f32[1024,1152]{1,0:T(8,128)}, f32[1024,1]{1,0:T(8,128)S(1)}, bf16[1536,1152]{1,0:T(8,128)(2,1)}, bf16[384,1536]{1,0:T(8,128)(2,1)}, bf16[1024,384]{1...) custom-call(bf16[1024,1536]{1,0:T(8,128)(2,1)} %copy-done.68, ...), custom_call_target="tpu_custom_call" | custom-call | flops 17179869184 | bytes 50331648 | tf_op jit(solution)/shard_map/front/pallas_call | solution.py:339
  136.0 11.8 %psum.7.earlier_ref = f32[8,128]{1,0:T(8,128)S(1)} all-reduce(f32[8,128]{1,0:T(8,128)S(1)} %bitcast.257), channel_id=1, replica_groups=mesh['seq'=8,'shard'=16] {'seq'}, use_global_device_ids=true, to_apply=%region_2.3 | all-reduce | flops 1024 | bytes 8192 | tf_op jit(solution)/shard_map/psum | solution.py:1113
  148.6 5.0 expert_early.1.raw_ref
  155.4 12.7 %reduce-scatter.4.cloned.1.call-done.out_ref = bf16[128,1536]{1,0:T(8,128)(2,1)} async-done(((bf16[1024,1536]{1,0:T(8,128)(2,1)}), bf16[128,1536]{1,0:T(8,128)(2,1)}) %reduce-scatter.4.cloned.1.call-update) | async-done | bytes 393232 | tf_op jit(solution)/shard_map/reduce_scatter | solution.py:1112
  173.1 6.8 %all-to-all-start.1 = ((bf16[16,64,1536]{2,1,0:T(8,128)(2,1)}), bf16[16,64,1536]{2,1,0:T(8,128)(2,1)}, u32[]{:S(2)}, u32[]{:S(2)}) async-start(bf16[16,64,1536]{2,1,0:T(8,128)(2,1)} %bitcast.205), calls=%async_computation.2 | async-start | bytes 6291456 | tf_op jit(solution)/shard_map/all_to_all | solution.py:987
  186.1 29.3 %all-to-all-done.1 = bf16[16,64,1536]{2,1,0:T(8,128)(2,1)} async-done(((bf16[16,64,1536]{2,1,0:T(8,128)(2,1)}), bf16[16,64,1536]{2,1,0:T(8,128)(2,1)}, u32[]{:S(2)}, u32[]{:S(2)}) %all-to-all-start.1) | async-done | bytes 3145760 | tf_op jit(solution)/shard_map/all_to_all | solution.py:987
  215.4 19.3 %expert_main.1 = (bf16[16,2,32,1664]{3,2,1,0:T(8,128)(2,1)}, bf16[2,512,512]{2,1,0:T(8,128)(2,1)}, bf16[2,512,512]{2,1,0:T(8,128)(2,1)}, bf16[2,512,512]{2,1,0:T...) custom-call(bf16[16,2,32,1536]{3,2,1,0:T(8,128)(2,1)} %bitcast.44.ro, ...), custom_call_target="tpu_custom_call" | custom-call | flops 8589934592 | bytes 20971520 | tf_op jit(solution)/shard_map/expert_main/pallas_call | solution.py:660
  239.2 9.4 %all-to-all-start.2 = ((bf16[16,64,1664]{2,1,0:T(8,128)(2,1)}), bf16[16,64,1664]{2,1,0:T(8,128)(2,1)}, u32[]{:S(2)}, u32[]{:S(2)}) async-start(bf16[16,64,1664]{2,1,0:T(8,128)(2,1)} %bitcast.232), calls=%async_computation.4 | async-start | bytes 6815744 | tf_op jit(solution)/shard_map/all_to_all | solution.py:987
  248.6 12.6 %expert_late.1 = (bf16[16,2,32,1536]{3,2,1,0:T(8,128)(2,1)}, bf16[2,1536,512]{2,1,0:T(8,128)(2,1)}, bf16[2,1536,512]{2,1,0:T(8,128)(2,1)}, bf16[2,1536,512]{2,1,0:T(8,128)(2,1)}) custom-call(bf16[16,2,32,1536]{3,2,1,0:T(8,128)(2,1)} %bitcast.44.rows_ref, bf16[16,2,32,1664]{3,2,1,0:T(8,128)(2,1)} %bitcast.41.cot_ref.routed_ref, ...), custom_call_target="tpu_custom_call" | custom-call | flops 7516192768 | bytes 25165824 | tf_op jit(solution)/shard_map/expert_late/pallas_call | solution.py:694
  279.0 7.7 %all-to-all-done.2 = bf16[16,64,1664]{2,1,0:T(8,128)(2,1)} async-done(((bf16[16,64,1664]{2,1,0:T(8,128)(2,1)}), bf16[16,64,1664]{2,1,0:T(8,128)(2,1)}, u32[]{:S(2)}, u32[]{:S(2)}) %all-to-all-start.2) | async-done | bytes 3407904 | tf_op jit(solution)/shard_map/all_to_all | solution.py:987
  310.9 4.0 pad_maximum_fusion.3
  315.0 6.7 %all-to-all-start.3 = ((bf16[16,64,1536]{2,1,0:T(8,128)(2,1)}), bf16[16,64,1536]{2,1,0:T(8,128)(2,1)}, u32[]{:S(2)}, u32[]{:S(2)}) async-start(bf16[16,64,1536]{2,1,0:T(8,128)(2,1)} %bitcast.233), calls=%async_computation.5 | async-start | bytes 6291456 | tf_op jit(solution)/shard_map/all_to_all | solution.py:987
  325.5 34.2 %all-gather.11.cloned.1.call-done.d_o_ref = bf16[1024,1664]{1,0:T(8,128)(2,1)} async-done(((bf16[128,1664]{1,0:T(8,128)(2,1)}), bf16[1024,1664]{1,0:T(8,128)(2,1)}) %all-gather.11.cloned.1.call-update) | async-done | bytes 3407888 | tf_op jit(solution)/shard_map/all_gather | solution.py:1179
  372.9 19.0 %scan_backward.2 = (bf16[1024,1152]{1,0:T(8,128)(2,1)}, bf16[1024,1536]{1,0:T(8,128)(2,1)}, f32[136,640]{1,0:T(8,128)S(1)}, f32[24,640]{1,0:T(8,128)S(1)}) custom-call(f32[1024,1152]{1,0:T(8,128)} %get-tuple-element.90.proj_ref.prev_ref, f32[1024,1152]{1,0:T(8,128)} %get-tuple-element.90.proj_ref.prev_ref, bf16[1024,384]{1,0:T(8,128)(2,1)S(1)} %copy-done.31, ...), custom_call_target="tpu_custom_call" | custom-call | flops 10737418240 | bytes 1048576 | tf_op jit(solution)/shard_map/scan_backward/pallas_call | solution.py:394
  392.3 6.6 %all-to-all-start.4 = ((bf16[16,224,384]{2,1,0:T(8,128)(2,1)}), bf16[16,224,384]{2,1,0:T(8,128)(2,1)}, u32[]{:S(2)}, u32[]{:S(2)}) async-start(bf16[16,224,384]{2,1,0:T(8,128)(2,1)} %copy-done.49), calls=%async_computation.7 | async-start | bytes 5505024 | tf_op jit(solution)/shard_map/all_to_all | solution.py:987
  401.1 18.9 %scan_backward.3 = (bf16[1024,1152]{1,0:T(8,128)(2,1)}, bf16[1024,1536]{1,0:T(8,128)(2,1)}, f32[136,640]{1,0:T(8,128)}, f32[24,640]{1,0:T(8,128)S(1)}) custom-call(f32[1024,1152]{1,0:T(8,128)} %get-tuple-element.90.proj_ref.prev_ref, f32[1024,1152]{1,0:T(8,128)} %get-tuple-element.90.proj_ref.prev_ref, ...), custom_call_target="tpu_custom_call", output_to_operand_aliasing={{0}: (13, {}), {1}: (14, {})} | custom-call | flops 1048576 | bytes 1048576 | tf_op jit(solution)/shard_map/scan_backward/pallas_call | solution.py:394
  425.3 8.7 %convolution_convert_fusion = bf16[1536,1152]{1,0:T(8,128)(2,1)} fusion(bf16[1024,1536]{1,0:T(8,128)(2,1)} %copy-done.68, bf16[1024,1152]{1,0:T(8,128)(2,1)} %get-tuple-element.104), kind=kOutput, calls=%fused_computation | convolution fusion | flops 3625648128 | bytes 9043968 | tf_op jit(solution)/shard_map/dot_general | solution.py:29
  441.5 5.5 all-to-all-start.5
  449.6 10.2 %collective-permute-done.16 = bf16[576,512]{1,0:T(8,128)(2,1)S(1)} collective-permute-done((bf16[576,512]{1,0:T(8,128)(2,1)S(1)}, bf16[576,512]{1,0:T(8,128)(2,1)S(1)}, u32[]{:S(2)}, u32[]{:S(2)}) %collective-permute-start.16) | collective-permute-done | bytes 589856 | tf_op jit(solution)/shard_map/ppermute | solution.py:852
  461.0 6.7 %collective-permute-done.19 = bf16[576,512]{1,0:T(8,128)(2,1)} collective-permute-done((bf16[576,512]{1,0:T(8,128)(2,1)S(1)}, bf16[576,512]{1,0:T(8,128)(2,1)}, u32[]{:S(2)}, u32[]{:S(2)}) %collective-permute-start.19) | collective-permute-done | bytes 589856 | tf_op jit(solution)/shard_map/ppermute | solution.py:852
  473.5 8.8 %collective-permute-start.14 = (bf16[128,384]{1,0:T(8,128)(2,1)S(1)}, bf16[128,384]{1,0:T(8,128)(2,1)S(1)}, u32[]{:S(2)}, u32[]{:S(2)}) collective-permute-start(bf16[128,384]{1,0:T(8,128)(2,1)S(1)} %slice.389), channel_id=1, source_target_pairs={{0,0},{1,16},{2,32},{3,48},{4,64},{5,80},{6,96},{7,112},{8,1},{9,1... | collective-permute-start | bytes 294920 | tf_op jit(solution)/shard_map/ppermute | solution.py:1271
  482.3 11.1 %collective-permute-done.14 = bf16[128,384]{1,0:T(8,128)(2,1)S(1)} collective-permute-done((bf16[128,384]{1,0:T(8,128)(2,1)S(1)}, bf16[128,384]{1,0:T(8,128)(2,1)S(1)}, u32[]{:S(2)}, u32[]{:S(2)}) %collective-permute-start.14) | collective-permute-done | bytes 98336 | tf_op jit(solution)/shard_map/ppermute | solution.py:1271
  508.6 3.8 pad_maximum_fusion.own_ref
  523.3 14.3 %unpack_expert_grads.1 = (f32[2,1536,512]{2,1,0:T(8,128)}, f32[2,1536,512]{2,1,0:T(8,128)}, f32[2,512,1536]{2,1,0:T(8,128)}) custom-call(s32[1]{0:T(128)} %bitcast.93.core_ref, bf16[4608,512]{1,0:T(8,128)(2,1)} %pad_maximum_fusion.own_ref, bf16[4608,512]{1,0:T(8,128)(2,1)} %collective-permute-done.21.other_ref), custom_call_target="tpu_custom_call" | custom-call | flops 1048576 | bytes 29360128 | tf_op jit(solution)/shard_map/unpack_expert_grads/pallas_call | solution.py:881
  537.6 4.3 all-gather.15.cloned.1.call-done
  (468 shorter events, 180.9 us)
Async XLA Ops:
  7.3 103.6 %all-gather.13.cloned.1.call-start = ((), (), s32[]{:S(2)}) async-start(), calls=%async_computation.14 | async-start | bytes 6266880 | tf_op jit(solution)/shard_map/all_gather | solution.py:1025
  9.2 10.4 %collective-permute-start.4 = (bf16[32,1536]{1,0:T(8,128)(2,1)S(1)}, bf16[32,1536]{1,0:T(8,128)(2,1)S(1)}, u32[]{:S(2)}, u32[]{:S(2)}) collective-permute-start(bf16[32,1536]{1,0:T(8,128)(2,1)S(1)} %pad_maximum_fusion.11), channel_id=1, source_target_pairs={{0,0},{16,1},{32,2},{48,3},{64,4},{80,5},{96,6},{112,7},{1,8},{17,... | collective-permute-start | bytes 294920 | tf_op jit(solution)/shard_map/ppermute | solution.py:1011
  20.5 27.5 %collective-permute-start.2 = (bf16[128,1536]{1,0:T(8,128)(2,1)S(1)}, bf16[128,1536]{1,0:T(8,128)(2,1)S(1)}, u32[]{:S(2)}, u32[]{:S(2)}) collective-permute-start(bf16[128,1536]{1,0:T(8,128)(2,1)S(1)} %bitcast.195), channel_id=1, source_target_pairs={{0,96},{16,112},{32,0},{48,16},{64,32},{80,48},{96,64},{112,80},{1... | collective-permute-start | bytes 1179656 | tf_op jit(solution)/shard_map/ppermute | solution.py:828
  29.1 18.9 %collective-permute-start.1 = (bf16[128,1536]{1,0:T(8,128)(2,1)S(1)}, bf16[128,1536]{1,0:T(8,128)(2,1)S(1)}, u32[]{:S(2)}, u32[]{:S(2)}) collective-permute-start(bf16[128,1536]{1,0:T(8,128)(2,1)S(1)} %bitcast.196), channel_id=1, source_target_pairs={{0,64},{16,80},{32,96},{48,112},{64,0},{80,16},{96,32},{112,48},{1... | collective-permute-start | bytes 1179656 | tf_op jit(solution)/shard_map/ppermute | solution.py:828
  29.1 20.7 %collective-permute-start = (bf16[128,1536]{1,0:T(8,128)(2,1)S(1)}, bf16[128,1536]{1,0:T(8,128)(2,1)S(1)}, u32[]{:S(2)}, u32[]{:S(2)}) collective-permute-start(bf16[128,1536]{1,0:T(8,128)(2,1)S(1)} %bitcast.197), channel_id=1, source_target_pairs={{0,32},{16,48},{32,64},{48,80},{64,96},{80,112},{96,0},{112,16},{1... | collective-permute-start | bytes 1179656 | tf_op jit(solution)/shard_map/ppermute | solution.py:828
  63.0 11.6 %collective-permute-start.7 = (bf16[128,1536]{1,0:T(8,128)(2,1)S(1)}, bf16[128,1536]{1,0:T(8,128)(2,1)S(1)}, u32[]{:S(2)}, u32[]{:S(2)}) collective-permute-start(bf16[128,1536]{1,0:T(8,128)(2,1)S(1)} %get-tuple-element.216), channel_id=1, source_target_pairs={{0,96},{16,112},{32,0},{48,16},{64,32},{80,48},{96,64},{112,80},{1... | collective-permute-start | bytes 1179656 | tf_op jit(solution)/shard_map/ppermute | solution.py:828
  65.0 11.6 %collective-permute-start.6 = (bf16[128,1536]{1,0:T(8,128)(2,1)S(1)}, bf16[128,1536]{1,0:T(8,128)(2,1)S(1)}, u32[]{:S(2)}, u32[]{:S(2)}) collective-permute-start(bf16[128,1536]{1,0:T(8,128)(2,1)S(1)} %get-tuple-element.216), channel_id=1, source_target_pairs={{0,64},{16,80},{32,96},{48,112},{64,0},{80,16},{96,32},{112,48},{1... | collective-permute-start | bytes 1179656 | tf_op jit(solution)/shard_map/ppermute | solution.py:828
  67.1 18.9 %collective-permute-start.5 = (bf16[128,1536]{1,0:T(8,128)(2,1)S(1)}, bf16[128,1536]{1,0:T(8,128)(2,1)S(1)}, u32[]{:S(2)}, u32[]{:S(2)}) collective-permute-start(bf16[128,1536]{1,0:T(8,128)(2,1)S(1)} %get-tuple-element.216), channel_id=1, source_target_pairs={{0,32},{16,48},{32,64},{48,80},{64,96},{80,112},{96,0},{112,16},{1... | collective-permute-start | bytes 1179656 | tf_op jit(solution)/shard_map/ppermute | solution.py:828
  87.4 11.7 %collective-permute-start.8 = (bf16[4,128,1536]{2,1,0:T(8,128)(2,1)}, bf16[4,128,1536]{2,1,0:T(8,128)(2,1)}, u32[]{:S(2)}, u32[]{:S(2)}) collective-permute-start(bf16[4,128,1536]{2,1,0:T(8,128)(2,1)} %get-tuple-element.232), channel_id=1, source_target_pairs={{0,16},{16,0},{32,48},{48,32},{64,80},{80,64},{96,112},{112,96},{1... | collective-permute-start | bytes 4718600 | tf_op jit(solution)/shard_map/ppermute | solution.py:830
  94.3 54.3 %all-to-all-start = ((bf16[16,64,1664]{2,1,0:T(8,128)(2,1)}), bf16[16,64,1664]{2,1,0:T(8,128)(2,1)}, u32[]{:S(2)}, u32[]{:S(2)}) async-start(bf16[16,64,1664]{2,1,0:T(8,128)(2,1)} %bitcast.207), calls=%async_computation.1 | async-start | bytes 6815744 | tf_op jit(solution)/shard_map/all_to_all | solution.py:987
  98.8 69.3 %reduce-scatter.4.cloned.1.call-start = ((), (), s32[]{:S(2)}) async-start(), calls=%async_computation.9 | async-start | bytes 3538944 | tf_op jit(solution)/shard_map/reduce_scatter | solution.py:1112
  135.8 79.7 %all-gather.9.cloned.1.call-start = ((), (), s32[]{:S(2)}) async-start(), calls=%async_computation.10 | async-start | bytes 3538944 | tf_op jit(solution)/shard_map/all_gather | solution.py:1120
  173.1 42.4 %all-to-all-start.1 = ((bf16[16,64,1536]{2,1,0:T(8,128)(2,1)}), bf16[16,64,1536]{2,1,0:T(8,128)(2,1)}, u32[]{:S(2)}, u32[]{:S(2)}) async-start(bf16[16,64,1536]{2,1,0:T(8,128)(2,1)} %bitcast.205), calls=%async_computation.2 | async-start | bytes 6291456 | tf_op jit(solution)/shard_map/all_to_all | solution.py:987
  179.9 109.0 %reduce-scatter.6.cloned.1.call-start = ((), (), s32[]{:S(2)}) async-start(), calls=%async_computation.11 | async-start | bytes 7077888 | tf_op jit(solution)/shard_map/reduce_scatter | solution.py:1148
  239.2 47.5 %all-to-all-start.2 = ((bf16[16,64,1664]{2,1,0:T(8,128)(2,1)}), bf16[16,64,1664]{2,1,0:T(8,128)(2,1)}, u32[]{:S(2)}, u32[]{:S(2)}) async-start(bf16[16,64,1664]{2,1,0:T(8,128)(2,1)} %bitcast.232), calls=%async_computation.4 | async-start | bytes 6815744 | tf_op jit(solution)/shard_map/all_to_all | solution.py:987
  248.6 111.2 %all-gather.11.cloned.1.call-start = ((), (), s32[]{:S(2)}) async-start(), calls=%async_computation.12 | async-start | bytes 3833856 | tf_op jit(solution)/shard_map/all_gather | solution.py:1179
  263.0 11.2 %collective-permute-start.11 = (bf16[1536,512]{1,0:T(8,128)(2,1)S(1)}, bf16[1536,512]{1,0:T(8,128)(2,1)S(1)}, u32[]{:S(2)}, u32[]{:S(2)}) collective-permute-start(bf16[1536,512]{1,0:T(8,128)(2,1)S(1)} %dynamic-slice_bitcast_fusion), channel_id=1, source_target_pairs={{0,16},{16,0},{32,48},{48,32},{64,80},{80,64},{96,112},{112,96},{1... | collective-permute-start | bytes 4718600 | tf_op jit(solution)/shard_map/ppermute | solution.py:847
  315.0 77.3 %all-to-all-start.3 = ((bf16[16,64,1536]{2,1,0:T(8,128)(2,1)}), bf16[16,64,1536]{2,1,0:T(8,128)(2,1)}, u32[]{:S(2)}, u32[]{:S(2)}) async-start(bf16[16,64,1536]{2,1,0:T(8,128)(2,1)} %bitcast.233), calls=%async_computation.5 | async-start | bytes 6291456 | tf_op jit(solution)/shard_map/all_to_all | solution.py:987
  363.2 28.8 %collective-permute-start.12 = (bf16[1152,512]{1,0:T(8,128)(2,1)S(1)}, bf16[1152,512]{1,0:T(8,128)(2,1)S(1)}, u32[]{:S(2)}, u32[]{:S(2)}) collective-permute-start(bf16[1152,512]{1,0:T(8,128)(2,1)S(1)} %fusion.13), channel_id=1, source_target_pairs={{0,32},{16,48},{32,0},{48,16},{64,96},{80,112},{96,64},{112,80},{1... | collective-permute-start | bytes 3538952 | tf_op jit(solution)/shard_map/ppermute | solution.py:847
  364.6 34.4 %collective-permute-start.13 = (bf16[1152,512]{1,0:T(8,128)(2,1)}, bf16[1152,512]{1,0:T(8,128)(2,1)}, u32[]{:S(2)}, u32[]{:S(2)}) collective-permute-start(bf16[1152,512]{1,0:T(8,128)(2,1)} %fusion.14), channel_id=1, source_target_pairs={{0,96},{16,112},{32,64},{48,80},{64,32},{80,48},{96,0},{112,16},{1... | collective-permute-start | bytes 3538952 | tf_op jit(solution)/shard_map/ppermute | solution.py:847
  392.3 42.7 %all-to-all-start.4 = ((bf16[16,224,384]{2,1,0:T(8,128)(2,1)}), bf16[16,224,384]{2,1,0:T(8,128)(2,1)}, u32[]{:S(2)}, u32[]{:S(2)}) async-start(bf16[16,224,384]{2,1,0:T(8,128)(2,1)} %copy-done.49), calls=%async_computation.7 | async-start | bytes 5505024 | tf_op jit(solution)/shard_map/all_to_all | solution.py:987
  398.9 105.7 %reduce-scatter.8.cloned.1.call-start = ((), (), s32[]{:S(2)}) async-start(), calls=%async_computation.13 | async-start | bytes 3538944 | tf_op jit(solution)/shard_map/reduce_scatter | solution.py:1234
  420.9 17.9 %collective-permute-start.15 = (bf16[576,512]{1,0:T(8,128)(2,1)}, bf16[576,512]{1,0:T(8,128)(2,1)}, u32[]{:S(2)}, u32[]{:S(2)}) collective-permute-start(bf16[576,512]{1,0:T(8,128)(2,1)} %dynamic-slice_bitcast_fusion.4), channel_id=1, source_target_pairs={{0,96},{16,112},{32,64},{48,80},{64,32},{80,48},{96,0},{112,16},{1... | collective-permute-start | bytes 1769480 | tf_op jit(solution)/shard_map/ppermute | solution.py:847
  422.9 24.3 %collective-permute-start.18 = (bf16[576,512]{1,0:T(8,128)(2,1)}, bf16[576,512]{1,0:T(8,128)(2,1)}, u32[]{:S(2)}, u32[]{:S(2)}) collective-permute-start(bf16[576,512]{1,0:T(8,128)(2,1)} %dynamic-slice_bitcast_fusion.3), channel_id=1, source_target_pairs={{0,32},{16,48},{32,0},{48,16},{64,96},{80,112},{96,64},{112,80},{1... | collective-permute-start | bytes 1769480 | tf_op jit(solution)/shard_map/ppermute | solution.py:847
  440.0 19.8 %collective-permute-start.16 = (bf16[576,512]{1,0:T(8,128)(2,1)S(1)}, bf16[576,512]{1,0:T(8,128)(2,1)S(1)}, u32[]{:S(2)}, u32[]{:S(2)}) collective-permute-start(bf16[576,512]{1,0:T(8,128)(2,1)S(1)} %add_convert_fusion.5), channel_id=1, source_target_pairs={{0,96},{16,112},{32,64},{48,80},{64,32},{80,48},{96,0},{112,16},{1... | collective-permute-start | bytes 1769480 | tf_op jit(solution)/shard_map/ppermute | solution.py:852
  441.5 60.5 %all-to-all-start.5 = ((bf16[16,96,1152]{2,1,0:T(8,128)(2,1)}), bf16[16,96,1152]{2,1,0:T(8,128)(2,1)}, u32[]{:S(2)}, u32[]{:S(2)}) async-start(bf16[16,96,1152]{2,1,0:T(8,128)(2,1)} %bitcast.206), calls=%async_computation.8 | async-start | bytes 7077888 | tf_op jit(solution)/shard_map/all_to_all | solution.py:987
  447.1 94.9 %all-gather.15.cloned.1.call-start = ((), (), s32[]{:S(2)}) async-start(), calls=%async_computation.15 | async-start | bytes 3538944 | tf_op jit(solution)/shard_map/all_gather | solution.py:1281
  448.4 19.3 %collective-permute-start.19 = (bf16[576,512]{1,0:T(8,128)(2,1)S(1)}, bf16[576,512]{1,0:T(8,128)(2,1)}, u32[]{:S(2)}, u32[]{:S(2)}) collective-permute-start(bf16[576,512]{1,0:T(8,128)(2,1)S(1)} %add_convert_fusion.4), channel_id=1, source_target_pairs={{0,32},{16,48},{32,0},{48,16},{64,96},{80,112},{96,64},{112,80},{1... | collective-permute-start | bytes 1769480 | tf_op jit(solution)/shard_map/ppermute | solution.py:852
  461.0 33.1 %collective-permute-start.17 = (bf16[1152,512]{1,0:T(8,128)(2,1)}, bf16[1152,512]{1,0:T(8,128)(2,1)}, u32[]{:S(2)}, u32[]{:S(2)}) collective-permute-start(bf16[1152,512]{1,0:T(8,128)(2,1)} %pad_maximum_fusion.8), channel_id=1, source_target_pairs={{0,32},{16,48},{32,0},{48,16},{64,96},{80,112},{96,64},{112,80},{1... | collective-permute-start | bytes 3538952 | tf_op jit(solution)/shard_map/ppermute | solution.py:852
  469.9 27.2 %collective-permute-start.20 = (bf16[1152,512]{1,0:T(8,128)(2,1)}, bf16[1152,512]{1,0:T(8,128)(2,1)}, u32[]{:S(2)}, u32[]{:S(2)}) collective-permute-start(bf16[1152,512]{1,0:T(8,128)(2,1)} %pad_maximum_fusion.9), channel_id=1, source_target_pairs={{0,96},{16,112},{32,64},{48,80},{64,32},{80,48},{96,0},{112,16},{1... | collective-permute-start | bytes 3538952 | tf_op jit(solution)/shard_map/ppermute | solution.py:852
  473.5 19.9 %collective-permute-start.14 = (bf16[128,384]{1,0:T(8,128)(2,1)S(1)}, bf16[128,384]{1,0:T(8,128)(2,1)S(1)}, u32[]{:S(2)}, u32[]{:S(2)}) collective-permute-start(bf16[128,384]{1,0:T(8,128)(2,1)S(1)} %slice.389), channel_id=1, source_target_pairs={{0,0},{1,16},{2,32},{3,48},{4,64},{5,80},{6,96},{7,112},{8,1},{9,1... | collective-permute-start | bytes 294920 | tf_op jit(solution)/shard_map/ppermute | solution.py:1271
  512.4 10.9 %collective-permute-start.21 = (bf16[4608,512]{1,0:T(8,128)(2,1)}, bf16[4608,512]{1,0:T(8,128)(2,1)}, u32[]{:S(2)}, u32[]{:S(2)}) collective-permute-start(bf16[4608,512]{1,0:T(8,128)(2,1)} %pad_maximum_fusion.own_ref), channel_id=1, source_target_pairs={{0,16},{16,0},{32,48},{48,32},{64,80},{80,64},{96,112},{112,96},{1... | collective-permute-start | bytes 14155784 | tf_op jit(solution)/shard_map/ppermute | solution.py:1279
  (94 other events, 815.7 us)
Sparse Core Ops, SparseCore 0:
  20.6 63.9 all-gather.12
  135.9 32.2 reduce-scatter.3
  173.2 30.2 all-gather.8
  234.9 53.9 reduce-scatter.5
  308.8 50.9 all-gather.10
  423.4 43.9 reduce-scatter.7
  508.6 33.2 all-gather.14

commit v9 on v8

--- a/solution.py
+++ b/solution.py
@@ -8,6 +8,7 @@
 from jax.sharding import PartitionSpec as P
 
 CAP = 32
+VMEM_LIMIT = 60 << 20
 
 
 epsilon = 1e-05
@@ -31,9 +32,9 @@
     )
 
 
-def after(value, other):
-    corner = other[(0,) * (other.ndim - 1)][:1].astype(jnp.float32)
-    return (value.astype(jnp.float32) + 0.0 * corner).astype(value.dtype)
+def after(value, *others):
+    corners = [o[(0,) * (o.ndim - 1)][:1].astype(jnp.float32) for o in others]
+    return (value.astype(jnp.float32) + 0.0 * sum(corners)).astype(value.dtype)
 
 
 def silu_slope(values):
@@ -138,7 +139,7 @@
 
 
 def front_kernel(
-    x_ref, w_in_ref, rows_in_ref, place_ref, taps_ref, head_ref, skip_ref, earlier_0, earlier_1,
+    x_ref, w_in_ref, rows_in_ref, place_ref, taps_ref, head_ref, skip_ref,
     proj_ref, scale_ref, w_ref, out_w_ref, mixed_ref, q_ref, out_ref, square_ref, start_ref,
     state_ref, pad_ref,
 ):
@@ -318,7 +319,7 @@
     return pl.BlockSpec(shape, lambda step: (0,) * len(shape))
 
 
-def front(x_all, weights, rows_w, taps, head, skip, *earlier):
+def front(x_all, weights, rows_w, taps, head, skip):
     f32, bf = jnp.float32, jnp.bfloat16
     rows, dim = x_all.shape
     sources, _, width = weights.shape
@@ -347,7 +348,6 @@
             whole(taps.shape),
             whole(head.shape),
             whole(skip.shape),
-            *map(corner_of, earlier),
         ],
         out_specs=[
             pl.BlockSpec((tile, width), by_tile),
@@ -375,15 +375,15 @@
             pltpu.VMEM((128, WIDE), f32),
             pltpu.VMEM((CHUNK + 8, CONVW), f32),
         ],
-        compiler_params=pltpu.CompilerParams(vmem_limit_bytes=52 << 20),
+        compiler_params=pltpu.CompilerParams(vmem_limit_bytes=VMEM_LIMIT),
         cost_estimate=pl.CostEstimate(
             flops=16 << 30, bytes_accessed=48 << 20, transcendentals=4 << 20
         ),
         name="front",
-    )(x_all, weights, weights, place, taps, head, skip, *earlier)
-
-
-def scan_backward(chunks, inputs, held, carry, sums, earlier):
+    )(x_all, weights, weights, place, taps, head, skip)
+
+
+def scan_backward(chunks, inputs, held, carry, sums):
     proj, mixed, d_o_all, row_values, starts, taps, head, skip, w_all, w_out = inputs
     rows, width = proj.shape
     dim = w_all.shape[0]
@@ -392,7 +392,7 @@
     given = (proj, proj, mixed, d_o_all, row_values, starts, taps, head, skip, w_all, w_out)
     given = given + (carry, sums)
     return pl.pallas_call(
-        functools.partial(scan_backward_kernel, chunks, len(held) + len(earlier)),
+        functools.partial(scan_backward_kernel, chunks, len(held)),
         grid=(chunks[1] - chunks[0],),
         in_specs=[
             pl.BlockSpec((CHUNK, width), by_chunk),
@@ -411,7 +411,6 @@
             whole(carry.shape),
             whole(sums.shape),
             *[pl.BlockSpec(memory_space=pl.ANY) for _ in held],
-            *map(corner_of, earlier),
         ],
         out_specs=[
             pl.BlockSpec((CHUNK, width), by_chunk),
@@ -431,44 +430,68 @@
             pltpu.VMEM((CHUNK + 8, CONVW), jnp.float32),
         ],
         input_output_aliases={len(given) + i: i for i in range(len(held))},
-        compiler_params=pltpu.CompilerParams(vmem_limit_bytes=48 << 20),
+        compiler_params=pltpu.CompilerParams(vmem_limit_bytes=VMEM_LIMIT),
         cost_estimate=pl.CostEstimate(
             flops=(1 << 20) if held else (10 << 30), bytes_accessed=1 << 20, transcendentals=0
         ),
         name="scan_backward",
-    )(*given, *held, *earlier)
-
-
-def token_front_kernel(x_ref, out_ref, scale_ref, gain_ref, slots_ref, resid_ref, moe_ref, sent_ref):
+    )(*given, *held)
+
+
+def token_front_kernel(
+    x_ref, out_ref, scale_ref, gain_ref, slots_ref, router_ref, named_ref,
+    resid_ref, moe_ref, sent_ref, gates_ref,
+):
     f32, bf = jnp.float32, jnp.bfloat16
     resid = x_ref[...].astype(f32) + out_ref[...].astype(f32) * scale_ref[...]
     resid_ref[...] = resid
     moe_in = (resid * row_scale(resid) * gain_ref[0:1, :]).astype(bf)
     moe_ref[...] = moe_in
     sent_ref[...] = times(slots_ref[...], moe_in).astype(bf)
-
-
-def token_front(x, out_sum, scale, gain, slots):
+    named = named_ref[...] > 0.0
+    logits = times(moe_in, router_ref[...])
+    top = jnp.max(jnp.where(named, logits, -1e30), axis=1, keepdims=True)
+    powers = jnp.where(named, jnp.exp(jnp.where(named, logits - top, 0.0)), 0.0)
+    gates_ref[...] = powers / jnp.sum(powers, axis=1, keepdims=True)
+
+
+def token_front(x, out_sum, scale, gain, slots, w_all, named):
     rows, dim = x.shape
     return pl.pallas_call(
         token_front_kernel,
+        grid=(1,),
+        in_specs=[
+            whole(x.shape),
+            whole(out_sum.shape),
+            whole(scale.shape),
+            whole(gain.shape),
+            whole(slots.shape),
+            pl.BlockSpec((dim, 128), lambda step: (0, w_all.shape[1] // 128 - 1)),
+            whole(named.shape),
+        ],
+        out_specs=[
+            whole((rows, dim)),
+            whole((rows, dim)),
+            whole((slots.shape[0], dim)),
+            whole((rows, 128)),
+        ],
         out_shape=[
             jax.ShapeDtypeStruct((rows, dim), jnp.float32),
             jax.ShapeDtypeStruct((rows, dim), jnp.bfloat16),
             jax.ShapeDtypeStruct((slots.shape[0], dim), jnp.bfloat16),
-        ],
-        compiler_params=pltpu.CompilerParams(vmem_limit_bytes=24 << 20),
+            jax.ShapeDtypeStruct((rows, 128), jnp.float32),
+        ],
+        compiler_params=pltpu.CompilerParams(vmem_limit_bytes=VMEM_LIMIT),
         cost_estimate=pl.CostEstimate(flops=1 << 28, bytes_accessed=5 << 20, transcendentals=0),
         name="token_front",
-    )(x, out_sum, scale, gain, slots)
+    )(x, out_sum, scale, gain, slots, w_all, named)
 
 
 def token_back_kernel(
     back_ref, slots_ref, shared_ref, x_ref, resid_ref, gates_ref, router_ref, gain_ref, cot_ref,
-    *refs,
+    d_o_ref, d_resid_ref, d_logits_ref, d_gain_ref,
 ):
     f32, bf = jnp.float32, jnp.bfloat16
-    d_o_ref, d_resid_ref, d_logits_ref, d_gain_ref = refs[-4:]
     dim = x_ref.shape[1]
     sums = transposed_times(slots_ref[...], back_ref[...])
     scalars = sums[:, dim:]
@@ -503,7 +526,7 @@
     d_o_ref[:, dim:] = both.astype(bf)
 
 
-def token_back(back, slots, shared_both, x, resid, gates, w_all, gain, cot, earlier):
+def token_back(back, slots, shared_both, x, resid, gates, w_all, gain, cot):
     rows, dim = x.shape
     return pl.pallas_call(
         token_back_kernel,
@@ -518,7 +541,6 @@
             pl.BlockSpec((dim, 128), lambda step: (0, w_all.shape[1] // 128 - 1)),
             whole(gain.shape),
             whole(cot.shape),
-            *map(corner_of, earlier),
         ],
         out_specs=[
             whole((rows, dim + 128)),
@@ -532,10 +554,10 @@
             jax.ShapeDtypeStruct((rows, 128), jnp.float32),
             jax.ShapeDtypeStruct((8, dim), jnp.float32),
         ],
-        compiler_params=pltpu.CompilerParams(vmem_limit_bytes=32 << 20),
+        compiler_params=pltpu.CompilerParams(vmem_limit_bytes=VMEM_LIMIT),
         cost_estimate=pl.CostEstimate(flops=1 << 29, bytes_accessed=8 << 20, transcendentals=0),
         name="token_back",
-    )(back, slots, shared_both, x, resid, gates, w_all, gain, cot, *earlier)
+    )(back, slots, shared_both, x, resid, gates, w_all, gain, cot)
 
 
 def expert_early_kernel(cot_ref, down_ref, earlier_ref, raw_ref):
@@ -625,7 +647,7 @@
 
 def expert_params(flops, moved):
     return dict(
-        compiler_params=pltpu.CompilerParams(vmem_limit_bytes=56 << 20),
+        compiler_params=pltpu.CompilerParams(vmem_limit_bytes=VMEM_LIMIT),
         cost_estimate=pl.CostEstimate(flops=flops, bytes_accessed=moved, transcendentals=1 << 19),
     )
 
@@ -796,7 +818,7 @@
         in_specs=[pl.BlockSpec(memory_space=pltpu.VMEM)] * 5,
         out_specs=[pl.BlockSpec(memory_space=pltpu.VMEM)] * len(shapes),
         out_shape=[jax.ShapeDtypeStruct(shape, jnp.float32) for shape in shapes],
-        compiler_params=pltpu.CompilerParams(vmem_limit_bytes=40 << 20),
+        compiler_params=pltpu.CompilerParams(vmem_limit_bytes=VMEM_LIMIT),
         cost_estimate=pl.CostEstimate(flops=8 << 20, bytes_accessed=12 << 20, transcendentals=0),
         name="assemble",
     )(side, in_weight, in_gain, out_weight, out_gain)
@@ -898,7 +920,7 @@
             jax.ShapeDtypeStruct((2, dim, units), jnp.float32),
             jax.ShapeDtypeStruct((2, units, dim), jnp.float32),
         ],
-        compiler_params=pltpu.CompilerParams(vmem_limit_bytes=40 << 20),
+        compiler_params=pltpu.CompilerParams(vmem_limit_bytes=VMEM_LIMIT),
         cost_estimate=pl.CostEstimate(flops=1 << 20, bytes_accessed=28 << 20, transcendentals=0),
         name="unpack_expert_grads",
     )(core.reshape(1), own, other)
@@ -1072,7 +1094,6 @@
     router_lane = at_router - (total - 128)
     lanes = jnp.arange(128, dtype=jnp.int32)
     named_lanes = jnp.pad(named, ((0, 0), (router_lane, 128 - router_lane - experts)))
-    cot_all = gather_rows(after(cot_low, x_all), core, z_at, mates)
     cot_sent = in_slots(jnp.concatenate([cot_low, named_lanes.astype(bf)], axis=1))
     cot_rows = dispatched(cot_sent)
 
@@ -1106,25 +1127,23 @@
     head_in = jnp.pad(jnp.stack([bias_local, decay_rate]), ((0, 6), (0, 128 - gh)))
     skip_in = jnp.broadcast_to(jnp.repeat(skip_local, per_head)[None], (8, gw))
     proj, x_r, w_all, w_out, mixed, q_low, out_part, square_part, starts = front(
-        x_all, weights, rows_w, taps_in, head_in, skip_in, cot_sent, cot_all
-    )
-
+        x_all, weights, rows_w, taps_in, after(head_in, cot_sent), skip_in
+    )
+
+    cot_all = lax.all_gather(after(cot_low, weights), "seq", axis=0, tiled=True)
+    square_part = after(square_part.reshape(sq, toks), cot_all)
     out_sum = lax.psum_scatter(out_part, "seq", scatter_dimension=0, tiled=True)
-    square = lax.psum(square_part.reshape(sq, toks), "seq")
+    square = lax.psum(square_part, "seq")
     q_r = lax.rsqrt(square / inner + epsilon).reshape(seq_rows, 1)
     d_raw = expert_early(cot_rows, expert_down, square)
     tok_r = after(lax.dynamic_slice_in_dim(q_r, q * toks, toks, 0), d_raw)
     x_tok = x_low.astype(f32)
-    resid, moe_in, moe_sent = token_front(x_low, out_sum, tok_r, moe_gain_rows, dispatch_flat)
+    resid, moe_in, moe_sent, gates = token_front(
+        x_low, out_sum, tok_r, moe_gain_rows, dispatch_flat, w_all, named_lanes
+    )
 
     moe_all = lax.all_gather(moe_in, "seq", axis=0, tiled=True)
 
-    logits = times(moe_in, w_all[:, total - 128 :])
-    top = jnp.max(jnp.where(named_lanes > 0.0, logits, -1e30), axis=1, keepdims=True)
-    powers = jnp.where(
-        named_lanes > 0.0, jnp.exp(jnp.where(named_lanes > 0.0, logits - top, 0.0)), 0.0
-    )
-    gates = powers / jnp.sum(powers, axis=1, keepdims=True)
     rows = dispatched(moe_sent.reshape(sh, local_e * CAP, dim))
     own_ids = lax.axis_index("shard") * local_e + jnp.arange(local_e, dtype=jnp.int32)
     marks = jnp.stack(
@@ -1156,7 +1175,11 @@
     far = [(i, 2 * (sq // 2 - 1 - i // 2) + i % 2) for i in range(sq)]
     is_inner = ((z_at == 1) | (z_at == 2)).astype(jnp.int32)
     is_high = (z_at >= 2).astype(jnp.int32)
-    e_parts = [halve(part.reshape(-1, part.shape[2]), core, mates) for part in e_grads]
+    e_parts = [
+        halve(part[:, at : at + dim // 2].reshape(dim, -1), core, mates)
+        for part in e_grads
+        for at in (0, dim // 2)
+    ]
     e_mine = jnp.concatenate(e_parts, axis=0)
     cutoff = e_mine.shape[0] // 2
 
@@ -1168,11 +1191,10 @@
         shared_both,
         x_low,
         resid,
-        gates,
+        after(gates, grad_down_part, grad_shared_part, *e_parts),
         w_all,
         moe_gain_rows,
         cot_low,
-        (grad_down_part, grad_shared_part, *e_parts),
     )
     grad_router = jnp.dot(moe_in.astype(f32).T, d_logits, precision=highest)
     grad_router = grad_router + jnp.pad(d_moe_gain[0][:, None], ((0, 0), (0, 127)))
@@ -1210,7 +1232,8 @@
     row_values = jnp.concatenate(
         [q_r, x_r, jnp.zeros((seq_rows, 6), f32)], axis=1
     )
-    scan_inputs = (proj, mixed, d_o_all, row_values, starts, taps_in, head_in, skip_in, w_all, w_out)
+    scan_inputs = (proj, mixed, d_o_all, row_values, starts, taps_in)
+    scan_inputs = scan_inputs + (head_in, skip_in, w_all, w_out)
     chunks = seq_rows // CHUNK
     middle = chunks // 2
     *held, carry, sums = scan_backward(
@@ -1219,10 +1242,13 @@
         (),
         jnp.zeros((136, gw + keys_w), f32),
         jnp.zeros((24, gw + keys_w), f32),
-        (),
-    )
+    )
+    route_gates = after(gates, carry)[:, router_lane : router_lane + experts]
+    weighted = (route_gates.T[:, None, :] * dispatch.astype(f32)).reshape(slots, toks)
+    combined = transposed_times(weighted.astype(bf), returned.reshape(slots, dim))
+    carry = after(carry, combined, early_part, e_one, e_two)
     d_proj, back_part, carry, sums = scan_backward(
-        (0, middle), scan_inputs, held, carry, sums, (returned, early_part, e_one, e_two)
+        (0, middle), scan_inputs, held, carry, sums
     )
     d_taps, d_head, d_skip = sums[0:8], sums[8:16, :128], sums[16:24, :gw]
     grad_conv_local = d_taps[:taps]
@@ -1232,9 +1258,6 @@
     grad_skip_local = jnp.sum(d_skip[0].reshape(gh, per_head), axis=1)
     e_one, e_two = halve(e_one, is_high, far), halve(e_two, is_inner, near)
     back_sum = lax.psum_scatter(back_part, "seq", scatter_dimension=0, tiled=True).astype(f32)
-    route_gates = gates[:, router_lane : router_lane + experts]
-    weighted = (route_gates.T[:, None, :] * dispatch.astype(f32)).reshape(slots, toks)
-    combined = transposed_times(weighted.astype(bf), returned.reshape(slots, dim))
     block_output = ((resid + shared_sum.astype(f32) + combined) * live[:, None]).astype(bf)[None]
     tok_x_r = row_scale(x_tok)
     x_n = x_tok * tok_x_r

time: 567 us -> 604 us (1.065)
  the two profiles are of different devices: /device:TPU:1 before, /device:TPU:33 now
where the time goes in v9:
time: 604 us; the launch traced here: 592 us
  Pallas kernels  128 us (21%)
  waiting for transfers between devices  119 us (20%)
  starting transfers between devices  94.6 us (16%)
  local copies, waits for them, and re-layouts  92.8 us (15%)
  other arithmetic  76.4 us (13%)
  between operations  31.7 us (5%)
  blocking collectives  27.9 us (5%)
  matrix products  21.2 us (4%)
    all_to_all x6, starting transfers between devices, to_shards(): lax.all_to_all(values, 'shard', split_axis=0, concat_axis=0, tiled=True)  39.6 us
    pallas_call x2, Pallas kernels, scan_backward(): pl.pallas_call(functools.partial(scan_backward_kernel, chunks, len(held))...  39 us
    all_to_all x6, waiting for transfers between devices, to_shards(): lax.all_to_all(values, 'shard', split_axis=0, concat_axis=0, tiled=True)  35.2 us
    all_gather x1, waiting for transfers between devices, on_device(): d_o_all = lax.all_gather(d_o_ext, 'seq', axis=0, tiled=True)  27 us
    pallas_call x1, Pallas kernels, front(): pl.pallas_call(front_kernel, grid=(rows // tile,), in_specs=[pl.BlockSpec...  23.2 us
    all_gather x1, waiting for transfers between devices, on_device(): lax.all_gather(jnp.concatenate([packed, fold_rows(piece[:own_out], total)...  20.1 us
    pallas_call x1, Pallas kernels, expert_main(): pl.pallas_call(expert_main_kernel, grid=(local,), in_specs=[expert_slots(...  19.2 us
    unnamed x171, local copies, waits for them, and re-layouts  18.1 us
  transfers between devices with their start and end apart: 35, of which 10 were waited for; matrix products, arithmetic and copies ran while one was open for 28% of the time, Pallas kernels for 16%

profile of v9, /device:TPU:33, one launch (start us, length us, event | category | flops | bytes accessed | tf_op | source)
XLA Modules:
  0.0 592.1 jit_solution(797803607062017478)
XLA Ops:
  9.2 4.7 collective-permute-start.4
  20.8 6.6 %collective-permute-start.1 = (bf16[128,1536]{1,0:T(8,128)(2,1)S(1)}, bf16[128,1536]{1,0:T(8,128)(2,1)S(1)}, u32[]{:S(2)}, u32[]{:S(2)}) collective-permute-start(bf16[128,1536]{1,0:T(8,128)(2,1)S(1)} %bitcast.204), channel_id=1, source_target_pairs={{0,64},{16,80},{32,96},{48,112},{64,0},{80,16},{96,32},{112,48},{1... | collective-permute-start | bytes 1179656 | tf_op jit(solution)/shard_map/ppermute | solution.py:850
  30.2 17.2 %all-gather.3 = bf16[16,1,1152]{2,1,0:T(2,128)(2,1)S(1)} all-gather(bf16[1,1,1152]{2,1,0:T(2,128)(2,1)S(1)} %reshape.1021), channel_id=3, replica_groups=mesh['seq'=8,'shard'=16] {'shard'}, dimensions={0}, use_global_device_ids=true | all-gather | bytes 39168 | tf_op jit(solution)/shard_map/all_gather | solution.py:1006
  55.7 7.6 %collective-permute-start.3 = (bf16[4,128,1536]{2,1,0:T(8,128)(2,1)S(1)}, bf16[4,128,1536]{2,1,0:T(8,128)(2,1)}, u32[]{:S(2)}, u32[]{:S(2)}) collective-permute-start(bf16[4,128,1536]{2,1,0:T(8,128)(2,1)S(1)} %get-tuple-element.238), channel_id=1, source_target_pairs={{0,16},{16,0},{32,48},{48,32},{64,80},{80,64},{96,112},{112,96},{1... | collective-permute-start | bytes 4718600 | tf_op jit(solution)/shard_map/ppermute | solution.py:852
  63.3 20.1 %all-gather.16.cloned.1.call-done = bf16[2560,1152]{1,0:T(8,128)(2,1)} async-done(((bf16[160,1152]{1,0:T(8,128)(2,1)}), bf16[2560,1152]{1,0:T(8,128)(2,1)}) %all-gather.16.cloned.1.call-update) | async-done | bytes 5898256 | tf_op jit(solution)/shard_map/all_gather | solution.py:1047
  124.1 5.0 all-to-all-start
  136.2 23.2 %front.1 = (f32[1024,1152]{1,0:T(8,128)}, f32[1024,1]{1,0:T(8,128)}, bf16[1536,1152]{1,0:T(8,128)(2,1)}, bf16[384,1536]{1,0:T(8,128)(2,1)}, bf16[1024,384]{1,0:T...) custom-call(bf16[1024,1536]{1,0:T(8,128)(2,1)} %bitcast_dynamic-upda, ...), custom_call_target="tpu_custom_call" | custom-call | flops 17179869184 | bytes 50331648 | tf_op jit(solution)/shard_map/front/pallas_call | solution.py:340
  161.7 10.7 %psum.7.earlier_ref = f32[8,128]{1,0:T(8,128)S(1)} all-reduce(f32[8,128]{1,0:T(8,128)S(1)} %bitcast.246), channel_id=1, replica_groups=mesh['seq'=8,'shard'=16] {'seq'}, use_global_device_ids=true, to_apply=%region_2.3 | all-reduce | flops 1024 | bytes 8192 | tf_op jit(solution)/shard_map/psum | solution.py:1136
  173.1 4.9 expert_early.1.raw_ref
  180.5 13.5 %reduce-scatter.4.cloned.1.call-done.out_ref = bf16[128,1536]{1,0:T(8,128)(2,1)} async-done(((bf16[1024,1536]{1,0:T(8,128)(2,1)}), bf16[128,1536]{1,0:T(8,128)(2,1)}) %reduce-scatter.4.cloned.1.call-update) | async-done | bytes 393232 | tf_op jit(solution)/shard_map/reduce_scatter | solution.py:1135
  194.6 4.3 token_front.1
  199.0 6.6 %all-to-all-start.1 = ((bf16[16,64,1536]{2,1,0:T(8,128)(2,1)}), bf16[16,64,1536]{2,1,0:T(8,128)(2,1)}, u32[]{:S(2)}, u32[]{:S(2)}) async-start(bf16[16,64,1536]{2,1,0:T(8,128)(2,1)} %bitcast.219), calls=%async_computation.2 | async-start | bytes 6291456 | tf_op jit(solution)/shard_map/all_to_all | solution.py:1009
  211.6 34.4 %all-to-all-done.1 = bf16[16,64,1536]{2,1,0:T(8,128)(2,1)} async-done(((bf16[16,64,1536]{2,1,0:T(8,128)(2,1)}), bf16[16,64,1536]{2,1,0:T(8,128)(2,1)}, u32[]{:S(2)}, u32[]{:S(2)}) %all-to-all-start.1) | async-done | bytes 3145760 | tf_op jit(solution)/shard_map/all_to_all | solution.py:1009
  245.9 19.2 %expert_main.1 = (bf16[16,2,32,1664]{3,2,1,0:T(8,128)(2,1)}, bf16[2,512,512]{2,1,0:T(8,128)(2,1)}, bf16[2,512,512]{2,1,0:T(8,128)(2,1)}, bf16[2,512,512]{2,1,0:T...) custom-call(bf16[16,2,32,1536]{3,2,1,0:T(8,128)(2,1)} %bitcast.32.ro, ...), custom_call_target="tpu_custom_call" | custom-call | flops 8589934592 | bytes 20971520 | tf_op jit(solution)/shard_map/expert_main/pallas_call | solution.py:682
  265.2 8.0 %all-to-all-start.2 = ((bf16[16,64,1664]{2,1,0:T(8,128)(2,1)}), bf16[16,64,1664]{2,1,0:T(8,128)(2,1)S(1)}, u32[]{:S(2)}, u32[]{:S(2)}) async-start(bf16[16,64,1664]{2,1,0:T(8,128)(2,1)} %bitcast.216), calls=%async_computation.4 | async-start | bytes 6815744 | tf_op jit(solution)/shard_map/all_to_all | solution.py:1009
  276.2 12.8 %expert_late.1 = (bf16[16,2,32,1536]{3,2,1,0:T(8,128)(2,1)}, bf16[2,1536,512]{2,1,0:T(8,128)(2,1)}, bf16[2,1536,512]{2,1,0:T(8,128)(2,1)}, bf16[2,1536,512]{2,1,0:T(8,128)(2,1)}) custom-call(bf16[16,2,32,1536]{3,2,1,0:T(8,128)(2,1)} %bitcast.32.rows_ref, bf16[16,2,32,1664]{3,2,1,0:T(8,128)(2,1)} %bitcast.29.cot_ref.routed_ref, ...), custom_call_target="tpu_custom_call" | custom-call | flops 7516192768 | bytes 25165824 | tf_op jit(solution)/shard_map/expert_late/pallas_call | solution.py:716
  314.9 5.3 token_back.1
  327.6 6.8 %all-to-all-start.3 = ((bf16[16,64,1536]{2,1,0:T(8,128)(2,1)}), bf16[16,64,1536]{2,1,0:T(8,128)(2,1)S(1)}, u32[]{:S(2)}, u32[]{:S(2)}) async-start(bf16[16,64,1536]{2,1,0:T(8,128)(2,1)} %bitcast.217), calls=%async_computation.5 | async-start | bytes 6291456 | tf_op jit(solution)/shard_map/all_to_all | solution.py:1009
  340.5 27.0 %all-gather.14.cloned.1.call-done.d_o_ref = bf16[1024,1664]{1,0:T(8,128)(2,1)} async-done(((bf16[128,1664]{1,0:T(8,128)(2,1)}), bf16[1024,1664]{1,0:T(8,128)(2,1)}) %all-gather.14.cloned.1.call-update) | async-done | bytes 3407888 | tf_op jit(solution)/shard_map/all_gather | solution.py:1201
  376.5 19.5 %scan_backward.2 = (bf16[1024,1152]{1,0:T(8,128)(2,1)}, bf16[1024,1536]{1,0:T(8,128)(2,1)}, f32[136,640]{1,0:T(8,128)}, f32[24,640]{1,0:T(8,128)}) custom-call(f32[1024,1152]{1,0:T(8,128)} %get-tuple-element.78.proj_ref.prev_ref, f32[1024,1152]{1,0:T(8,128)} %get-tuple-element.78.proj_ref.prev_ref, bf16[1024,384]{1,0:T(8,128)(2,1)} %get-tuple-element.79.mixed_ref, ...), custom_call_target="tpu_custom_call" | custom-call | flops 10737418240 | bytes 1048576 | tf_op jit(solution)/shard_map/scan_backward/pallas_call | solution.py:394
  405.4 6.6 %all-to-all-start.4 = ((bf16[16,224,384]{2,1,0:T(8,128)(2,1)}), bf16[16,224,384]{2,1,0:T(8,128)(2,1)}, u32[]{:S(2)}, u32[]{:S(2)}) async-start(bf16[16,224,384]{2,1,0:T(8,128)(2,1)} %copy-done.17), calls=%async_computation.7 | async-start | bytes 5505024 | tf_op jit(solution)/shard_map/all_to_all | solution.py:1009
  421.7 19.5 %scan_backward.3 = (bf16[1024,1152]{1,0:T(8,128)(2,1)}, bf16[1024,1536]{1,0:T(8,128)(2,1)}, f32[136,640]{1,0:T(8,128)}, f32[24,640]{1,0:T(8,128)}) custom-call(f32[1024,1152]{1,0:T(8,128)} %get-tuple-element.78.proj_ref.prev_ref, f32[1024,1152]{1,0:T(8,128)} %get-tuple-element.78.proj_ref.prev_ref, ...), custom_call_target="tpu_custom_call", output_to_operand_aliasing={{0}: (13, {}), {1}: (14, {})} | custom-call | flops 1048576 | bytes 1048576 | tf_op jit(solution)/shard_map/scan_backward/pallas_call | solution.py:394
  450.7 8.7 %convolution_convert_fusion = bf16[1536,1152]{1,0:T(8,128)(2,1)} fusion(bf16[1024,1536]{1,0:T(8,128)(2,1)} %bitcast_dynamic-update-slice_fusion.x_ref, bf16[1024,1152]{1,0:T(8,128)(2,1)} %get-tuple-element.104), kind=kOutput, calls=%fused_computation | convolution fusion | flops 3625648128 | bytes 9043968 | tf_op jit(solution)/shard_map/dot_general | solution.py:30
  459.4 4.2 add_convert_fusion
  467.5 6.6 %all-to-all-start.5 = ((bf16[16,96,1152]{2,1,0:T(8,128)(2,1)}), bf16[16,96,1152]{2,1,0:T(8,128)(2,1)S(1)}, u32[]{:S(2)}, u32[]{:S(2)}) async-start(bf16[16,96,1152]{2,1,0:T(8,128)(2,1)} %bitcast.80), calls=%async_computation.8 | async-start | bytes 7077888 | tf_op jit(solution)/shard_map/all_to_all | solution.py:1009
  477.3 10.0 %collective-permute-done.15 = bf16[576,512]{1,0:T(8,128)(2,1)} collective-permute-done((bf16[576,512]{1,0:T(8,128)(2,1)}, bf16[576,512]{1,0:T(8,128)(2,1)}, u32[]{:S(2)}, u32[]{:S(2)}) %collective-permute-start.15) | collective-permute-done | bytes 589856 | tf_op jit(solution)/shard_map/ppermute | solution.py:874
  501.0 9.7 %collective-permute-start.13 = (bf16[128,384]{1,0:T(8,128)(2,1)S(1)}, bf16[128,384]{1,0:T(8,128)(2,1)S(1)}, u32[]{:S(2)}, u32[]{:S(2)}) collective-permute-start(bf16[128,384]{1,0:T(8,128)(2,1)S(1)} %slice.526), channel_id=1, source_target_pairs={{0,0},{1,16},{2,32},{3,48},{4,64},{5,80},{6,96},{7,112},{8,1},{9,1... | collective-permute-start | bytes 294920 | tf_op jit(solution)/shard_map/ppermute | solution.py:1294
  510.7 4.8 collective-permute-done.13
  534.1 4.1 pad_maximum_fusion.own_ref
  538.2 10.3 %collective-permute-start.20 = (bf16[4608,512]{1,0:T(8,128)(2,1)}, bf16[4608,512]{1,0:T(8,128)(2,1)}, u32[]{:S(2)}, u32[]{:S(2)}) collective-permute-start(bf16[4608,512]{1,0:T(8,128)(2,1)} %pad_maximum_fusion.own_ref), channel_id=1, source_target_pairs={{0,16},{16,0},{32,48},{48,32},{64,80},{80,64},{96,112},{112,96},{1... | collective-permute-start | bytes 14155784 | tf_op jit(solution)/shard_map/ppermute | solution.py:1302
  556.4 13.9 %unpack_expert_grads.1 = (f32[2,1536,512]{2,1,0:T(8,128)}, f32[2,1536,512]{2,1,0:T(8,128)}, f32[2,512,1536]{2,1,0:T(8,128)}) custom-call(s32[1]{0:T(128)} %bitcast.94.core_ref, bf16[4608,512]{1,0:T(8,128)(2,1)} %pad_maximum_fusion.own_ref, bf16[4608,512]{1,0:T(8,128)(2,1)} %collective-permute-done.20.other_ref), custom_call_target="tpu_custom_call" | custom-call | flops 1048576 | bytes 29360128 | tf_op jit(solution)/shard_map/unpack_expert_grads/pallas_call | solution.py:903
  570.3 5.5 assemble.1
  (445 shorter events, 198.8 us)
Async XLA Ops:
  7.3 76.0 %all-gather.16.cloned.1.call-start = ((), (), s32[]{:S(2)}) async-start(), calls=%async_computation.15 | async-start | bytes 6266880 | tf_op jit(solution)/shard_map/all_gather | solution.py:1047
  9.2 10.5 %collective-permute-start.4 = (bf16[32,1536]{1,0:T(8,128)(2,1)S(1)}, bf16[32,1536]{1,0:T(8,128)(2,1)S(1)}, u32[]{:S(2)}, u32[]{:S(2)}) collective-permute-start(bf16[32,1536]{1,0:T(8,128)(2,1)S(1)} %pad_maximum_fusion.9), channel_id=1, source_target_pairs={{0,0},{16,1},{32,2},{48,3},{64,4},{80,5},{96,6},{112,7},{1,8},{17,... | collective-permute-start | bytes 294920 | tf_op jit(solution)/shard_map/ppermute | solution.py:1033
  20.6 139.1 %all-gather.10.cloned.1.call-start = ((), (), s32[]{:S(2)}) async-start(), calls=%async_computation.10 | async-start | bytes 3538944 | tf_op jit(solution)/shard_map/all_gather | solution.py:1133
  20.7 32.4 %collective-permute-start.2 = (bf16[128,1536]{1,0:T(8,128)(2,1)S(1)}, bf16[128,1536]{1,0:T(8,128)(2,1)S(1)}, u32[]{:S(2)}, u32[]{:S(2)}) collective-permute-start(bf16[128,1536]{1,0:T(8,128)(2,1)S(1)} %bitcast.203), channel_id=1, source_target_pairs={{0,96},{16,112},{32,0},{48,16},{64,32},{80,48},{96,64},{112,80},{1... | collective-permute-start | bytes 1179656 | tf_op jit(solution)/shard_map/ppermute | solution.py:850
  20.8 32.4 %collective-permute-start.1 = (bf16[128,1536]{1,0:T(8,128)(2,1)S(1)}, bf16[128,1536]{1,0:T(8,128)(2,1)S(1)}, u32[]{:S(2)}, u32[]{:S(2)}) collective-permute-start(bf16[128,1536]{1,0:T(8,128)(2,1)S(1)} %bitcast.204), channel_id=1, source_target_pairs={{0,64},{16,80},{32,96},{48,112},{64,0},{80,16},{96,32},{112,48},{1... | collective-permute-start | bytes 1179656 | tf_op jit(solution)/shard_map/ppermute | solution.py:850
  27.3 25.8 %collective-permute-start = (bf16[128,1536]{1,0:T(8,128)(2,1)S(1)}, bf16[128,1536]{1,0:T(8,128)(2,1)S(1)}, u32[]{:S(2)}, u32[]{:S(2)}) collective-permute-start(bf16[128,1536]{1,0:T(8,128)(2,1)S(1)} %bitcast.205), channel_id=1, source_target_pairs={{0,32},{16,48},{32,64},{48,80},{64,96},{80,112},{96,0},{112,16},{1... | collective-permute-start | bytes 1179656 | tf_op jit(solution)/shard_map/ppermute | solution.py:850
  55.7 61.2 %collective-permute-start.3 = (bf16[4,128,1536]{2,1,0:T(8,128)(2,1)S(1)}, bf16[4,128,1536]{2,1,0:T(8,128)(2,1)}, u32[]{:S(2)}, u32[]{:S(2)}) collective-permute-start(bf16[4,128,1536]{2,1,0:T(8,128)(2,1)S(1)} %get-tuple-element.238), channel_id=1, source_target_pairs={{0,16},{16,0},{32,48},{48,32},{64,80},{80,64},{96,112},{112,96},{1... | collective-permute-start | bytes 4718600 | tf_op jit(solution)/shard_map/ppermute | solution.py:852
  124.1 48.5 %all-to-all-start = ((bf16[16,64,1664]{2,1,0:T(8,128)(2,1)}), bf16[16,64,1664]{2,1,0:T(8,128)(2,1)}, u32[]{:S(2)}, u32[]{:S(2)}) async-start(bf16[16,64,1664]{2,1,0:T(8,128)(2,1)} %bitcast.24), calls=%async_computation.1 | async-start | bytes 6815744 | tf_op jit(solution)/shard_map/all_to_all | solution.py:1009
  129.2 64.8 %reduce-scatter.4.cloned.1.call-start = ((), (), s32[]{:S(2)}) async-start(), calls=%async_computation.9 | async-start | bytes 3538944 | tf_op jit(solution)/shard_map/reduce_scatter | solution.py:1135
  159.4 86.5 %all-gather.12.cloned.1.call-start = ((), (), s32[]{:S(2)}) async-start(), calls=%async_computation.11 | async-start | bytes 3538944 | tf_op jit(solution)/shard_map/all_gather | solution.py:1145
  199.0 47.0 %all-to-all-start.1 = ((bf16[16,64,1536]{2,1,0:T(8,128)(2,1)}), bf16[16,64,1536]{2,1,0:T(8,128)(2,1)}, u32[]{:S(2)}, u32[]{:S(2)}) async-start(bf16[16,64,1536]{2,1,0:T(8,128)(2,1)} %bitcast.219), calls=%async_computation.2 | async-start | bytes 6291456 | tf_op jit(solution)/shard_map/all_to_all | solution.py:1009
  205.6 109.3 %reduce-scatter.6.cloned.1.call-start = ((), (), s32[]{:S(2)}) async-start(), calls=%async_computation.12 | async-start | bytes 7077888 | tf_op jit(solution)/shard_map/reduce_scatter | solution.py:1167
  265.2 47.2 %all-to-all-start.2 = ((bf16[16,64,1664]{2,1,0:T(8,128)(2,1)}), bf16[16,64,1664]{2,1,0:T(8,128)(2,1)S(1)}, u32[]{:S(2)}, u32[]{:S(2)}) async-start(bf16[16,64,1664]{2,1,0:T(8,128)(2,1)} %bitcast.216), calls=%async_computation.4 | async-start | bytes 6815744 | tf_op jit(solution)/shard_map/all_to_all | solution.py:1009
  273.2 94.3 %all-gather.14.cloned.1.call-start = ((), (), s32[]{:S(2)}) async-start(), calls=%async_computation.13 | async-start | bytes 3833856 | tf_op jit(solution)/shard_map/all_gather | solution.py:1201
  294.3 7.5 %collective-permute-start.5 = (bf16[768,512]{1,0:T(8,128)(2,1)S(1)}, bf16[768,512]{1,0:T(8,128)(2,1)S(1)}, u32[]{:S(2)}, u32[]{:S(2)}) collective-permute-start(bf16[768,512]{1,0:T(8,128)(2,1)S(1)} %dynamic-slice_bitcast_fusion.5), channel_id=1, source_target_pairs={{0,16},{16,0},{32,48},{48,32},{64,80},{80,64},{96,112},{112,96},{1... | collective-permute-start | bytes 2359304 | tf_op jit(solution)/shard_map/ppermute | solution.py:869
  297.2 6.3 %collective-permute-start.7 = (bf16[768,512]{1,0:T(8,128)(2,1)S(1)}, bf16[768,512]{1,0:T(8,128)(2,1)S(1)}, u32[]{:S(2)}, u32[]{:S(2)}) collective-permute-start(bf16[768,512]{1,0:T(8,128)(2,1)S(1)} %dynamic-slice_bitcast_fusion.3), channel_id=1, source_target_pairs={{0,16},{16,0},{32,48},{48,32},{64,80},{80,64},{96,112},{112,96},{1... | collective-permute-start | bytes 2359304 | tf_op jit(solution)/shard_map/ppermute | solution.py:869
  298.4 6.0 %collective-permute-start.8 = (bf16[768,512]{1,0:T(8,128)(2,1)S(1)}, bf16[768,512]{1,0:T(8,128)(2,1)S(1)}, u32[]{:S(2)}, u32[]{:S(2)}) collective-permute-start(bf16[768,512]{1,0:T(8,128)(2,1)S(1)} %dynamic-slice_bitcast_fusion.2), channel_id=1, source_target_pairs={{0,16},{16,0},{32,48},{48,32},{64,80},{80,64},{96,112},{112,96},{1... | collective-permute-start | bytes 2359304 | tf_op jit(solution)/shard_map/ppermute | solution.py:869
  327.6 77.8 %all-to-all-start.3 = ((bf16[16,64,1536]{2,1,0:T(8,128)(2,1)}), bf16[16,64,1536]{2,1,0:T(8,128)(2,1)S(1)}, u32[]{:S(2)}, u32[]{:S(2)}) async-start(bf16[16,64,1536]{2,1,0:T(8,128)(2,1)} %bitcast.217), calls=%async_computation.5 | async-start | bytes 6291456 | tf_op jit(solution)/shard_map/all_to_all | solution.py:1009
  372.0 43.3 %collective-permute-start.11 = (bf16[1152,512]{1,0:T(8,128)(2,1)}, bf16[1152,512]{1,0:T(8,128)(2,1)}, u32[]{:S(2)}, u32[]{:S(2)}) collective-permute-start(bf16[1152,512]{1,0:T(8,128)(2,1)} %fusion.13), channel_id=1, source_target_pairs={{0,32},{16,48},{32,0},{48,16},{64,96},{80,112},{96,64},{112,80},{1... | collective-permute-start | bytes 3538952 | tf_op jit(solution)/shard_map/ppermute | solution.py:869
  374.8 42.7 %collective-permute-start.12 = (bf16[1152,512]{1,0:T(8,128)(2,1)}, bf16[1152,512]{1,0:T(8,128)(2,1)}, u32[]{:S(2)}, u32[]{:S(2)}) collective-permute-start(bf16[1152,512]{1,0:T(8,128)(2,1)} %fusion.14), channel_id=1, source_target_pairs={{0,96},{16,112},{32,64},{48,80},{64,32},{80,48},{96,0},{112,16},{1... | collective-permute-start | bytes 3538952 | tf_op jit(solution)/shard_map/ppermute | solution.py:869
  405.4 54.0 %all-to-all-start.4 = ((bf16[16,224,384]{2,1,0:T(8,128)(2,1)}), bf16[16,224,384]{2,1,0:T(8,128)(2,1)}, u32[]{:S(2)}, u32[]{:S(2)}) async-start(bf16[16,224,384]{2,1,0:T(8,128)(2,1)} %copy-done.17), calls=%async_computation.7 | async-start | bytes 5505024 | tf_op jit(solution)/shard_map/all_to_all | solution.py:1009
  412.0 117.2 %reduce-scatter.8.cloned.1.call-start = ((), (), s32[]{:S(2)}) async-start(), calls=%async_computation.14 | async-start | bytes 3538944 | tf_op jit(solution)/shard_map/reduce_scatter | solution.py:1260
  443.5 22.0 %collective-permute-start.14 = (bf16[576,512]{1,0:T(8,128)(2,1)}, bf16[576,512]{1,0:T(8,128)(2,1)S(1)}, u32[]{:S(2)}, u32[]{:S(2)}) collective-permute-start(bf16[576,512]{1,0:T(8,128)(2,1)} %dynamic-slice_bitcast_fusion.7), channel_id=1, source_target_pairs={{0,96},{16,112},{32,64},{48,80},{64,32},{80,48},{96,0},{112,16},{1... | collective-permute-start | bytes 1769480 | tf_op jit(solution)/shard_map/ppermute | solution.py:869
  445.4 28.8 %collective-permute-start.17 = (bf16[576,512]{1,0:T(8,128)(2,1)}, bf16[576,512]{1,0:T(8,128)(2,1)}, u32[]{:S(2)}, u32[]{:S(2)}) collective-permute-start(bf16[576,512]{1,0:T(8,128)(2,1)} %dynamic-slice_bitcast_fusion.6), channel_id=1, source_target_pairs={{0,32},{16,48},{32,0},{48,16},{64,96},{80,112},{96,64},{112,80},{1... | collective-permute-start | bytes 1769480 | tf_op jit(solution)/shard_map/ppermute | solution.py:869
  466.5 20.8 %collective-permute-start.15 = (bf16[576,512]{1,0:T(8,128)(2,1)}, bf16[576,512]{1,0:T(8,128)(2,1)}, u32[]{:S(2)}, u32[]{:S(2)}) collective-permute-start(bf16[576,512]{1,0:T(8,128)(2,1)} %add_convert_fusion.5), channel_id=1, source_target_pairs={{0,96},{16,112},{32,64},{48,80},{64,32},{80,48},{96,0},{112,16},{1... | collective-permute-start | bytes 1769480 | tf_op jit(solution)/shard_map/ppermute | solution.py:874
  467.5 60.5 %all-to-all-start.5 = ((bf16[16,96,1152]{2,1,0:T(8,128)(2,1)}), bf16[16,96,1152]{2,1,0:T(8,128)(2,1)S(1)}, u32[]{:S(2)}, u32[]{:S(2)}) async-start(bf16[16,96,1152]{2,1,0:T(8,128)(2,1)} %bitcast.80), calls=%async_computation.8 | async-start | bytes 7077888 | tf_op jit(solution)/shard_map/all_to_all | solution.py:1009
  474.1 96.2 %all-gather.18.cloned.1.call-start = ((), (), s32[]{:S(2)}) async-start(), calls=%async_computation.16 | async-start | bytes 3538944 | tf_op jit(solution)/shard_map/all_gather | solution.py:1304
  476.4 16.5 %collective-permute-start.18 = (bf16[576,512]{1,0:T(8,128)(2,1)}, bf16[576,512]{1,0:T(8,128)(2,1)}, u32[]{:S(2)}, u32[]{:S(2)}) collective-permute-start(bf16[576,512]{1,0:T(8,128)(2,1)} %add_convert_fusion.4), channel_id=1, source_target_pairs={{0,32},{16,48},{32,0},{48,16},{64,96},{80,112},{96,64},{112,80},{1... | collective-permute-start | bytes 1769480 | tf_op jit(solution)/shard_map/ppermute | solution.py:874
  492.0 27.3 %collective-permute-start.16 = (bf16[1152,512]{1,0:T(8,128)(2,1)}, bf16[1152,512]{1,0:T(8,128)(2,1)}, u32[]{:S(2)}, u32[]{:S(2)}) collective-permute-start(bf16[1152,512]{1,0:T(8,128)(2,1)} %pad_maximum_fusion.6), channel_id=1, source_target_pairs={{0,32},{16,48},{32,0},{48,16},{64,96},{80,112},{96,64},{112,80},{1... | collective-permute-start | bytes 3538952 | tf_op jit(solution)/shard_map/ppermute | solution.py:874
  496.2 27.3 %collective-permute-start.19 = (bf16[1152,512]{1,0:T(8,128)(2,1)}, bf16[1152,512]{1,0:T(8,128)(2,1)}, u32[]{:S(2)}, u32[]{:S(2)}) collective-permute-start(bf16[1152,512]{1,0:T(8,128)(2,1)} %pad_maximum_fusion.7), channel_id=1, source_target_pairs={{0,96},{16,112},{32,64},{48,80},{64,32},{80,48},{96,0},{112,16},{1... | collective-permute-start | bytes 3538952 | tf_op jit(solution)/shard_map/ppermute | solution.py:874
  501.0 14.6 %collective-permute-start.13 = (bf16[128,384]{1,0:T(8,128)(2,1)S(1)}, bf16[128,384]{1,0:T(8,128)(2,1)S(1)}, u32[]{:S(2)}, u32[]{:S(2)}) collective-permute-start(bf16[128,384]{1,0:T(8,128)(2,1)S(1)} %slice.526), channel_id=1, source_target_pairs={{0,0},{1,16},{2,32},{3,48},{4,64},{5,80},{6,96},{7,112},{8,1},{9,1... | collective-permute-start | bytes 294920 | tf_op jit(solution)/shard_map/ppermute | solution.py:1294
  538.2 18.2 %collective-permute-start.20 = (bf16[4608,512]{1,0:T(8,128)(2,1)}, bf16[4608,512]{1,0:T(8,128)(2,1)}, u32[]{:S(2)}, u32[]{:S(2)}) collective-permute-start(bf16[4608,512]{1,0:T(8,128)(2,1)} %pad_maximum_fusion.own_ref), channel_id=1, source_target_pairs={{0,16},{16,0},{32,48},{48,32},{64,80},{80,64},{96,112},{112,96},{1... | collective-permute-start | bytes 14155784 | tf_op jit(solution)/shard_map/ppermute | solution.py:1302
  (75 other events, 641.2 us)
Sparse Core Ops, SparseCore 0:
  20.7 62.5 all-gather.15
  87.2 27.0 all-gather.9
  159.6 34.4 reduce-scatter.3
  199.1 29.5 all-gather.11
  265.3 49.5 reduce-scatter.5
  320.4 47.0 all-gather.13
  446.8 44.1 reduce-scatter.7
  534.2 33.2 all-gather.17

commit v10 on v9

--- a/solution.py
+++ b/solution.py
@@ -8,7 +8,6 @@
 from jax.sharding import PartitionSpec as P
 
 CAP = 32
-VMEM_LIMIT = 60 << 20
 
 
 epsilon = 1e-05
@@ -35,6 +34,11 @@
 def after(value, *others):
     corners = [o[(0,) * (o.ndim - 1)][:1].astype(jnp.float32) for o in others]
     return (value.astype(jnp.float32) + 0.0 * sum(corners)).astype(value.dtype)
+
+
+def corner_after(values, other):
+    at = (0.0 * other[(0,) * other.ndim]).astype(jnp.int32)
+    return lax.dynamic_slice(values, (at,) * values.ndim, (1,) * values.ndim)
 
 
 def silu_slope(values):
@@ -139,8 +143,8 @@
 
 
 def front_kernel(
-    x_ref, w_in_ref, rows_in_ref, place_ref, taps_ref, head_ref, skip_ref,
-    proj_ref, scale_ref, w_ref, out_w_ref, mixed_ref, q_ref, out_ref, square_ref, start_ref,
+    here_ref, column_ref, other_ref, w_in_ref, rows_in_ref, place_ref, taps_ref, head_ref, skip_ref,
+    x_ref, proj_ref, scale_ref, w_ref, out_w_ref, mixed_ref, q_ref, out_ref, square_ref, start_ref,
     state_ref, pad_ref,
 ):
     f32, bf = jnp.float32, jnp.bfloat16
@@ -159,7 +163,12 @@
             tail = tail + times(place_ref[1 + part], folded[:, rest * part : rest * part + rest])
         out_w_ref[:, width:] = tail.astype(bf)
 
-    x = x_ref[...]
+    column, other = column_ref[0].astype(f32), other_ref[0].astype(f32)
+    first = here_ref[1] == 0
+    x = jnp.concatenate(
+        [jnp.where(first, column, other), jnp.where(first, other, column)], axis=0
+    ).astype(bf)
+    x_ref[...] = x
     scale = row_scale(x.astype(f32))
     proj = times(x, w_ref[...]) * scale
     proj_ref[...] = proj
@@ -316,16 +325,17 @@
 
 
 def whole(shape):
-    return pl.BlockSpec(shape, lambda step: (0,) * len(shape))
-
-
-def front(x_all, weights, rows_w, taps, head, skip):
+    return pl.BlockSpec(shape, lambda *step: (0,) * len(shape))
+
+
+def front(here, column, other, weights, rows_w, taps, head, skip):
     f32, bf = jnp.float32, jnp.bfloat16
-    rows, dim = x_all.shape
+    chips, block, dim = column.shape
+    rows = 2 * chips * block
     sources, _, width = weights.shape
     own = WIDE // sources
     count = own * dim // width
-    tile = 2 * CHUNK
+    tile = 2 * block
     row = jnp.arange(WIDE)[:, None]
     slot = jnp.arange(sources * count)[None, :]
     same = row // own == slot // count
@@ -335,21 +345,26 @@
         for part in range(own // deep)
     ]
     place = jnp.stack(place).astype(bf)
-    by_tile = lambda step: (step, 0)
+    by_tile = lambda step, here: (step, 0)
+    by_chip = lambda step, here: ((here[0] + chips - step) % chips, 0, 0)
     chunks = rows // CHUNK
     return pl.pallas_call(
         front_kernel,
+        grid_spec=pltpu.PrefetchScalarGridSpec(
+            num_scalar_prefetch=1,
         grid=(rows // tile,),
         in_specs=[
-            pl.BlockSpec((tile, dim), by_tile),
-            pl.BlockSpec((sources, rows_w, width), lambda step: (0, 0, 0)),
-            pl.BlockSpec((sources, count, width), lambda step: (0, rows_w // count, 0)),
+            pl.BlockSpec((1, block, dim), by_chip),
+            pl.BlockSpec((1, block, dim), by_chip),
+            pl.BlockSpec((sources, rows_w, width), lambda *step: (0, 0, 0)),
+            pl.BlockSpec((sources, count, width), lambda *step: (0, rows_w // count, 0)),
             whole(place.shape),
             whole(taps.shape),
             whole(head.shape),
             whole(skip.shape),
         ],
         out_specs=[
+            pl.BlockSpec((tile, dim), by_tile),
             pl.BlockSpec((tile, width), by_tile),
             pl.BlockSpec((tile, 1), by_tile),
             whole((dim, width)),
@@ -358,9 +373,15 @@
             pl.BlockSpec((tile, WIDE), by_tile),
             pl.BlockSpec((tile, dim), by_tile),
             pl.BlockSpec((tile, 1), by_tile),
-            pl.BlockSpec((tile // CHUNK, 128, WIDE), lambda step: (step, 0, 0)),
-        ],
+            pl.BlockSpec((tile // CHUNK, 128, WIDE), lambda step, here: (step, 0, 0)),
+        ],
+        scratch_shapes=[
+            pltpu.VMEM((128, WIDE), f32),
+            pltpu.VMEM((CHUNK + 8, CONVW), f32),
+        ],
+        ),
         out_shape=[
+            jax.ShapeDtypeStruct((rows, dim), bf),
             jax.ShapeDtypeStruct((rows, width), f32),
             jax.ShapeDtypeStruct((rows, 1), f32),
             jax.ShapeDtypeStruct((dim, width), bf),
@@ -371,16 +392,12 @@
             jax.ShapeDtypeStruct((rows, 1), f32),
             jax.ShapeDtypeStruct((chunks, 128, WIDE), f32),
         ],
-        scratch_shapes=[
-            pltpu.VMEM((128, WIDE), f32),
-            pltpu.VMEM((CHUNK + 8, CONVW), f32),
-        ],
-        compiler_params=pltpu.CompilerParams(vmem_limit_bytes=VMEM_LIMIT),
+        compiler_params=pltpu.CompilerParams(vmem_limit_bytes=52 << 20),
         cost_estimate=pl.CostEstimate(
             flops=16 << 30, bytes_accessed=48 << 20, transcendentals=4 << 20
         ),
         name="front",
-    )(x_all, weights, weights, place, taps, head, skip)
+    )(here, column, other, weights, weights, place, taps, head, skip)
 
 
 def scan_backward(chunks, inputs, held, carry, sums):
@@ -430,9 +447,9 @@
             pltpu.VMEM((CHUNK + 8, CONVW), jnp.float32),
         ],
         input_output_aliases={len(given) + i: i for i in range(len(held))},
-        compiler_params=pltpu.CompilerParams(vmem_limit_bytes=VMEM_LIMIT),
+        compiler_params=pltpu.CompilerParams(vmem_limit_bytes=48 << 20),
         cost_estimate=pl.CostEstimate(
-            flops=(1 << 20) if held else (10 << 30), bytes_accessed=1 << 20, transcendentals=0
+            flops=20 << 30, bytes_accessed=40 << 20, transcendentals=16 << 20
         ),
         name="scan_backward",
     )(*given, *held)
@@ -481,7 +498,7 @@
             jax.ShapeDtypeStruct((slots.shape[0], dim), jnp.bfloat16),
             jax.ShapeDtypeStruct((rows, 128), jnp.float32),
         ],
-        compiler_params=pltpu.CompilerParams(vmem_limit_bytes=VMEM_LIMIT),
+        compiler_params=pltpu.CompilerParams(vmem_limit_bytes=60 << 20),
         cost_estimate=pl.CostEstimate(flops=1 << 28, bytes_accessed=5 << 20, transcendentals=0),
         name="token_front",
     )(x, out_sum, scale, gain, slots, w_all, named)
@@ -554,7 +571,7 @@
             jax.ShapeDtypeStruct((rows, 128), jnp.float32),
             jax.ShapeDtypeStruct((8, dim), jnp.float32),
         ],
-        compiler_params=pltpu.CompilerParams(vmem_limit_bytes=VMEM_LIMIT),
+        compiler_params=pltpu.CompilerParams(vmem_limit_bytes=60 << 20),
         cost_estimate=pl.CostEstimate(flops=1 << 29, bytes_accessed=8 << 20, transcendentals=0),
         name="token_back",
     )(back, slots, shared_both, x, resid, gates, w_all, gain, cot)
@@ -647,7 +664,7 @@
 
 def expert_params(flops, moved):
     return dict(
-        compiler_params=pltpu.CompilerParams(vmem_limit_bytes=VMEM_LIMIT),
+        compiler_params=pltpu.CompilerParams(vmem_limit_bytes=56 << 20),
         cost_estimate=pl.CostEstimate(flops=flops, bytes_accessed=moved, transcendentals=1 << 19),
     )
 
@@ -818,7 +835,7 @@
         in_specs=[pl.BlockSpec(memory_space=pltpu.VMEM)] * 5,
         out_specs=[pl.BlockSpec(memory_space=pltpu.VMEM)] * len(shapes),
         out_shape=[jax.ShapeDtypeStruct(shape, jnp.float32) for shape in shapes],
-        compiler_params=pltpu.CompilerParams(vmem_limit_bytes=VMEM_LIMIT),
+        compiler_params=pltpu.CompilerParams(vmem_limit_bytes=40 << 20),
         cost_estimate=pl.CostEstimate(flops=8 << 20, bytes_accessed=12 << 20, transcendentals=0),
         name="assemble",
     )(side, in_weight, in_gain, out_weight, out_gain)
@@ -839,7 +856,7 @@
     return jnp.concatenate([values[:, :count], jnp.concatenate(parts, axis=1)], axis=2)
 
 
-def gather_rows(values, core, z_at, mates):
+def gather_blocks(values, mates):
     cores = 2
     chips = len(mates) // cores
     column = [values]
@@ -849,25 +866,23 @@
         ]
         column.append(lax.ppermute(values, "seq", pairs))
     column = jnp.stack(column)
-    both = jnp.stack([column, lax.ppermute(column, "seq", mates)], axis=1)
-    both = both.reshape((len(mates),) + values.shape)
-    ordered = [
-        lax.dynamic_index_in_dim(both, (z_at - z) % chips * cores + (c ^ core), 0, keepdims=False)
-        for z in range(chips)
-        for c in range(cores)
-    ]
-    return jnp.concatenate(ordered, axis=0)
-
-
-def halve(values, bit, pairs, start=None):
-    f32 = jnp.float32
+    return column, lax.ppermute(column, "seq", mates)
+
+
+def halves(values, bit):
     parts = values.reshape(2, values.shape[0] // 2, values.shape[1])
     sent = lax.dynamic_index_in_dim(parts, 1 - bit, 0, keepdims=False)
-    kept = lax.dynamic_index_in_dim(parts, bit, 0, keepdims=False)
-    if start is not None:
-        sent = after(sent, start)
+    return sent, lax.dynamic_index_in_dim(parts, bit, 0, keepdims=False)
+
+
+def add_other(kept, sent, pairs):
     other = lax.ppermute(sent, "seq", pairs)
-    return (kept.astype(f32) + other.astype(f32)).astype(jnp.bfloat16)
+    return (kept.astype(jnp.float32) + other.astype(jnp.float32)).astype(jnp.bfloat16)
+
+
+def halve(values, bit, pairs):
+    sent, kept = halves(values, bit)
+    return add_other(kept, sent, pairs)
 
 
 def double(values, bit, pairs):
@@ -920,7 +935,7 @@
             jax.ShapeDtypeStruct((2, dim, units), jnp.float32),
             jax.ShapeDtypeStruct((2, units, dim), jnp.float32),
         ],
-        compiler_params=pltpu.CompilerParams(vmem_limit_bytes=VMEM_LIMIT),
+        compiler_params=pltpu.CompilerParams(vmem_limit_bytes=40 << 20),
         cost_estimate=pl.CostEstimate(flops=1 << 20, bytes_accessed=28 << 20, transcendentals=0),
         name="unpack_expert_grads",
     )(core.reshape(1), own, other)
@@ -1003,14 +1018,13 @@
         ],
         axis=1,
     )
-    small_all = lax.all_gather(jnp.pad(small, (0, total - small.shape[0])), "shard", axis=0)
 
     def to_shards(values):
         return lax.all_to_all(values, "shard", split_axis=0, concat_axis=0, tiled=True)
 
     core, z_at = q % 2, q // 2
     mates = [(i, i ^ 1) for i in range(sq)]
-    x_all = gather_rows(x_low, core, z_at, mates)
+    x_column, x_other = gather_blocks(x_low, mates)
 
     out_scaled = (norm_gain.astype(f32)[:, None] * out_weight.astype(f32)).astype(bf)
     own_out = out_weight.shape[0] // sq
@@ -1095,7 +1109,10 @@
     lanes = jnp.arange(128, dtype=jnp.int32)
     named_lanes = jnp.pad(named, ((0, 0), (router_lane, 128 - router_lane - experts)))
     cot_sent = in_slots(jnp.concatenate([cot_low, named_lanes.astype(bf)], axis=1))
-    cot_rows = dispatched(cot_sent)
+    weights, cot_late = lax.optimization_barrier((weights, cot_sent))
+    cot_rows = dispatched(cot_late)
+    small = after(jnp.pad(small, (0, total - small.shape[0])), cot_sent)
+    small_all = to_shards(jnp.broadcast_to(small[None, None], (sh, 1, total)))[:, 0]
 
     at = taps * conv_own
     conv_full = (
@@ -1126,17 +1143,20 @@
     decay_rate = -jnp.exp(decay_local)
     head_in = jnp.pad(jnp.stack([bias_local, decay_rate]), ((0, 6), (0, 128 - gh)))
     skip_in = jnp.broadcast_to(jnp.repeat(skip_local, per_head)[None], (8, gw))
-    proj, x_r, w_all, w_out, mixed, q_low, out_part, square_part, starts = front(
-        x_all, weights, rows_w, taps_in, after(head_in, cot_sent), skip_in
-    )
-
-    cot_all = lax.all_gather(after(cot_low, weights), "seq", axis=0, tiled=True)
-    square_part = after(square_part.reshape(sq, toks), cot_all)
+    place_here = jnp.stack([z_at, core]).astype(jnp.int32)
+    x_all, proj, x_r, w_all, w_out, mixed, q_low, out_part, square_part, starts = front(
+        place_here, x_column, x_other, weights, rows_w, taps_in, head_in, skip_in
+    )
+
+    cot_all = lax.all_gather(after(cot_low, x_column), "seq", axis=0, tiled=True)
+    square_part = square_part.reshape(sq, toks)
+    square_part = after(square_part, corner_after(cot_all, square_part))
     out_sum = lax.psum_scatter(out_part, "seq", scatter_dimension=0, tiled=True)
     square = lax.psum(square_part, "seq")
     q_r = lax.rsqrt(square / inner + epsilon).reshape(seq_rows, 1)
     d_raw = expert_early(cot_rows, expert_down, square)
-    tok_r = after(lax.dynamic_slice_in_dim(q_r, q * toks, toks, 0), d_raw)
+    tok_r = lax.dynamic_slice_in_dim(q_r, q * toks, toks, 0)
+    tok_r = after(tok_r, d_raw)
     x_tok = x_low.astype(f32)
     resid, moe_in, moe_sent, gates = token_front(
         x_low, out_sum, tok_r, moe_gain_rows, dispatch_flat, w_all, named_lanes
@@ -1200,42 +1220,18 @@
     grad_router = grad_router + jnp.pad(d_moe_gain[0][:, None], ((0, 0), (0, 127)))
     d_o_all = lax.all_gather(d_o_ext, "seq", axis=0, tiled=True)
 
+    sent_one, kept_one = halves(e_mine[:cutoff], is_inner)
+    sent_two, kept_two = halves(e_mine[cutoff:], is_high)
+    d_o_all, sent_one, sent_two = lax.optimization_barrier((d_o_all, sent_one, sent_two))
     grad_out_part = transposed_times(q_low, (q_r * d_o_all[:, :dim].astype(f32)).astype(bf))
 
-    mid_part = jnp.concatenate(
-        [
-            grad_shared_part,
-            grad_router.astype(bf),
-        ],
-        axis=1,
-    )
-    lane_w = mid_part.shape[1]
-    bands = dim // lane_w
-
-    def to_bands(values):
-        return jnp.concatenate(
-            [values[:, :, band * lane_w : band * lane_w + lane_w] for band in range(bands)], axis=1
-        )
-
-    early_part = jnp.concatenate(
-        [
-            to_bands(grad_out_part.astype(bf).reshape(sh, own_out, dim)),
-            to_bands(grad_down_part.reshape(sh, own_down, dim)),
-            mid_part.reshape(sh, rows_w, lane_w),
-        ],
-        axis=1,
-    )
-    moved_early = to_shards(early_part)
-
-    e_one = halve(e_mine[:cutoff], is_inner, near, d_o_all)
-    e_two = halve(e_mine[cutoff:], is_high, far, d_o_all)
     row_values = jnp.concatenate(
         [q_r, x_r, jnp.zeros((seq_rows, 6), f32)], axis=1
     )
     scan_inputs = (proj, mixed, d_o_all, row_values, starts, taps_in)
     scan_inputs = scan_inputs + (head_in, skip_in, w_all, w_out)
     chunks = seq_rows // CHUNK
-    middle = chunks // 2
+    middle = chunks - 2
     *held, carry, sums = scan_backward(
         (middle, chunks),
         scan_inputs,
@@ -1243,13 +1239,34 @@
         jnp.zeros((136, gw + keys_w), f32),
         jnp.zeros((24, gw + keys_w), f32),
     )
-    route_gates = after(gates, carry)[:, router_lane : router_lane + experts]
-    weighted = (route_gates.T[:, None, :] * dispatch.astype(f32)).reshape(slots, toks)
-    combined = transposed_times(weighted.astype(bf), returned.reshape(slots, dim))
-    carry = after(carry, combined, early_part, e_one, e_two)
-    d_proj, back_part, carry, sums = scan_backward(
-        (0, middle), scan_inputs, held, carry, sums
-    )
+    mid_part = jnp.concatenate(
+        [
+            grad_shared_part,
+            after(grad_router, corner_after(returned, carry)).astype(bf),
+        ],
+        axis=1,
+    )
+    lane_w = mid_part.shape[1]
+    bands = dim // lane_w
+
+    def to_bands(values):
+        return jnp.concatenate(
+            [values[:, :, band * lane_w : band * lane_w + lane_w] for band in range(bands)], axis=1
+        )
+
+    early_part = jnp.concatenate(
+        [
+            to_bands(grad_out_part.astype(bf).reshape(sh, own_out, dim)),
+            to_bands(grad_down_part.reshape(sh, own_down, dim)),
+            mid_part.reshape(sh, rows_w, lane_w),
+        ],
+        axis=1,
+    )
+    moved_early = to_shards(early_part)
+    d_proj, back_part, carry, sums = scan_backward((0, middle), scan_inputs, held, carry, sums)
+    d_proj, moved_early = lax.optimization_barrier((d_proj, moved_early))
+    e_one = add_other(after(kept_one, d_proj), sent_one, near)
+    e_two = add_other(after(kept_two, d_proj), sent_two, far)
     d_taps, d_head, d_skip = sums[0:8], sums[8:16, :128], sums[16:24, :gw]
     grad_conv_local = d_taps[:taps]
     grad_offset_local = d_taps[taps]
@@ -1258,6 +1275,9 @@
     grad_skip_local = jnp.sum(d_skip[0].reshape(gh, per_head), axis=1)
     e_one, e_two = halve(e_one, is_high, far), halve(e_two, is_inner, near)
     back_sum = lax.psum_scatter(back_part, "seq", scatter_dimension=0, tiled=True).astype(f32)
+    route_gates = gates[:, router_lane : router_lane + experts]
+    weighted = (route_gates.T[:, None, :] * dispatch.astype(f32)).reshape(slots, toks)
+    combined = transposed_times(weighted.astype(bf), returned.reshape(slots, dim))
     block_output = ((resid + shared_sum.astype(f32) + combined) * live[:, None]).astype(bf)[None]
     tok_x_r = row_scale(x_tok)
     x_n = x_tok * tok_x_r
@@ -1266,7 +1286,6 @@
     )[None]
 
     grad_in_part = transposed_times(x_all, d_proj).astype(bf)
-    grad_in_part, moved_early = lax.optimization_barrier((grad_in_part, moved_early))
 
     def spread(local, count):
         wide = jnp.zeros(local.shape[:-1] + (count,), f32)

time: 604 us -> 551 us (0.912)
  the two profiles are of different devices: /device:TPU:33 before, /device:TPU:1 now
where the time goes in v10:
time: 551 us; the launch traced here: 541 us
  waiting for transfers between devices  150 us (27%)
  Pallas kernels  125 us (23%)
  starting transfers between devices  81.1 us (15%)
  local copies, waits for them, and re-layouts  72.8 us (13%)
  other arithmetic  48.5 us (9%)
  between operations  29.8 us (5%)
  matrix products  19.8 us (4%)
  blocking collectives  13.7 us (2%)
    all_to_all x7, starting transfers between devices, to_shards(): lax.all_to_all(values, 'shard', split_axis=0, concat_axis=0, tiled=True)  42.1 us
    pallas_call x2, Pallas kernels, scan_backward(): pl.pallas_call(functools.partial(scan_backward_kernel, chunks, len(held))...  37.4 us
    all_to_all x7, waiting for transfers between devices, to_shards(): lax.all_to_all(values, 'shard', split_axis=0, concat_axis=0, tiled=True)  35.3 us
    all_gather x1, waiting for transfers between devices, on_device(): d_o_all = lax.all_gather(d_o_ext, 'seq', axis=0, tiled=True)  31.5 us
    all_gather x1, waiting for transfers between devices, on_device(): lax.all_gather(jnp.concatenate([packed, fold_rows(piece[:own_out], total)...  29.4 us
    unnamed x171, local copies, waits for them, and re-layouts  24.7 us
    pallas_call x1, Pallas kernels, front(): pl.pallas_call(front_kernel, grid_spec=pltpu.PrefetchScalarGridSpec(num_s...  24.2 us
    pallas_call x1, Pallas kernels, expert_main(): pl.pallas_call(expert_main_kernel, grid=(local,), in_specs=[expert_slots(...  19.3 us
  transfers between devices with their start and end apart: 36, of which 17 were waited for; matrix products, arithmetic and copies ran while one was open for 21% of the time, Pallas kernels for 17%

profile of v10, /device:TPU:1, one launch (start us, length us, event | category | flops | bytes accessed | tf_op | source)
XLA Modules:
  0.0 540.9 jit_solution(13907722529001264714)
XLA Ops:
  9.1 4.6 collective-permute-start.4
  23.3 8.6 %collective-permute-start.2 = (bf16[128,1536]{1,0:T(8,128)(2,1)S(1)}, bf16[128,1536]{1,0:T(8,128)(2,1)S(1)}, u32[]{:S(2)}, u32[]{:S(2)}) collective-permute-start(bf16[128,1536]{1,0:T(8,128)(2,1)S(1)} %bitcast.174), channel_id=1, source_target_pairs={{0,96},{16,112},{32,0},{48,16},{64,32},{80,48},{96,64},{112,80},{1... | collective-permute-start | bytes 1179656 | tf_op jit(solution)/shard_map/ppermute | solution.py:867
  55.1 29.4 %all-gather.14.cloned.1.call-done = bf16[2560,1152]{1,0:T(8,128)(2,1)} async-done(((bf16[160,1152]{1,0:T(8,128)(2,1)}), bf16[2560,1152]{1,0:T(8,128)(2,1)}) %all-gather.14.cloned.1.call-update) | async-done | bytes 5898256 | tf_op jit(solution)/shard_map/all_gather | solution.py:1061
  84.5 5.0 all-to-all-start.1
  91.1 24.2 %front.1 = (bf16[1024,1536]{1,0:T(8,128)(2,1)}, f32[1024,1152]{1,0:T(8,128)}, f32[1024,1]{1,0:T(8,128)S(1)}, bf16[1536,1152]{1,0:T(8,128)(2,1)}, bf16[384,1536]{...) custom-call(s32[2]{0:T(128)S(1)} %pad_add_fusion.here_ref, ...), custom_call_target="tpu_custom_call" | custom-call | flops 17179869184 | bytes 50331648 | tf_op jit(solution)/shard_map/front/pallas_call | solution.py:351
  118.7 13.7 %psum.7.earlier_ref = f32[8,128]{1,0:T(8,128)S(1)} all-reduce(f32[8,128]{1,0:T(8,128)S(1)} %broadcast_add_fusion.2), channel_id=1, replica_groups=mesh['seq'=8,'shard'=16] {'seq'}, use_global_device_ids=true, to_apply=%region_2.3 | all-reduce | flops 1024 | bytes 8192 | tf_op jit(solution)/shard_map/psum | solution.py:1155
  133.0 5.0 expert_early.1.raw_ref
  140.5 11.5 %reduce-scatter.4.cloned.1.call-done.out_ref = bf16[128,1536]{1,0:T(8,128)(2,1)} async-done(((bf16[1024,1536]{1,0:T(8,128)(2,1)}), bf16[128,1536]{1,0:T(8,128)(2,1)}) %reduce-scatter.4.cloned.1.call-update) | async-done | bytes 393232 | tf_op jit(solution)/shard_map/reduce_scatter | solution.py:1154
  152.6 4.3 token_front.1
  156.9 6.6 %all-to-all-start.2 = ((bf16[16,64,1536]{2,1,0:T(8,128)(2,1)}), bf16[16,64,1536]{2,1,0:T(8,128)(2,1)}, u32[]{:S(2)}, u32[]{:S(2)}) async-start(bf16[16,64,1536]{2,1,0:T(8,128)(2,1)} %bitcast.190), calls=%async_computation.3 | async-start | bytes 6291456 | tf_op jit(solution)/shard_map/all_to_all | solution.py:1023
  173.4 25.8 %all-to-all-done.2 = bf16[16,64,1536]{2,1,0:T(8,128)(2,1)} async-done(((bf16[16,64,1536]{2,1,0:T(8,128)(2,1)}), bf16[16,64,1536]{2,1,0:T(8,128)(2,1)}, u32[]{:S(2)}, u32[]{:S(2)}) %all-to-all-start.2) | async-done | bytes 3145760 | tf_op jit(solution)/shard_map/all_to_all | solution.py:1023
  199.2 19.3 %expert_main.1 = (bf16[16,2,32,1664]{3,2,1,0:T(8,128)(2,1)}, bf16[2,512,512]{2,1,0:T(8,128)(2,1)}, bf16[2,512,512]{2,1,0:T(8,128)(2,1)}, bf16[2,512,512]{2,1,0:T...) custom-call(bf16[16,2,32,1536]{3,2,1,0:T(8,128)(2,1)} %bitcast.24.ro, ...), custom_call_target="tpu_custom_call" | custom-call | flops 8589934592 | bytes 20971520 | tf_op jit(solution)/shard_map/expert_main/pallas_call | solution.py:699
  218.6 9.8 %all-to-all-start.3 = ((bf16[16,64,1664]{2,1,0:T(8,128)(2,1)}), bf16[16,64,1664]{2,1,0:T(8,128)(2,1)}, u32[]{:S(2)}, u32[]{:S(2)}) async-start(bf16[16,64,1664]{2,1,0:T(8,128)(2,1)} %bitcast.188), calls=%async_computation.5 | async-start | bytes 6815744 | tf_op jit(solution)/shard_map/all_to_all | solution.py:1023
  231.2 12.7 %expert_late.1 = (bf16[16,2,32,1536]{3,2,1,0:T(8,128)(2,1)}, bf16[2,1536,512]{2,1,0:T(8,128)(2,1)}, bf16[2,1536,512]{2,1,0:T(8,128)(2,1)}, bf16[2,1536,512]{2,1,0:T(8,128)(2,1)}) custom-call(bf16[16,2,32,1536]{3,2,1,0:T(8,128)(2,1)} %bitcast.24.rows_ref, bf16[16,2,32,1664]{3,2,1,0:T(8,128)(2,1)} %bitcast.21.cot_ref.routed_ref, ...), custom_call_target="tpu_custom_call" | custom-call | flops 7516192768 | bytes 25165824 | tf_op jit(solution)/shard_map/expert_late/pallas_call | solution.py:733
  266.0 4.0 all-to-all-done.3
  272.7 5.4 %token_back.1 = (bf16[128,1664]{1,0:T(8,128)(2,1)}, f32[128,1536]{1,0:T(8,128)}, f32[128,128]{1,0:T(8,128)}, f32[8,1536]{1,0:T(8,128)}) custom-call(bf16[1024,1664]{1,0:T(8,128)(2,1)} %bitcast.34.back_ref, bf16[1024,128]{1,0:T(8,128)(2,1)} %get-tuple-element.281.slots_ref, bf16[128,3072]{1,0:T(8,128)(2,1)} %reduce-scatter.6.cloned.1.call-done.shared_ref, ...), custom_call_target="tpu_custom_call" | custom-call | flops 536870912 | bytes 8388608 | tf_op jit(solution)/shard_map/token_back/pallas_call | solution.py:548
  284.6 6.9 %all-to-all-start.4 = ((bf16[16,64,1536]{2,1,0:T(8,128)(2,1)}), bf16[16,64,1536]{2,1,0:T(8,128)(2,1)}, u32[]{:S(2)}, u32[]{:S(2)}) async-start(bf16[16,64,1536]{2,1,0:T(8,128)(2,1)} %bitcast.189), calls=%async_computation.6 | async-start | bytes 6291456 | tf_op jit(solution)/shard_map/all_to_all | solution.py:1023
  293.6 31.5 %all-gather.12.cloned.1.call-done.d_o_ref = bf16[1024,1664]{1,0:T(8,128)(2,1)} async-done(((bf16[128,1664]{1,0:T(8,128)(2,1)}), bf16[1024,1664]{1,0:T(8,128)(2,1)}) %all-gather.12.cloned.1.call-update) | async-done | bytes 3407888 | tf_op jit(solution)/shard_map/all_gather | solution.py:1221
  326.4 10.9 %scan_backward.2 = (bf16[1024,1152]{1,0:T(8,128)(2,1)}, bf16[1024,1536]{1,0:T(8,128)(2,1)}, f32[136,640]{1,0:T(8,128)S(1)}, f32[24,640]{1,0:T(8,128)S(1)}) custom-call(f32[1024,1152]{1,0:T(8,128)} %get-tuple-element.100.proj_ref.prev_ref, f32[1024,1152]{1,0:T(8,128)} %get-tuple-element.100.proj_ref.prev_ref, ...), custom_call_target="tpu_custom_call" | custom-call | flops 21474836480 | bytes 41943040 | tf_op jit(solution)/shard_map/scan_backward/pallas_call | solution.py:411
  355.5 6.6 %all-to-all-start.5 = ((bf16[16,224,384]{2,1,0:T(8,128)(2,1)}), bf16[16,224,384]{2,1,0:T(8,128)(2,1)}, u32[]{:S(2)}, u32[]{:S(2)}) async-start(bf16[16,224,384]{2,1,0:T(8,128)(2,1)} %constant_dynamic-update-slice_fusion.9), calls=%async_computation.8 | async-start | bytes 5505024 | tf_op jit(solution)/shard_map/all_to_all | solution.py:1023
  363.4 26.5 %scan_backward.3 = (bf16[1024,1152]{1,0:T(8,128)(2,1)}, bf16[1024,1536]{1,0:T(8,128)(2,1)}, f32[136,640]{1,0:T(8,128)}, f32[24,640]{1,0:T(8,128)S(1)}) custom-call(f32[1024,1152]{1,0:T(8,128)} %get-tuple-element.100.proj_ref.prev_ref, f32[1024,1152]{1,0:T(8,128)} %get-tuple-element.100.proj_ref.prev_ref, ...), custom_call_target="tpu_custom_call", output_to_operand_aliasing={{0}: (13, {}), {1}: (14, {})} | custom-call | flops 21474836480 | bytes 41943040 | tf_op jit(solution)/shard_map/scan_backward/pallas_call | solution.py:411
  393.0 5.2 all-to-all-done.5
  407.4 4.6 fusion.2
  413.3 7.4 %collective-permute-done.13 = bf16[576,512]{1,0:T(8,128)(2,1)S(1)} collective-permute-done((bf16[576,512]{1,0:T(8,128)(2,1)S(1)}, bf16[576,512]{1,0:T(8,128)(2,1)S(1)}, u32[]{:S(2)}, u32[]{:S(2)}) %collective-permute-start.13) | collective-permute-done | bytes 589856 | tf_op jit(solution)/shard_map/ppermute | solution.py:879
  424.7 3.8 all-to-all-start.6
  430.8 10.1 %collective-permute-done.14 = bf16[576,512]{1,0:T(8,128)(2,1)} collective-permute-done((bf16[576,512]{1,0:T(8,128)(2,1)}, bf16[576,512]{1,0:T(8,128)(2,1)}, u32[]{:S(2)}, u32[]{:S(2)}) %collective-permute-start.14) | collective-permute-done | bytes 589856 | tf_op jit(solution)/shard_map/ppermute | solution.py:889
  454.5 6.9 %collective-permute-start.11 = (bf16[128,384]{1,0:T(8,128)(2,1)S(1)}, bf16[128,384]{1,0:T(8,128)(2,1)S(1)}, u32[]{:S(2)}, u32[]{:S(2)}) collective-permute-start(bf16[128,384]{1,0:T(8,128)(2,1)S(1)} %slice.479), channel_id=1, source_target_pairs={{0,0},{1,16},{2,32},{3,48},{4,64},{5,80},{6,96},{7,112},{8,1},{9,1... | collective-permute-start | bytes 294920 | tf_op jit(solution)/shard_map/ppermute | solution.py:1313
  461.5 6.5 %collective-permute-done.11 = bf16[128,384]{1,0:T(8,128)(2,1)S(1)} collective-permute-done((bf16[128,384]{1,0:T(8,128)(2,1)S(1)}, bf16[128,384]{1,0:T(8,128)(2,1)S(1)}, u32[]{:S(2)}, u32[]{:S(2)}) %collective-permute-start.11) | collective-permute-done | bytes 98336 | tf_op jit(solution)/shard_map/ppermute | solution.py:1313
  485.7 4.1 pad_maximum_fusion.own_ref
  489.8 4.3 collective-permute-start.20
  501.9 14.0 %unpack_expert_grads.1 = (f32[2,1536,512]{2,1,0:T(8,128)}, f32[2,1536,512]{2,1,0:T(8,128)}, f32[2,512,1536]{2,1,0:T(8,128)}) custom-call(s32[1]{0:T(128)} %bitcast.2.core_ref, bf16[4608,512]{1,0:T(8,128)(2,1)} %pad_maximum_fusion.own_ref, bf16[4608,512]{1,0:T(8,128)(2,1)} %collective-permute-done.20.other_ref), custom_call_target="tpu_custom_call" | custom-call | flops 1048576 | bytes 29360128 | tf_op jit(solution)/shard_map/unpack_expert_grads/pallas_call | solution.py:918
  515.9 7.8 %all-gather.16.cloned.1.call-done = bf16[4096,384]{1,0:T(8,128)(2,1)} async-done(((bf16[512,384]{1,0:T(8,128)(2,1)}), bf16[4096,384]{1,0:T(8,128)(2,1)}) %all-gather.16.cloned.1.call-update) | async-done | bytes 3145744 | tf_op jit(solution)/shard_map/all_gather | solution.py:1323
  (443 shorter events, 164.1 us)
Async XLA Ops:
  7.2 77.3 %all-gather.14.cloned.1.call-start = ((), (), s32[]{:S(2)}) async-start(), calls=%async_computation.16 | async-start | bytes 6266880 | tf_op jit(solution)/shard_map/all_gather | solution.py:1061
  9.1 10.4 %collective-permute-start.4 = (bf16[32,1536]{1,0:T(8,128)(2,1)S(1)}, bf16[32,1536]{1,0:T(8,128)(2,1)S(1)}, u32[]{:S(2)}, u32[]{:S(2)}) collective-permute-start(bf16[32,1536]{1,0:T(8,128)(2,1)S(1)} %pad_maximum_fusion.8), channel_id=1, source_target_pairs={{0,0},{16,1},{32,2},{48,3},{64,4},{80,5},{96,6},{112,7},{1,8},{17,... | collective-permute-start | bytes 294920 | tf_op jit(solution)/shard_map/ppermute | solution.py:1047
  20.4 96.4 %all-gather.8.cloned.1.call-start = ((), (), s32[]{:S(2)}) async-start(), calls=%async_computation.11 | async-start | bytes 3538944 | tf_op jit(solution)/shard_map/all_gather | solution.py:1151
  23.3 25.5 %collective-permute-start.2 = (bf16[128,1536]{1,0:T(8,128)(2,1)S(1)}, bf16[128,1536]{1,0:T(8,128)(2,1)S(1)}, u32[]{:S(2)}, u32[]{:S(2)}) collective-permute-start(bf16[128,1536]{1,0:T(8,128)(2,1)S(1)} %bitcast.174), channel_id=1, source_target_pairs={{0,96},{16,112},{32,0},{48,16},{64,32},{80,48},{96,64},{112,80},{1... | collective-permute-start | bytes 1179656 | tf_op jit(solution)/shard_map/ppermute | solution.py:867
  31.9 16.9 %collective-permute-start.1 = (bf16[128,1536]{1,0:T(8,128)(2,1)S(1)}, bf16[128,1536]{1,0:T(8,128)(2,1)S(1)}, u32[]{:S(2)}, u32[]{:S(2)}) collective-permute-start(bf16[128,1536]{1,0:T(8,128)(2,1)S(1)} %bitcast.175), channel_id=1, source_target_pairs={{0,64},{16,80},{32,96},{48,112},{64,0},{80,16},{96,32},{112,48},{1... | collective-permute-start | bytes 1179656 | tf_op jit(solution)/shard_map/ppermute | solution.py:867
  31.9 20.4 %collective-permute-start = (bf16[128,1536]{1,0:T(8,128)(2,1)S(1)}, bf16[128,1536]{1,0:T(8,128)(2,1)S(1)}, u32[]{:S(2)}, u32[]{:S(2)}) collective-permute-start(bf16[128,1536]{1,0:T(8,128)(2,1)S(1)} %bitcast.176), channel_id=1, source_target_pairs={{0,32},{16,48},{32,64},{48,80},{64,96},{80,112},{96,0},{112,16},{1... | collective-permute-start | bytes 1179656 | tf_op jit(solution)/shard_map/ppermute | solution.py:867
  42.6 12.2 %all-to-all-start = ((bf16[16,2,576]{2,1,0:T(2,128)(2,1)}), bf16[16,2,576]{2,1,0:T(2,128)(2,1)S(1)}, u32[]{:S(2)}, u32[]{:S(2)}) async-start(bf16[16,2,576]{2,1,0:T(2,128)(2,1)} %reshape.1012), calls=%async_computation | async-start | bytes 81920 | tf_op jit(solution)/shard_map/all_to_all | solution.py:1023
  54.2 36.8 %collective-permute-start.3 = (bf16[4,128,1536]{2,1,0:T(8,128)(2,1)S(1)}, bf16[4,128,1536]{2,1,0:T(8,128)(2,1)}, u32[]{:S(2)}, u32[]{:S(2)}) collective-permute-start(bf16[4,128,1536]{2,1,0:T(8,128)(2,1)S(1)} %pad_maximum_fusion.3.column_ref), channel_id=1, source_target_pairs={{0,16},{16,0},{32,48},{48,32},{64,80},{80,64},{96,112},{112,96},{1... | collective-permute-start | bytes 4718600 | tf_op jit(solution)/shard_map/ppermute | solution.py:869
  84.5 48.3 %all-to-all-start.1 = ((bf16[16,64,1664]{2,1,0:T(8,128)(2,1)}), bf16[16,64,1664]{2,1,0:T(8,128)(2,1)}, u32[]{:S(2)}, u32[]{:S(2)}) async-start(bf16[16,64,1664]{2,1,0:T(8,128)(2,1)} %bitcast.12), calls=%async_computation.2 | async-start | bytes 6815744 | tf_op jit(solution)/shard_map/all_to_all | solution.py:1023
  89.5 62.4 %reduce-scatter.4.cloned.1.call-start = ((), (), s32[]{:S(2)}) async-start(), calls=%async_computation.10 | async-start | bytes 3538944 | tf_op jit(solution)/shard_map/reduce_scatter | solution.py:1154
  116.7 82.5 %all-gather.10.cloned.1.call-start = ((), (), s32[]{:S(2)}) async-start(), calls=%async_computation.12 | async-start | bytes 3538944 | tf_op jit(solution)/shard_map/all_gather | solution.py:1165
  156.9 42.4 %all-to-all-start.2 = ((bf16[16,64,1536]{2,1,0:T(8,128)(2,1)}), bf16[16,64,1536]{2,1,0:T(8,128)(2,1)}, u32[]{:S(2)}, u32[]{:S(2)}) async-start(bf16[16,64,1536]{2,1,0:T(8,128)(2,1)} %bitcast.190), calls=%async_computation.3 | async-start | bytes 6291456 | tf_op jit(solution)/shard_map/all_to_all | solution.py:1023
  163.5 109.2 %reduce-scatter.6.cloned.1.call-start = ((), (), s32[]{:S(2)}) async-start(), calls=%async_computation.13 | async-start | bytes 7077888 | tf_op jit(solution)/shard_map/reduce_scatter | solution.py:1187
  218.6 51.4 %all-to-all-start.3 = ((bf16[16,64,1664]{2,1,0:T(8,128)(2,1)}), bf16[16,64,1664]{2,1,0:T(8,128)(2,1)}, u32[]{:S(2)}, u32[]{:S(2)}) async-start(bf16[16,64,1664]{2,1,0:T(8,128)(2,1)} %bitcast.188), calls=%async_computation.5 | async-start | bytes 6815744 | tf_op jit(solution)/shard_map/all_to_all | solution.py:1023
  228.5 96.7 %all-gather.12.cloned.1.call-start = ((), (), s32[]{:S(2)}) async-start(), calls=%async_computation.14 | async-start | bytes 3833856 | tf_op jit(solution)/shard_map/all_gather | solution.py:1221
  249.1 7.1 %collective-permute-start.5 = (bf16[768,512]{1,0:T(8,128)(2,1)S(1)}, bf16[768,512]{1,0:T(8,128)(2,1)S(1)}, u32[]{:S(2)}, u32[]{:S(2)}) collective-permute-start(bf16[768,512]{1,0:T(8,128)(2,1)S(1)} %dynamic-slice_bitcast_fusion.7), channel_id=1, source_target_pairs={{0,16},{16,0},{32,48},{48,32},{64,80},{80,64},{96,112},{112,96},{1... | collective-permute-start | bytes 2359304 | tf_op jit(solution)/shard_map/ppermute | solution.py:879
  251.7 6.3 %collective-permute-start.7 = (bf16[768,512]{1,0:T(8,128)(2,1)S(1)}, bf16[768,512]{1,0:T(8,128)(2,1)S(1)}, u32[]{:S(2)}, u32[]{:S(2)}) collective-permute-start(bf16[768,512]{1,0:T(8,128)(2,1)S(1)} %dynamic-slice_bitcast_fusion.5), channel_id=1, source_target_pairs={{0,16},{16,0},{32,48},{48,32},{64,80},{80,64},{96,112},{112,96},{1... | collective-permute-start | bytes 2359304 | tf_op jit(solution)/shard_map/ppermute | solution.py:879
  284.6 64.8 %all-to-all-start.4 = ((bf16[16,64,1536]{2,1,0:T(8,128)(2,1)}), bf16[16,64,1536]{2,1,0:T(8,128)(2,1)}, u32[]{:S(2)}, u32[]{:S(2)}) async-start(bf16[16,64,1536]{2,1,0:T(8,128)(2,1)} %bitcast.189), calls=%async_computation.6 | async-start | bytes 6291456 | tf_op jit(solution)/shard_map/all_to_all | solution.py:1023
  338.5 61.6 %collective-permute-start.12 = (bf16[1152,512]{1,0:T(8,128)(2,1)}, bf16[1152,512]{1,0:T(8,128)(2,1)}, u32[]{:S(2)}, u32[]{:S(2)}) collective-permute-start(bf16[1152,512]{1,0:T(8,128)(2,1)} %dynamic-slice_bitcast_fusion.1), channel_id=1, source_target_pairs={{0,32},{16,48},{32,0},{48,16},{64,96},{80,112},{96,64},{112,80},{1... | collective-permute-start | bytes 3538952 | tf_op jit(solution)/shard_map/ppermute | solution.py:879
  338.6 65.2 %collective-permute-start.16 = (bf16[1152,512]{1,0:T(8,128)(2,1)}, bf16[1152,512]{1,0:T(8,128)(2,1)}, u32[]{:S(2)}, u32[]{:S(2)}) collective-permute-start(bf16[1152,512]{1,0:T(8,128)(2,1)} %dynamic-slice_bitcast_fusion), channel_id=1, source_target_pairs={{0,96},{16,112},{32,64},{48,80},{64,32},{80,48},{96,0},{112,16},{1... | collective-permute-start | bytes 3538952 | tf_op jit(solution)/shard_map/ppermute | solution.py:879
  355.5 42.7 %all-to-all-start.5 = ((bf16[16,224,384]{2,1,0:T(8,128)(2,1)}), bf16[16,224,384]{2,1,0:T(8,128)(2,1)}, u32[]{:S(2)}, u32[]{:S(2)}) async-start(bf16[16,224,384]{2,1,0:T(8,128)(2,1)} %constant_dynamic-update-slice_fusion.9), calls=%async_computation.8 | async-start | bytes 5505024 | tf_op jit(solution)/shard_map/all_to_all | solution.py:1023
  362.1 118.7 %reduce-scatter.8.cloned.1.call-start = ((), (), s32[]{:S(2)}) async-start(), calls=%async_computation.15 | async-start | bytes 3538944 | tf_op jit(solution)/shard_map/reduce_scatter | solution.py:1277
  402.0 18.6 %collective-permute-start.13 = (bf16[576,512]{1,0:T(8,128)(2,1)S(1)}, bf16[576,512]{1,0:T(8,128)(2,1)S(1)}, u32[]{:S(2)}, u32[]{:S(2)}) collective-permute-start(bf16[576,512]{1,0:T(8,128)(2,1)S(1)} %dynamic-slice_bitcast_fusion.9), channel_id=1, source_target_pairs={{0,96},{16,112},{32,64},{48,80},{64,32},{80,48},{96,0},{112,16},{1... | collective-permute-start | bytes 1769480 | tf_op jit(solution)/shard_map/ppermute | solution.py:879
  407.3 21.2 %collective-permute-start.17 = (bf16[576,512]{1,0:T(8,128)(2,1)}, bf16[576,512]{1,0:T(8,128)(2,1)}, u32[]{:S(2)}, u32[]{:S(2)}) collective-permute-start(bf16[576,512]{1,0:T(8,128)(2,1)} %dynamic-slice_bitcast_fusion.8), channel_id=1, source_target_pairs={{0,32},{16,48},{32,0},{48,16},{64,96},{80,112},{96,64},{112,80},{1... | collective-permute-start | bytes 1769480 | tf_op jit(solution)/shard_map/ppermute | solution.py:879
  421.6 19.2 %collective-permute-start.14 = (bf16[576,512]{1,0:T(8,128)(2,1)}, bf16[576,512]{1,0:T(8,128)(2,1)}, u32[]{:S(2)}, u32[]{:S(2)}) collective-permute-start(bf16[576,512]{1,0:T(8,128)(2,1)} %add_convert_fusion.4), channel_id=1, source_target_pairs={{0,96},{16,112},{32,64},{48,80},{64,32},{80,48},{96,0},{112,16},{1... | collective-permute-start | bytes 1769480 | tf_op jit(solution)/shard_map/ppermute | solution.py:889
  424.7 54.8 %all-to-all-start.6 = ((bf16[16,96,1152]{2,1,0:T(8,128)(2,1)}), bf16[16,96,1152]{2,1,0:T(8,128)(2,1)S(1)}, u32[]{:S(2)}, u32[]{:S(2)}) async-start(bf16[16,96,1152]{2,1,0:T(8,128)(2,1)} %bitcast.187), calls=%async_computation.9 | async-start | bytes 7077888 | tf_op jit(solution)/shard_map/all_to_all | solution.py:1023
  428.5 95.3 %all-gather.16.cloned.1.call-start = ((), (), s32[]{:S(2)}) async-start(), calls=%async_computation.17 | async-start | bytes 3538944 | tf_op jit(solution)/shard_map/all_gather | solution.py:1323
  430.8 15.1 %collective-permute-start.18 = (bf16[576,512]{1,0:T(8,128)(2,1)}, bf16[576,512]{1,0:T(8,128)(2,1)}, u32[]{:S(2)}, u32[]{:S(2)}) collective-permute-start(bf16[576,512]{1,0:T(8,128)(2,1)} %add_convert_fusion.3), channel_id=1, source_target_pairs={{0,32},{16,48},{32,0},{48,16},{64,96},{80,112},{96,64},{112,80},{1... | collective-permute-start | bytes 1769480 | tf_op jit(solution)/shard_map/ppermute | solution.py:889
  445.5 24.6 %collective-permute-start.15 = (bf16[1152,512]{1,0:T(8,128)(2,1)}, bf16[1152,512]{1,0:T(8,128)(2,1)}, u32[]{:S(2)}, u32[]{:S(2)}) collective-permute-start(bf16[1152,512]{1,0:T(8,128)(2,1)} %pad_maximum_fusion.5), channel_id=1, source_target_pairs={{0,32},{16,48},{32,0},{48,16},{64,96},{80,112},{96,64},{112,80},{1... | collective-permute-start | bytes 3538952 | tf_op jit(solution)/shard_map/ppermute | solution.py:889
  449.1 25.9 %collective-permute-start.19 = (bf16[1152,512]{1,0:T(8,128)(2,1)}, bf16[1152,512]{1,0:T(8,128)(2,1)}, u32[]{:S(2)}, u32[]{:S(2)}) collective-permute-start(bf16[1152,512]{1,0:T(8,128)(2,1)} %pad_maximum_fusion.6), channel_id=1, source_target_pairs={{0,96},{16,112},{32,64},{48,80},{64,32},{80,48},{96,0},{112,16},{1... | collective-permute-start | bytes 3538952 | tf_op jit(solution)/shard_map/ppermute | solution.py:889
  454.5 13.4 %collective-permute-start.11 = (bf16[128,384]{1,0:T(8,128)(2,1)S(1)}, bf16[128,384]{1,0:T(8,128)(2,1)S(1)}, u32[]{:S(2)}, u32[]{:S(2)}) collective-permute-start(bf16[128,384]{1,0:T(8,128)(2,1)S(1)} %slice.479), channel_id=1, source_target_pairs={{0,0},{1,16},{2,32},{3,48},{4,64},{5,80},{6,96},{7,112},{8,1},{9,1... | collective-permute-start | bytes 294920 | tf_op jit(solution)/shard_map/ppermute | solution.py:1313
  489.8 12.1 %collective-permute-start.20 = (bf16[4608,512]{1,0:T(8,128)(2,1)}, bf16[4608,512]{1,0:T(8,128)(2,1)}, u32[]{:S(2)}, u32[]{:S(2)}) collective-permute-start(bf16[4608,512]{1,0:T(8,128)(2,1)} %pad_maximum_fusion.own_ref), channel_id=1, source_target_pairs={{0,16},{16,0},{32,48},{48,32},{64,80},{80,64},{96,112},{112,96},{1... | collective-permute-start | bytes 14155784 | tf_op jit(solution)/shard_map/ppermute | solution.py:1321
  (79 other events, 613.1 us)
Sparse Core Ops, SparseCore 0:
  20.5 63.9 all-gather.13
  86.8 28.0 all-gather.7
  117.3 34.5 reduce-scatter.3
  157.0 30.2 all-gather.9
  218.7 53.9 reduce-scatter.5
  278.3 46.7 all-gather.11
  390.1 44.0 reduce-scatter.7
  485.7 37.9 all-gather.15

commit v11 on v10

--- a/solution.py
+++ b/solution.py
@@ -1217,7 +1217,7 @@
         cot_low,
     )
     grad_router = jnp.dot(moe_in.astype(f32).T, d_logits, precision=highest)
-    grad_router = grad_router + jnp.pad(d_moe_gain[0][:, None], ((0, 0), (0, 127)))
+    grad_router = lax.optimization_barrier(grad_router)
     d_o_all = lax.all_gather(d_o_ext, "seq", axis=0, tiled=True)
 
     sent_one, kept_one = halves(e_mine[:cutoff], is_inner)
@@ -1239,10 +1239,12 @@
         jnp.zeros((136, gw + keys_w), f32),
         jnp.zeros((24, gw + keys_w), f32),
     )
+    moe_column = jnp.pad(d_moe_gain[0][:, None], ((0, 0), (0, 127)))
+    grad_router = grad_router + after(moe_column, corner_after(returned, carry))
     mid_part = jnp.concatenate(
         [
             grad_shared_part,
-            after(grad_router, corner_after(returned, carry)).astype(bf),
+            grad_router.astype(bf),
         ],
         axis=1,
     )
@@ -1263,17 +1265,20 @@
         axis=1,
     )
     moved_early = to_shards(early_part)
+    e_one = add_other(kept_one, sent_one, near)
+    e_two = add_other(kept_two, sent_two, far)
+    carry = after(carry, e_one, e_two)
     d_proj, back_part, carry, sums = scan_backward((0, middle), scan_inputs, held, carry, sums)
-    d_proj, moved_early = lax.optimization_barrier((d_proj, moved_early))
-    e_one = add_other(after(kept_one, d_proj), sent_one, near)
-    e_two = add_other(after(kept_two, d_proj), sent_two, far)
     d_taps, d_head, d_skip = sums[0:8], sums[8:16, :128], sums[16:24, :gw]
     grad_conv_local = d_taps[:taps]
     grad_offset_local = d_taps[taps]
     grad_bias_local = d_head[0, :gh]
     grad_decay_local = d_head[1, :gh] * decay_rate
     grad_skip_local = jnp.sum(d_skip[0].reshape(gh, per_head), axis=1)
-    e_one, e_two = halve(e_one, is_high, far), halve(e_two, is_inner, near)
+    sent_one, kept_one = halves(e_one, is_high)
+    sent_two, kept_two = halves(e_two, is_inner)
+    e_one = add_other(kept_one, sent_one, far)
+    e_two = add_other(kept_two, sent_two, near)
     back_sum = lax.psum_scatter(back_part, "seq", scatter_dimension=0, tiled=True).astype(f32)
     route_gates = gates[:, router_lane : router_lane + experts]
     weighted = (route_gates.T[:, None, :] * dispatch.astype(f32)).reshape(slots, toks)
@@ -1301,6 +1306,7 @@
         ],
         axis=1,
     )
+    small_part = after(small_part, e_one, e_two)
     small_count = small_part.shape[1]
     small_part = jnp.pad(
         small_part, ((0, 0), (0, rows_w * small_cols - small_count))
@@ -1309,14 +1315,16 @@
         small_part.reshape(dim, small_cols), ((0, 0), (used, total - used - small_cols))
     )
     last_part = last_part.astype(bf)
+    last_part, moved_early = lax.optimization_barrier((last_part, moved_early))
     early_sum = jnp.sum(moved_early.astype(f32), axis=0).astype(bf)
     rows_sum = lax.ppermute(early_sum[: bands * own_rows], both_axes, backward_pairs)
-    e_one, e_two = after(e_one, last_part), after(e_two, last_part)
+    e_one, e_two, last_part = lax.optimization_barrier((e_one, e_two, last_part))
     e_one, e_two = double(e_one, is_high, far), double(e_two, is_inner, near)
     e_one, e_two = double(e_one, is_inner, near), double(e_two, is_high, far)
     moved_last = to_shards(last_part.reshape(sh, rows_w, total))
     last_sum = jnp.sum(moved_last.astype(f32), axis=0)
-    last_sum = after(after(after(last_sum, e_one), e_two), back_sum).astype(bf)
+    last_sum = after(last_sum, e_one, e_two).astype(bf)
+    rows_sum = after(rows_sum, e_one)
     e_mine = jnp.concatenate([e_one, e_two], axis=0)
     e_other = lax.ppermute(e_mine, "seq", mates)
     grad_e_gate, grad_e_up, grad_e_down = unpack_expert_grads(e_mine, e_other, core)

time: 551 us -> 543 us (0.985)
  waiting for transfers between devices: 150 us -> 128 us
  starting transfers between devices: 81.1 us -> 88.8 us
    all_to_all x7, waiting for transfers between devices: 35.3 us -> 26.1 us  [to_shards(): lax.all_to_all(values, 'shard', split_axis=0, concat_axis=0, tiled=True)]
    ppermute x10, waiting for transfers between devices: 7.4 us -> 0.03 us  [add_other(): other = lax.ppermute(sent, 'seq', pairs)]
    ppermute x4, waiting for transfers between devices: 11.3 us -> 18.2 us  [double(): other = lax.ppermute(values, 'seq', pairs)]
    ppermute x1, waiting for transfers between devices: 6.47 us -> 0.01 us  [on_device(): lax.ppermute(early_sum[:bands * own_rows], both_axes, backward_pairs)]
    unnamed x171 -> x168, local copies, waits for them, and re-layouts: 24.7 us -> 21.6 us
    slice x16 -> x17, local copies, waits for them, and re-layouts: 11.2 us -> 11.2 us  [after(): corners = [o[(0,) * (o.ndim - 1)][:1].astype(jnp.float32) for o in others]]
  transfers between devices with their start and end apart: 36 -> 36, of which waited for: 17 -> 13; matrix products, arithmetic and copies ran while one was open for 21% -> 24% of each run, Pallas kernels for 17% -> 18%
where the time goes in v11:
time: 543 us; the launch traced here: 533 us
  waiting for transfers between devices  128 us (24%)
  Pallas kernels  126 us (23%)
  starting transfers between devices  88.8 us (16%)
  local copies, waits for them, and re-layouts  71.1 us (13%)
  other arithmetic  51.8 us (10%)
  between operations  31.2 us (6%)
  matrix products  23.4 us (4%)
  blocking collectives  13.4 us (2%)
    all_to_all x7, starting transfers between devices, to_shards(): lax.all_to_all(values, 'shard', split_axis=0, concat_axis=0, tiled=True)  44.5 us
    pallas_call x2, Pallas kernels, scan_backward(): pl.pallas_call(functools.partial(scan_backward_kernel, chunks, len(held))...  37.5 us
    all_gather x1, waiting for transfers between devices, on_device(): lax.all_gather(jnp.concatenate([packed, fold_rows(piece[:own_out], total)...  29.4 us
    all_gather x1, waiting for transfers between devices, on_device(): d_o_all = lax.all_gather(d_o_ext, 'seq', axis=0, tiled=True)  28.1 us
    all_to_all x7, waiting for transfers between devices, to_shards(): lax.all_to_all(values, 'shard', split_axis=0, concat_axis=0, tiled=True)  26.1 us
    pallas_call x1, Pallas kernels, front(): pl.pallas_call(front_kernel, grid_spec=pltpu.PrefetchScalarGridSpec(num_s...  24.2 us
    unnamed x168, local copies, waits for them, and re-layouts  21.6 us
    pallas_call x1, Pallas kernels, expert_main(): pl.pallas_call(expert_main_kernel, grid=(local,), in_specs=[expert_slots(...  19.3 us
  transfers between devices with their start and end apart: 36, of which 13 were waited for; matrix products, arithmetic and copies ran while one was open for 24% of the time, Pallas kernels for 18%

profile of v11, /device:TPU:1, one launch (start us, length us, event | category | flops | bytes accessed | tf_op | source)
XLA Modules:
  0.0 533.0 jit_solution(5083017270062062709)
XLA Ops:
  9.1 4.6 collective-permute-start.4
  23.3 8.6 %collective-permute-start.2 = (bf16[128,1536]{1,0:T(8,128)(2,1)S(1)}, bf16[128,1536]{1,0:T(8,128)(2,1)S(1)}, u32[]{:S(2)}, u32[]{:S(2)}) collective-permute-start(bf16[128,1536]{1,0:T(8,128)(2,1)S(1)} %bitcast.169), channel_id=1, source_target_pairs={{0,96},{16,112},{32,0},{48,16},{64,32},{80,48},{96,64},{112,80},{1... | collective-permute-start | bytes 1179656 | tf_op jit(solution)/shard_map/ppermute | solution.py:867
  42.6 3.5 all-to-all-start
  48.8 3.5 collective-permute-done
  55.1 29.4 %all-gather.14.cloned.1.call-done = bf16[2560,1152]{1,0:T(8,128)(2,1)} async-done(((bf16[160,1152]{1,0:T(8,128)(2,1)}), bf16[2560,1152]{1,0:T(8,128)(2,1)}) %all-gather.14.cloned.1.call-update) | async-done | bytes 5898256 | tf_op jit(solution)/shard_map/all_gather | solution.py:1061
  84.5 5.0 all-to-all-start.1
  91.1 24.2 %front.1 = (bf16[1024,1536]{1,0:T(8,128)(2,1)}, f32[1024,1152]{1,0:T(8,128)}, f32[1024,1]{1,0:T(8,128)S(1)}, bf16[1536,1152]{1,0:T(8,128)(2,1)}, bf16[384,1536]{...) custom-call(s32[2]{0:T(128)S(1)} %pad_add_fusion.here_ref, ...), custom_call_target="tpu_custom_call" | custom-call | flops 17179869184 | bytes 50331648 | tf_op jit(solution)/shard_map/front/pallas_call | solution.py:351
  118.7 13.4 %psum.7.earlier_ref = f32[8,128]{1,0:T(8,128)S(1)} all-reduce(f32[8,128]{1,0:T(8,128)S(1)} %broadcast_add_fusion.3), channel_id=1, replica_groups=mesh['seq'=8,'shard'=16] {'seq'}, use_global_device_ids=true, to_apply=%region_2.3 | all-reduce | flops 1024 | bytes 8192 | tf_op jit(solution)/shard_map/psum | solution.py:1155
  132.9 5.0 expert_early.1.raw_ref
  140.3 11.7 %reduce-scatter.4.cloned.1.call-done.out_ref = bf16[128,1536]{1,0:T(8,128)(2,1)} async-done(((bf16[1024,1536]{1,0:T(8,128)(2,1)}), bf16[128,1536]{1,0:T(8,128)(2,1)}) %reduce-scatter.4.cloned.1.call-update) | async-done | bytes 393232 | tf_op jit(solution)/shard_map/reduce_scatter | solution.py:1154
  152.6 4.3 token_front.1
  156.9 6.6 %all-to-all-start.2 = ((bf16[16,64,1536]{2,1,0:T(8,128)(2,1)}), bf16[16,64,1536]{2,1,0:T(8,128)(2,1)}, u32[]{:S(2)}, u32[]{:S(2)}) async-start(bf16[16,64,1536]{2,1,0:T(8,128)(2,1)} %bitcast.183), calls=%async_computation.3 | async-start | bytes 6291456 | tf_op jit(solution)/shard_map/all_to_all | solution.py:1023
  173.5 25.6 %all-to-all-done.2 = bf16[16,64,1536]{2,1,0:T(8,128)(2,1)} async-done(((bf16[16,64,1536]{2,1,0:T(8,128)(2,1)}), bf16[16,64,1536]{2,1,0:T(8,128)(2,1)}, u32[]{:S(2)}, u32[]{:S(2)}) %all-to-all-start.2) | async-done | bytes 3145760 | tf_op jit(solution)/shard_map/all_to_all | solution.py:1023
  199.1 19.3 %expert_main.1 = (bf16[16,2,32,1664]{3,2,1,0:T(8,128)(2,1)}, bf16[2,512,512]{2,1,0:T(8,128)(2,1)}, bf16[2,512,512]{2,1,0:T(8,128)(2,1)}, bf16[2,512,512]{2,1,0:T...) custom-call(bf16[16,2,32,1536]{3,2,1,0:T(8,128)(2,1)} %bitcast.24.ro, ...), custom_call_target="tpu_custom_call" | custom-call | flops 8589934592 | bytes 20971520 | tf_op jit(solution)/shard_map/expert_main/pallas_call | solution.py:699
  218.4 9.5 %all-to-all-start.3 = ((bf16[16,64,1664]{2,1,0:T(8,128)(2,1)}), bf16[16,64,1664]{2,1,0:T(8,128)(2,1)}, u32[]{:S(2)}, u32[]{:S(2)}) async-start(bf16[16,64,1664]{2,1,0:T(8,128)(2,1)} %bitcast.181), calls=%async_computation.5 | async-start | bytes 6815744 | tf_op jit(solution)/shard_map/all_to_all | solution.py:1023
  230.9 12.7 %expert_late.1 = (bf16[16,2,32,1536]{3,2,1,0:T(8,128)(2,1)}, bf16[2,1536,512]{2,1,0:T(8,128)(2,1)}, bf16[2,1536,512]{2,1,0:T(8,128)(2,1)}, bf16[2,1536,512]{2,1,0:T(8,128)(2,1)}) custom-call(bf16[16,2,32,1536]{3,2,1,0:T(8,128)(2,1)} %bitcast.24.rows_ref, bf16[16,2,32,1664]{3,2,1,0:T(8,128)(2,1)} %bitcast.21.cot_ref.routed_ref, ...), custom_call_target="tpu_custom_call" | custom-call | flops 7516192768 | bytes 25165824 | tf_op jit(solution)/shard_map/expert_late/pallas_call | solution.py:733
  266.8 5.7 %reduce-scatter.6.cloned.1.call-done.shared_ref = bf16[128,3072]{1,0:T(8,128)(2,1)} async-done(((bf16[1024,3072]{1,0:T(8,128)(2,1)}), bf16[128,3072]{1,0:T(8,128)(2,1)}) %reduce-scatter.6.cloned.1.call-update) | async-done | bytes 786448 | tf_op jit(solution)/shard_map/reduce_scatter | solution.py:1187
  272.5 5.5 %token_back.1 = (bf16[128,1664]{1,0:T(8,128)(2,1)}, f32[128,1536]{1,0:T(8,128)}, f32[128,128]{1,0:T(8,128)}, f32[8,1536]{1,0:T(8,128)}) custom-call(bf16[1024,1664]{1,0:T(8,128)(2,1)} %bitcast.34.back_ref, bf16[1024,128]{1,0:T(8,128)(2,1)} %get-tuple-element.287.slots_ref, bf16[128,3072]{1,0:T(8,128)(2,1)} %reduce-scatter.6.cloned.1.call-done.shared_ref, ...), custom_call_target="tpu_custom_call" | custom-call | flops 536870912 | bytes 8388608 | tf_op jit(solution)/shard_map/token_back/pallas_call | solution.py:548
  286.7 6.7 %all-to-all-start.4 = ((bf16[16,64,1536]{2,1,0:T(8,128)(2,1)}), bf16[16,64,1536]{2,1,0:T(8,128)(2,1)}, u32[]{:S(2)}, u32[]{:S(2)}) async-start(bf16[16,64,1536]{2,1,0:T(8,128)(2,1)} %bitcast.182), calls=%async_computation.6 | async-start | bytes 6291456 | tf_op jit(solution)/shard_map/all_to_all | solution.py:1023
  296.8 28.1 %all-gather.12.cloned.1.call-done.d_o_ref = bf16[1024,1664]{1,0:T(8,128)(2,1)} async-done(((bf16[128,1664]{1,0:T(8,128)(2,1)}), bf16[1024,1664]{1,0:T(8,128)(2,1)}) %all-gather.12.cloned.1.call-update) | async-done | bytes 3407888 | tf_op jit(solution)/shard_map/all_gather | solution.py:1221
  334.7 11.0 %scan_backward.2 = (bf16[1024,1152]{1,0:T(8,128)(2,1)}, bf16[1024,1536]{1,0:T(8,128)(2,1)}, f32[136,640]{1,0:T(8,128)S(1)}, f32[24,640]{1,0:T(8,128)S(1)}) custom-call(f32[1024,1152]{1,0:T(8,128)} %get-tuple-element.103.proj_ref.prev_ref, f32[1024,1152]{1,0:T(8,128)} %get-tuple-element.103.proj_ref.prev_ref, ...), custom_call_target="tpu_custom_call" | custom-call | flops 21474836480 | bytes 41943040 | tf_op jit(solution)/shard_map/scan_backward/pallas_call | solution.py:411
  353.8 6.6 %all-to-all-start.5 = ((bf16[16,224,384]{2,1,0:T(8,128)(2,1)}), bf16[16,224,384]{2,1,0:T(8,128)(2,1)}, u32[]{:S(2)}, u32[]{:S(2)}) async-start(bf16[16,224,384]{2,1,0:T(8,128)(2,1)} %constant_dynamic-update-slice_fusion.9), calls=%async_computation.8 | async-start | bytes 5505024 | tf_op jit(solution)/shard_map/all_to_all | solution.py:1023
  369.9 26.5 %scan_backward.3 = (bf16[1024,1152]{1,0:T(8,128)(2,1)}, bf16[1024,1536]{1,0:T(8,128)(2,1)}, f32[136,640]{1,0:T(8,128)}, f32[24,640]{1,0:T(8,128)S(1)}) custom-call(f32[1024,1152]{1,0:T(8,128)} %get-tuple-element.103.proj_ref.prev_ref, f32[1024,1152]{1,0:T(8,128)} %get-tuple-element.103.proj_ref.prev_ref, ...), custom_call_target="tpu_custom_call", output_to_operand_aliasing={{0}: (13, {}), {1}: (14, {})} | custom-call | flops 21474836480 | bytes 41943040 | tf_op jit(solution)/shard_map/scan_backward/pallas_call | solution.py:411
  405.8 8.7 %fusion.2 = bf16[1536,1152]{1,0:T(8,128)(2,1)} fusion(bf16[1024,1536]{1,0:T(8,128)(2,1)} %get-tuple-element.117, bf16[1024,1152]{1,0:T(8,128)(2,1)} %get-tuple-element.118, f32[1536,11]{1,0:T(8,128)S(1)} %reshape_reshape.3), kind=kOutput, calls=%fused_computation.3 | convolution fusion | flops 3630956544 | bytes 9111552 | tf_op jit(solution)/shard_map/dot_general | solution.py:29
  415.9 6.6 %all-to-all-start.6 = ((bf16[16,96,1152]{2,1,0:T(8,128)(2,1)}), bf16[16,96,1152]{2,1,0:T(8,128)(2,1)S(1)}, u32[]{:S(2)}, u32[]{:S(2)}) async-start(bf16[16,96,1152]{2,1,0:T(8,128)(2,1)} %bitcast.180), calls=%async_computation.9 | async-start | bytes 7077888 | tf_op jit(solution)/shard_map/all_to_all | solution.py:1023
  423.4 10.3 %collective-permute-done.16 = bf16[576,512]{1,0:T(8,128)(2,1)} collective-permute-done((bf16[576,512]{1,0:T(8,128)(2,1)}, bf16[576,512]{1,0:T(8,128)(2,1)}, u32[]{:S(2)}, u32[]{:S(2)}) %collective-permute-start.16) | collective-permute-done | bytes 589856 | tf_op jit(solution)/shard_map/ppermute | solution.py:889
  448.9 10.3 %collective-permute-start.15 = (bf16[128,384]{1,0:T(8,128)(2,1)S(1)}, bf16[128,384]{1,0:T(8,128)(2,1)S(1)}, u32[]{:S(2)}, u32[]{:S(2)}) collective-permute-start(bf16[128,384]{1,0:T(8,128)(2,1)S(1)} %slice.488), channel_id=1, source_target_pairs={{0,0},{1,16},{2,32},{3,48},{4,64},{5,80},{6,96},{7,112},{8,1},{9,1... | collective-permute-start | bytes 294920 | tf_op jit(solution)/shard_map/ppermute | solution.py:1320
  459.2 5.8 %collective-permute-done.17 = bf16[1152,512]{1,0:T(8,128)(2,1)} collective-permute-done((bf16[1152,512]{1,0:T(8,128)(2,1)}, bf16[1152,512]{1,0:T(8,128)(2,1)}, u32[]{:S(2)}, u32[]{:S(2)}) %collective-permute-start.17) | collective-permute-done | bytes 1179680 | tf_op jit(solution)/shard_map/ppermute | solution.py:889
  479.1 4.1 pad_maximum_fusion.own_ref
  483.2 6.5 %collective-permute-start.20 = (bf16[4608,512]{1,0:T(8,128)(2,1)}, bf16[4608,512]{1,0:T(8,128)(2,1)}, u32[]{:S(2)}, u32[]{:S(2)}) collective-permute-start(bf16[4608,512]{1,0:T(8,128)(2,1)} %pad_maximum_fusion.own_ref), channel_id=1, source_target_pairs={{0,16},{16,0},{32,48},{48,32},{64,80},{80,64},{96,112},{112,96},{1... | collective-permute-start | bytes 14155784 | tf_op jit(solution)/shard_map/ppermute | solution.py:1329
  497.6 14.2 %unpack_expert_grads.1 = (f32[2,1536,512]{2,1,0:T(8,128)}, f32[2,1536,512]{2,1,0:T(8,128)}, f32[2,512,1536]{2,1,0:T(8,128)}) custom-call(s32[1]{0:T(128)} %bitcast.2.core_ref, bf16[4608,512]{1,0:T(8,128)(2,1)} %pad_maximum_fusion.own_ref, bf16[4608,512]{1,0:T(8,128)(2,1)} %collective-permute-done.20.other_ref), custom_call_target="tpu_custom_call" | custom-call | flops 1048576 | bytes 29360128 | tf_op jit(solution)/shard_map/unpack_expert_grads/pallas_call | solution.py:918
  511.8 4.0 all-gather.16.cloned.1.call-done
  (445 shorter events, 154.3 us)
Async XLA Ops:
  7.2 77.3 %all-gather.14.cloned.1.call-start = ((), (), s32[]{:S(2)}) async-start(), calls=%async_computation.16 | async-start | bytes 6266880 | tf_op jit(solution)/shard_map/all_gather | solution.py:1061
  9.1 10.4 %collective-permute-start.4 = (bf16[32,1536]{1,0:T(8,128)(2,1)S(1)}, bf16[32,1536]{1,0:T(8,128)(2,1)S(1)}, u32[]{:S(2)}, u32[]{:S(2)}) collective-permute-start(bf16[32,1536]{1,0:T(8,128)(2,1)S(1)} %pad_maximum_fusion.8), channel_id=1, source_target_pairs={{0,0},{16,1},{32,2},{48,3},{64,4},{80,5},{96,6},{112,7},{1,8},{17,... | collective-permute-start | bytes 294920 | tf_op jit(solution)/shard_map/ppermute | solution.py:1047
  20.4 96.4 %all-gather.8.cloned.1.call-start = ((), (), s32[]{:S(2)}) async-start(), calls=%async_computation.11 | async-start | bytes 3538944 | tf_op jit(solution)/shard_map/all_gather | solution.py:1151
  23.3 25.5 %collective-permute-start.2 = (bf16[128,1536]{1,0:T(8,128)(2,1)S(1)}, bf16[128,1536]{1,0:T(8,128)(2,1)S(1)}, u32[]{:S(2)}, u32[]{:S(2)}) collective-permute-start(bf16[128,1536]{1,0:T(8,128)(2,1)S(1)} %bitcast.169), channel_id=1, source_target_pairs={{0,96},{16,112},{32,0},{48,16},{64,32},{80,48},{96,64},{112,80},{1... | collective-permute-start | bytes 1179656 | tf_op jit(solution)/shard_map/ppermute | solution.py:867
  31.9 16.9 %collective-permute-start.1 = (bf16[128,1536]{1,0:T(8,128)(2,1)S(1)}, bf16[128,1536]{1,0:T(8,128)(2,1)S(1)}, u32[]{:S(2)}, u32[]{:S(2)}) collective-permute-start(bf16[128,1536]{1,0:T(8,128)(2,1)S(1)} %bitcast.170), channel_id=1, source_target_pairs={{0,64},{16,80},{32,96},{48,112},{64,0},{80,16},{96,32},{112,48},{1... | collective-permute-start | bytes 1179656 | tf_op jit(solution)/shard_map/ppermute | solution.py:867
  31.9 20.4 %collective-permute-start = (bf16[128,1536]{1,0:T(8,128)(2,1)S(1)}, bf16[128,1536]{1,0:T(8,128)(2,1)S(1)}, u32[]{:S(2)}, u32[]{:S(2)}) collective-permute-start(bf16[128,1536]{1,0:T(8,128)(2,1)S(1)} %bitcast.171), channel_id=1, source_target_pairs={{0,32},{16,48},{32,64},{48,80},{64,96},{80,112},{96,0},{112,16},{1... | collective-permute-start | bytes 1179656 | tf_op jit(solution)/shard_map/ppermute | solution.py:867
  42.6 12.2 %all-to-all-start = ((bf16[16,2,576]{2,1,0:T(2,128)(2,1)}), bf16[16,2,576]{2,1,0:T(2,128)(2,1)S(1)}, u32[]{:S(2)}, u32[]{:S(2)}) async-start(bf16[16,2,576]{2,1,0:T(2,128)(2,1)} %reshape.1006), calls=%async_computation | async-start | bytes 81920 | tf_op jit(solution)/shard_map/all_to_all | solution.py:1023
  54.2 36.8 %collective-permute-start.3 = (bf16[4,128,1536]{2,1,0:T(8,128)(2,1)S(1)}, bf16[4,128,1536]{2,1,0:T(8,128)(2,1)}, u32[]{:S(2)}, u32[]{:S(2)}) collective-permute-start(bf16[4,128,1536]{2,1,0:T(8,128)(2,1)S(1)} %pad_maximum_fusion.3.column_ref), channel_id=1, source_target_pairs={{0,16},{16,0},{32,48},{48,32},{64,80},{80,64},{96,112},{112,96},{1... | collective-permute-start | bytes 4718600 | tf_op jit(solution)/shard_map/ppermute | solution.py:869
  84.5 48.3 %all-to-all-start.1 = ((bf16[16,64,1664]{2,1,0:T(8,128)(2,1)}), bf16[16,64,1664]{2,1,0:T(8,128)(2,1)}, u32[]{:S(2)}, u32[]{:S(2)}) async-start(bf16[16,64,1664]{2,1,0:T(8,128)(2,1)} %bitcast.12), calls=%async_computation.2 | async-start | bytes 6815744 | tf_op jit(solution)/shard_map/all_to_all | solution.py:1023
  89.5 62.4 %reduce-scatter.4.cloned.1.call-start = ((), (), s32[]{:S(2)}) async-start(), calls=%async_computation.10 | async-start | bytes 3538944 | tf_op jit(solution)/shard_map/reduce_scatter | solution.py:1154
  116.7 82.3 %all-gather.10.cloned.1.call-start = ((), (), s32[]{:S(2)}) async-start(), calls=%async_computation.12 | async-start | bytes 3538944 | tf_op jit(solution)/shard_map/all_gather | solution.py:1165
  156.9 42.2 %all-to-all-start.2 = ((bf16[16,64,1536]{2,1,0:T(8,128)(2,1)}), bf16[16,64,1536]{2,1,0:T(8,128)(2,1)}, u32[]{:S(2)}, u32[]{:S(2)}) async-start(bf16[16,64,1536]{2,1,0:T(8,128)(2,1)} %bitcast.183), calls=%async_computation.3 | async-start | bytes 6291456 | tf_op jit(solution)/shard_map/all_to_all | solution.py:1023
  163.5 109.0 %reduce-scatter.6.cloned.1.call-start = ((), (), s32[]{:S(2)}) async-start(), calls=%async_computation.13 | async-start | bytes 7077888 | tf_op jit(solution)/shard_map/reduce_scatter | solution.py:1187
  218.4 48.4 %all-to-all-start.3 = ((bf16[16,64,1664]{2,1,0:T(8,128)(2,1)}), bf16[16,64,1664]{2,1,0:T(8,128)(2,1)}, u32[]{:S(2)}, u32[]{:S(2)}) async-start(bf16[16,64,1664]{2,1,0:T(8,128)(2,1)} %bitcast.181), calls=%async_computation.5 | async-start | bytes 6815744 | tf_op jit(solution)/shard_map/all_to_all | solution.py:1023
  228.0 96.9 %all-gather.12.cloned.1.call-start = ((), (), s32[]{:S(2)}) async-start(), calls=%async_computation.14 | async-start | bytes 3833856 | tf_op jit(solution)/shard_map/all_gather | solution.py:1221
  248.8 8.1 %collective-permute-start.5 = (bf16[768,512]{1,0:T(8,128)(2,1)S(1)}, bf16[768,512]{1,0:T(8,128)(2,1)S(1)}, u32[]{:S(2)}, u32[]{:S(2)}) collective-permute-start(bf16[768,512]{1,0:T(8,128)(2,1)S(1)} %dynamic-slice_bitcast_fusion.7), channel_id=1, source_target_pairs={{0,16},{16,0},{32,48},{48,32},{64,80},{80,64},{96,112},{112,96},{1... | collective-permute-start | bytes 2359304 | tf_op jit(solution)/shard_map/ppermute | solution.py:879
  252.4 6.3 %collective-permute-start.7 = (bf16[768,512]{1,0:T(8,128)(2,1)S(1)}, bf16[768,512]{1,0:T(8,128)(2,1)S(1)}, u32[]{:S(2)}, u32[]{:S(2)}) collective-permute-start(bf16[768,512]{1,0:T(8,128)(2,1)S(1)} %dynamic-slice_bitcast_fusion.5), channel_id=1, source_target_pairs={{0,16},{16,0},{32,48},{48,32},{64,80},{80,64},{96,112},{112,96},{1... | collective-permute-start | bytes 2359304 | tf_op jit(solution)/shard_map/ppermute | solution.py:879
  286.7 60.8 %all-to-all-start.4 = ((bf16[16,64,1536]{2,1,0:T(8,128)(2,1)}), bf16[16,64,1536]{2,1,0:T(8,128)(2,1)}, u32[]{:S(2)}, u32[]{:S(2)}) async-start(bf16[16,64,1536]{2,1,0:T(8,128)(2,1)} %bitcast.182), calls=%async_computation.6 | async-start | bytes 6291456 | tf_op jit(solution)/shard_map/all_to_all | solution.py:1023
  324.9 35.6 %collective-permute-start.11 = (bf16[1152,512]{1,0:T(8,128)(2,1)}, bf16[1152,512]{1,0:T(8,128)(2,1)}, u32[]{:S(2)}, u32[]{:S(2)}) collective-permute-start(bf16[1152,512]{1,0:T(8,128)(2,1)} %dynamic-slice_bitcast_fusion.1), channel_id=1, source_target_pairs={{0,32},{16,48},{32,0},{48,16},{64,96},{80,112},{96,64},{112,80},{1... | collective-permute-start | bytes 3538952 | tf_op jit(solution)/shard_map/ppermute | solution.py:879
  325.1 40.1 %collective-permute-start.12 = (bf16[1152,512]{1,0:T(8,128)(2,1)}, bf16[1152,512]{1,0:T(8,128)(2,1)}, u32[]{:S(2)}, u32[]{:S(2)}) collective-permute-start(bf16[1152,512]{1,0:T(8,128)(2,1)} %dynamic-slice_bitcast_fusion), channel_id=1, source_target_pairs={{0,96},{16,112},{32,64},{48,80},{64,32},{80,48},{96,0},{112,16},{1... | collective-permute-start | bytes 3538952 | tf_op jit(solution)/shard_map/ppermute | solution.py:879
  353.8 60.6 %all-to-all-start.5 = ((bf16[16,224,384]{2,1,0:T(8,128)(2,1)}), bf16[16,224,384]{2,1,0:T(8,128)(2,1)}, u32[]{:S(2)}, u32[]{:S(2)}) async-start(bf16[16,224,384]{2,1,0:T(8,128)(2,1)} %constant_dynamic-update-slice_fusion.9), calls=%async_computation.8 | async-start | bytes 5505024 | tf_op jit(solution)/shard_map/all_to_all | solution.py:1023
  360.4 133.3 %reduce-scatter.8.cloned.1.call-start = ((), (), s32[]{:S(2)}) async-start(), calls=%async_computation.15 | async-start | bytes 3538944 | tf_op jit(solution)/shard_map/reduce_scatter | solution.py:1282
  364.0 33.8 %collective-permute-start.13 = (bf16[576,512]{1,0:T(8,128)(2,1)}, bf16[576,512]{1,0:T(8,128)(2,1)}, u32[]{:S(2)}, u32[]{:S(2)}) collective-permute-start(bf16[576,512]{1,0:T(8,128)(2,1)} %dynamic-slice_bitcast_fusion.9), channel_id=1, source_target_pairs={{0,96},{16,112},{32,64},{48,80},{64,32},{80,48},{96,0},{112,16},{1... | collective-permute-start | bytes 1769480 | tf_op jit(solution)/shard_map/ppermute | solution.py:879
  369.5 31.6 %collective-permute-start.14 = (bf16[576,512]{1,0:T(8,128)(2,1)}, bf16[576,512]{1,0:T(8,128)(2,1)}, u32[]{:S(2)}, u32[]{:S(2)}) collective-permute-start(bf16[576,512]{1,0:T(8,128)(2,1)} %dynamic-slice_bitcast_fusion.8), channel_id=1, source_target_pairs={{0,32},{16,48},{32,0},{48,16},{64,96},{80,112},{96,64},{112,80},{1... | collective-permute-start | bytes 1769480 | tf_op jit(solution)/shard_map/ppermute | solution.py:879
  414.5 19.3 %collective-permute-start.16 = (bf16[576,512]{1,0:T(8,128)(2,1)}, bf16[576,512]{1,0:T(8,128)(2,1)}, u32[]{:S(2)}, u32[]{:S(2)}) collective-permute-start(bf16[576,512]{1,0:T(8,128)(2,1)} %fusion.16), channel_id=1, source_target_pairs={{0,96},{16,112},{32,64},{48,80},{64,32},{80,48},{96,0},{112,16},{1... | collective-permute-start | bytes 1769480 | tf_op jit(solution)/shard_map/ppermute | solution.py:889
  415.9 60.6 %all-to-all-start.6 = ((bf16[16,96,1152]{2,1,0:T(8,128)(2,1)}), bf16[16,96,1152]{2,1,0:T(8,128)(2,1)S(1)}, u32[]{:S(2)}, u32[]{:S(2)}) async-start(bf16[16,96,1152]{2,1,0:T(8,128)(2,1)} %bitcast.180), calls=%async_computation.9 | async-start | bytes 7077888 | tf_op jit(solution)/shard_map/all_to_all | solution.py:1023
  422.5 93.4 %all-gather.16.cloned.1.call-start = ((), (), s32[]{:S(2)}) async-start(), calls=%async_computation.17 | async-start | bytes 3538944 | tf_op jit(solution)/shard_map/all_gather | solution.py:1331
  422.5 18.3 %collective-permute-start.18 = (bf16[576,512]{1,0:T(8,128)(2,1)}, bf16[576,512]{1,0:T(8,128)(2,1)}, u32[]{:S(2)}, u32[]{:S(2)}) collective-permute-start(bf16[576,512]{1,0:T(8,128)(2,1)} %copy-done.37), channel_id=1, source_target_pairs={{0,32},{16,48},{32,0},{48,16},{64,96},{80,112},{96,64},{112,80},{1... | collective-permute-start | bytes 1769480 | tf_op jit(solution)/shard_map/ppermute | solution.py:889
  438.4 26.6 %collective-permute-start.17 = (bf16[1152,512]{1,0:T(8,128)(2,1)}, bf16[1152,512]{1,0:T(8,128)(2,1)}, u32[]{:S(2)}, u32[]{:S(2)}) collective-permute-start(bf16[1152,512]{1,0:T(8,128)(2,1)} %pad_maximum_fusion.5), channel_id=1, source_target_pairs={{0,32},{16,48},{32,0},{48,16},{64,96},{80,112},{96,64},{112,80},{1... | collective-permute-start | bytes 3538952 | tf_op jit(solution)/shard_map/ppermute | solution.py:889
  444.1 24.0 %collective-permute-start.19 = (bf16[1152,512]{1,0:T(8,128)(2,1)}, bf16[1152,512]{1,0:T(8,128)(2,1)}, u32[]{:S(2)}, u32[]{:S(2)}) collective-permute-start(bf16[1152,512]{1,0:T(8,128)(2,1)} %pad_maximum_fusion.6), channel_id=1, source_target_pairs={{0,96},{16,112},{32,64},{48,80},{64,32},{80,48},{96,0},{112,16},{1... | collective-permute-start | bytes 3538952 | tf_op jit(solution)/shard_map/ppermute | solution.py:889
  448.9 25.4 %collective-permute-start.15 = (bf16[128,384]{1,0:T(8,128)(2,1)S(1)}, bf16[128,384]{1,0:T(8,128)(2,1)S(1)}, u32[]{:S(2)}, u32[]{:S(2)}) collective-permute-start(bf16[128,384]{1,0:T(8,128)(2,1)S(1)} %slice.488), channel_id=1, source_target_pairs={{0,0},{1,16},{2,32},{3,48},{4,64},{5,80},{6,96},{7,112},{8,1},{9,1... | collective-permute-start | bytes 294920 | tf_op jit(solution)/shard_map/ppermute | solution.py:1320
  483.2 14.4 %collective-permute-start.20 = (bf16[4608,512]{1,0:T(8,128)(2,1)}, bf16[4608,512]{1,0:T(8,128)(2,1)}, u32[]{:S(2)}, u32[]{:S(2)}) collective-permute-start(bf16[4608,512]{1,0:T(8,128)(2,1)} %pad_maximum_fusion.own_ref), channel_id=1, source_target_pairs={{0,16},{16,0},{32,48},{48,32},{64,80},{80,64},{96,112},{112,96},{1... | collective-permute-start | bytes 14155784 | tf_op jit(solution)/shard_map/ppermute | solution.py:1329
  (78 other events, 644.8 us)
Sparse Core Ops, SparseCore 0:
  20.5 63.9 all-gather.13
  86.8 28.0 all-gather.7
  117.3 34.6 reduce-scatter.3
  157.0 30.0 all-gather.9
  218.5 53.9 reduce-scatter.5
  278.1 46.7 all-gather.11
  396.6 46.1 reduce-scatter.7
  479.1 36.6 all-gather.15
